TPU v7x, 32 devices: a whole 2x2x4 slice. The times are simulated.
32 devices in a mesh: dp: 8 (over y, x, core), expert: 4 (over z).
Axes of the slice: x: 2, y: 2, z: 4, core: 2. Of those that a mesh axis runs over, the one named last changes fastest.
Arguments:
- tokens: bfloat16 [8192, 1536], P(('dp', 'expert')), may hold values from -6 to 6
- first_gain: float32 [1536], replicated, may hold values from 0.5 to 1.5
- query_weight: bfloat16 [1536, 1536], replicated, may hold values from -2 to 2
- key_weight: bfloat16 [1536, 512], replicated, may hold values from -2 to 2
- value_weight: bfloat16 [1536, 512], replicated, may hold values from -0.15625 to 0.15625
- output_weight: bfloat16 [1536, 1536], replicated, may hold values from -1.5 to 1.5
- second_gain: float32 [1536], replicated, may hold values from 0.5 to 1.5
- router_weight: bfloat16 [1536, 20], replicated, may hold values from -0.078125 to 0.078125
- gate_weight: bfloat16 [20, 1536, 512], P('expert'), may hold values from -0.15625 to 0.15625
- up_weight: bfloat16 [20, 1536, 512], P('expert'), may hold values from -0.15625 to 0.15625
- down_weight: bfloat16 [20, 1536, 512], P('expert'), may hold values from -3 to 3
- cotangent: bfloat16 [8192, 1536], P(('dp', 'expert')), may hold values from -6 to 6
- routes: int32 [8192, 8], P(('dp', 'expert')), may hold values from 0 to 19, all different within a row; in each aligned block of 256 rows (0 to 255, 256 to 511, ...) at most 115 rows name the same one
- segments: int32 [8192], P(('dp', 'expert')), may hold values from 0 to 4, as said below
- threshold: float32 [24], replicated, may hold values from 5 to 10
Outputs:
- block_out: bfloat16 [8192, 1536], P(('dp', 'expert'))
- input_grad: float32 [8192, 1536], P(('dp', 'expert'))
- first_gain_grad: float32 [1536], P(('dp', 'expert'))
- query_grad: float32 [1536, 1536], P(('dp', 'expert'))
- key_grad: float32 [1536, 512], P(('dp', 'expert'))
- value_grad: float32 [1536, 512], P(('dp', 'expert'))
- projection_grad: float32 [1536, 1536], P(('dp', 'expert'))
- second_gain_grad: float32 [1536], P(('dp', 'expert'))
- router_grad: float32 [1536, 20], P(('dp', 'expert'))
- gate_grad: float32 [20, 1536, 512], P('expert', 'dp')
- up_grad: float32 [20, 1536, 512], P('expert', 'dp')
- down_grad: float32 [20, 1536, 512], P('expert', 'dp')
- head_scale: float32 [24], replicated
- query_clipped: bfloat16 [1536, 1536], P(('dp', 'expert'))
- key_clipped: bfloat16 [1536, 512], P(('dp', 'expert'))
Inputs may be any that keep to these rules, and one draw needn't show every extreme that they name: `routes`: among the tokens of one device (aligned blocks of 256 tokens) no expert is named more than 115 times, and some expert reaches 115 in some block; a token's 8 experts differ. `segments`: segment numbers never fall within a sequence of 1024 tokens, are 0 at each sequence's first token, and each sequence holds all of 0 to 4.
All inputs are finite; a program needn't handle non-finite values.
Results may differ from a plain program's by a relative error of at most 0.018.
Values may be sent and summed in bfloat16 or wider, within the bound.
No kernel may reach another device: no remote copies, remote signals or barrier semaphores. Data moves between devices by JAX's collectives and lax.ppermute only.
A program may use at most 320 MiB of HBM per device.

v0:
```python
import jax
import jax.numpy as jnp
from jax import lax
from jax.sharding import PartitionSpec as P

HDIM = 64


ATTENTION_SCALE = 0.015625
RESIDUAL_SCALE = 0.22
NORM_EPSILON = 1e-06
ROTARY_BASE = 10000.0
MASKED_SCORE = -1e30
CONTRACT_ROWS = (((0,), (0,)), ((), ()))
CONTRACT_COLUMNS = (((1,), (1,)), ((), ()))


def rotary_tables(positions, head_dim):
    half_dim = head_dim // 2
    inverse = ROTARY_BASE ** (-2.0 * jnp.arange(half_dim, dtype=jnp.float32) / head_dim)
    angles = positions.astype(jnp.float32)[:, None] * inverse[None, :]
    return (jnp.cos(angles)[:, None, :], jnp.sin(angles)[:, None, :])


def rotate(row_data, cosine, sine_table):
    half_dim = row_data.shape[-1] // 2
    lower_half = row_data[..., :half_dim]
    upper_half = row_data[..., half_dim:]
    return jnp.concatenate(
        [
            lower_half * cosine - upper_half * sine_table,
            upper_half * cosine + lower_half * sine_table,
        ],
        axis=-1,
    )


def rotate_back(grad_in, cosine, sine_table):
    half_dim = grad_in.shape[-1] // 2
    lower_half = grad_in[..., :half_dim]
    upper_half = grad_in[..., half_dim:]
    return jnp.concatenate(
        [
            lower_half * cosine + upper_half * sine_table,
            upper_half * cosine - lower_half * sine_table,
        ],
        axis=-1,
    )


def rms_factor(hidden):
    return lax.rsqrt(jnp.mean(hidden * hidden, axis=-1, keepdims=True) + NORM_EPSILON)


def norm_backward(hidden, factor, gain_vec, grad_in):
    scaled = grad_in * gain_vec
    hidden_grad = factor * scaled - hidden * factor**3 * jnp.mean(
        scaled * hidden, axis=-1, keepdims=True
    )
    return (hidden_grad, jnp.sum(grad_in * hidden * factor, axis=0))


def slot_rows(row_data, source, occupied, expert_total, capacity):
    picked = jnp.where(occupied[:, None], row_data[source], jnp.zeros((), row_data.dtype))
    return picked.reshape(expert_total, capacity, row_data.shape[-1])


def cut_window(gathered, group_count, head_dim, seq_len):
    keys_all, values_all, segments_all = gathered
    key_groups = keys_all.reshape(seq_len, group_count, head_dim).transpose(1, 0, 2)
    value_groups = values_all.reshape(seq_len, group_count, head_dim).transpose(1, 0, 2)
    return (key_groups, value_groups, segments_all)


def expert_front(received, gate_weight, up_weight):
    gate_pre = jnp.einsum("erd,edf->erf", received, gate_weight, preferred_element_type=jnp.float32)
    up_pre = jnp.einsum("erd,edf->erf", received, up_weight, preferred_element_type=jnp.float32)
    expert_hidden = (jax.nn.silu(gate_pre) * up_pre).astype(jnp.bfloat16)
    return (gate_pre, up_pre, expert_hidden)


def local(
    tokens,
    first_gain,
    query_weight,
    key_weight,
    value_weight,
    output_weight,
    second_gain,
    router_weight,
    gate_weight,
    up_weight,
    down_weight,
    cotangent,
    routes,
    segments,
    threshold,
):
    tok_count, model_width = tokens.shape
    head_dim = HDIM
    query_width = query_weight.shape[1]
    kv_width = key_weight.shape[1]
    head_count = query_width // head_dim
    group_count = kv_width // head_dim
    group_ratio = head_count // group_count
    local_experts = gate_weight.shape[0]
    expert_devices = lax.axis_size("expert")
    expert_total = local_experts * expert_devices
    seq_len = tok_count * expert_devices
    top_count = routes.shape[1]
    capacity = tok_count * top_count * 9 // (expert_total * 8)
    route_count = tok_count * top_count
    device_place = lax.axis_index("expert")
    offsets = device_place * tok_count + jnp.arange(tok_count, dtype=jnp.int32)
    positions = offsets % seq_len
    cosine, sine_table = rotary_tables(positions, head_dim)
    hidden_in = tokens.astype(jnp.float32)
    first_factor = rms_factor(hidden_in)
    first_normed = (hidden_in * first_factor * first_gain).astype(jnp.bfloat16)
    query_raw = jnp.dot(first_normed, query_weight, preferred_element_type=jnp.float32)
    queries = rotate(query_raw.reshape(tok_count, head_count, head_dim), cosine, sine_table).astype(
        jnp.bfloat16
    )
    key_raw = jnp.dot(first_normed, key_weight, preferred_element_type=jnp.float32)
    keys_local = (
        rotate(key_raw.reshape(tok_count, group_count, head_dim), cosine, sine_table)
        .astype(jnp.bfloat16)
        .reshape(tok_count, kv_width)
    )
    values_local = jnp.dot(first_normed, value_weight, preferred_element_type=jnp.float32).astype(
        jnp.bfloat16
    )
    segment_values = segments.astype(jnp.bfloat16)
    gathered = (
        lax.all_gather(keys_local, "expert", axis=0, tiled=True),
        lax.all_gather(values_local, "expert", axis=0, tiled=True),
        lax.all_gather(segment_values, "expert", axis=0, tiled=True),
    )
    key_groups, value_groups, segment_window = cut_window(gathered, group_count, head_dim, seq_len)
    key_positions = jnp.arange(seq_len, dtype=jnp.int32)
    allowed = (segment_values[:, None] == segment_window[None, :]) & (
        key_positions[None, :] <= positions[:, None]
    )
    query_groups = queries.reshape(tok_count, group_count, group_ratio, head_dim).transpose(
        1, 0, 2, 3
    )

    def forward_group(group_parts):
        query_part, key_part, value_part = group_parts
        scores = (
            jnp.einsum("trd,sd->rts", query_part, key_part, preferred_element_type=jnp.float32)
            * ATTENTION_SCALE
        )
        scores = jnp.where(allowed[None], scores, MASKED_SCORE)
        row_top = jnp.max(scores, axis=-1, keepdims=True)
        exponent = jnp.exp(scores - row_top)
        row_total = jnp.sum(exponent, axis=-1, keepdims=True)
        weights = (exponent / row_total).astype(jnp.bfloat16)
        mixed_rows = jnp.einsum(
            "rts,sd->trd", weights, value_part, preferred_element_type=jnp.float32
        )
        log_total = row_top[..., 0] + jnp.log(row_total[..., 0])
        return (mixed_rows, log_total, jnp.max(row_top[..., 0], axis=1))

    mixed_groups, log_totals, group_top = lax.map(
        forward_group, (query_groups, key_groups, value_groups)
    )
    attended = (
        mixed_groups.transpose(1, 0, 2, 3).reshape(tok_count, query_width).astype(jnp.bfloat16)
    )
    head_top = lax.pmax(group_top.reshape(head_count), ("dp", "expert"))
    attention_out = lax.dot_general(
        attended, output_weight, CONTRACT_COLUMNS, preferred_element_type=jnp.float32
    )
    hidden_mid = hidden_in + RESIDUAL_SCALE * attention_out
    second_factor = rms_factor(hidden_mid)
    second_normed = (hidden_mid * second_factor * second_gain).astype(jnp.bfloat16)
    router_logits = jnp.dot(second_normed, router_weight, preferred_element_type=jnp.float32)
    expert_ids = jnp.arange(expert_total, dtype=jnp.int32)
    chosen = (routes[:, :, None] == expert_ids[None, None, :]).astype(jnp.float32)
    picked_logits = jnp.sum(chosen * router_logits[:, None, :], axis=-1)
    gate_values = jax.nn.softmax(picked_logits, axis=-1)
    flat_routes = routes.reshape(route_count)
    route_hits = (flat_routes[:, None] == expert_ids[None, :]).astype(jnp.int32)
    route_rank = jnp.sum(jnp.cumsum(route_hits, axis=0) * route_hits, axis=1) - 1
    route_slot = flat_routes * capacity + route_rank
    slot_owner = (
        jnp.full((expert_total * capacity,), -1, dtype=jnp.int32)
        .at[route_slot]
        .set(jnp.arange(route_count, dtype=jnp.int32))
    )
    occupied = slot_owner >= 0
    owner_route = jnp.where(occupied, slot_owner, 0)
    owner_token = owner_route // top_count
    outgoing = slot_rows(second_normed, owner_token, occupied, expert_total, capacity)
    received = lax.all_to_all(outgoing, "expert", split_axis=0, concat_axis=1, tiled=True)
    gate_pre, up_pre, expert_hidden = expert_front(received, gate_weight, up_weight)
    expert_out = jnp.einsum(
        "erf,edf->erd", expert_hidden, down_weight, preferred_element_type=jnp.float32
    ).astype(jnp.bfloat16)
    returned = lax.all_to_all(expert_out, "expert", split_axis=1, concat_axis=0, tiled=True)
    route_out = returned.reshape(expert_total * capacity, model_width)[route_slot].reshape(
        tok_count, top_count, model_width
    )
    mixture = jnp.sum(gate_values[:, :, None] * route_out, axis=1)
    block_out = (hidden_mid + RESIDUAL_SCALE * mixture).astype(jnp.bfloat16)
    out_grad = cotangent.astype(jnp.float32)
    mixture_grad = RESIDUAL_SCALE * out_grad
    gate_back = jnp.sum(route_out * mixture_grad[:, None, :], axis=-1)
    picked_grad = gate_values * (
        gate_back - jnp.sum(gate_values * gate_back, axis=-1, keepdims=True)
    )
    logit_grad = jnp.sum(chosen * picked_grad[:, :, None], axis=1).astype(jnp.bfloat16)
    route_grad = (
        (gate_values[:, :, None] * mixture_grad[:, None, :])
        .astype(jnp.bfloat16)
        .reshape(route_count, model_width)
    )
    outgoing_grad = slot_rows(route_grad, owner_route, occupied, expert_total, capacity)
    received_grad = lax.all_to_all(outgoing_grad, "expert", split_axis=0, concat_axis=1, tiled=True)
    received = lax.all_to_all(
        slot_rows(second_normed, owner_token, occupied, expert_total, capacity),
        "expert",
        split_axis=0,
        concat_axis=1,
        tiled=True,
    )
    gate_pre, up_pre, expert_hidden = expert_front(received, gate_weight, up_weight)
    hidden_grad = jnp.einsum(
        "erd,edf->erf", received_grad, down_weight, preferred_element_type=jnp.float32
    )
    sigmoid_gate = jax.nn.sigmoid(gate_pre)
    activated = gate_pre * sigmoid_gate
    gate_pre_grad = (
        hidden_grad * up_pre * sigmoid_gate * (1.0 + gate_pre * (1.0 - sigmoid_gate))
    ).astype(jnp.bfloat16)
    up_pre_grad = (hidden_grad * activated).astype(jnp.bfloat16)
    down_partial = jnp.einsum(
        "erd,erf->edf", received_grad, expert_hidden, preferred_element_type=jnp.float32
    )
    gate_partial = jnp.einsum(
        "erd,erf->edf", received, gate_pre_grad, preferred_element_type=jnp.float32
    )
    up_partial = jnp.einsum(
        "erd,erf->edf", received, up_pre_grad, preferred_element_type=jnp.float32
    )
    slot_grad = jnp.einsum(
        "erf,edf->erd", gate_pre_grad, gate_weight, preferred_element_type=jnp.float32
    ) + jnp.einsum("erf,edf->erd", up_pre_grad, up_weight, preferred_element_type=jnp.float32)
    returned_grad = lax.all_to_all(
        slot_grad.astype(jnp.bfloat16), "expert", split_axis=1, concat_axis=0, tiled=True
    ).astype(slot_grad.dtype)
    normed_grad = jnp.sum(
        returned_grad.reshape(expert_total * capacity, model_width)[route_slot].reshape(
            tok_count, top_count, model_width
        ),
        axis=1,
    )
    normed_grad = normed_grad + lax.dot_general(
        logit_grad, router_weight, CONTRACT_COLUMNS, preferred_element_type=jnp.float32
    )
    router_partial = lax.dot_general(
        second_normed, logit_grad, CONTRACT_ROWS, preferred_element_type=jnp.float32
    )
    mid_back, second_gain_partial = norm_backward(
        hidden_mid, second_factor, second_gain, normed_grad
    )
    mid_grad = out_grad + mid_back
    branch_grad = (RESIDUAL_SCALE * mid_grad).astype(jnp.bfloat16)
    projection_partial = lax.dot_general(
        branch_grad, attended, CONTRACT_ROWS, preferred_element_type=jnp.float32
    )
    attended_grad = jnp.dot(branch_grad, output_weight, preferred_element_type=jnp.float32).astype(
        jnp.bfloat16
    )
    key_groups, value_groups, segment_window = cut_window(
        (
            lax.all_gather(keys_local, "expert", axis=0, tiled=True),
            lax.all_gather(values_local, "expert", axis=0, tiled=True),
            lax.all_gather(segment_values, "expert", axis=0, tiled=True),
        ),
        group_count,
        head_dim,
        seq_len,
    )
    grad_groups = attended_grad.reshape(tok_count, group_count, group_ratio, head_dim).transpose(
        1, 0, 2, 3
    )

    def backward_group(group_parts):
        query_part, key_part, value_part, grad_part, log_part = group_parts
        scores = (
            jnp.einsum("trd,sd->rts", query_part, key_part, preferred_element_type=jnp.float32)
            * ATTENTION_SCALE
        )
        weights_full = jnp.where(allowed[None], jnp.exp(scores - log_part[..., None]), 0.0)
        weight_grad = jnp.einsum(
            "trd,sd->rts", grad_part, value_part, preferred_element_type=jnp.float32
        )
        row_dot = jnp.sum(weights_full * weight_grad, axis=-1, keepdims=True)
        score_grad = (weights_full * (weight_grad - row_dot)).astype(jnp.bfloat16)
        query_part_grad = (
            jnp.einsum("rts,sd->trd", score_grad, key_part, preferred_element_type=jnp.float32)
            * ATTENTION_SCALE
        )
        key_part_grad = (
            jnp.einsum("rts,trd->sd", score_grad, query_part, preferred_element_type=jnp.float32)
            * ATTENTION_SCALE
        )
        value_part_grad = jnp.einsum(
            "rts,trd->sd",
            weights_full.astype(jnp.bfloat16),
            grad_part,
            preferred_element_type=jnp.float32,
        )
        return (query_part_grad, key_part_grad, value_part_grad)

    query_raw_grad, key_raw_grad, value_raw_grad = lax.map(
        backward_group, (query_groups, key_groups, value_groups, grad_groups, log_totals)
    )
    query_back = (
        rotate_back(
            query_raw_grad.transpose(1, 0, 2, 3).reshape(tok_count, head_count, head_dim),
            cosine,
            sine_table,
        )
        .reshape(tok_count, query_width)
        .astype(jnp.bfloat16)
    )
    key_full = key_raw_grad.transpose(1, 0, 2).reshape(seq_len, kv_width)
    value_full = value_raw_grad.transpose(1, 0, 2).reshape(seq_len, kv_width)
    key_summed, value_summed = (
        lax.psum_scatter(
            key_full.astype(jnp.bfloat16), "expert", scatter_dimension=0, tiled=True
        ).astype(jnp.float32),
        lax.psum_scatter(
            value_full.astype(jnp.bfloat16), "expert", scatter_dimension=0, tiled=True
        ).astype(jnp.float32),
    )
    key_back = (
        rotate_back(key_summed.reshape(tok_count, group_count, head_dim), cosine, sine_table)
        .reshape(tok_count, kv_width)
        .astype(jnp.bfloat16)
    )
    value_back = value_summed.astype(jnp.bfloat16)
    query_partial = lax.dot_general(
        first_normed, query_back, CONTRACT_ROWS, preferred_element_type=jnp.float32
    )
    key_partial = lax.dot_general(
        first_normed, key_back, CONTRACT_ROWS, preferred_element_type=jnp.float32
    )
    value_partial = lax.dot_general(
        first_normed, value_back, CONTRACT_ROWS, preferred_element_type=jnp.float32
    )
    first_grad = lax.dot_general(
        query_back, query_weight, CONTRACT_COLUMNS, preferred_element_type=jnp.float32
    )
    first_grad = first_grad + lax.dot_general(
        key_back, key_weight, CONTRACT_COLUMNS, preferred_element_type=jnp.float32
    )
    first_grad = first_grad + lax.dot_general(
        value_back, value_weight, CONTRACT_COLUMNS, preferred_element_type=jnp.float32
    )
    input_back, first_gain_partial = norm_backward(hidden_in, first_factor, first_gain, first_grad)
    input_grad = mid_grad + input_back
    dense_sums = (
        lax.psum_scatter(query_partial, ("dp", "expert"), scatter_dimension=0, tiled=True),
        lax.psum_scatter(key_partial, ("dp", "expert"), scatter_dimension=0, tiled=True),
        lax.psum_scatter(value_partial, ("dp", "expert"), scatter_dimension=0, tiled=True),
        lax.psum_scatter(projection_partial, ("dp", "expert"), scatter_dimension=0, tiled=True),
        lax.psum_scatter(router_partial, ("dp", "expert"), scatter_dimension=0, tiled=True),
        lax.psum_scatter(first_gain_partial, ("dp", "expert"), scatter_dimension=0, tiled=True),
        lax.psum_scatter(second_gain_partial, ("dp", "expert"), scatter_dimension=0, tiled=True),
    )
    expert_sums = (
        lax.psum_scatter(
            gate_partial.astype(jnp.bfloat16), "dp", scatter_dimension=1, tiled=True
        ).astype(jnp.float32),
        lax.psum_scatter(
            up_partial.astype(jnp.bfloat16), "dp", scatter_dimension=1, tiled=True
        ).astype(jnp.float32),
        lax.psum_scatter(
            down_partial.astype(jnp.bfloat16), "dp", scatter_dimension=1, tiled=True
        ).astype(jnp.float32),
    )
    head_scale = threshold / jnp.maximum(head_top, threshold)
    group_scale = jnp.min(head_scale.reshape(group_count, group_ratio), axis=1)
    device_count = lax.axis_size(("dp", "expert"))
    row_count = model_width // device_count
    row_start = lax.axis_index(("dp", "expert")) * row_count
    query_rows = lax.dynamic_slice_in_dim(query_weight, row_start, row_count, 0).astype(jnp.float32)
    key_rows = lax.dynamic_slice_in_dim(key_weight, row_start, row_count, 0).astype(jnp.float32)
    query_clipped = (query_rows * jnp.repeat(jnp.sqrt(head_scale), head_dim)[None, :]).astype(
        jnp.bfloat16
    )
    key_clipped = (key_rows * jnp.repeat(jnp.sqrt(group_scale), head_dim)[None, :]).astype(
        jnp.bfloat16
    )
    return (
        block_out,
        input_grad,
        dense_sums[5],
        dense_sums[0],
        dense_sums[1],
        dense_sums[2],
        dense_sums[3],
        dense_sums[6],
        dense_sums[4],
        expert_sums[0],
        expert_sums[1],
        expert_sums[2],
        head_scale,
        query_clipped,
        key_clipped,
    )


def solution(mesh):
    placed = (
        P(("dp", "expert"), None),
        P(),
        P(),
        P(),
        P(),
        P(),
        P(),
        P(),
        P("expert", None, None),
        P("expert", None, None),
        P("expert", None, None),
        P(("dp", "expert"), None),
        P(("dp", "expert"), None),
        P(("dp", "expert")),
        P(),
    )
    return jax.shard_map(
        local,
        mesh=mesh,
        in_specs=placed,
        out_specs=(
            P(("dp", "expert"), None),
            P(("dp", "expert"), None),
            P(("dp", "expert")),
            P(("dp", "expert"), None),
            P(("dp", "expert"), None),
            P(("dp", "expert"), None),
            P(("dp", "expert"), None),
            P(("dp", "expert")),
            P(("dp", "expert"), None),
            P("expert", "dp", None),
            P("expert", "dp", None),
            P("expert", "dp", None),
            P(),
            P(("dp", "expert"), None),
            P(("dp", "expert"), None),
        ),
        check_vma=False,
    )
```

profile of v0, /device:TPU:24, one launch (start us, length us, event | category | flops | bytes accessed | tf_op | source)
XLA Modules:
  0.0 2144.7 jit_solution(8307564205942316128)
XLA Ops:
  15.9 5.7 reduce-window.6
  22.4 8.1 scatter_custom_fusion
  30.6 7.4 all-gather
  39.1 4.3 fusion.96
  48.4 21.6 %all-gather.6.cloned.1.call-done = bf16[1024,512]{0,1:T(8,128)(2,1)} async-done(((bf16[256,512]{0,1:T(8,128)(2,1)}), bf16[1024,512]{0,1:T(8,128)(2,1)}) %all-gather.6.cloned.1.call-update) | async-done | bytes 1048592 | tf_op jit(solution)/shard_map/all_gather | solution.py:135
  70.0 59.8 %while.32 = (s32[]{:T(128)}, bf16[8,256,3,64]{1,3,2,0:T(8,128)(2,1)}, f32[8,3,256]{2,1,0:T(4,128)}, f32[8,3]{1,0:T(8,128)}, bf16[8,1024,64]{1,2,0:T(8,128)(2,1)}...) while((s32[]{:T(128)}, ...), condition=%wide.region_5.6_spmd.clone.clone, body=%wide.region_1.5_spmd.clone.sunk.clone | while | flops 212860160 | bytes 11074201 | solution.py:165
  129.8 4.5 multiply_reduce_fusion.2
  137.5 5.0 fusion.63
  142.5 18.5 gather_fusion.2
  161.0 6.6 gather.21
  167.6 8.7 gather_fusion
  176.3 6.6 gather.18
  182.9 8.8 broadcast_select_fusion
  191.7 165.0 %all_to_all.65 = bf16[20,115,1536]{2,1,0:T(8,128)(2,1)} all-to-all(bf16[20,115,1536]{2,1,0:T(8,128)(2,1)S(1)} %get-tuple-element.248), channel_id=1, replica_groups=mesh['dp'=8,'expert'=4] {'expert'}, dimensions={0} | all-to-all | bytes 14131200 | tf_op jit(solution)/shard_map/all_to_all | solution.py:220
  356.7 7.8 all-to-all-start
  364.5 6.8 copy.154
  371.3 8.4 all_to_all.59
  379.7 142.7 %all-to-all-done = bf16[20,115,1536]{2,1,0:T(8,128)(2,1)} async-done(((bf16[20,115,1536]{2,1,0:T(8,128)(2,1)}), bf16[20,115,1536]{2,1,0:T(8,128)(2,1)}, u32[]{:S(2)}, u32[]{:S(2)}) %all-to-all-start) | async-done | bytes 7065632 | tf_op jit(solution)/shard_map/all_to_all | solution.py:196
  522.4 6.9 copy.149
  529.3 8.5 all_to_all.52
  537.8 11.4 fusion.104
  549.3 8.8 fusion.103
  558.1 11.2 multiply_convert_fusion
  570.7 9.5 convolution_convert_fusion.3
  580.2 11.6 copy.150
  591.9 8.6 all-to-all-start.1
  600.4 13.1 fusion.105
  613.5 11.6 add_convert_fusion
  625.1 11.8 copy.155
  636.9 206.3 %all-to-all-done.1 = bf16[5,460,1536]{2,0,1:T(8,128)(2,1)} async-done(((bf16[5,460,1536]{2,0,1:T(8,128)(2,1)}), bf16[5,460,1536]{2,0,1:T(8,128)(2,1)}, u32[]{:S(2)}, u32[]{:S(2)}) %all-to-all-start.1) | async-done | bytes 7065632 | tf_op jit(solution)/shard_map/all_to_all | solution.py:201
  843.2 8.5 all-to-all-start.3
  851.7 10.0 copy.152
  861.7 6.9 reshape.411
  868.6 17.3 gather_fusion.1
  886.0 9.5 fusion.62
  895.6 198.8 %all-to-all-done.3 = bf16[5,460,1536]{2,0,1:T(8,128)(2,1)} async-done(((bf16[5,460,1536]{2,0,1:T(8,128)(2,1)}), bf16[5,460,1536]{2,0,1:T(8,128)(2,1)}, u32[]{:S(2)}, u32[]{:S(2)}) %all-to-all-start.3) | async-done | bytes 7065632 | tf_op jit(solution)/shard_map/all_to_all | solution.py:250
  1094.4 12.0 copy_convert_fusion
  1106.4 12.4 reshape.423
  1118.9 12.2 copy.157
  1131.0 15.5 reshape.420
  1146.6 19.6 gather_fusion.3
  1166.2 7.9 bitcast_reduce_fusion
  1178.4 3.7 convolution_convert_fusion.4
  1182.4 82.4 %while.33 = (s32[]{:T(128)}, f32[8,256,3,64]{1,3,2,0:T(8,128)}, bf16[8,1024,64]{1,2,0:T(8,128)(2,1)}, bf16[8,1024,64]{1,2,0:T(8,128)(2,1)}, bf16[8,1024,64]{1,2,...) while((s32[]{:T(128)}, f32[8,256,3,64]{1,3,2,0:T(8,128)}, ...), condition=%wide.region_22.23_spmd.clone.clone, body=%wide.region_20.22_spmd.clone.sunk.clone | while | flops 511819008 | bytes 25648768 | solution.py:318
  1267.0 11.3 convolution_convert_fusion
  1278.4 11.2 convolution_convert_fusion.2
  1289.9 11.2 convolution_convert_fusion.1
  1302.3 3.3 fusion.90
  1305.6 14.4 reduce-scatter.13.cloned.1.call-done
  1323.7 6.5 fusion.74
  1332.0 5.2 fusion.94
  1337.9 40.4 %pmax.7 = f32[24]{0:T(128)S(1)} all-reduce(f32[24]{0:T(128)S(1)} %reshape.417), channel_id=1, replica_groups=mesh['dp'=8,'expert'=4] {'dp','expert'}, use_global_device_ids=true, to_apply=%region_38.39 | all-reduce | flops 24 | bytes 192 | tf_op jit(solution)/shard_map/pmax | solution.py:171
  1381.9 5.0 fusion.106
  1386.8 34.3 %reduce-scatter.31.cloned.1.call-done = f32[48,20]{1,0:T(8,128)} async-done(((f32[1536,20]{1,0:T(8,128)}), f32[48,20]{1,0:T(8,128)}) %reduce-scatter.31.cloned.1.call-update) | async-done | bytes 3856
  1422.6 71.3 %reduce-scatter.29.cloned.1.call-done = bf16[5,192,512]{2,1,0:T(8,128)(2,1)} async-done(((bf16[5,1536,512]{2,1,0:T(8,128)(2,1)}), bf16[5,192,512]{2,1,0:T(8,128)(2,1)}) %reduce-scatter.29.cloned.1.call-update) | async-done | bytes 983056 | tf_op jit(solution)/shard_map/reduce_scatter | solution.py:382
  1496.6 70.5 %reduce-scatter.25.cloned.1.call-done = bf16[5,192,512]{2,1,0:T(8,128)(2,1)} async-done(((bf16[5,1536,512]{2,1,0:T(8,128)(2,1)}), bf16[5,192,512]{2,1,0:T(8,128)(2,1)}) %reduce-scatter.25.cloned.1.call-update) | async-done | bytes 983056 | tf_op jit(solution)/shard_map/reduce_scatter | solution.py:376
  1569.9 70.1 %reduce-scatter.27.cloned.1.call-done = bf16[5,192,512]{2,1,0:T(8,128)(2,1)} async-done(((bf16[5,1536,512]{2,1,0:T(8,128)(2,1)}), bf16[5,192,512]{2,1,0:T(8,128)(2,1)}) %reduce-scatter.27.cloned.1.call-update) | async-done | bytes 983056 | tf_op jit(solution)/shard_map/reduce_scatter | solution.py:379
  1640.0 2.9 convert_element_type.210
  1647.0 38.4 %all-reduce.2 = (f32[1536]{0:T(1024)S(1)}, f32[1536]{0:T(1024)S(1)}) all-reduce(f32[1536]{0:T(1024)S(1)} %get-tuple-element.179, f32[1536]{0:T(1024)S(1)} %get-tuple-element.177), channel_id=4, replica_groups=mesh['dp'=8,'expert'=4] {'dp','expert'}, use_global_device_ids=true, to_apply=%region_27.28.clone | all-reduce | flops 3072 | bytes 24576
  1686.6 3.5 fusion.70
  1690.1 57.4 %reduce-scatter.21.cloned.1.call-done = f32[48,512]{1,0:T(8,128)} async-done(((f32[1536,512]{1,0:T(8,128)}), f32[48,512]{1,0:T(8,128)}) %reduce-scatter.21.cloned.1.call-update) | async-done | bytes 98320 | tf_op jit(solution)/shard_map/reduce_scatter | solution.py:369
  1747.4 107.3 %reduce-scatter.19.cloned.1.call-done = f32[48,512]{1,0:T(8,128)} async-done(((f32[1536,512]{1,0:T(8,128)}), f32[48,512]{1,0:T(8,128)}) %reduce-scatter.19.cloned.1.call-update) | async-done | bytes 98320 | tf_op jit(solution)/shard_map/reduce_scatter | solution.py:368
  1854.7 142.0 %reduce-scatter.23.cloned.1.call-done = f32[48,1536]{1,0:T(8,128)} async-done(((f32[1536,1536]{1,0:T(8,128)}), f32[48,1536]{1,0:T(8,128)}) %reduce-scatter.23.cloned.1.call-update) | async-done | bytes 294928 | tf_op jit(solution)/shard_map/reduce_scatter | solution.py:370
  1996.7 140.9 %reduce-scatter.17.cloned.1.call-done = f32[48,1536]{1,0:T(8,128)} async-done(((f32[1536,1536]{1,0:T(8,128)}), f32[48,1536]{1,0:T(8,128)}) %reduce-scatter.17.cloned.1.call-update) | async-done | bytes 294928 | tf_op jit(solution)/shard_map/reduce_scatter | solution.py:367
  (346 shorter events, 191.9 us)
Async XLA Ops:
  7.2 2.2 copy-start
  7.2 5.0 copy-start.3
  7.2 5.0 copy-start.30
  7.2 38.8 %all-gather.4.cloned.1.call-start = ((), (), s32[]{:S(2)}) async-start(), calls=%async_computation.14 | async-start | bytes 1310720 | tf_op jit(solution)/shard_map/all_gather | solution.py:136
  9.4 29.8 %copy-start.40 = (f32[256]{0:T(256)}, f32[256]{0:T(256)S(1)}, u32[]{:S(2)}) copy-start(f32[256]{0:T(256)S(1)} %get-tuple-element.253) | copy-start | bytes 3076
  11.8 3.4 copy-start.32
  11.9 58.1 %all-gather.6.cloned.1.call-start = ((), (), s32[]{:S(2)}) async-start(), calls=%async_computation.15 | async-start | bytes 1310720 | tf_op jit(solution)/shard_map/all_gather | solution.py:135
  12.2 31.3 %copy-start.20 = (f32[256,32]{0,1:T(8,128)}, f32[256,32]{0,1:T(8,128)S(1)}, u32[]{:S(2)}) copy-start(f32[256,32]{0,1:T(8,128)S(1)} %get-tuple-element.250) | copy-start | bytes 98308
  12.2 31.3 %copy-start.22 = (f32[256,32]{0,1:T(8,128)}, f32[256,32]{0,1:T(8,128)S(1)}, u32[]{:S(2)}) copy-start(f32[256,32]{0,1:T(8,128)S(1)} %get-tuple-element.251) | copy-start | bytes 98308
  14.4 16.1 copy-start.55
  22.4 21.1 copy-start.42
  129.8 4.5 copy-start.12
  129.8 4.5 copy-start.28
  129.8 4.5 copy-start.34
  129.8 4.5 copy-start.38
  129.8 5.7 copy-start.36
  129.8 5.9 copy-start.26
  134.9 7.5 copy-start.48
  135.6 31.9 %copy-start.1 = (bf16[256,1536]{1,0:T(8,128)(2,1)}, bf16[256,1536]{1,0:T(8,128)(2,1)S(1)}, u32[]{:S(2)}) copy-start(bf16[256,1536]{1,0:T(8,128)(2,1)S(1)} %multiply_convert_fusion.4) | copy-start | bytes 2359300
  137.4 5.1 copy-start.17
  356.7 165.7 %all-to-all-start = ((bf16[20,115,1536]{2,1,0:T(8,128)(2,1)}), bf16[20,115,1536]{2,1,0:T(8,128)(2,1)}, u32[]{:S(2)}, u32[]{:S(2)}) async-start(bf16[20,115,1536]{2,1,0:T(8,128)(2,1)} %get-tuple-element.249), calls=%async_computation | async-start | bytes 14745600 | tf_op jit(solution)/shard_map/all_to_all | solution.py:196
  537.8 11.4 copy-start.9
  537.8 20.3 slice-start
  549.2 8.9 slice-start.1
  569.3 1.4 copy-start.56
  591.9 251.3 %all-to-all-start.1 = ((bf16[5,460,1536]{2,0,1:T(8,128)(2,1)}), bf16[5,460,1536]{2,0,1:T(8,128)(2,1)}, u32[]{:S(2)}, u32[]{:S(2)}) async-start(bf16[5,460,1536]{2,0,1:T(8,128)(2,1)} %copy.150), calls=%async_computation.1 | async-start | bytes 22609920 | tf_op jit(solution)/shard_map/all_to_all | solution.py:201
  600.4 13.1 copy-start.11
  636.9 214.8 %copy-start.43 = (s32[2048,1]{0,1:T(1,128)S(1)}, s32[2048,1]{0,1:T(1,128)}, u32[]{:S(2)}) copy-start(s32[2048,1]{0,1:T(1,128)} %copy-done.42) | copy-start | bytes 24580
  843.2 251.2 %all-to-all-start.3 = ((bf16[5,460,1536]{2,0,1:T(8,128)(2,1)}), bf16[5,460,1536]{2,0,1:T(8,128)(2,1)}, u32[]{:S(2)}, u32[]{:S(2)}) async-start(bf16[5,460,1536]{2,0,1:T(8,128)(2,1)} %copy.155), calls=%async_computation.3 | async-start | bytes 22609920 | tf_op jit(solution)/shard_map/all_to_all | solution.py:250
  851.7 449.6 %reduce-scatter.15.cloned.1.call-start = ((), (), s32[]{:S(2)}) async-start(), calls=%async_computation.17 | async-start | bytes 1310720 | tf_op jit(solution)/shard_map/reduce_scatter | solution.py:336
  868.6 17.3 copy-start.6
  868.6 17.3 copy-start.18
  885.9 9.6 copy-start.25
  885.9 9.6 copy-start.45
  885.9 9.6 copy-start.47
  886.0 9.6 copy-start.33
  1166.2 7.9 copy-start.8
  1166.2 7.9 copy-start.27
  1166.2 7.9 copy-start.37
  1166.2 7.9 copy-start.49
  1174.1 1.4 copy-start.10
  1174.1 1.6 copy-start.15
  1174.2 1.6 copy-start.52
  1178.4 4.0 copy-start.29
  1178.4 4.0 copy-start.35
  1178.4 4.0 copy-start.39
  1182.4 83.1 %copy-start.2 = (bf16[256,1536]{1,0:T(8,128)(2,1)S(1)}, bf16[256,1536]{1,0:T(8,128)(2,1)}, u32[]{:S(2)}) copy-start(bf16[256,1536]{1,0:T(8,128)(2,1)} %copy-done.1) | copy-start | bytes 2359300
  1264.8 55.2 %reduce-scatter.13.cloned.1.call-start = ((), (), s32[]{:S(2)}) async-start(), calls=%async_computation.16 | async-start | bytes 1310720 | tf_op jit(solution)/shard_map/reduce_scatter | solution.py:333
  1265.4 155.7 %reduce-scatter.31.cloned.1.call-start = ((), (), s32[]{:S(2)}) async-start(), calls=%async_computation.25 | async-start | bytes 811008
  1266.8 227.1 %reduce-scatter.29.cloned.1.call-start = ((), (), s32[]{:S(2)}) async-start(), calls=%async_computation.24 | async-start | bytes 8847360 | tf_op jit(solution)/shard_map/reduce_scatter | solution.py:382
  1278.3 288.8 %reduce-scatter.25.cloned.1.call-start = ((), (), s32[]{:S(2)}) async-start(), calls=%async_computation.22 | async-start | bytes 8847360 | tf_op jit(solution)/shard_map/reduce_scatter | solution.py:376
  1289.6 350.4 %reduce-scatter.27.cloned.1.call-start = ((), (), s32[]{:S(2)}) async-start(), calls=%async_computation.23 | async-start | bytes 8847360 | tf_op jit(solution)/shard_map/reduce_scatter | solution.py:379
  1301.1 19.9 copy-start.21
  1301.1 19.9 copy-start.23
  1301.1 446.3 %reduce-scatter.21.cloned.1.call-start = ((), (), s32[]{:S(2)}) async-start(), calls=%async_computation.20 | async-start | bytes 3244032 | tf_op jit(solution)/shard_map/reduce_scatter | solution.py:369
  1305.6 549.1 %reduce-scatter.19.cloned.1.call-start = ((), (), s32[]{:S(2)}) async-start(), calls=%async_computation.19 | async-start | bytes 3244032 | tf_op jit(solution)/shard_map/reduce_scatter | solution.py:368
  1321.2 2.5 copy-start.13
  1323.6 673.1 %reduce-scatter.23.cloned.1.call-start = ((), (), s32[]{:S(2)}) async-start(), calls=%async_computation.21 | async-start | bytes 9732096 | tf_op jit(solution)/shard_map/reduce_scatter | solution.py:370
  1330.2 807.4 %reduce-scatter.17.cloned.1.call-start = ((), (), s32[]{:S(2)}) async-start(), calls=%async_computation.18 | async-start | bytes 9732096 | tf_op jit(solution)/shard_map/reduce_scatter | solution.py:367
  1337.2 41.1 %copy-start.54 = (f32[24]{0:T(128)S(1)}, f32[24]{0:T(128)}, u32[]{:S(2)}) copy-start(f32[24]{0:T(128)} %param.33) | copy-start | bytes 292
  1378.3 8.5 copy-start.53
  1640.0 2.9 copy-start.16
  1642.9 2.1 copy-start.19
  1645.0 41.6 %copy-start.51 = (f32[256]{0:T(256)S(1)}, f32[256]{0:T(256)}, u32[]{:S(2)}) copy-start(f32[256]{0:T(256)} %get-tuple-element.252) | copy-start | bytes 3076
  (10 other events, 9.4 us)
Sparse Core Ops, SparseCore 0:
  12.0 27.5 all-gather.3
  41.7 28.1 all-gather.5
  1265.0 26.9 reduce-scatter.14
  1294.2 25.7 reduce-scatter.12
  1325.6 95.5 reduce-scatter.30
  1424.5 69.4 reduce-scatter.28
  1497.7 69.3 reduce-scatter.24
  1570.6 69.3 reduce-scatter.26
  1646.9 100.4 reduce-scatter.20
  1754.2 100.4 reduce-scatter.18
  1862.2 134.4 reduce-scatter.22
  2003.0 134.5 reduce-scatter.16
where the time goes:
time: 2160 us; the launch traced here: 2140 us
  waiting for transfers between devices  1280 us (59%)
  blocking collectives  251 us (12%)
  matrix products  250 us (12%)
  local copies, waits for them, and re-layouts  227 us (11%)
  other arithmetic  96.8 us (4%)
  starting transfers between devices  25.7 us (1%)
    all_to_all x1, waiting for transfers between devices, local(): lax.all_to_all(expert_out, 'expert', split_axis=1, concat_axis=0, tiled=T...  206 us
    all_to_all x1, waiting for transfers between devices, local(): lax.all_to_all(slot_grad.astype(jnp.bfloat16), 'expert', split_axis=1, co...  199 us
    all_to_all x1, blocking collectives, local(): lax.all_to_all(outgoing_grad, 'expert', split_axis=0, concat_axis=1, tile...  165 us
    all_to_all x1, waiting for transfers between devices, local(): lax.all_to_all(outgoing, 'expert', split_axis=0, concat_axis=1, tiled=True)  143 us
    reduce_scatter x1, waiting for transfers between devices, local(): lax.psum_scatter(projection_partial, ('dp', 'expert'), scatter_dimension=...  142 us
    reduce_scatter x1, waiting for transfers between devices, local(): lax.psum_scatter(query_partial, ('dp', 'expert'), scatter_dimension=0, ti...  141 us
    reduce_scatter x1, waiting for transfers between devices, local(): lax.psum_scatter(key_partial, ('dp', 'expert'), scatter_dimension=0, tile...  107 us
    reduce_scatter x1, waiting for transfers between devices, local(): lax.psum_scatter(down_partial.astype(jnp.bfloat16), 'dp', scatter_dimensi...  71.3 us
  transfers between devices with their start and end apart: 15, of which 13 were waited for; matrix products, arithmetic and copies ran while one was open for 9% of the time, Pallas kernels for 0%

commit v1 on v0

v1 whole, which is shorter than its diff:
```python
import functools

import jax
import jax.numpy as jnp
import numpy as np
from jax import lax
from jax.experimental import pallas as pl
from jax.experimental.pallas import tpu as pltpu
from jax.sharding import PartitionSpec as P

HDIM = 64
LANES = 128
ATTENTION_SCALE = 0.015625
RESIDUAL_SCALE = 0.22
NORM_EPSILON = 1e-06
ROTARY_BASE = 10000.0
MASKED_SCORE = -1e30
BF16 = jnp.bfloat16
F32 = jnp.float32
NN = (((1,), (0,)), ((), ()))
NT = (((1,), (1,)), ((), ()))
TN = (((0,), (0,)), ((), ()))
VMEM_LIMIT = 56 * 1024 * 1024


def dot(left, right, dims=NN):
    return lax.dot_general(left, right, dims, preferred_element_type=F32)


def round_up(count, unit):
    return (count + unit - 1) // unit * unit


def low_lanes(rows):
    return lax.broadcasted_iota(jnp.int32, (rows, LANES), 1) < HDIM


def partner_lanes(slab):
    lane = lax.broadcasted_iota(jnp.int32, slab.shape, 1) % HDIM
    half = HDIM // 2
    return jnp.where(lane < half, pltpu.roll(slab, LANES - half, 1), pltpu.roll(slab, half, 1))


def vmem():
    return pl.BlockSpec(memory_space=pltpu.VMEM)


def params(**more):
    return pltpu.CompilerParams(vmem_limit_bytes=VMEM_LIMIT, **more)


def info_kernel(expert_pad, routes_ref, segments_ref, info_ref):
    rows, top_count = routes_ref.shape
    lane = lax.broadcasted_iota(jnp.int32, (rows, LANES), 1)
    chosen = jnp.zeros((rows, LANES), F32)
    for k in range(top_count):
        chosen = chosen + jnp.where(routes_ref[:, k : k + 1] == lane, 1.0, 0.0)
    chosen = chosen.astype(BF16)
    first = lax.broadcasted_iota(jnp.int32, (rows, rows), 0)
    second = lax.broadcasted_iota(jnp.int32, (rows, rows), 1)
    earlier = jnp.where(first < second, 1.0, 0.0).astype(BF16)
    same = jnp.where(first == second, 1.0, 0.0).astype(BF16)
    rank = dot(chosen, earlier, TN)
    named = dot(chosen, same, TN)
    table = jnp.where(named > 0.5, rank, -1.0).astype(jnp.int32)
    info_ref[:expert_pad, :] = table[:expert_pad]
    info_ref[expert_pad:, :] = jnp.broadcast_to(segments_ref[...], (8, rows))


def front_kernel(tokens_ref, gain_ref, key_ref, value_ref, cos_ref, sin_ref, normed_ref, factor_ref, kv_ref):
    hidden = tokens_ref[...].astype(F32)
    factor = lax.rsqrt(jnp.mean(hidden * hidden, axis=-1, keepdims=True) + NORM_EPSILON)
    normed = (hidden * factor * gain_ref[...]).astype(BF16)
    normed_ref[...] = normed
    factor_ref[...] = factor
    keys = dot(normed, key_ref[...])
    values = dot(normed, value_ref[...])
    cosine, sine = cos_ref[...], sin_ref[...]
    low = low_lanes(hidden.shape[0])
    for i in range(keys.shape[1] // LANES):
        slab = keys[:, i * LANES : (i + 1) * LANES]
        slab = slab * cosine + partner_lanes(slab) * sine
        value_slab = values[:, i * LANES : (i + 1) * LANES]
        kv_ref[2 * i] = jnp.where(low, slab, pltpu.roll(value_slab, HDIM, 1)).astype(BF16)
        kv_ref[2 * i + 1] = jnp.where(low, pltpu.roll(slab, HDIM, 1), value_slab).astype(BF16)


def query_kernel(normed_ref, query_ref, cos_ref, sin_ref, out_ref):
    raw = dot(normed_ref[...], query_ref[...])
    cosine, sine = cos_ref[...], sin_ref[...]
    for i in range(raw.shape[1] // LANES):
        slab = raw[:, i * LANES : (i + 1) * LANES]
        slab = slab * cosine + partner_lanes(slab) * sine
        out_ref[:, i * LANES : (i + 1) * LANES] = (slab.astype(BF16).astype(F32) * ATTENTION_SCALE).astype(BF16)


def fill_bias(bias_ref, seg_column, seg_rows):
    slots, rows, keys = bias_ref.shape
    for k in range(slots):
        allowed = seg_column == seg_rows[k : k + 1, :]
        if k == 0:
            allowed = allowed & (
                lax.broadcasted_iota(jnp.int32, (rows, keys), 1)
                <= lax.broadcasted_iota(jnp.int32, (rows, keys), 0)
            )
        bias_ref[k] = jnp.where(allowed, 0.0, MASKED_SCORE)


def head_slab(block, head, upper):
    slab = block[:, (head // 2) * LANES : (head // 2 + 1) * LANES].astype(F32)
    low = low_lanes(slab.shape[0])
    if (head % 2 == 1) != upper:
        slab = pltpu.roll(slab, HDIM, 1)
    return jnp.where(low != upper, slab, 0.0)


def attend_kernel(slots, ratio, need_ref, query_ref, seg_column_ref, seg_rows_ref, *refs):
    kv_refs = refs[:slots]
    attended_ref, lse_ref, top_ref, bias_ref, stacked_ref, acc_ref, max_ref, sum_ref = refs[slots:]
    rows = query_ref.shape[0]
    low = low_lanes(rows)
    lane = lax.broadcasted_iota(jnp.int32, (rows, LANES), 1)
    need = need_ref[0]

    @pl.when(pl.program_id(0) == 0)
    def _():
        fill_bias(bias_ref, seg_column_ref[...], seg_rows_ref[...])

    outs = []
    lse_all = jnp.zeros((rows, LANES), F32)
    top_all = jnp.zeros((8, LANES), F32)
    for group in range(2):
        for r in range(ratio):
            stacked_ref[r * rows : (r + 1) * rows, :] = head_slab(
                query_ref, group * ratio + r, False
            ).astype(BF16)
        for k in range(slots):

            def step(k=k):
                kv = kv_refs[k][group]
                scores = dot(stacked_ref[...], kv, NT).reshape(ratio, rows, rows)
                scores = (scores + bias_ref[k][None]).reshape(ratio * rows, rows)
                top = jnp.max(scores, axis=-1, keepdims=True)
                if k == 0:
                    weights = jnp.exp(scores - top)
                    max_ref[...] = top
                    sum_ref[...] = jnp.sum(weights, axis=-1, keepdims=True)
                    acc_ref[...] = dot(weights.astype(BF16), kv)
                else:
                    before = max_ref[...]
                    top = jnp.maximum(top, before)
                    shrink = jnp.exp(before - top)
                    weights = jnp.exp(scores - top)
                    max_ref[...] = top
                    sum_ref[...] = sum_ref[...] * shrink + jnp.sum(weights, axis=-1, keepdims=True)
                    acc_ref[...] = acc_ref[...] * shrink + dot(weights.astype(BF16), kv)

            if k == 0:
                step()
            else:
                pl.when(k < need)(step)
        total = sum_ref[...]
        mixed = acc_ref[...] / total
        lse = max_ref[...] + jnp.log(total)
        for r in range(ratio):
            head = group * ratio + r
            outs.append(mixed[r * rows : (r + 1) * rows])
            lse_all = jnp.where(lane == head, lse[r * rows : (r + 1) * rows], lse_all)
            peak = jnp.max(max_ref[r * rows : (r + 1) * rows, :], axis=0, keepdims=True)
            top_all = jnp.where(lane[:8] == head, peak, top_all)
    for i in range(len(outs) // 2):
        attended_ref[:, i * LANES : (i + 1) * LANES] = jnp.where(
            low, pltpu.roll(outs[2 * i], HDIM, 1), outs[2 * i + 1]
        ).astype(BF16)
    lse_ref[0] = lse_all
    top_ref[0] = top_all


def attend(queries, kv_slots, seg_column, seg_rows, need, ratio):
    slots = len(kv_slots)
    rows, width = queries.shape
    groups = kv_slots[0].shape[0]
    steps = groups // 2
    block = 2 * ratio * HDIM
    return pl.pallas_call(
        functools.partial(attend_kernel, slots, ratio),
        out_shape=(
            jax.ShapeDtypeStruct((rows, width), BF16),
            jax.ShapeDtypeStruct((steps, rows, LANES), F32),
            jax.ShapeDtypeStruct((steps, 8, LANES), F32),
        ),
        grid=(steps,),
        in_specs=[
            pl.BlockSpec(memory_space=pltpu.SMEM),
            pl.BlockSpec((rows, block), lambda s: (0, s)),
            pl.BlockSpec((rows, 1), lambda s: (0, 0)),
            pl.BlockSpec(seg_rows.shape, lambda s: (0, 0)),
        ]
        + [pl.BlockSpec((2, rows, LANES), lambda s: (s, 0, 0))] * slots,
        out_specs=(
            pl.BlockSpec((rows, block), lambda s: (0, s)),
            pl.BlockSpec((1, rows, LANES), lambda s: (s, 0, 0)),
            pl.BlockSpec((1, 8, LANES), lambda s: (s, 0, 0)),
        ),
        scratch_shapes=[
            pltpu.VMEM((slots, rows, rows), F32),
            pltpu.VMEM((ratio * rows, LANES), BF16),
            pltpu.VMEM((ratio * rows, LANES), F32),
            pltpu.VMEM((ratio * rows, 1), F32),
            pltpu.VMEM((ratio * rows, 1), F32),
        ],
        compiler_params=params(),
        name="attend",
    )(need, queries, seg_column, seg_rows, *kv_slots)


def attend_back_kernel(slots, ratio, need_ref, query_ref, attended_ref, grad_ref, lse_ref, cos_ref, sin_ref, seg_column_ref, seg_rows_ref, *refs):
    kv_refs = refs[:slots]
    back_ref = refs[slots]
    dkv_refs = refs[slots + 1 : 2 * slots + 1]
    bias_ref, query_s, grad_s, acc_ref, lse_s, delta_s = refs[2 * slots + 1 :]
    rows = query_ref.shape[0]
    low = low_lanes(rows)
    need = need_ref[0]

    @pl.when(pl.program_id(0) == 0)
    def _():
        fill_bias(bias_ref, seg_column_ref[...], seg_rows_ref[...])

    outs = []
    for group in range(2):
        for r in range(ratio):
            head = group * ratio + r
            part = slice(r * rows, (r + 1) * rows)
            query_s[part, :] = head_slab(query_ref, head, False).astype(BF16)
            grad = head_slab(grad_ref, head, True)
            grad_s[part, :] = grad.astype(BF16)
            delta_s[part, :] = jnp.sum(grad * head_slab(attended_ref, head, True), axis=-1, keepdims=True)
            lse_s[part, :] = lse_ref[0, :, head : head + 1]
        for k in range(slots):

            def step(k=k):
                kv = kv_refs[k][group]
                scores = dot(query_s[...], kv, NT).reshape(ratio, rows, rows)
                scores = (scores + bias_ref[k][None]).reshape(ratio * rows, rows)
                weights = jnp.exp(scores - lse_s[...])
                weight_grad = dot(grad_s[...], kv, NT)
                score_grad = (weights * (weight_grad - delta_s[...])).astype(BF16)
                query_part = dot(score_grad, kv)
                if k == 0:
                    acc_ref[...] = query_part
                else:
                    acc_ref[...] += query_part
                dkv_refs[k][group] = (
                    dot(score_grad, query_s[...], TN) + dot(weights.astype(BF16), grad_s[...], TN)
                ).astype(BF16)

            if k == 0:
                step()
            else:
                pl.when(k < need)(step)

                @pl.when(k >= need)
                def _(k=k):
                    dkv_refs[k][group] = jnp.zeros((rows, LANES), BF16)

        for r in range(ratio):
            outs.append(acc_ref[r * rows : (r + 1) * rows, :] * ATTENTION_SCALE)
    cosine, sine = cos_ref[...], sin_ref[...]
    for i in range(len(outs) // 2):
        slab = jnp.where(low, outs[2 * i], pltpu.roll(outs[2 * i + 1], HDIM, 1))
        slab = slab * cosine - partner_lanes(slab) * sine
        back_ref[:, i * LANES : (i + 1) * LANES] = slab.astype(BF16)


def attend_back(queries, attended, grad, lse, tables, kv_slots, seg_column, seg_rows, need, ratio):
    slots = len(kv_slots)
    rows, width = queries.shape
    groups = kv_slots[0].shape[0]
    steps = groups // 2
    block = 2 * ratio * HDIM
    whole = pl.BlockSpec((rows, LANES), lambda s: (0, 0))
    wide = pl.BlockSpec((rows, block), lambda s: (0, s))
    pair = pl.BlockSpec((2, rows, LANES), lambda s: (s, 0, 0))
    out = pl.pallas_call(
        functools.partial(attend_back_kernel, slots, ratio),
        out_shape=(jax.ShapeDtypeStruct((rows, width), BF16),)
        + (jax.ShapeDtypeStruct((groups, rows, LANES), BF16),) * slots,
        grid=(steps,),
        in_specs=[
            pl.BlockSpec(memory_space=pltpu.SMEM),
            wide,
            wide,
            wide,
            pl.BlockSpec((1, rows, LANES), lambda s: (s, 0, 0)),
            whole,
            whole,
            pl.BlockSpec((rows, 1), lambda s: (0, 0)),
            pl.BlockSpec(seg_rows.shape, lambda s: (0, 0)),
        ]
        + [pair] * slots,
        out_specs=(wide,) + (pair,) * slots,
        scratch_shapes=[
            pltpu.VMEM((slots, rows, rows), F32),
            pltpu.VMEM((ratio * rows, LANES), BF16),
            pltpu.VMEM((ratio * rows, LANES), BF16),
            pltpu.VMEM((ratio * rows, LANES), F32),
            pltpu.VMEM((ratio * rows, 1), F32),
            pltpu.VMEM((ratio * rows, 1), F32),
        ],
        compiler_params=params(),
        name="attend_back",
    )(need, queries, attended, grad, lse, *tables, seg_column, seg_rows, *kv_slots)
    return out[0], out[1:]


def unpack_kernel(dkv_ref, cos_ref, sin_ref, key_ref, value_ref):
    groups, rows, _ = dkv_ref.shape
    low = low_lanes(rows)
    cosine, sine = cos_ref[...], sin_ref[...]
    for i in range(groups // 2):
        even, odd = dkv_ref[2 * i], dkv_ref[2 * i + 1]
        slab = jnp.where(low, even, pltpu.roll(odd, HDIM, 1))
        slab = slab * cosine - partner_lanes(slab) * sine
        key_ref[:, i * LANES : (i + 1) * LANES] = slab.astype(BF16)
        value_ref[:, i * LANES : (i + 1) * LANES] = jnp.where(
            low, pltpu.roll(even, HDIM, 1), odd
        ).astype(BF16)


def expert_kernel(blocks, slot_rows, local_experts, place_ref, router_ref, gate_ref, up_ref, down_ref, *refs):
    sources = 2 * blocks - 1
    normed_in, cot_in, info_in = (refs[i * sources : (i + 1) * sources] for i in range(3))
    refs = refs[3 * sources :]
    xs_ref, cs_ref, hs_ref, gate_grad_ref, up_grad_ref, hit_ref = refs[:6]
    grad_out = refs[6 : 6 + sources]
    router_grad_ref = refs[6 + sources]
    x_all, c_all, info, gates, back, grad_acc, grad_low, sems, out_sem = refs[7 + sources :]
    step = pl.program_id(0)
    rows = x_all.shape[1]
    expert_pad = router_ref.shape[0]
    first_expert = place_ref[0]
    mine = pl.ds(first_expert + step, 1)

    def source_copies(i, s):
        return (
            pltpu.make_async_copy(normed_in[s], x_all.at[i], sems.at[0, i]),
            pltpu.make_async_copy(cot_in[s], c_all.at[i], sems.at[1, i]),
            pltpu.make_async_copy(info_in[s], info.at[i], sems.at[2, i]),
        )

    @pl.when(step == 0)
    def _():
        for i in range(blocks):
            for s in range(sources):

                @pl.when(place_ref[1 + i] == s)
                def _(i=i, s=s):
                    for copy in source_copies(i, s):
                        copy.start()

        for i in range(blocks):
            for copy in source_copies(i, 0):
                copy.wait()
        for i in range(blocks):
            logits = dot(router_ref[...], x_all[i], NT)
            logits = jnp.where(info[i, :expert_pad, :] >= 0, logits, MASKED_SCORE)
            weights = jnp.exp(logits - jnp.max(logits, axis=0, keepdims=True))
            gates[i] = weights / jnp.sum(weights, axis=0, keepdims=True)
        back[...] = jnp.zeros_like(back)
        grad_acc[...] = jnp.zeros_like(grad_acc)

    slot_ids = lax.broadcasted_iota(jnp.int32, (slot_rows, rows), 0)
    gate_slots = []
    for i in range(blocks):
        hit = slot_ids == info[i, mine, :]
        part = slice(i * slot_rows, (i + 1) * slot_rows)
        gate_slots.append(
            jnp.sum(jnp.where(hit, gates[i, mine, :], 0.0), axis=-1, keepdims=True)
        )
        hit = jnp.where(hit, 1.0, 0.0).astype(BF16)
        hit_ref[0, part, :] = hit
        xs_ref[0, part, :] = dot(hit, x_all[i]).astype(BF16)
        cs_ref[0, part, :] = dot(hit, c_all[i]).astype(BF16)
    gate_slot = jnp.concatenate(gate_slots, axis=0) * RESIDUAL_SCALE
    gate_pre = dot(xs_ref[0], gate_ref[0])
    up_pre = dot(xs_ref[0], up_ref[0])
    raw_grad = dot(cs_ref[0], down_ref[0])
    sigmoid = 1.0 / (1.0 + jnp.exp(-gate_pre))
    active = gate_pre * sigmoid
    expert_hidden = (active * up_pre).astype(BF16).astype(F32)
    hs_ref[0] = (expert_hidden * gate_slot).astype(BF16)
    back_slot = jnp.sum(expert_hidden * raw_grad, axis=-1, keepdims=True) * RESIDUAL_SCALE
    hidden_grad = raw_grad * gate_slot
    gate_grad_ref[0] = (hidden_grad * up_pre * sigmoid * (1.0 + gate_pre * (1.0 - sigmoid))).astype(BF16)
    up_grad_ref[0] = (hidden_grad * active).astype(BF16)
    slot_grad = (
        dot(gate_grad_ref[0], gate_ref[0], NT) + dot(up_grad_ref[0], up_ref[0], NT)
    ).astype(BF16)
    for i in range(blocks):
        part = slice(i * slot_rows, (i + 1) * slot_rows)
        hit = hit_ref[0, part, :]
        back_row = jnp.sum(hit.astype(F32) * back_slot[part], axis=0, keepdims=True)
        back[i, mine, :] = back_row * gates[i, mine, :]
        grad_acc[i] += dot(hit, slot_grad[part], TN)

    @pl.when(step == local_experts - 1)
    def _():
        router_sum = None
        for i in range(blocks):
            share = back[i]
            logit_grad = (share - gates[i] * jnp.sum(share, axis=0, keepdims=True)).astype(BF16)
            grad_low[i] = (grad_acc[i] + dot(logit_grad, router_ref[...], TN)).astype(BF16)
            part = dot(logit_grad, x_all[i])
            router_sum = part if router_sum is None else router_sum + part
        router_grad_ref[...] = router_sum
        for i in range(blocks):
            for s in range(sources):

                @pl.when(place_ref[1 + i] == s)
                def _(i=i, s=s):
                    pltpu.make_async_copy(grad_low.at[i], grad_out[s], out_sem.at[i]).start()

        for i in range(blocks):
            pltpu.make_async_copy(grad_low.at[i], grad_out[0], out_sem.at[i]).wait()


def run_experts(place, router_t, gate_weight, up_weight, down_weight, normed, cots, infos, slot_rows):
    local_experts, width, hidden = gate_weight.shape
    sources = len(normed)
    blocks = (sources + 1) // 2
    rows = normed[0].shape[0]
    expert_pad = router_t.shape[0]
    slots = blocks * slot_rows
    anywhere = pl.BlockSpec(memory_space=pl.ANY)
    weight_spec = pl.BlockSpec((1, width, hidden), lambda e, place: (e, 0, 0))

    def slot_spec(columns):
        return pl.BlockSpec((1, slots, columns), lambda e, place: (e, 0, 0))

    def slot_shape(columns):
        return jax.ShapeDtypeStruct((local_experts, slots, columns), BF16)

    out = pl.pallas_call(
        functools.partial(expert_kernel, blocks, slot_rows, local_experts),
        out_shape=(
            slot_shape(width),
            slot_shape(width),
            slot_shape(hidden),
            slot_shape(hidden),
            slot_shape(hidden),
            slot_shape(rows),
        )
        + (jax.ShapeDtypeStruct((rows, width), BF16),) * sources
        + (jax.ShapeDtypeStruct((expert_pad, width), F32),),
        grid_spec=pltpu.PrefetchScalarGridSpec(
            num_scalar_prefetch=1,
            grid=(local_experts,),
            in_specs=[pl.BlockSpec((expert_pad, width), lambda e, place: (0, 0))]
            + [weight_spec] * 3
            + [anywhere] * (3 * sources),
            out_specs=(
                slot_spec(width),
                slot_spec(width),
                slot_spec(hidden),
                slot_spec(hidden),
                slot_spec(hidden),
                slot_spec(rows),
            )
            + (anywhere,) * sources
            + (pl.BlockSpec((expert_pad, width), lambda e, place: (0, 0)),),
            scratch_shapes=[
                pltpu.VMEM((blocks, rows, width), BF16),
                pltpu.VMEM((blocks, rows, width), BF16),
                pltpu.VMEM((blocks,) + infos[0].shape, jnp.int32),
                pltpu.VMEM((blocks, expert_pad, rows), F32),
                pltpu.VMEM((blocks, expert_pad, rows), F32),
                pltpu.VMEM((blocks, rows, width), F32),
                pltpu.VMEM((blocks, rows, width), BF16),
                pltpu.SemaphoreType.DMA((3, blocks)),
                pltpu.SemaphoreType.DMA((blocks,)),
            ],
        ),
        compiler_params=params(),
        name="experts",
    )(place, router_t, gate_weight, up_weight, down_weight, *normed, *cots, *infos)
    return out[:6], out[6 : 6 + sources], out[6 + sources]


def expert_grad_kernel(blocks, slot_rows, local_experts, owners, chunk, place_ref, down_ref, xs_ref, cs_ref, hs_ref, gate_grad_ref, up_grad_ref, hit_ref, *refs):
    keep_refs, send_refs = refs[:3], refs[3:6]
    sources = 2 * blocks - 1
    mix_out = refs[6 : 6 + sources]
    mix_acc, mix_low, out_sem = refs[6 + sources :]
    step = pl.program_id(0)
    width = xs_ref.shape[2]
    owned = width // owners
    mine = place_ref[0]
    my_pair, my_bit = mine // 2, mine % 2

    @pl.when(step == 0)
    def _():
        mix_acc[...] = jnp.zeros_like(mix_acc)

    slot_out = dot(hs_ref[0], down_ref[0], NT).astype(BF16)
    for i in range(blocks):
        part = slice(i * slot_rows, (i + 1) * slot_rows)
        mix_acc[i] += dot(hit_ref[0, part, :], slot_out[part], TN)

    pairs = ((xs_ref, gate_grad_ref), (xs_ref, up_grad_ref), (cs_ref, hs_ref))
    for w, (left_ref, right_ref) in enumerate(pairs):
        for c in range(width // chunk):
            grad = dot(left_ref[0, :, c * chunk : (c + 1) * chunk], right_ref[0], TN).astype(BF16)
            for o in range(chunk // owned):
                owner = c * (chunk // owned) + o
                piece = grad[o * owned : (o + 1) * owned]
                spot = (owner // 2) ^ my_pair

                @pl.when(my_bit == owner % 2)
                def _(w=w, spot=spot, piece=piece):
                    keep_refs[w][0, spot] = piece

                @pl.when(my_bit != owner % 2)
                def _(w=w, spot=spot, piece=piece):
                    send_refs[w][0, spot] = piece

    @pl.when(step == local_experts - 1)
    def _():
        for i in range(blocks):
            mix_low[i] = mix_acc[i].astype(BF16)
        for i in range(blocks):
            for s in range(sources):

                @pl.when(place_ref[1 + i] == s)
                def _(i=i, s=s):
                    pltpu.make_async_copy(mix_low.at[i], mix_out[s], out_sem.at[i]).start()

        for i in range(blocks):
            pltpu.make_async_copy(mix_low.at[i], mix_out[0], out_sem.at[i]).wait()


def run_expert_grads(place, down_weight, saved, rows, slot_rows, owners):
    local_experts, width, hidden = down_weight.shape
    slots = saved[0].shape[1]
    blocks = slots // slot_rows
    sources = 2 * blocks - 1
    owned = width // owners
    chunk = int(np.lcm(2 * owned, LANES))
    anywhere = pl.BlockSpec(memory_space=pl.ANY)

    def slot_spec(columns):
        return pl.BlockSpec((1, slots, columns), lambda e, place: (e, 0, 0))

    half_shape = jax.ShapeDtypeStruct((local_experts, owners // 2, owned, hidden), BF16)
    half_spec = pl.BlockSpec((1, owners // 2, owned, hidden), lambda e, place: (e, 0, 0, 0))
    out = pl.pallas_call(
        functools.partial(expert_grad_kernel, blocks, slot_rows, local_experts, owners, chunk),
        out_shape=(half_shape,) * 6 + (jax.ShapeDtypeStruct((rows, width), BF16),) * sources,
        grid_spec=pltpu.PrefetchScalarGridSpec(
            num_scalar_prefetch=1,
            grid=(local_experts,),
            in_specs=[
                pl.BlockSpec((1, width, hidden), lambda e, place: (e, 0, 0)),
                slot_spec(width),
                slot_spec(width),
                slot_spec(hidden),
                slot_spec(hidden),
                slot_spec(hidden),
                slot_spec(rows),
            ],
            out_specs=(half_spec,) * 6 + (anywhere,) * sources,
            scratch_shapes=[
                pltpu.VMEM((blocks, rows, width), F32),
                pltpu.VMEM((blocks, rows, width), BF16),
                pltpu.SemaphoreType.DMA((blocks,)),
            ],
        ),
        compiler_params=params(),
        name="expert_grads",
    )(place, down_weight, *saved)
    return out[:3], out[3:6], out[6:]


def line_up(value, size):
    return lax.ppermute(value, "expert", [(i, i + 1) for i in range(size - 1)])


def line_down(value, size):
    return lax.ppermute(value, "expert", [(i + 1, i) for i in range(size - 1)])


def line_gather(value, size):
    below, above = [], []
    up, down = value, value
    for _ in range(size - 1):
        up = line_up(up, size)
        down = line_down(down, size)
        below.append(up)
        above.append(down)
    return [value] + below + above


def add_low(*terms):
    total = terms[0].astype(F32)
    for term in terms[1:]:
        total = total + term.astype(F32)
    return total.astype(BF16)


def line_reduce(parts, size):
    down = parts[size - 1]
    up = parts[2 * size - 2]
    for k in range(1, size):
        from_above = line_down(down, size)
        from_below = line_up(up, size)
        if k < size - 1:
            down = add_low(from_above, parts[size - 1 - k])
            up = add_low(from_below, parts[2 * size - 2 - k])
    return parts[0].astype(F32) + from_above.astype(F32) + from_below.astype(F32)


def flip(value, bit, size):
    return lax.ppermute(value, "dp", [(i, i ^ bit) for i in range(size)])


def halve_rows(value, order, dp_size, dp_place):
    left = list(range(dp_size.bit_length() - 2, -1, -1))
    for bit in order:
        axis = left.index(bit)
        own = (dp_place >> bit) & 1
        keep = lax.dynamic_index_in_dim(value, own, axis, keepdims=False)
        send = lax.dynamic_index_in_dim(value, 1 - own, axis, keepdims=False)
        value = add_low(keep, flip(send, 1 << bit, dp_size))
        left.pop(axis)
    return value


def reduce_dense(partial, dp_size, dp_place, size, place):
    depth, columns = partial.shape
    bits = dp_size.bit_length() - 1
    rows = depth // (dp_size * size)
    cube = partial.astype(BF16).reshape((2,) * bits + (size, rows, columns))
    half = columns // 2 // LANES * LANES
    outs = []
    rest = list(range(1, bits))
    for part, order in ((cube[..., :half], rest), (cube[..., half:], rest[::-1])):
        block = halve_rows(part, [0] + order, dp_size, dp_place)

        def pick(index, block=block):
            return lax.dynamic_index_in_dim(block, jnp.clip(index, 0, size - 1), 0, keepdims=False)

        down, up = pick(1 + place - size), pick(place + size - 1)
        for k in range(1, size):
            from_above = line_down(down, size)
            from_below = line_up(up, size)
            if k < size - 1:
                down = add_low(from_above, pick(k + 1 + place - size))
                up = add_low(from_below, pick(place + size - k - 1))
        outs.append(pick(place).astype(F32) + from_above.astype(F32) + from_below.astype(F32))
    return jnp.concatenate(outs, axis=-1)


def reduce_experts(keep, send, dp_size):
    bits = dp_size.bit_length() - 1
    local_experts, _, rows, hidden = keep.shape
    received = flip(send, 1, dp_size)
    cube = (local_experts,) + (2,) * (bits - 1) + (rows, hidden)
    keep, received = keep.reshape(cube), received.reshape(cube)
    half = rows // 2
    outs = []
    rest = list(range(1, bits))
    for lo, hi, order in ((0, half, rest), (half, rows, rest[::-1])):
        value = (keep[..., lo:hi, :], received[..., lo:hi, :])
        left = list(range(bits - 1, 0, -1))
        for bit in order:
            axis = 1 + left.index(bit)
            send_part = add_low(*(lax.index_in_dim(v, 1, axis, keepdims=False) for v in value))
            keep_parts = tuple(lax.index_in_dim(v, 0, axis, keepdims=False) for v in value)
            value = (add_low(*keep_parts), flip(send_part, 1 << bit, dp_size))
            left.pop(axis - 1)
        outs.append(value[0].astype(F32) + value[1].astype(F32))
    return jnp.concatenate(outs, axis=1)


def reduce_top(top, dp_size, size):
    for bit in range(dp_size.bit_length() - 1):
        top = jnp.maximum(top, flip(top, 1 << bit, dp_size))
    place = lax.axis_index("expert")
    up, down = top, top
    for k in range(1, size):
        up = line_up(up, size)
        down = line_down(down, size)
        top = jnp.maximum(top, jnp.where(place >= k, up, top))
        top = jnp.maximum(top, jnp.where(place + k < size, down, top))
    return top


def arrival_order(size):
    table = np.zeros((size, size), np.int32)
    for place in range(size):
        spots = [0]
        for k in range(1, size):
            if place - k >= 0:
                spots.append(k)
            if place + k < size:
                spots.append(size - 1 + k)
        table[place] = spots
    return table


def norm_backward(hidden, factor, gain_vec, grad_in):
    scaled = grad_in * gain_vec
    hidden_grad = factor * scaled - hidden * factor**3 * jnp.mean(
        scaled * hidden, axis=-1, keepdims=True
    )
    return hidden_grad, jnp.sum(grad_in * hidden * factor, axis=0)


def local(
    tokens,
    first_gain,
    query_weight,
    key_weight,
    value_weight,
    output_weight,
    second_gain,
    router_weight,
    gate_weight,
    up_weight,
    down_weight,
    cotangent,
    routes,
    segments,
    threshold,
):
    rows, width = tokens.shape
    query_width, kv_width = query_weight.shape[1], key_weight.shape[1]
    heads, groups = query_width // HDIM, kv_width // HDIM
    ratio = heads // groups
    local_experts = gate_weight.shape[0]
    size, dp_size = lax.axis_size("expert"), lax.axis_size("dp")
    place, dp_place = lax.axis_index("expert"), lax.axis_index("dp")
    experts = local_experts * size
    expert_pad = round_up(experts, 16)
    capacity = rows * routes.shape[1] * 9 // (experts * 8)
    slot_rows = round_up(capacity, 64)

    positions = (place * rows + jnp.arange(rows, dtype=jnp.int32)).astype(F32)
    half = HDIM // 2
    inverse = ROTARY_BASE ** (-2.0 * jnp.arange(half, dtype=F32) / HDIM)
    angles = positions[:, None] * jnp.tile(inverse, LANES // half)[None, :]
    sign = jnp.where(jnp.arange(LANES) % HDIM < half, -1.0, 1.0).astype(F32)
    tables = (jnp.cos(angles), jnp.sin(angles) * sign[None, :])

    info = pl.pallas_call(
        functools.partial(info_kernel, expert_pad),
        out_shape=jax.ShapeDtypeStruct((expert_pad + 8, rows), jnp.int32),
        in_specs=[vmem()] * 2,
        out_specs=vmem(),
        compiler_params=params(),
        name="info",
    )(routes, segments.reshape(1, rows))
    infos = line_gather(info, size)

    normed, first_factor, kv_own = pl.pallas_call(
        front_kernel,
        out_shape=(
            jax.ShapeDtypeStruct((rows, width), BF16),
            jax.ShapeDtypeStruct((rows, 1), F32),
            jax.ShapeDtypeStruct((groups, rows, LANES), BF16),
        ),
        in_specs=[vmem()] * 6,
        out_specs=(vmem(),) * 3,
        compiler_params=params(),
        name="front",
    )(tokens, first_gain.reshape(1, width), key_weight, value_weight, *tables)
    kv_slots = [kv_own]
    for _ in range(size - 1):
        kv_slots.append(line_up(kv_slots[-1], size))
    cots = line_gather(cotangent, size)

    query_block = 512
    queries = pl.pallas_call(
        query_kernel,
        out_shape=jax.ShapeDtypeStruct((rows, query_width), BF16),
        grid=(query_width // query_block,),
        in_specs=[
            pl.BlockSpec((rows, width), lambda s: (0, 0)),
            pl.BlockSpec((width, query_block), lambda s: (0, s)),
            pl.BlockSpec((rows, LANES), lambda s: (0, 0)),
            pl.BlockSpec((rows, LANES), lambda s: (0, 0)),
        ],
        out_specs=pl.BlockSpec((rows, query_block), lambda s: (0, s)),
        compiler_params=params(),
        name="queries",
    )(normed, query_weight, *tables)

    seg_rows = jnp.concatenate([infos[k][expert_pad : expert_pad + 1] for k in range(size)], axis=0)
    reach = jnp.arange(size, dtype=jnp.int32)
    wanted = (reach <= place) & (seg_rows[:, -1] >= segments[0])
    need = jnp.sum(wanted.astype(jnp.int32)).reshape(1)
    seg_rows = jnp.where((reach <= place)[:, None], seg_rows, -1)
    seg_column = segments.reshape(rows, 1)

    attended, lse, top = attend(queries, kv_slots, seg_column, seg_rows, need, ratio)
    head_top = reduce_top(top[:, 0, : 2 * ratio].reshape(1, heads), dp_size, size).reshape(heads)

    hidden_in = tokens.astype(F32)
    hidden_mid = hidden_in + RESIDUAL_SCALE * dot(attended, output_weight, NT)
    second_factor = lax.rsqrt(jnp.mean(hidden_mid * hidden_mid, axis=-1, keepdims=True) + NORM_EPSILON)
    second_normed = (hidden_mid * second_factor * second_gain).astype(BF16)
    normed_blocks = line_gather(second_normed, size)

    router_t = jnp.pad(router_weight.T, ((0, expert_pad - experts), (0, 0)))
    order = lax.dynamic_index_in_dim(jnp.asarray(arrival_order(size)), place, 0, keepdims=False)
    expert_place = jnp.concatenate([(place * local_experts).reshape(1), order]).astype(jnp.int32)
    saved, grad_blocks, router_part = run_experts(
        expert_place, router_t, gate_weight, up_weight, down_weight, normed_blocks, cots, infos, slot_rows
    )
    normed_grad = line_reduce(grad_blocks, size)

    grad_place = jnp.concatenate([dp_place.reshape(1), order]).astype(jnp.int32)
    keep, send, mix_blocks = run_expert_grads(grad_place, down_weight, saved, rows, slot_rows, dp_size)
    expert_sums = [reduce_experts(k, s, dp_size) for k, s in zip(keep, send)]
    block_out = (hidden_mid + line_reduce(mix_blocks, size)).astype(BF16)

    out_grad = cotangent.astype(F32)
    mid_back, second_gain_part = norm_backward(hidden_mid, second_factor, second_gain, normed_grad)
    mid_grad = out_grad + mid_back
    branch_grad = (RESIDUAL_SCALE * mid_grad).astype(BF16)
    attended_grad = dot(branch_grad, output_weight).astype(BF16)
    projection_part = dot(branch_grad, attended, TN)
    projection_grad = reduce_dense(projection_part, dp_size, dp_place, size, place)

    query_back, dkv = attend_back(
        queries, attended, attended_grad, lse, tables, kv_slots, seg_column, seg_rows, need, ratio
    )
    down = dkv[size - 1]
    for k in range(1, size):
        from_above = line_down(down, size)
        if k < size - 1:
            down = add_low(from_above, dkv[size - 1 - k])
    dkv_sum = dkv[0].astype(F32) + from_above.astype(F32)
    key_back, value_back = pl.pallas_call(
        unpack_kernel,
        out_shape=(jax.ShapeDtypeStruct((rows, kv_width), BF16),) * 2,
        in_specs=[vmem()] * 3,
        out_specs=(vmem(),) * 2,
        compiler_params=params(),
        name="unpack",
    )(dkv_sum, *tables)

    first_grad = dot(query_back, query_weight, NT)
    first_grad = first_grad + dot(key_back, key_weight, NT)
    first_grad = first_grad + dot(value_back, value_weight, NT)
    input_back, first_gain_part = norm_backward(hidden_in, first_factor, first_gain, first_grad)
    input_grad = mid_grad + input_back
    small = jnp.concatenate(
        [router_part[:experts], second_gain_part[None], first_gain_part[None]], axis=0
    )
    small = jnp.pad(small, ((0, LANES - small.shape[0]), (0, 0))).T
    query_grad = reduce_dense(dot(normed, query_back, TN), dp_size, dp_place, size, place)
    rest_grad = reduce_dense(
        jnp.concatenate(
            [dot(normed, key_back, TN).astype(BF16), dot(normed, value_back, TN).astype(BF16), small.astype(BF16)],
            axis=1,
        ),
        dp_size,
        dp_place,
        size,
        place,
    )
    key_grad = rest_grad[:, :kv_width]
    value_grad = rest_grad[:, kv_width : 2 * kv_width]
    small_grad = rest_grad[:, 2 * kv_width :]

    head_scale = threshold / jnp.maximum(head_top, threshold)
    group_scale = jnp.min(head_scale.reshape(groups, ratio), axis=1)
    row_count = width // (dp_size * size)
    row_start = (dp_place * size + place) * row_count
    query_rows = lax.dynamic_slice_in_dim(query_weight, row_start, row_count, 0).astype(F32)
    key_rows = lax.dynamic_slice_in_dim(key_weight, row_start, row_count, 0).astype(F32)
    query_clipped = (query_rows * jnp.repeat(jnp.sqrt(head_scale), HDIM)[None, :]).astype(BF16)
    key_clipped = (key_rows * jnp.repeat(jnp.sqrt(group_scale), HDIM)[None, :]).astype(BF16)
    return (
        block_out,
        input_grad,
        small_grad[:, experts + 1],
        query_grad,
        key_grad,
        value_grad,
        projection_grad,
        small_grad[:, experts],
        small_grad[:, :experts],
        expert_sums[0],
        expert_sums[1],
        expert_sums[2],
        head_scale,
        query_clipped,
        key_clipped,
    )


def solution(mesh):
    row = P(("dp", "expert"), None)
    vector = P(("dp", "expert"))
    expert_in = P("expert", None, None)
    expert_out = P("expert", "dp", None)
    return jax.shard_map(
        local,
        mesh=mesh,
        in_specs=(row,) + (P(),) * 7 + (expert_in,) * 3 + (row, row, vector, P()),
        out_specs=(row, row, vector)
        + (row,) * 4
        + (vector, row)
        + (expert_out,) * 3
        + (P(), row, row),
        check_vma=False,
    )
```

time: 2160 us -> 816 us (0.38)
  waiting for transfers between devices: 1280 us -> 279 us
  blocking collectives: 251 us -> 0 us
  matrix products: 250 us -> 15.5 us
  starting transfers between devices: 25.7 us -> 246 us
  Pallas kernels: 0 us -> 170 us
  local copies, waits for them, and re-layouts: 227 us -> 65.1 us
  other arithmetic: 96.8 us -> 37 us
    reduce_scatter x9 -> x0, waiting for transfers between devices: 674 us -> none  [the longest x1 142 us: local(): lax.psum_scatter(projection_partial, ('dp', 'expert'), scatter_dimension=...]
    all_to_all x3 -> x0, waiting for transfers between devices: 548 us -> none  [the longest x1 206 us: local(): lax.all_to_all(expert_out, 'expert', split_axis=1, concat_axis=0, tiled=T...]
    ppermute x0 -> x114, waiting for transfers between devices: none -> 279 us  [the longest x39 102 us: line_down(): return lax.ppermute(value, 'expert', [(i + 1, i) for i in range(size - 1)])]
    ppermute x0 -> x114, starting transfers between devices: none -> 246 us  [the longest x39 161 us: line_down(): return lax.ppermute(value, 'expert', [(i + 1, i) for i in range(size - 1)])]
    dot_general x79 -> x9, matrix products: 249 us -> 15.5 us  [dot(): return lax.dot_general(left, right, dims, preferred_element_type=F32)]
    pallas_call x0 -> x8, Pallas kernels: none -> 170 us  [the longest x1 45.5 us: run_experts(): pl.pallas_call(functools.partial(expert_kernel, blocks, slot_rows, local_...]
    all_to_all x1 -> x0, blocking collectives: 165 us -> none  [local(): lax.all_to_all(outgoing_grad, 'expert', split_axis=0, concat_axis=1, tile...]
    gather x6 -> x0, local copies, waits for them, and re-layouts: 77.3 us -> none  [the longest x4 40.4 us: slot_rows(): row_data[source]]
  transfers between devices with their start and end apart: 15 -> 114, of which waited for: 13 -> 55; matrix products, arithmetic and copies ran while one was open for 9% -> 12% of each run, Pallas kernels for 0% -> 15%
where the time goes in v1:
time: 816 us
  waiting for transfers between devices  279 us (34%)
  starting transfers between devices  246 us (30%)
  Pallas kernels  170 us (21%)
  local copies, waits for them, and re-layouts  65.1 us (8%)
  other arithmetic  37 us (5%)
  matrix products  15.5 us (2%)
    ppermute x39, starting transfers between devices, line_down(): return lax.ppermute(value, 'expert', [(i + 1, i) for i in range(size - 1)])  161 us
    ppermute x39, waiting for transfers between devices, line_down(): return lax.ppermute(value, 'expert', [(i + 1, i) for i in range(size - 1)])  102 us
    ppermute x36, waiting for transfers between devices, flip(): return lax.ppermute(value, 'dp', [(i, i ^ bit) for i in range(size)])  101 us
    ppermute x39, waiting for transfers between devices, line_up(): return lax.ppermute(value, 'expert', [(i, i + 1) for i in range(size - 1)])  75.6 us
    ppermute x39, starting transfers between devices, line_up(): return lax.ppermute(value, 'expert', [(i, i + 1) for i in range(size - 1)])  52.1 us
    pallas_call x1, Pallas kernels, run_experts(): pl.pallas_call(functools.partial(expert_kernel, blocks, slot_rows, local_...  45.5 us
    pallas_call x1, Pallas kernels, run_expert_grads(): pl.pallas_call(functools.partial(expert_grad_kernel, blocks, slot_rows, l...  42.9 us
    pallas_call x1, Pallas kernels, attend(): pl.pallas_call(functools.partial(attend_kernel, slots, ratio), out_shape=...  39.4 us
  transfers between devices with their start and end apart: 114, of which 55 were waited for; matrix products, arithmetic and copies ran while one was open for 12% of the time, Pallas kernels for 15%

profile of v1, /device:TPU:24, one launch (start us, length us, event | category | flops | bytes accessed | tf_op | source)
XLA Modules:
  0.0 815.9 jit_solution(2174184611768477252)
XLA Ops:
  3.3 4.3 front.1
  8.9 14.5 %collective-permute-done.3.refs_1_ = bf16[8,256,128]{2,1,0:T(8,128)(2,1)S(1)} collective-permute-done((bf16[8,256,128]{2,1,0:T(8,128)(2,1)}, bf16[8,256,128]{2,1,0:T(8,128)(2,1)S(1)}, u32[]{:S(2)}, u32[]{:S(2)}) %collective-permute-start.3) | collective-permute-done | bytes 524320 | tf_op jit(solution)/shard_map/ppermute | solution.py:585
  28.8 10.1 %collective-permute-done.refs_15_ = s32[40,256]{1,0:T(8,128)S(1)} collective-permute-done((s32[40,256]{1,0:T(8,128)}, s32[40,256]{1,0:T(8,128)S(1)}, u32[]{:S(2)}, u32[]{:S(2)}) %collective-permute-start) | collective-permute-done | bytes 40992 | tf_op jit(solution)/shard_map/ppermute | solution.py:585
  40.2 5.4 collective-permute-start.15
  52.2 5.6 queries.1.query_ref
  57.8 11.1 %collective-permute-done.2.refs_17_ = s32[40,256]{1,0:T(8,128)S(1)} collective-permute-done((s32[40,256]{1,0:T(8,128)S(1)}, s32[40,256]{1,0:T(8,128)S(1)}, u32[]{:S(2)}, u32[]{:S(2)}) %collective-permute-start.2) | collective-permute-done | bytes 40992 | tf_op jit(solution)/shard_map/ppermute | solution.py:585
  71.0 5.5 collective-permute-done.5.refs_3_
  77.4 39.4 %attend.1 = (bf16[256,1536]{1,0:T(8,128)(2,1)}, f32[4,256,128]{2,1,0:T(8,128)}, f32[4,8,128]{2,1,0:T(8,128)}) custom-call(s32[1]{0:T(128)} %bitcast.2.need_ref, bf16[256,1536]{1,0:T(8,128)(2,1)} %queries.1.query_ref, s32[256,1]{1,0:T(8,128)} %copy.97.seg_column_ref, s32[4,256]{1,0:T(4,128)} %get-tuple-element.220.seg_rows_ref, ...), custom_call_target="tpu_custom_call" | custom-call | tf_op jit(solution)/shard_map/attend/pallas_call | solution.py:185
  116.8 4.1 multiply_reduce_fusion.2
  124.7 5.4 collective-permute-start.16
  131.4 9.1 %collective-permute-done.9.refs_4_ = bf16[256,1536]{1,0:T(8,128)(2,1)} collective-permute-done((bf16[256,1536]{1,0:T(8,128)(2,1)S(1)}, bf16[256,1536]{1,0:T(8,128)(2,1)}, u32[]{:S(2)}, u32[]{:S(2)}) %collective-permute-start.9) | collective-permute-done | bytes 786464 | tf_op jit(solution)/shard_map/ppermute | solution.py:589
  140.5 5.4 collective-permute-start.10
  149.3 4.7 collective-permute-start.18
  154.7 16.1 %collective-permute-done.18.refs_18_ = s32[40,256]{1,0:T(8,128)S(1)} collective-permute-done((s32[40,256]{1,0:T(8,128)S(1)}, s32[40,256]{1,0:T(8,128)S(1)}, u32[]{:S(2)}, u32[]{:S(2)}) %collective-permute-start.18) | collective-permute-done | bytes 40992 | tf_op jit(solution)/shard_map/ppermute | solution.py:589
  174.4 4.4 collective-permute-start.19
  183.9 4.2 collective-permute-start.20
  191.5 4.5 collective-permute-start.111
  197.3 4.5 collective-permute-start.113
  203.2 5.4 collective-permute-start.17
  209.9 5.5 collective-permute-start.11
  220.5 4.4 collective-permute-done.17.refs_13_
  224.9 4.8 collective-permute-done.14.refs_10_
  233.3 4.8 collective-permute-done.8.refs_3_
  238.1 45.5 %experts.1 = (bf16[5,512,1536]{2,1,0:T(8,128)(2,1)}, bf16[5,512,1536]{2,1,0:T(8,128)(2,1)}, bf16[5,512,512]{2,1,0:T(8,128)(2,1)}, bf16[5,512,512]{2,1,0:T(8,128)...) custom-call(s32[5]{0:T(128)} %get-tuple-element.226.place_ref, ...), custom_call_target="tpu_custom_call" | custom-call | tf_op jit(solution)/shard_map/experts/pallas_call | solution.py:444
  286.6 42.9 %expert_grads.1 = (bf16[5,4,192,512]{3,2,1,0:T(8,128)(2,1)}, bf16[5,4,192,512]{3,2,1,0:T(8,128)(2,1)}, bf16[5,4,192,512]{3,2,1,0:T(8,128)(2,1)}, bf16[5,4,192,51...) custom-call(s32[5]{0:T(128)} %get-tuple-element.227.place_ref, ...), custom_call_target="tpu_custom_call" | custom-call | tf_op jit(solution)/shard_map/expert_grads/pallas_call | solution.py:556
  329.5 4.6 collective-permute-start.21
  343.2 4.7 collective-permute-start.28
  349.8 4.7 collective-permute-start.22
  356.2 9.5 %collective-permute-done.28 = bf16[256,1536]{1,0:T(8,128)(2,1)S(1)} collective-permute-done((bf16[256,1536]{1,0:T(8,128)(2,1)S(1)}, bf16[256,1536]{1,0:T(8,128)(2,1)S(1)}, u32[]{:S(2)}, u32[]{:S(2)}) %collective-permute-start.28) | collective-permute-done | bytes 786464 | tf_op jit(solution)/shard_map/ppermute | solution.py:589
  365.9 4.6 collective-permute-start.29
  372.2 10.4 %collective-permute-done.22 = bf16[256,1536]{1,0:T(8,128)(2,1)S(1)} collective-permute-done((bf16[256,1536]{1,0:T(8,128)(2,1)S(1)}, bf16[256,1536]{1,0:T(8,128)(2,1)S(1)}, u32[]{:S(2)}, u32[]{:S(2)}) %collective-permute-start.22) | collective-permute-done | bytes 786464 | tf_op jit(solution)/shard_map/ppermute | solution.py:589
  382.7 4.4 collective-permute-start.23
  390.9 8.5 %collective-permute-done.29 = bf16[256,1536]{1,0:T(8,128)(2,1)S(1)} collective-permute-done((bf16[256,1536]{1,0:T(8,128)(2,1)S(1)}, bf16[256,1536]{1,0:T(8,128)(2,1)S(1)}, u32[]{:S(2)}, u32[]{:S(2)}) %collective-permute-start.29) | collective-permute-done | bytes 786464 | tf_op jit(solution)/shard_map/ppermute | solution.py:589
  399.4 4.8 collective-permute-done.32
  404.9 10.9 %collective-permute-done.23 = bf16[256,1536]{1,0:T(8,128)(2,1)S(1)} collective-permute-done((bf16[256,1536]{1,0:T(8,128)(2,1)S(1)}, bf16[256,1536]{1,0:T(8,128)(2,1)S(1)}, u32[]{:S(2)}, u32[]{:S(2)}) %collective-permute-start.23) | collective-permute-done | bytes 786464 | tf_op jit(solution)/shard_map/ppermute | solution.py:589
  415.8 4.5 collective-permute-done.26
  426.0 27.9 %attend_back.1 = (bf16[256,1536]{1,0:T(8,128)(2,1)}, bf16[8,256,128]{2,1,0:T(8,128)(2,1)}, bf16[8,256,128]{2,1,0:T(8,128)(2,1)}, bf16[8,256,128]{2,1,0:T(8,128)(2,1)}, bf16[8,256,128]{2,1,0:T(8,128)(2,1)}) custom-call(s32[1]{0:T(128)} %bitcast.2.need_ref, bf16[256,1536]{1,0:T(8,128)(2,1)} %queries.1.query_ref, ...), custom_call_target="tpu_custom_call" | custom-call | tf_op jit(solution)/shard_map/attend_back/pallas_call | solution.py:285
  459.5 7.9 collective-permute-done.33
  467.6 4.3 collective-permute-start.34
  476.4 6.5 collective-permute-done.34
  486.3 4.4 collective-permute-start.35
  494.2 8.3 %collective-permute-done.35 = bf16[8,256,128]{2,1,0:T(8,128)(2,1)S(1)} collective-permute-done((bf16[8,256,128]{2,1,0:T(8,128)(2,1)S(1)}, bf16[8,256,128]{2,1,0:T(8,128)(2,1)S(1)}, u32[]{:S(2)}, u32[]{:S(2)}) %collective-permute-start.35) | collective-permute-done | bytes 524320 | tf_op jit(solution)/shard_map/ppermute | solution.py:589
  534.3 5.8 copy.99
  567.3 21.5 %collective-permute-done.83 = bf16[4,48,768]{2,1,0:T(8,128)(2,1)S(1)} collective-permute-done((bf16[4,48,768]{2,1,0:T(8,128)(2,1)S(1)}, bf16[4,48,768]{2,1,0:T(8,128)(2,1)S(1)}, u32[]{:S(2)}, u32[]{:S(2)}) %collective-permute-start.83) | collective-permute-done | bytes 294944 | tf_op jit(solution)/shard_map/ppermute | solution.py:623
  591.4 5.1 collective-permute-done.74
  596.4 4.4 collective-permute-start.84
  602.8 4.3 collective-permute-start.48
  609.0 4.3 collective-permute-start.75
  615.3 4.4 collective-permute-start.57
  622.1 4.4 collective-permute-start.85
  628.4 4.3 collective-permute-start.49
  634.6 4.3 collective-permute-start.76
  640.9 4.3 collective-permute-start.58
  647.1 4.3 collective-permute-start.86
  653.3 4.3 collective-permute-start.77
  659.6 4.4 collective-permute-start.50
  667.0 4.5 collective-permute-start.59
  682.8 15.3 %collective-permute-done.93 = bf16[5,2,96,512]{3,2,0,1:T(8,128)(2,1)S(1)} collective-permute-done((bf16[5,2,96,512]{3,2,0,1:T(8,128)(2,1)S(1)}, bf16[5,2,96,512]{3,2,0,1:T(8,128)(2,1)S(1)}, u32[]{:S(2)}, u32[]{:S(2)}) %collective-permute-start.93) | collective-permute-done | bytes 983072 | tf_op jit(solution)/shard_map/ppermute | solution.py:623
  704.3 14.9 %collective-permute-done.98 = bf16[5,2,96,512]{3,2,0,1:T(8,128)(2,1)S(1)} collective-permute-done((bf16[5,2,96,512]{3,2,0,1:T(8,128)(2,1)S(1)}, bf16[5,2,96,512]{3,2,0,1:T(8,128)(2,1)S(1)}, u32[]{:S(2)}, u32[]{:S(2)}) %collective-permute-start.98) | collective-permute-done | bytes 983072 | tf_op jit(solution)/shard_map/ppermute | solution.py:623
  726.0 30.9 %collective-permute-done.65 = bf16[4,48,512]{2,1,0:T(8,128)(2,1)S(1)} collective-permute-done((bf16[4,48,512]{2,1,0:T(8,128)(2,1)S(1)}, bf16[4,48,512]{2,1,0:T(8,128)(2,1)S(1)}, u32[]{:S(2)}, u32[]{:S(2)}) %collective-permute-start.65) | collective-permute-done | bytes 196640 | tf_op jit(solution)/shard_map/ppermute | solution.py:623
  757.0 4.3 collective-permute-start.66
  797.0 4.5 collective-permute-start.68
  802.9 4.5 collective-permute-start.41
  809.4 4.1 collective-permute-done.44
  (524 shorter events, 247.0 us)
Async XLA Ops:
  7.6 15.8 %collective-permute-start.3 = (bf16[8,256,128]{2,1,0:T(8,128)(2,1)}, bf16[8,256,128]{2,1,0:T(8,128)(2,1)S(1)}, u32[]{:S(2)}, u32[]{:S(2)}) collective-permute-start(bf16[8,256,128]{2,1,0:T(8,128)(2,1)} %get-tuple-element.56.refs_0_), channel_id=1, source_target_pairs={{0,1},{1,2},{2,3},{4,5},{5,6},{6,7},{8,9},{9,10},{10,11},{12,13},{... | collective-permute-start | bytes 1572872 | tf_op jit(solution)/shard_map/ppermute | solution.py:585
  23.4 24.9 %collective-permute-start.4 = (bf16[8,256,128]{2,1,0:T(8,128)(2,1)S(1)}, bf16[8,256,128]{2,1,0:T(8,128)(2,1)S(1)}, u32[]{:S(2)}, u32[]{:S(2)}) collective-permute-start(bf16[8,256,128]{2,1,0:T(8,128)(2,1)S(1)} %collective-permute-done.3.refs_1_), channel_id=1, source_target_pairs={{0,1},{1,2},{2,3},{4,5},{5,6},{6,7},{8,9},{9,10},{10,11},{12,13},{... | collective-permute-start | bytes 1572872 | tf_op jit(solution)/shard_map/ppermute | solution.py:585
  27.5 11.4 %collective-permute-start = (s32[40,256]{1,0:T(8,128)}, s32[40,256]{1,0:T(8,128)S(1)}, u32[]{:S(2)}, u32[]{:S(2)}) collective-permute-start(s32[40,256]{1,0:T(8,128)} %info.1.refs_14_), channel_id=1, source_target_pairs={{0,1},{1,2},{2,3},{4,5},{5,6},{6,7},{8,9},{9,10},{10,11},{12,13},{... | collective-permute-start | bytes 122888 | tf_op jit(solution)/shard_map/ppermute | solution.py:585
  40.2 84.5 %collective-permute-start.15 = (bf16[256,1536]{1,0:T(8,128)(2,1)S(1)}, bf16[256,1536]{1,0:T(8,128)(2,1)}, u32[]{:S(2)}, u32[]{:S(2)}) collective-permute-start(bf16[256,1536]{1,0:T(8,128)(2,1)S(1)} %copy-done.43), channel_id=1, source_target_pairs={{1,0},{2,1},{3,2},{5,4},{6,5},{7,6},{9,8},{10,9},{11,10},{13,12},{... | collective-permute-start | bytes 2359304 | tf_op jit(solution)/shard_map/ppermute | solution.py:589
  45.7 84.5 %collective-permute-start.12 = (bf16[256,1536]{1,0:T(8,128)(2,1)S(1)}, bf16[256,1536]{1,0:T(8,128)(2,1)}, u32[]{:S(2)}, u32[]{:S(2)}) collective-permute-start(bf16[256,1536]{1,0:T(8,128)(2,1)S(1)} %copy-done.43), channel_id=1, source_target_pairs={{0,1},{1,2},{2,3},{4,5},{5,6},{6,7},{8,9},{9,10},{10,11},{12,13},{... | collective-permute-start | bytes 2359304 | tf_op jit(solution)/shard_map/ppermute | solution.py:585
  47.0 21.9 %collective-permute-start.2 = (s32[40,256]{1,0:T(8,128)S(1)}, s32[40,256]{1,0:T(8,128)S(1)}, u32[]{:S(2)}, u32[]{:S(2)}) collective-permute-start(s32[40,256]{1,0:T(8,128)S(1)} %collective-permute-done.1.refs_16_), channel_id=1, source_target_pairs={{0,1},{1,2},{2,3},{4,5},{5,6},{6,7},{8,9},{9,10},{10,11},{12,13},{... | collective-permute-start | bytes 122888 | tf_op jit(solution)/shard_map/ppermute | solution.py:585
  48.3 28.3 %collective-permute-start.5 = (bf16[8,256,128]{2,1,0:T(8,128)(2,1)S(1)}, bf16[8,256,128]{2,1,0:T(8,128)(2,1)S(1)}, u32[]{:S(2)}, u32[]{:S(2)}) collective-permute-start(bf16[8,256,128]{2,1,0:T(8,128)(2,1)S(1)} %collective-permute-done.4.refs_2_), channel_id=1, source_target_pairs={{0,1},{1,2},{2,3},{4,5},{5,6},{6,7},{8,9},{9,10},{10,11},{12,13},{... | collective-permute-start | bytes 1572872 | tf_op jit(solution)/shard_map/ppermute | solution.py:585
  121.2 19.3 %collective-permute-start.9 = (bf16[256,1536]{1,0:T(8,128)(2,1)S(1)}, bf16[256,1536]{1,0:T(8,128)(2,1)}, u32[]{:S(2)}, u32[]{:S(2)}) collective-permute-start(bf16[256,1536]{1,0:T(8,128)(2,1)S(1)} %multiply_convert_fusion.1.refs_0_), channel_id=1, source_target_pairs={{1,0},{2,1},{3,2},{5,4},{6,5},{7,6},{9,8},{10,9},{11,10},{13,12},{... | collective-permute-start | bytes 2359304 | tf_op jit(solution)/shard_map/ppermute | solution.py:589
  123.4 22.5 %collective-permute-start.6 = (bf16[256,1536]{1,0:T(8,128)(2,1)S(1)}, bf16[256,1536]{1,0:T(8,128)(2,1)}, u32[]{:S(2)}, u32[]{:S(2)}) collective-permute-start(bf16[256,1536]{1,0:T(8,128)(2,1)S(1)} %multiply_convert_fusion.1.refs_0_), channel_id=1, source_target_pairs={{0,1},{1,2},{2,3},{4,5},{5,6},{6,7},{8,9},{9,10},{10,11},{12,13},{... | collective-permute-start | bytes 2359304 | tf_op jit(solution)/shard_map/ppermute | solution.py:585
  124.7 63.5 %collective-permute-start.16 = (bf16[256,1536]{1,0:T(8,128)(2,1)}, bf16[256,1536]{1,0:T(8,128)(2,1)}, u32[]{:S(2)}, u32[]{:S(2)}) collective-permute-start(bf16[256,1536]{1,0:T(8,128)(2,1)} %collective-permute-done.15.refs_11_), channel_id=1, source_target_pairs={{1,0},{2,1},{3,2},{5,4},{6,5},{7,6},{9,8},{10,9},{11,10},{13,12},{... | collective-permute-start | bytes 2359304 | tf_op jit(solution)/shard_map/ppermute | solution.py:589
  130.1 60.0 %collective-permute-start.13 = (bf16[256,1536]{1,0:T(8,128)(2,1)}, bf16[256,1536]{1,0:T(8,128)(2,1)S(1)}, u32[]{:S(2)}, u32[]{:S(2)}) collective-permute-start(bf16[256,1536]{1,0:T(8,128)(2,1)} %collective-permute-done.12.refs_8_), channel_id=1, source_target_pairs={{0,1},{1,2},{2,3},{4,5},{5,6},{6,7},{8,9},{9,10},{10,11},{12,13},{... | collective-permute-start | bytes 2359304 | tf_op jit(solution)/shard_map/ppermute | solution.py:585
  140.5 69.5 %collective-permute-start.10 = (bf16[256,1536]{1,0:T(8,128)(2,1)}, bf16[256,1536]{1,0:T(8,128)(2,1)}, u32[]{:S(2)}, u32[]{:S(2)}) collective-permute-start(bf16[256,1536]{1,0:T(8,128)(2,1)} %collective-permute-done.9.refs_4_), channel_id=1, source_target_pairs={{1,0},{2,1},{3,2},{5,4},{6,5},{7,6},{9,8},{10,9},{11,10},{13,12},{... | collective-permute-start | bytes 2359304 | tf_op jit(solution)/shard_map/ppermute | solution.py:589
  145.9 69.6 %collective-permute-start.7 = (bf16[256,1536]{1,0:T(8,128)(2,1)}, bf16[256,1536]{1,0:T(8,128)(2,1)}, u32[]{:S(2)}, u32[]{:S(2)}) collective-permute-start(bf16[256,1536]{1,0:T(8,128)(2,1)} %collective-permute-done.6.refs_1_), channel_id=1, source_target_pairs={{0,1},{1,2},{2,3},{4,5},{5,6},{6,7},{8,9},{9,10},{10,11},{12,13},{... | collective-permute-start | bytes 2359304 | tf_op jit(solution)/shard_map/ppermute | solution.py:585
  149.3 21.5 %collective-permute-start.18 = (s32[40,256]{1,0:T(8,128)S(1)}, s32[40,256]{1,0:T(8,128)S(1)}, u32[]{:S(2)}, u32[]{:S(2)}) collective-permute-start(s32[40,256]{1,0:T(8,128)S(1)} %copy-done.65), channel_id=1, source_target_pairs={{1,0},{2,1},{3,2},{5,4},{6,5},{7,6},{9,8},{10,9},{11,10},{13,12},{... | collective-permute-start | bytes 122888 | tf_op jit(solution)/shard_map/ppermute | solution.py:589
  183.9 36.5 %collective-permute-start.20 = (s32[40,256]{1,0:T(8,128)S(1)}, s32[40,256]{1,0:T(8,128)S(1)}, u32[]{:S(2)}, u32[]{:S(2)}) collective-permute-start(s32[40,256]{1,0:T(8,128)S(1)} %collective-permute-done.19.refs_19_), channel_id=1, source_target_pairs={{1,0},{2,1},{3,2},{5,4},{6,5},{7,6},{9,8},{10,9},{11,10},{13,12},{... | collective-permute-start | bytes 122888 | tf_op jit(solution)/shard_map/ppermute | solution.py:589
  203.2 21.7 %collective-permute-start.17 = (bf16[256,1536]{1,0:T(8,128)(2,1)}, bf16[256,1536]{1,0:T(8,128)(2,1)}, u32[]{:S(2)}, u32[]{:S(2)}) collective-permute-start(bf16[256,1536]{1,0:T(8,128)(2,1)} %collective-permute-done.16.refs_12_), channel_id=1, source_target_pairs={{1,0},{2,1},{3,2},{5,4},{6,5},{7,6},{9,8},{10,9},{11,10},{13,12},{... | collective-permute-start | bytes 2359304 | tf_op jit(solution)/shard_map/ppermute | solution.py:589
  208.6 21.0 %collective-permute-start.14 = (bf16[256,1536]{1,0:T(8,128)(2,1)S(1)}, bf16[256,1536]{1,0:T(8,128)(2,1)}, u32[]{:S(2)}, u32[]{:S(2)}) collective-permute-start(bf16[256,1536]{1,0:T(8,128)(2,1)S(1)} %collective-permute-done.13.refs_9_), channel_id=1, source_target_pairs={{0,1},{1,2},{2,3},{4,5},{5,6},{6,7},{8,9},{9,10},{10,11},{12,13},{... | collective-permute-start | bytes 2359304 | tf_op jit(solution)/shard_map/ppermute | solution.py:585
  209.9 23.3 %collective-permute-start.11 = (bf16[256,1536]{1,0:T(8,128)(2,1)}, bf16[256,1536]{1,0:T(8,128)(2,1)}, u32[]{:S(2)}, u32[]{:S(2)}) collective-permute-start(bf16[256,1536]{1,0:T(8,128)(2,1)} %collective-permute-done.10.refs_5_), channel_id=1, source_target_pairs={{1,0},{2,1},{3,2},{5,4},{6,5},{7,6},{9,8},{10,9},{11,10},{13,12},{... | collective-permute-start | bytes 2359304 | tf_op jit(solution)/shard_map/ppermute | solution.py:589
  215.5 22.6 %collective-permute-start.8 = (bf16[256,1536]{1,0:T(8,128)(2,1)}, bf16[256,1536]{1,0:T(8,128)(2,1)}, u32[]{:S(2)}, u32[]{:S(2)}) collective-permute-start(bf16[256,1536]{1,0:T(8,128)(2,1)} %collective-permute-done.7.refs_2_), channel_id=1, source_target_pairs={{0,1},{1,2},{2,3},{4,5},{5,6},{6,7},{8,9},{9,10},{10,11},{12,13},{... | collective-permute-start | bytes 2359304 | tf_op jit(solution)/shard_map/ppermute | solution.py:585
  283.6 59.3 %collective-permute-start.27 = (bf16[256,1536]{1,0:T(8,128)(2,1)}, bf16[256,1536]{1,0:T(8,128)(2,1)S(1)}, u32[]{:S(2)}, u32[]{:S(2)}) collective-permute-start(bf16[256,1536]{1,0:T(8,128)(2,1)} %get-tuple-element.72), channel_id=1, source_target_pairs={{1,0},{2,1},{3,2},{5,4},{6,5},{7,6},{9,8},{10,9},{11,10},{13,12},{... | collective-permute-start | bytes 2359304 | tf_op jit(solution)/shard_map/ppermute | solution.py:589
  285.0 62.9 %collective-permute-start.30 = (bf16[256,1536]{1,0:T(8,128)(2,1)}, bf16[256,1536]{1,0:T(8,128)(2,1)S(1)}, u32[]{:S(2)}, u32[]{:S(2)}) collective-permute-start(bf16[256,1536]{1,0:T(8,128)(2,1)} %get-tuple-element.75), channel_id=1, source_target_pairs={{0,1},{1,2},{2,3},{4,5},{5,6},{6,7},{8,9},{9,10},{10,11},{12,13},{... | collective-permute-start | bytes 2359304 | tf_op jit(solution)/shard_map/ppermute | solution.py:585
  329.5 20.1 %collective-permute-start.21 = (bf16[256,1536]{1,0:T(8,128)(2,1)}, bf16[256,1536]{1,0:T(8,128)(2,1)S(1)}, u32[]{:S(2)}, u32[]{:S(2)}) collective-permute-start(bf16[256,1536]{1,0:T(8,128)(2,1)} %get-tuple-element.65), channel_id=1, source_target_pairs={{1,0},{2,1},{3,2},{5,4},{6,5},{7,6},{9,8},{10,9},{11,10},{13,12},{... | collective-permute-start | bytes 2359304 | tf_op jit(solution)/shard_map/ppermute | solution.py:589
  334.0 20.5 %collective-permute-start.24 = (bf16[256,1536]{1,0:T(8,128)(2,1)}, bf16[256,1536]{1,0:T(8,128)(2,1)S(1)}, u32[]{:S(2)}, u32[]{:S(2)}) collective-permute-start(bf16[256,1536]{1,0:T(8,128)(2,1)} %get-tuple-element.68), channel_id=1, source_target_pairs={{0,1},{1,2},{2,3},{4,5},{5,6},{6,7},{8,9},{9,10},{10,11},{12,13},{... | collective-permute-start | bytes 2359304 | tf_op jit(solution)/shard_map/ppermute | solution.py:585
  335.3 173.2 %collective-permute-start.90 = (bf16[5,4,192,512]{3,2,1,0:T(8,128)(2,1)}, bf16[5,4,192,512]{3,2,1,0:T(8,128)(2,1)}, u32[]{:S(2)}, u32[]{:S(2)}) collective-permute-start(bf16[5,4,192,512]{3,2,1,0:T(8,128)(2,1)} %get-tuple-element.89), channel_id=1, source_target_pairs={{0,4},{4,0},{8,12},{12,8},{16,20},{20,16},{24,28},{28,24},{1,5},{5... | collective-permute-start | bytes 11796488 | tf_op jit(solution)/shard_map/ppermute | solution.py:623
  343.2 22.5 %collective-permute-start.28 = (bf16[256,1536]{1,0:T(8,128)(2,1)S(1)}, bf16[256,1536]{1,0:T(8,128)(2,1)S(1)}, u32[]{:S(2)}, u32[]{:S(2)}) collective-permute-start(bf16[256,1536]{1,0:T(8,128)(2,1)S(1)} %add_convert_fusion.15), channel_id=1, source_target_pairs={{1,0},{2,1},{3,2},{5,4},{6,5},{7,6},{9,8},{10,9},{11,10},{13,12},{... | collective-permute-start | bytes 2359304 | tf_op jit(solution)/shard_map/ppermute | solution.py:589
  348.1 22.4 %collective-permute-start.31 = (bf16[256,1536]{1,0:T(8,128)(2,1)S(1)}, bf16[256,1536]{1,0:T(8,128)(2,1)S(1)}, u32[]{:S(2)}, u32[]{:S(2)}) collective-permute-start(bf16[256,1536]{1,0:T(8,128)(2,1)S(1)} %add_convert_fusion.13), channel_id=1, source_target_pairs={{0,1},{1,2},{2,3},{4,5},{5,6},{6,7},{8,9},{9,10},{10,11},{12,13},{... | collective-permute-start | bytes 2359304 | tf_op jit(solution)/shard_map/ppermute | solution.py:585
  349.8 32.8 %collective-permute-start.22 = (bf16[256,1536]{1,0:T(8,128)(2,1)S(1)}, bf16[256,1536]{1,0:T(8,128)(2,1)S(1)}, u32[]{:S(2)}, u32[]{:S(2)}) collective-permute-start(bf16[256,1536]{1,0:T(8,128)(2,1)S(1)} %add_convert_fusion.20), channel_id=1, source_target_pairs={{1,0},{2,1},{3,2},{5,4},{6,5},{7,6},{9,8},{10,9},{11,10},{13,12},{... | collective-permute-start | bytes 2359304 | tf_op jit(solution)/shard_map/ppermute | solution.py:589
  354.7 32.6 %collective-permute-start.25 = (bf16[256,1536]{1,0:T(8,128)(2,1)S(1)}, bf16[256,1536]{1,0:T(8,128)(2,1)S(1)}, u32[]{:S(2)}, u32[]{:S(2)}) collective-permute-start(bf16[256,1536]{1,0:T(8,128)(2,1)S(1)} %add_convert_fusion.18), channel_id=1, source_target_pairs={{0,1},{1,2},{2,3},{4,5},{5,6},{6,7},{8,9},{9,10},{10,11},{12,13},{... | collective-permute-start | bytes 2359304 | tf_op jit(solution)/shard_map/ppermute | solution.py:585
  365.9 33.5 %collective-permute-start.29 = (bf16[256,1536]{1,0:T(8,128)(2,1)S(1)}, bf16[256,1536]{1,0:T(8,128)(2,1)S(1)}, u32[]{:S(2)}, u32[]{:S(2)}) collective-permute-start(bf16[256,1536]{1,0:T(8,128)(2,1)S(1)} %add_convert_fusion.14), channel_id=1, source_target_pairs={{1,0},{2,1},{3,2},{5,4},{6,5},{7,6},{9,8},{10,9},{11,10},{13,12},{... | collective-permute-start | bytes 2359304 | tf_op jit(solution)/shard_map/ppermute | solution.py:589
  370.7 33.5 %collective-permute-start.32 = (bf16[256,1536]{1,0:T(8,128)(2,1)S(1)}, bf16[256,1536]{1,0:T(8,128)(2,1)S(1)}, u32[]{:S(2)}, u32[]{:S(2)}) collective-permute-start(bf16[256,1536]{1,0:T(8,128)(2,1)S(1)} %add_convert_fusion.12), channel_id=1, source_target_pairs={{0,1},{1,2},{2,3},{4,5},{5,6},{6,7},{8,9},{9,10},{10,11},{12,13},{... | collective-permute-start | bytes 2359304 | tf_op jit(solution)/shard_map/ppermute | solution.py:585
  382.7 33.1 %collective-permute-start.23 = (bf16[256,1536]{1,0:T(8,128)(2,1)S(1)}, bf16[256,1536]{1,0:T(8,128)(2,1)S(1)}, u32[]{:S(2)}, u32[]{:S(2)}) collective-permute-start(bf16[256,1536]{1,0:T(8,128)(2,1)S(1)} %add_convert_fusion.19), channel_id=1, source_target_pairs={{1,0},{2,1},{3,2},{5,4},{6,5},{7,6},{9,8},{10,9},{11,10},{13,12},{... | collective-permute-start | bytes 2359304 | tf_op jit(solution)/shard_map/ppermute | solution.py:589
  387.6 32.8 %collective-permute-start.26 = (bf16[256,1536]{1,0:T(8,128)(2,1)S(1)}, bf16[256,1536]{1,0:T(8,128)(2,1)S(1)}, u32[]{:S(2)}, u32[]{:S(2)}) collective-permute-start(bf16[256,1536]{1,0:T(8,128)(2,1)S(1)} %add_convert_fusion.17), channel_id=1, source_target_pairs={{0,1},{1,2},{2,3},{4,5},{5,6},{6,7},{8,9},{9,10},{10,11},{12,13},{... | collective-permute-start | bytes 2359304 | tf_op jit(solution)/shard_map/ppermute | solution.py:585
  453.9 13.5 %collective-permute-start.33 = (bf16[8,256,128]{2,1,0:T(8,128)(2,1)}, bf16[8,256,128]{2,1,0:T(8,128)(2,1)S(1)}, u32[]{:S(2)}, u32[]{:S(2)}) collective-permute-start(bf16[8,256,128]{2,1,0:T(8,128)(2,1)} %get-tuple-element.82), channel_id=1, source_target_pairs={{1,0},{2,1},{3,2},{5,4},{6,5},{7,6},{9,8},{10,9},{11,10},{13,12},{... | collective-permute-start | bytes 1572872 | tf_op jit(solution)/shard_map/ppermute | solution.py:589
  459.2 24.1 %collective-permute-start.45 = (bf16[2,2,4,48,768]{4,3,2,0,1:T(8,128)(2,1)S(1)}, bf16[2,2,4,48,768]{4,3,2,0,1:T(8,128)(2,1)S(1)}, u32[]{:S(2)}, u32[]{:S(2)}) collective-permute-start(bf16[2,2,4,48,768]{4,3,2,0,1:T(8,128)(2,1)S(1)} %bitcast.339), channel_id=1, source_target_pairs={{0,4},{4,0},{8,12},{12,8},{16,20},{20,16},{24,28},{28,24},{1,5},{5... | collective-permute-start | bytes 3538952 | tf_op jit(solution)/shard_map/ppermute | solution.py:623
  467.6 15.4 %collective-permute-start.34 = (bf16[8,256,128]{2,1,0:T(8,128)(2,1)S(1)}, bf16[8,256,128]{2,1,0:T(8,128)(2,1)S(1)}, u32[]{:S(2)}, u32[]{:S(2)}) collective-permute-start(bf16[8,256,128]{2,1,0:T(8,128)(2,1)S(1)} %add_convert_fusion.22), channel_id=1, source_target_pairs={{1,0},{2,1},{3,2},{5,4},{6,5},{7,6},{9,8},{10,9},{11,10},{13,12},{... | collective-permute-start | bytes 1572872 | tf_op jit(solution)/shard_map/ppermute | solution.py:589
  474.2 42.4 %collective-permute-start.95 = (bf16[5,4,192,512]{3,2,1,0:T(8,128)(2,1)}, bf16[5,4,192,512]{3,2,1,0:T(8,128)(2,1)S(1)}, u32[]{:S(2)}, u32[]{:S(2)}) collective-permute-start(bf16[5,4,192,512]{3,2,1,0:T(8,128)(2,1)} %get-tuple-element.91), channel_id=1, source_target_pairs={{0,4},{4,0},{8,12},{12,8},{16,20},{20,16},{24,28},{28,24},{1,5},{5... | collective-permute-start | bytes 11796488 | tf_op jit(solution)/shard_map/ppermute | solution.py:623
  474.4 10.6 %collective-permute-start.72 = (bf16[2,2,4,48,768]{4,3,2,0,1:T(8,128)(2,1)S(1)}, bf16[2,2,4,48,768]{4,3,2,0,1:T(8,128)(2,1)S(1)}, u32[]{:S(2)}, u32[]{:S(2)}) collective-permute-start(bf16[2,2,4,48,768]{4,3,2,0,1:T(8,128)(2,1)S(1)} %bitcast.340), channel_id=1, source_target_pairs={{0,4},{4,0},{8,12},{12,8},{16,20},{20,16},{24,28},{28,24},{1,5},{5... | collective-permute-start | bytes 3538952 | tf_op jit(solution)/shard_map/ppermute | solution.py:623
  485.0 37.3 %collective-permute-start.100 = (bf16[5,4,192,512]{3,2,1,0:T(8,128)(2,1)}, bf16[5,4,192,512]{3,2,1,0:T(8,128)(2,1)}, u32[]{:S(2)}, u32[]{:S(2)}) collective-permute-start(bf16[5,4,192,512]{3,2,1,0:T(8,128)(2,1)} %get-tuple-element.93), channel_id=1, source_target_pairs={{0,4},{4,0},{8,12},{12,8},{16,20},{20,16},{24,28},{28,24},{1,5},{5... | collective-permute-start | bytes 11796488 | tf_op jit(solution)/shard_map/ppermute | solution.py:623
  486.3 16.2 %collective-permute-start.35 = (bf16[8,256,128]{2,1,0:T(8,128)(2,1)S(1)}, bf16[8,256,128]{2,1,0:T(8,128)(2,1)S(1)}, u32[]{:S(2)}, u32[]{:S(2)}) collective-permute-start(bf16[8,256,128]{2,1,0:T(8,128)(2,1)S(1)} %add_convert_fusion.21), channel_id=1, source_target_pairs={{1,0},{2,1},{3,2},{5,4},{6,5},{7,6},{9,8},{10,9},{11,10},{13,12},{... | collective-permute-start | bytes 1572872 | tf_op jit(solution)/shard_map/ppermute | solution.py:589
  492.0 64.9 %collective-permute-start.82 = (bf16[2,4,48,768]{3,2,1,0:T(8,128)(2,1)}, bf16[2,4,48,768]{3,2,1,0:T(8,128)(2,1)}, u32[]{:S(2)}, u32[]{:S(2)}) collective-permute-start(bf16[2,4,48,768]{3,2,1,0:T(8,128)(2,1)} %dynamic-slice_bitcast_fusion.4), channel_id=1, source_target_pairs={{0,16},{4,20},{8,24},{12,28},{16,0},{20,4},{24,8},{28,12},{1,17},{... | collective-permute-start | bytes 1769480 | tf_op jit(solution)/shard_map/ppermute | solution.py:623
  502.5 56.8 %collective-permute-start.46 = (bf16[2,4,48,768]{3,2,1,0:T(8,128)(2,1)}, bf16[2,4,48,768]{3,2,1,0:T(8,128)(2,1)}, u32[]{:S(2)}, u32[]{:S(2)}) collective-permute-start(bf16[2,4,48,768]{3,2,1,0:T(8,128)(2,1)} %dynamic-slice_bitcast_fusion.7), channel_id=1, source_target_pairs={{0,8},{4,12},{8,0},{12,4},{16,24},{20,28},{24,16},{28,20},{1,9},{5... | collective-permute-start | bytes 1769480 | tf_op jit(solution)/shard_map/ppermute | solution.py:623
  508.6 53.1 %collective-permute-start.73 = (bf16[2,4,48,768]{3,2,1,0:T(8,128)(2,1)}, bf16[2,4,48,768]{3,2,1,0:T(8,128)(2,1)}, u32[]{:S(2)}, u32[]{:S(2)}) collective-permute-start(bf16[2,4,48,768]{3,2,1,0:T(8,128)(2,1)} %dynamic-slice_bitcast_fusion.5), channel_id=1, source_target_pairs={{0,8},{4,12},{8,0},{12,4},{16,24},{20,28},{24,16},{28,20},{1,9},{5... | collective-permute-start | bytes 1769480 | tf_op jit(solution)/shard_map/ppermute | solution.py:623
  516.6 47.3 %collective-permute-start.55 = (bf16[2,4,48,768]{3,2,1,0:T(8,128)(2,1)}, bf16[2,4,48,768]{3,2,1,0:T(8,128)(2,1)}, u32[]{:S(2)}, u32[]{:S(2)}) collective-permute-start(bf16[2,4,48,768]{3,2,1,0:T(8,128)(2,1)} %dynamic-slice_bitcast_fusion.6), channel_id=1, source_target_pairs={{0,16},{4,20},{8,24},{12,28},{16,0},{20,4},{24,8},{28,12},{1,17},{... | collective-permute-start | bytes 1769480 | tf_op jit(solution)/shard_map/ppermute | solution.py:623
  541.8 137.5 %collective-permute-start.63 = (bf16[2,2,4,48,512]{4,3,2,1,0:T(8,128)(2,1)S(1)}, bf16[2,2,4,48,512]{4,3,2,1,0:T(8,128)(2,1)S(1)}, u32[]{:S(2)}, u32[]{:S(2)}) collective-permute-start(bf16[2,2,4,48,512]{4,3,2,1,0:T(8,128)(2,1)S(1)} %dynamic-slice_bitcast_fusion.3), channel_id=1, source_target_pairs={{0,4},{4,0},{8,12},{12,8},{16,20},{20,16},{24,28},{28,24},{1,5},{5... | collective-permute-start | bytes 2359304 | tf_op jit(solution)/shard_map/ppermute | solution.py:623
  556.9 143.2 %collective-permute-start.36 = (bf16[2,2,4,48,640]{4,3,2,1,0:T(8,128)(2,1)S(1)}, bf16[2,2,4,48,640]{4,3,2,1,0:T(8,128)(2,1)S(1)}, u32[]{:S(2)}, u32[]{:S(2)}) collective-permute-start(bf16[2,2,4,48,640]{4,3,2,1,0:T(8,128)(2,1)S(1)} %dynamic-slice_bitcast_fusion.2), channel_id=1, source_target_pairs={{0,4},{4,0},{8,12},{12,8},{16,20},{20,16},{24,28},{28,24},{1,5},{5... | collective-permute-start | bytes 2949128 | tf_op jit(solution)/shard_map/ppermute | solution.py:623
  559.3 121.8 %collective-permute-start.91 = (bf16[5,2,96,512]{3,2,0,1:T(8,128)(2,1)S(1)}, bf16[5,2,96,512]{3,2,0,1:T(8,128)(2,1)S(1)}, u32[]{:S(2)}, u32[]{:S(2)}) collective-permute-start(bf16[5,2,96,512]{3,2,0,1:T(8,128)(2,1)S(1)} %fusion.18), channel_id=1, source_target_pairs={{0,8},{4,12},{8,0},{12,4},{16,24},{20,28},{24,16},{28,20},{1,9},{5... | collective-permute-start | bytes 2949128 | tf_op jit(solution)/shard_map/ppermute | solution.py:623
  561.7 27.0 %collective-permute-start.83 = (bf16[4,48,768]{2,1,0:T(8,128)(2,1)S(1)}, bf16[4,48,768]{2,1,0:T(8,128)(2,1)S(1)}, u32[]{:S(2)}, u32[]{:S(2)}) collective-permute-start(bf16[4,48,768]{2,1,0:T(8,128)(2,1)S(1)} %dynamic-slice_bitcast_fusion.10), channel_id=1, source_target_pairs={{0,8},{4,12},{8,0},{12,4},{16,24},{20,28},{24,16},{28,20},{1,9},{5... | collective-permute-start | bytes 884744 | tf_op jit(solution)/shard_map/ppermute | solution.py:623
  563.9 27.0 %collective-permute-start.47 = (bf16[4,48,768]{2,1,0:T(8,128)(2,1)S(1)}, bf16[4,48,768]{2,1,0:T(8,128)(2,1)S(1)}, u32[]{:S(2)}, u32[]{:S(2)}) collective-permute-start(bf16[4,48,768]{2,1,0:T(8,128)(2,1)S(1)} %dynamic-slice_bitcast_fusion.13), channel_id=1, source_target_pairs={{0,16},{4,20},{8,24},{12,28},{16,0},{20,4},{24,8},{28,12},{1,17},{... | collective-permute-start | bytes 884744 | tf_op jit(solution)/shard_map/ppermute | solution.py:623
  673.5 24.7 %collective-permute-start.93 = (bf16[5,2,96,512]{3,2,0,1:T(8,128)(2,1)S(1)}, bf16[5,2,96,512]{3,2,0,1:T(8,128)(2,1)S(1)}, u32[]{:S(2)}, u32[]{:S(2)}) collective-permute-start(bf16[5,2,96,512]{3,2,0,1:T(8,128)(2,1)S(1)} %fusion.20), channel_id=1, source_target_pairs={{0,16},{4,20},{8,24},{12,28},{16,0},{20,4},{24,8},{28,12},{1,17},{... | collective-permute-start | bytes 2949128 | tf_op jit(solution)/shard_map/ppermute | solution.py:623
  677.8 24.7 %collective-permute-start.96 = (bf16[5,2,96,512]{3,2,0,1:T(8,128)(2,1)S(1)}, bf16[5,2,96,512]{3,2,0,1:T(8,128)(2,1)S(1)}, u32[]{:S(2)}, u32[]{:S(2)}) collective-permute-start(bf16[5,2,96,512]{3,2,0,1:T(8,128)(2,1)S(1)} %fusion.22), channel_id=1, source_target_pairs={{0,8},{4,12},{8,0},{12,4},{16,24},{20,28},{24,16},{28,20},{1,9},{5... | collective-permute-start | bytes 2949128 | tf_op jit(solution)/shard_map/ppermute | solution.py:623
  679.4 39.8 %collective-permute-start.98 = (bf16[5,2,96,512]{3,2,0,1:T(8,128)(2,1)S(1)}, bf16[5,2,96,512]{3,2,0,1:T(8,128)(2,1)S(1)}, u32[]{:S(2)}, u32[]{:S(2)}) collective-permute-start(bf16[5,2,96,512]{3,2,0,1:T(8,128)(2,1)S(1)} %fusion.24), channel_id=1, source_target_pairs={{0,16},{4,20},{8,24},{12,28},{16,0},{20,4},{24,8},{28,12},{1,17},{... | collective-permute-start | bytes 2949128 | tf_op jit(solution)/shard_map/ppermute | solution.py:623
  681.1 42.9 %collective-permute-start.101 = (bf16[5,2,96,512]{3,2,0,1:T(8,128)(2,1)S(1)}, bf16[5,2,96,512]{3,2,0,1:T(8,128)(2,1)S(1)}, u32[]{:S(2)}, u32[]{:S(2)}) collective-permute-start(bf16[5,2,96,512]{3,2,0,1:T(8,128)(2,1)S(1)} %fusion.26), channel_id=1, source_target_pairs={{0,8},{4,12},{8,0},{12,4},{16,24},{20,28},{24,16},{28,20},{1,9},{5... | collective-permute-start | bytes 2949128 | tf_op jit(solution)/shard_map/ppermute | solution.py:623
  698.1 63.2 %collective-permute-start.103 = (bf16[5,2,96,512]{3,2,0,1:T(8,128)(2,1)S(1)}, bf16[5,2,96,512]{3,2,0,1:T(8,128)(2,1)S(1)}, u32[]{:S(2)}, u32[]{:S(2)}) collective-permute-start(bf16[5,2,96,512]{3,2,0,1:T(8,128)(2,1)S(1)} %fusion.28), channel_id=1, source_target_pairs={{0,16},{4,20},{8,24},{12,28},{16,0},{20,4},{24,8},{28,12},{1,17},{... | collective-permute-start | bytes 2949128 | tf_op jit(solution)/shard_map/ppermute | solution.py:623
  700.0 23.4 %collective-permute-start.64 = (bf16[2,4,48,512]{3,2,1,0:T(8,128)(2,1)S(1)}, bf16[2,4,48,512]{3,2,1,0:T(8,128)(2,1)S(1)}, u32[]{:S(2)}, u32[]{:S(2)}) collective-permute-start(bf16[2,4,48,512]{3,2,1,0:T(8,128)(2,1)S(1)} %dynamic-slice_bitcast_fusion.9), channel_id=1, source_target_pairs={{0,8},{4,12},{8,0},{12,4},{16,24},{20,28},{24,16},{28,20},{1,9},{5... | collective-permute-start | bytes 1179656 | tf_op jit(solution)/shard_map/ppermute | solution.py:623
  702.5 65.5 %collective-permute-start.37 = (bf16[2,4,48,640]{3,2,1,0:T(8,128)(2,1)S(1)}, bf16[2,4,48,640]{3,2,1,0:T(8,128)(2,1)S(1)}, u32[]{:S(2)}, u32[]{:S(2)}) collective-permute-start(bf16[2,4,48,640]{3,2,1,0:T(8,128)(2,1)S(1)} %dynamic-slice_bitcast_fusion.8), channel_id=1, source_target_pairs={{0,16},{4,20},{8,24},{12,28},{16,0},{20,4},{24,8},{28,12},{1,17},{... | collective-permute-start | bytes 1474568 | tf_op jit(solution)/shard_map/ppermute | solution.py:623
  719.2 50.6 %collective-permute-start.92 = (bf16[5,96,512]{2,1,0:T(8,128)(2,1)S(1)}, bf16[5,96,512]{2,1,0:T(8,128)(2,1)S(1)}, u32[]{:S(2)}, u32[]{:S(2)}) collective-permute-start(bf16[5,96,512]{2,1,0:T(8,128)(2,1)S(1)} %fusion.39), channel_id=1, source_target_pairs={{0,16},{4,20},{8,24},{12,28},{16,0},{20,4},{24,8},{28,12},{1,17},{... | collective-permute-start | bytes 1474568 | tf_op jit(solution)/shard_map/ppermute | solution.py:623
  723.4 48.2 %collective-permute-start.94 = (bf16[5,96,512]{2,1,0:T(8,128)(2,1)S(1)}, bf16[5,96,512]{2,1,0:T(8,128)(2,1)S(1)}, u32[]{:S(2)}, u32[]{:S(2)}) collective-permute-start(bf16[5,96,512]{2,1,0:T(8,128)(2,1)S(1)} %fusion.41), channel_id=1, source_target_pairs={{0,8},{4,12},{8,0},{12,4},{16,24},{20,28},{24,16},{28,20},{1,9},{5... | collective-permute-start | bytes 1474568 | tf_op jit(solution)/shard_map/ppermute | solution.py:623
  724.0 33.0 %collective-permute-start.65 = (bf16[4,48,512]{2,1,0:T(8,128)(2,1)S(1)}, bf16[4,48,512]{2,1,0:T(8,128)(2,1)S(1)}, u32[]{:S(2)}, u32[]{:S(2)}) collective-permute-start(bf16[4,48,512]{2,1,0:T(8,128)(2,1)S(1)} %dynamic-slice_bitcast_fusion.15), channel_id=1, source_target_pairs={{0,16},{4,20},{8,24},{12,28},{16,0},{20,4},{24,8},{28,12},{1,17},{... | collective-permute-start | bytes 589832 | tf_op jit(solution)/shard_map/ppermute | solution.py:623
  763.0 11.0 %collective-permute-start.97 = (bf16[5,96,512]{2,1,0:T(8,128)(2,1)S(1)}, bf16[5,96,512]{2,1,0:T(8,128)(2,1)S(1)}, u32[]{:S(2)}, u32[]{:S(2)}) collective-permute-start(bf16[5,96,512]{2,1,0:T(8,128)(2,1)S(1)} %fusion.43), channel_id=1, source_target_pairs={{0,16},{4,20},{8,24},{12,28},{16,0},{20,4},{24,8},{28,12},{1,17},{... | collective-permute-start | bytes 1474568 | tf_op jit(solution)/shard_map/ppermute | solution.py:623
  768.0 11.8 %collective-permute-start.102 = (bf16[5,96,512]{2,1,0:T(8,128)(2,1)S(1)}, bf16[5,96,512]{2,1,0:T(8,128)(2,1)S(1)}, u32[]{:S(2)}, u32[]{:S(2)}) collective-permute-start(bf16[5,96,512]{2,1,0:T(8,128)(2,1)S(1)} %fusion.47), channel_id=1, source_target_pairs={{0,16},{4,20},{8,24},{12,28},{16,0},{20,4},{24,8},{28,12},{1,17},{... | collective-permute-start | bytes 1474568 | tf_op jit(solution)/shard_map/ppermute | solution.py:623
  769.8 11.6 %collective-permute-start.104 = (bf16[5,96,512]{2,1,0:T(8,128)(2,1)S(1)}, bf16[5,96,512]{2,1,0:T(8,128)(2,1)S(1)}, u32[]{:S(2)}, u32[]{:S(2)}) collective-permute-start(bf16[5,96,512]{2,1,0:T(8,128)(2,1)S(1)} %fusion.49), channel_id=1, source_target_pairs={{0,8},{4,12},{8,0},{12,4},{16,24},{20,28},{24,16},{28,20},{1,9},{5... | collective-permute-start | bytes 1474568 | tf_op jit(solution)/shard_map/ppermute | solution.py:623
  771.6 25.3 %collective-permute-start.67 = (bf16[48,512]{1,0:T(8,128)(2,1)S(1)}, bf16[48,512]{1,0:T(8,128)(2,1)S(1)}, u32[]{:S(2)}, u32[]{:S(2)}) collective-permute-start(bf16[48,512]{1,0:T(8,128)(2,1)S(1)} %get-tuple-element.216), channel_id=1, source_target_pairs={{1,0},{2,1},{3,2},{5,4},{6,5},{7,6},{9,8},{10,9},{11,10},{13,12},{... | collective-permute-start | bytes 147464 | tf_op jit(solution)/shard_map/ppermute | solution.py:589
  774.0 22.9 %collective-permute-start.70 = (bf16[48,512]{1,0:T(8,128)(2,1)S(1)}, bf16[48,512]{1,0:T(8,128)(2,1)S(1)}, u32[]{:S(2)}, u32[]{:S(2)}) collective-permute-start(bf16[48,512]{1,0:T(8,128)(2,1)S(1)} %get-tuple-element.217), channel_id=1, source_target_pairs={{0,1},{1,2},{2,3},{4,5},{5,6},{6,7},{8,9},{9,10},{10,11},{12,13},{... | collective-permute-start | bytes 147464 | tf_op jit(solution)/shard_map/ppermute | solution.py:585
  797.0 11.8 %collective-permute-start.68 = (bf16[48,512]{1,0:T(8,128)(2,1)S(1)}, bf16[48,512]{1,0:T(8,128)(2,1)S(1)}, u32[]{:S(2)}, u32[]{:S(2)}) collective-permute-start(bf16[48,512]{1,0:T(8,128)(2,1)S(1)} %get-tuple-element.214), channel_id=1, source_target_pairs={{1,0},{2,1},{3,2},{5,4},{6,5},{7,6},{9,8},{10,9},{11,10},{13,12},{... | collective-permute-start | bytes 147464 | tf_op jit(solution)/shard_map/ppermute | solution.py:589
  (135 other events, 1420.5 us)

commit v2 on v1

v2 whole, which is shorter than its diff:
```python
import functools

import jax
import jax.numpy as jnp
import numpy as np
from jax import lax
from jax.experimental import pallas as pl
from jax.experimental.pallas import tpu as pltpu
from jax.sharding import PartitionSpec as P

HDIM = 64
LANES = 128
ATTENTION_SCALE = 0.015625
RESIDUAL_SCALE = 0.22
NORM_EPSILON = 1e-06
ROTARY_BASE = 10000.0
MASKED_SCORE = -1e30
BF16 = jnp.bfloat16
F32 = jnp.float32
NN = (((1,), (0,)), ((), ()))
NT = (((1,), (1,)), ((), ()))
TN = (((0,), (0,)), ((), ()))
VMEM_LIMIT = 56 * 1024 * 1024


def dot(left, right, dims=NN):
    return lax.dot_general(left, right, dims, preferred_element_type=F32)


def round_up(count, unit):
    return (count + unit - 1) // unit * unit


def low_lanes(rows):
    return lax.broadcasted_iota(jnp.int32, (rows, LANES), 1) < HDIM


def partner_lanes(slab):
    lane = lax.broadcasted_iota(jnp.int32, slab.shape, 1) % HDIM
    half = HDIM // 2
    return jnp.where(lane < half, pltpu.roll(slab, LANES - half, 1), pltpu.roll(slab, half, 1))


def vmem():
    return pl.BlockSpec(memory_space=pltpu.VMEM)


def params(**more):
    return pltpu.CompilerParams(vmem_limit_bytes=VMEM_LIMIT, **more)


def cost(microseconds):
    return pl.CostEstimate(flops=int(microseconds * 1e6), bytes_accessed=0, transcendentals=0)


def rotary_tables(length):
    half = HDIM // 2
    inverse = np.float32(ROTARY_BASE) ** (np.float32(-2.0) * np.arange(half, dtype=np.float32) / np.float32(HDIM))
    angles = np.arange(length, dtype=np.float32)[:, None] * np.tile(inverse, LANES // half)[None, :]
    angles = angles.astype(np.float32).astype(np.float64)
    sign = np.where(np.arange(LANES) % HDIM < half, -1.0, 1.0)
    return np.cos(angles).astype(np.float32), (np.sin(angles) * sign).astype(np.float32)


def extend_kernel(cotangent_ref, routes_ref, out_ref):
    rows, top_count = routes_ref.shape
    width = cotangent_ref.shape[1]
    lane = lax.broadcasted_iota(jnp.int32, (rows, LANES), 1)
    chosen = jnp.zeros((rows, LANES), F32)
    for k in range(top_count):
        chosen = chosen + jnp.where(routes_ref[:, k : k + 1] == lane, 1.0, 0.0)
    first = lax.broadcasted_iota(jnp.int32, (rows, rows), 0)
    second = lax.broadcasted_iota(jnp.int32, (rows, rows), 1)
    earlier = jnp.where(second < first, 1.0, 0.0).astype(BF16)
    rank = dot(earlier, chosen.astype(BF16))
    out_ref[:, :width] = cotangent_ref[...]
    out_ref[:, width:] = jnp.where(chosen > 0.5, rank, -1.0).astype(BF16)


def front_kernel(tokens_ref, gain_ref, key_ref, value_ref, cos_ref, sin_ref, segments_ref, normed_ref, factor_ref, kv_ref):
    hidden = tokens_ref[...].astype(F32)
    factor = lax.rsqrt(jnp.mean(hidden * hidden, axis=-1, keepdims=True) + NORM_EPSILON)
    normed = (hidden * factor * gain_ref[...]).astype(BF16)
    normed_ref[...] = normed
    factor_ref[...] = factor
    keys = dot(normed, key_ref[...])
    values = dot(normed, value_ref[...])
    cosine, sine = cos_ref[...], sin_ref[...]
    rows = hidden.shape[0]
    low = low_lanes(rows)
    for i in range(keys.shape[1] // LANES):
        slab = keys[:, i * LANES : (i + 1) * LANES]
        slab = slab * cosine + partner_lanes(slab) * sine
        value_slab = values[:, i * LANES : (i + 1) * LANES]
        even, odd = 2 * i * rows, (2 * i + 1) * rows
        kv_ref[even : even + rows, :] = jnp.where(low, slab, pltpu.roll(value_slab, HDIM, 1)).astype(BF16)
        kv_ref[odd : odd + rows, :] = jnp.where(low, pltpu.roll(slab, HDIM, 1), value_slab).astype(BF16)
    kv_ref[keys.shape[1] // HDIM * rows :, :] = segments_ref[...]


def query_kernel(normed_ref, query_ref, cos_ref, sin_ref, out_ref):
    raw = dot(normed_ref[...], query_ref[...])
    cosine, sine = cos_ref[...], sin_ref[...]
    for i in range(raw.shape[1] // LANES):
        slab = raw[:, i * LANES : (i + 1) * LANES]
        slab = slab * cosine + partner_lanes(slab) * sine
        out_ref[:, i * LANES : (i + 1) * LANES] = (slab.astype(BF16).astype(F32) * ATTENTION_SCALE).astype(BF16)


def fill_bias(bias_ref, need_ref, place_ref, seg_column, seg_refs):
    slots, rows, keys = bias_ref.shape
    for k in range(slots):
        for j in range(keys // LANES):
            lanes = slice(j * LANES, (j + 1) * LANES)
            allowed = seg_column == seg_refs[k][j : j + 1, :].astype(F32)
            if k == 0:
                allowed = allowed & (
                    lax.broadcasted_iota(jnp.int32, (rows, LANES), 1) + j * LANES
                    <= lax.broadcasted_iota(jnp.int32, (rows, LANES), 0)
                )
            bias_ref[k, :, lanes] = jnp.where(allowed, 0.0, MASKED_SCORE)
    first = jnp.min(seg_column)
    need = jnp.int32(1)
    for k in range(1, slots):
        last = jnp.max(seg_refs[k][: keys // LANES, :].astype(F32))
        need = jnp.where((last >= first) & (k <= place_ref[0]), k + 1, need)
    need_ref[0] = need


def head_slab(block, head, upper):
    slab = block[:, (head // 2) * LANES : (head // 2 + 1) * LANES].astype(F32)
    low = low_lanes(slab.shape[0])
    if (head % 2 == 1) != upper:
        slab = pltpu.roll(slab, HDIM, 1)
    return jnp.where(low != upper, slab, 0.0)


def attend_kernel(slots, ratio, place_ref, query_ref, seg_column_ref, *refs):
    kv_refs, seg_refs = refs[:slots], refs[slots : 2 * slots]
    attended_ref, lse_ref, top_ref, bias_ref, stacked_ref, acc_ref, max_ref, sum_ref, need_ref = refs[2 * slots :]
    rows = query_ref.shape[0]
    low = low_lanes(rows)
    lane = lax.broadcasted_iota(jnp.int32, (rows, LANES), 1)

    @pl.when(pl.program_id(0) == 0)
    def _():
        fill_bias(bias_ref, need_ref, place_ref, seg_column_ref[...], seg_refs)

    need = need_ref[0]

    outs = []
    lse_all = jnp.zeros((rows, LANES), F32)
    top_all = jnp.zeros((8, LANES), F32)
    for group in range(2):
        for r in range(ratio):
            stacked_ref[r * rows : (r + 1) * rows, :] = head_slab(
                query_ref, group * ratio + r, False
            ).astype(BF16)
        for k in range(slots):

            def step(k=k):
                kv = kv_refs[k][group * rows : (group + 1) * rows, :]
                scores = dot(stacked_ref[...], kv, NT).reshape(ratio, rows, rows)
                scores = (scores + bias_ref[k][None]).reshape(ratio * rows, rows)
                top = jnp.max(scores, axis=-1, keepdims=True)
                if k == 0:
                    weights = jnp.exp(scores - top)
                    max_ref[...] = top
                    sum_ref[...] = jnp.sum(weights, axis=-1, keepdims=True)
                    acc_ref[...] = dot(weights.astype(BF16), kv)
                else:
                    before = max_ref[...]
                    top = jnp.maximum(top, before)
                    shrink = jnp.exp(before - top)
                    weights = jnp.exp(scores - top)
                    max_ref[...] = top
                    sum_ref[...] = sum_ref[...] * shrink + jnp.sum(weights, axis=-1, keepdims=True)
                    acc_ref[...] = acc_ref[...] * shrink + dot(weights.astype(BF16), kv)

            if k == 0:
                step()
            else:
                pl.when(k < need)(step)
        total = sum_ref[...]
        mixed = acc_ref[...] / total
        lse = max_ref[...] + jnp.log(total)
        for r in range(ratio):
            head = group * ratio + r
            outs.append(mixed[r * rows : (r + 1) * rows])
            lse_all = jnp.where(lane == head, lse[r * rows : (r + 1) * rows], lse_all)
            peak = jnp.max(max_ref[r * rows : (r + 1) * rows, :], axis=0, keepdims=True)
            top_all = jnp.where(lane[:8] == head, peak, top_all)
    for i in range(len(outs) // 2):
        attended_ref[:, i * LANES : (i + 1) * LANES] = jnp.where(
            low, pltpu.roll(outs[2 * i], HDIM, 1), outs[2 * i + 1]
        ).astype(BF16)
    lse_ref[0] = lse_all
    top_ref[0] = top_all


def kv_specs(slots, groups, rows):
    return [pl.BlockSpec((2 * rows, LANES), lambda s: (s, 0))] * slots + [
        pl.BlockSpec((16, LANES), lambda s: (groups * rows // 16, 0))
    ] * slots


def attend(queries, kv_slots, seg_column, place, groups):
    slots = len(kv_slots)
    rows, width = queries.shape
    ratio = width // HDIM // groups
    steps = groups // 2
    block = 2 * ratio * HDIM
    return pl.pallas_call(
        functools.partial(attend_kernel, slots, ratio),
        out_shape=(
            jax.ShapeDtypeStruct((rows, width), BF16),
            jax.ShapeDtypeStruct((steps, rows, LANES), F32),
            jax.ShapeDtypeStruct((steps, 8, LANES), F32),
        ),
        grid=(steps,),
        in_specs=[
            pl.BlockSpec(memory_space=pltpu.SMEM),
            pl.BlockSpec((rows, block), lambda s: (0, s)),
            pl.BlockSpec((rows, 1), lambda s: (0, 0)),
        ]
        + kv_specs(slots, groups, rows),
        out_specs=(
            pl.BlockSpec((rows, block), lambda s: (0, s)),
            pl.BlockSpec((1, rows, LANES), lambda s: (s, 0, 0)),
            pl.BlockSpec((1, 8, LANES), lambda s: (s, 0, 0)),
        ),
        scratch_shapes=[
            pltpu.VMEM((slots, rows, rows), F32),
            pltpu.VMEM((ratio * rows, LANES), BF16),
            pltpu.VMEM((ratio * rows, LANES), F32),
            pltpu.VMEM((ratio * rows, 1), F32),
            pltpu.VMEM((ratio * rows, 1), F32),
            pltpu.SMEM((1,), jnp.int32),
        ],
        compiler_params=params(),
        cost_estimate=cost(20),
        name="attend",
    )(place, queries, seg_column, *kv_slots, *kv_slots)


def attend_back_kernel(slots, ratio, place_ref, query_ref, attended_ref, grad_ref, lse_ref, cos_ref, sin_ref, seg_column_ref, *refs):
    kv_refs, seg_refs = refs[:slots], refs[slots : 2 * slots]
    refs = refs[2 * slots :]
    back_ref, dkv_refs = refs[0], refs[1 : slots + 1]
    bias_ref, query_s, grad_s, acc_ref, lse_s, delta_s, need_ref = refs[slots + 1 :]
    rows = query_ref.shape[0]
    low = low_lanes(rows)

    @pl.when(pl.program_id(0) == 0)
    def _():
        fill_bias(bias_ref, need_ref, place_ref, seg_column_ref[...], seg_refs)

    need = need_ref[0]

    outs = []
    for group in range(2):
        for r in range(ratio):
            head = group * ratio + r
            part = slice(r * rows, (r + 1) * rows)
            query_s[part, :] = head_slab(query_ref, head, False).astype(BF16)
            grad = head_slab(grad_ref, head, True)
            grad_s[part, :] = grad.astype(BF16)
            delta_s[part, :] = jnp.sum(grad * head_slab(attended_ref, head, True), axis=-1, keepdims=True)
            lse_s[part, :] = lse_ref[0, :, head : head + 1]
        for k in range(slots):

            def step(k=k):
                kv = kv_refs[k][group * rows : (group + 1) * rows, :]
                scores = dot(query_s[...], kv, NT).reshape(ratio, rows, rows)
                scores = (scores + bias_ref[k][None]).reshape(ratio * rows, rows)
                weights = jnp.exp(scores - lse_s[...])
                weight_grad = dot(grad_s[...], kv, NT)
                score_grad = (weights * (weight_grad - delta_s[...])).astype(BF16)
                query_part = dot(score_grad, kv)
                if k == 0:
                    acc_ref[...] = query_part
                else:
                    acc_ref[...] += query_part
                dkv_refs[k][group * rows : (group + 1) * rows, :] = (
                    dot(score_grad, query_s[...], TN) + dot(weights.astype(BF16), grad_s[...], TN)
                ).astype(BF16)

            if k == 0:
                step()
            else:
                pl.when(k < need)(step)

                @pl.when(k >= need)
                def _(k=k):
                    dkv_refs[k][group * rows : (group + 1) * rows, :] = jnp.zeros((rows, LANES), BF16)

        for r in range(ratio):
            outs.append(acc_ref[r * rows : (r + 1) * rows, :] * ATTENTION_SCALE)
    cosine, sine = cos_ref[...], sin_ref[...]
    for i in range(len(outs) // 2):
        slab = jnp.where(low, outs[2 * i], pltpu.roll(outs[2 * i + 1], HDIM, 1))
        slab = slab * cosine - partner_lanes(slab) * sine
        back_ref[:, i * LANES : (i + 1) * LANES] = slab.astype(BF16)


def attend_back(queries, attended, grad, lse, tables, kv_slots, seg_column, place, groups):
    slots = len(kv_slots)
    rows, width = queries.shape
    ratio = width // HDIM // groups
    steps = groups // 2
    block = 2 * ratio * HDIM
    whole = pl.BlockSpec((rows, LANES), lambda s: (0, 0))
    wide = pl.BlockSpec((rows, block), lambda s: (0, s))
    out = pl.pallas_call(
        functools.partial(attend_back_kernel, slots, ratio),
        out_shape=(jax.ShapeDtypeStruct((rows, width), BF16),)
        + (jax.ShapeDtypeStruct((groups * rows, LANES), BF16),) * slots,
        grid=(steps,),
        in_specs=[
            pl.BlockSpec(memory_space=pltpu.SMEM),
            wide,
            wide,
            wide,
            pl.BlockSpec((1, rows, LANES), lambda s: (s, 0, 0)),
            whole,
            whole,
            pl.BlockSpec((rows, 1), lambda s: (0, 0)),
        ]
        + kv_specs(slots, groups, rows),
        out_specs=(wide,) + (pl.BlockSpec((2 * rows, LANES), lambda s: (s, 0)),) * slots,
        scratch_shapes=[
            pltpu.VMEM((slots, rows, rows), F32),
            pltpu.VMEM((ratio * rows, LANES), BF16),
            pltpu.VMEM((ratio * rows, LANES), BF16),
            pltpu.VMEM((ratio * rows, LANES), F32),
            pltpu.VMEM((ratio * rows, 1), F32),
            pltpu.VMEM((ratio * rows, 1), F32),
            pltpu.SMEM((1,), jnp.int32),
        ],
        compiler_params=params(),
        cost_estimate=cost(2),
        name="attend_back",
    )(place, queries, attended, grad, lse, *tables, seg_column, *kv_slots, *kv_slots)
    return out[0], out[1:]


def unpack_kernel(own_ref, above_ref, cos_ref, sin_ref, key_ref, value_ref):
    rows = cos_ref.shape[0]
    low = low_lanes(rows)
    cosine, sine = cos_ref[...], sin_ref[...]
    for i in range(key_ref.shape[1] // LANES):
        even, odd = (
            own_ref[g * rows : (g + 1) * rows, :].astype(F32) + above_ref[g * rows : (g + 1) * rows, :].astype(F32)
            for g in (2 * i, 2 * i + 1)
        )
        slab = jnp.where(low, even, pltpu.roll(odd, HDIM, 1))
        slab = slab * cosine - partner_lanes(slab) * sine
        key_ref[:, i * LANES : (i + 1) * LANES] = slab.astype(BF16)
        value_ref[:, i * LANES : (i + 1) * LANES] = jnp.where(
            low, pltpu.roll(even, HDIM, 1), odd
        ).astype(BF16)


def expert_kernel(blocks, slot_rows, local_experts, place_ref, router_ref, gate_ref, up_ref, down_ref, *refs):
    sources = 2 * blocks - 1
    normed_in, cot_in = refs[:sources], refs[sources : 2 * sources]
    refs = refs[2 * sources :]
    xs_ref, cs_ref, hs_ref, gate_grad_ref, up_grad_ref, hit_ref = refs[:6]
    grad_out, router_grad_ref = refs[6:8]
    x_all, c_all, info, gates, back, grad_acc, grad_low, sems, out_sem = refs[8:]
    step = pl.program_id(0)
    rows, width = x_all.shape[1:]
    expert_pad = router_ref.shape[0]
    first_expert = place_ref[0]
    mine = pl.ds(first_expert + step, 1)

    def source_copies(i, s):
        return (
            pltpu.make_async_copy(normed_in[s], x_all.at[i], sems.at[0, i]),
            pltpu.make_async_copy(cot_in[s], c_all.at[i], sems.at[1, i]),
        )

    @pl.when(step == 0)
    def _():
        for i in range(blocks):
            for s in range(sources):

                @pl.when(place_ref[1 + i] == s)
                def _(i=i, s=s):
                    for copy in source_copies(i, s):
                        copy.start()

        for i in range(blocks):
            for copy in source_copies(i, 0):
                copy.wait()
        same = jnp.where(
            lax.broadcasted_iota(jnp.int32, (rows, rows), 0) == lax.broadcasted_iota(jnp.int32, (rows, rows), 1),
            1.0,
            0.0,
        ).astype(BF16)
        for i in range(blocks):
            info[i] = dot(c_all[i, :, width:], same, TN)
            logits = dot(router_ref[...], x_all[i], NT)
            logits = jnp.where(info[i, :expert_pad, :] >= 0, logits, MASKED_SCORE)
            weights = jnp.exp(logits - jnp.max(logits, axis=0, keepdims=True))
            gates[i] = weights / jnp.sum(weights, axis=0, keepdims=True)
        back[...] = jnp.zeros_like(back)
        grad_acc[...] = jnp.zeros_like(grad_acc)

    slot_ids = lax.broadcasted_iota(jnp.int32, (slot_rows, rows), 0).astype(F32)
    gate_slots = []
    for i in range(blocks):
        hit = slot_ids == info[i, mine, :]
        part = slice(i * slot_rows, (i + 1) * slot_rows)
        gate_slots.append(
            jnp.sum(jnp.where(hit, gates[i, mine, :], 0.0), axis=-1, keepdims=True)
        )
        hit = jnp.where(hit, 1.0, 0.0).astype(BF16)
        hit_ref[0, part, :] = hit
        xs_ref[0, part, :] = dot(hit, x_all[i]).astype(BF16)
        cs_ref[0, part, :] = dot(hit, c_all[i, :, :width]).astype(BF16)
    gate_slot = jnp.concatenate(gate_slots, axis=0) * RESIDUAL_SCALE
    gate_pre = dot(xs_ref[0], gate_ref[0])
    up_pre = dot(xs_ref[0], up_ref[0])
    raw_grad = dot(cs_ref[0], down_ref[0])
    sigmoid = 1.0 / (1.0 + jnp.exp(-gate_pre))
    active = gate_pre * sigmoid
    expert_hidden = (active * up_pre).astype(BF16).astype(F32)
    hs_ref[0] = (expert_hidden * gate_slot).astype(BF16)
    back_slot = jnp.sum(expert_hidden * raw_grad, axis=-1, keepdims=True) * RESIDUAL_SCALE
    hidden_grad = raw_grad * gate_slot
    gate_grad_ref[0] = (hidden_grad * up_pre * sigmoid * (1.0 + gate_pre * (1.0 - sigmoid))).astype(BF16)
    up_grad_ref[0] = (hidden_grad * active).astype(BF16)
    slot_grad = (
        dot(gate_grad_ref[0], gate_ref[0], NT) + dot(up_grad_ref[0], up_ref[0], NT)
    ).astype(BF16)
    for i in range(blocks):
        part = slice(i * slot_rows, (i + 1) * slot_rows)
        hit = hit_ref[0, part, :]
        back_row = jnp.sum(hit.astype(F32) * back_slot[part], axis=0, keepdims=True)
        back[i, mine, :] = back_row * gates[i, mine, :]
        grad_acc[i] += dot(hit, slot_grad[part], TN)

    @pl.when(step == local_experts - 1)
    def _():
        router_sum = None
        for i in range(blocks):
            share = back[i]
            logit_grad = (share - gates[i] * jnp.sum(share, axis=0, keepdims=True)).astype(BF16)
            grad_low[i] = (grad_acc[i] + dot(logit_grad, router_ref[...], TN)).astype(BF16)
            part = dot(logit_grad, x_all[i])
            router_sum = part if router_sum is None else router_sum + part
        router_grad_ref[...] = router_sum

        def copy(i):
            return pltpu.make_async_copy(grad_low.at[i], grad_out.at[place_ref[1 + blocks + i]], out_sem.at[i])

        for i in range(blocks):
            copy(i).start()
        for i in range(blocks):
            copy(i).wait()


def run_experts(place, router_t, gate_weight, up_weight, down_weight, normed, cots, slot_rows):
    local_experts, width, hidden = gate_weight.shape
    sources = len(normed)
    blocks = (sources + 1) // 2
    rows = normed[0].shape[0]
    expert_pad = router_t.shape[0]
    slots = blocks * slot_rows
    anywhere = pl.BlockSpec(memory_space=pl.ANY)
    weight_spec = pl.BlockSpec((1, width, hidden), lambda e, place: (e, 0, 0))

    def slot_spec(columns):
        return pl.BlockSpec((1, slots, columns), lambda e, place: (e, 0, 0))

    def slot_shape(columns):
        return jax.ShapeDtypeStruct((local_experts, slots, columns), BF16)

    out = pl.pallas_call(
        functools.partial(expert_kernel, blocks, slot_rows, local_experts),
        out_shape=(
            slot_shape(width),
            slot_shape(width),
            slot_shape(hidden),
            slot_shape(hidden),
            slot_shape(hidden),
            slot_shape(rows),
        )
        + (jax.ShapeDtypeStruct((blocks, rows, width), BF16), jax.ShapeDtypeStruct((expert_pad, width), F32)),
        grid_spec=pltpu.PrefetchScalarGridSpec(
            num_scalar_prefetch=1,
            grid=(local_experts,),
            in_specs=[pl.BlockSpec((expert_pad, width), lambda e, place: (0, 0))]
            + [weight_spec] * 3
            + [anywhere] * (2 * sources),
            out_specs=(
                slot_spec(width),
                slot_spec(width),
                slot_spec(hidden),
                slot_spec(hidden),
                slot_spec(hidden),
                slot_spec(rows),
            )
            + (anywhere, pl.BlockSpec((expert_pad, width), lambda e, place: (0, 0))),
            scratch_shapes=[
                pltpu.VMEM((blocks, rows, width), BF16),
                pltpu.VMEM((blocks, rows, width + LANES), BF16),
                pltpu.VMEM((blocks, LANES, rows), F32),
                pltpu.VMEM((blocks, expert_pad, rows), F32),
                pltpu.VMEM((blocks, expert_pad, rows), F32),
                pltpu.VMEM((blocks, rows, width), F32),
                pltpu.VMEM((blocks, rows, width), BF16),
                pltpu.SemaphoreType.DMA((2, blocks)),
                pltpu.SemaphoreType.DMA((blocks,)),
            ],
        ),
        compiler_params=params(),
        cost_estimate=cost(45),
        name="experts",
    )(place, router_t, gate_weight, up_weight, down_weight, *normed, *cots)
    return out[:6], out[6], out[7]


def mixture_kernel(blocks, slot_rows, local_experts, order_ref, down_ref, hs_ref, hit_ref, mix_out, mix_acc, mix_low, out_sem):
    step = pl.program_id(0)

    @pl.when(step == 0)
    def _():
        mix_acc[...] = jnp.zeros_like(mix_acc)

    slot_out = dot(hs_ref[0], down_ref[0], NT).astype(BF16)
    for i in range(blocks):
        part = slice(i * slot_rows, (i + 1) * slot_rows)
        mix_acc[i] += dot(hit_ref[0, part, :], slot_out[part], TN)

    @pl.when(step == local_experts - 1)
    def _():
        def copy(i):
            return pltpu.make_async_copy(mix_low.at[i], mix_out.at[order_ref[i]], out_sem.at[i])

        for i in range(blocks):
            mix_low[i] = mix_acc[i].astype(BF16)
            copy(i).start()
        for i in range(blocks):
            copy(i).wait()


def run_mixture(order, down_weight, saved, slot_rows):
    hs, hit = saved[2], saved[5]
    local_experts, width, hidden = down_weight.shape
    slots, rows = hit.shape[1:]
    blocks = slots // slot_rows
    return pl.pallas_call(
        functools.partial(mixture_kernel, blocks, slot_rows, local_experts),
        out_shape=jax.ShapeDtypeStruct((blocks, rows, width), BF16),
        grid_spec=pltpu.PrefetchScalarGridSpec(
            num_scalar_prefetch=1,
            grid=(local_experts,),
            in_specs=[
                pl.BlockSpec((1, width, hidden), lambda e, order: (e, 0, 0)),
                pl.BlockSpec((1, slots, hidden), lambda e, order: (e, 0, 0)),
                pl.BlockSpec((1, slots, rows), lambda e, order: (e, 0, 0)),
            ],
            out_specs=pl.BlockSpec(memory_space=pl.ANY),
            scratch_shapes=[
                pltpu.VMEM((blocks, rows, width), F32),
                pltpu.VMEM((blocks, rows, width), BF16),
                pltpu.SemaphoreType.DMA((blocks,)),
            ],
        ),
        compiler_params=params(),
        cost_estimate=cost(10),
        name="mixture",
    )(order, down_weight, hs, hit)


def turn_rows(block, sides_ref, owned):
    width = block.shape[1]
    chunk = int(np.lcm(2 * owned, LANES))
    for c in range(width // chunk):
        turned = block[:, c * chunk : (c + 1) * chunk].T
        for o in range(chunk // owned):
            owner = c * (chunk // owned) + o
            spot = owner // 2 * owned
            sides_ref[owner % 2, spot : spot + owned, :] = turned[o * owned : (o + 1) * owned]


def expert_grad_kernel(xs_ref, cs_ref, hs_ref, gate_grad_ref, up_grad_ref, out_ref, turned):
    owners, owned = out_ref.shape[0], out_ref.shape[3]
    for left_ref, rights in ((xs_ref, ((0, gate_grad_ref), (1, up_grad_ref))), (cs_ref, ((2, hs_ref),))):
        turned[...] = left_ref[0].T
        for w, right_ref in rights:
            grad = dot(turned[...], right_ref[0]).astype(BF16)
            for o in range(owners):
                out_ref[o, w, 0] = grad[o * owned : (o + 1) * owned]


def run_expert_grads(saved, owners):
    xs, cs, hs, gate_grad, up_grad, _ = saved
    local_experts, slots, width = xs.shape
    hidden = hs.shape[2]
    owned = width // owners
    wide = pl.BlockSpec((1, slots, width), lambda e: (e, 0, 0))
    narrow = pl.BlockSpec((1, slots, hidden), lambda e: (e, 0, 0))
    return pl.pallas_call(
        expert_grad_kernel,
        out_shape=jax.ShapeDtypeStruct((owners, 3, local_experts, owned, hidden), BF16),
        grid=(local_experts,),
        in_specs=[wide, wide, narrow, narrow, narrow],
        out_specs=pl.BlockSpec((owners, 3, 1, owned, hidden), lambda e: (0, 0, e, 0, 0)),
        scratch_shapes=[pltpu.VMEM((width, slots), BF16)],
        compiler_params=params(),
        cost_estimate=cost(30),
        name="expert_grads",
    )(xs, cs, hs, gate_grad, up_grad)


def dense_grad_kernel(pairs, place_ref, *refs):
    lefts, rights = refs[:pairs], refs[pairs : 2 * pairs]
    smalls = refs[2 * pairs : -3]
    keep_ref, send_ref, sides = refs[-3:]
    owned = keep_ref.shape[1]
    bit = place_ref[0] % 2
    column = 0
    for i in range(pairs):
        if i == 0 or lefts[i] is not lefts[i - 1]:
            turn_rows(lefts[i][...], sides, owned)
        columns = rights[i].shape[1]
        for out_ref, side in ((send_ref, 1 - bit), (keep_ref, bit)):
            grad = dot(sides[side], rights[i][...]).astype(BF16)
            for q in range(keep_ref.shape[0]):
                out_ref[q, :, column : column + columns] = grad[q * owned : (q + 1) * owned]
        column += columns
    if smalls:
        rows = jnp.concatenate([ref[...] for ref in smalls], axis=0)
        rows = jnp.concatenate([rows, jnp.zeros((LANES - rows.shape[0], rows.shape[1]), F32)], axis=0)
        turned = rows.T.astype(BF16)
        for owner in range(2 * keep_ref.shape[0]):
            piece = turned[owner * owned : (owner + 1) * owned]

            @pl.when(bit == owner % 2)
            def _(owner=owner, piece=piece):
                keep_ref[owner // 2, :, column:] = piece

            @pl.when(bit != owner % 2)
            def _(owner=owner, piece=piece):
                send_ref[owner // 2, :, column:] = piece


def dense_grads(dp_word, pairs, owners, smalls=()):
    rows, width = pairs[0][0].shape
    columns = sum(right.shape[1] for _, right in pairs) + (LANES if smalls else 0)
    return pl.pallas_call(
        functools.partial(dense_grad_kernel, len(pairs)),
        out_shape=(jax.ShapeDtypeStruct((owners // 2, width // owners, columns), BF16),) * 2,
        in_specs=[pl.BlockSpec(memory_space=pltpu.SMEM)] + [vmem()] * (2 * len(pairs) + len(smalls)),
        out_specs=(vmem(),) * 2,
        scratch_shapes=[pltpu.VMEM((2, width // 2, rows), BF16)],
        compiler_params=params(),
        cost_estimate=cost(4),
        name="dense_grads",
    )(dp_word, *(left for left, _ in pairs), *(right for _, right in pairs), *smalls)


def line_up(value, size):
    return lax.ppermute(value, "expert", [(i, i + 1) for i in range(size - 1)])


def line_down(value, size):
    return lax.ppermute(value, "expert", [(i + 1, i) for i in range(size - 1)])


def line_gather(value, size):
    below, above = [], []
    up, down = value, value
    for _ in range(size - 1):
        up = line_up(up, size)
        down = line_down(down, size)
        below.append(up)
        above.append(down)
    return [value] + below + above


def add_low(*terms):
    total = terms[0].astype(F32)
    for term in terms[1:]:
        total = total + term.astype(F32)
    return total.astype(BF16)


def flip(value, bit, size):
    return lax.ppermute(value, "dp", [(i, i ^ bit) for i in range(size)])


def halve(terms, bit, left, dp_place):
    axis = left.index(bit)
    own = (dp_place >> bit) & 1
    return tuple(
        add_low(*(lax.dynamic_index_in_dim(t, side, axis, keepdims=False) for t in terms)) for side in (own, 1 - own)
    )


def start_spread(routes):
    return [
        tuple(t.reshape((2,) * (t.shape[0].bit_length() - 1) + t.shape[1:]) for t in terms) for terms in routes
    ]


def step_spread(routes, stage, dp_size, dp_place):
    bits = list(range(1, dp_size.bit_length() - 1))
    kept, sent = [], []
    for terms, order in zip(routes, (bits, bits[::-1])):
        left = [bit for bit in bits[::-1] if bit not in order[:stage]]
        keep, send = halve(terms, order[stage], left, dp_place)
        kept.append(keep)
        sent.append(flip(send, 1 << order[stage], dp_size))
    sent = lax.optimization_barrier(tuple(sent))
    return list(zip(kept, sent))


def start_dense(terms):
    half = terms[0].shape[2] // 2 // LANES * LANES
    return start_spread([tuple(t[..., :half] for t in terms), tuple(t[..., half:] for t in terms)])


def finish_dense(routes, size):
    block = jnp.concatenate([add_low(*terms) for terms in routes], axis=-1)
    parts = lax.all_to_all(block.reshape(size, -1, block.shape[-1]), "expert", 0, 0, tiled=True)
    return jnp.sum(parts.astype(F32), axis=0)


def reduce_top(top, dp_size, size):
    for bit in range(dp_size.bit_length() - 1):
        top = jnp.maximum(top, flip(top, 1 << bit, dp_size))
    for bit in range(size.bit_length() - 1):
        top = jnp.maximum(top, lax.ppermute(top, "expert", [(i, i ^ (1 << bit)) for i in range(size)]))
    return top


def arrival_order(size):
    sources, places = np.zeros((size, size), np.int32), np.zeros((size, size), np.int32)
    for place in range(size):
        spots = [(0, place)]
        for k in range(1, size):
            if place - k >= 0:
                spots.append((k, place - k))
            if place + k < size:
                spots.append((size - 1 + k, place + k))
        sources[place], places[place] = zip(*spots)
    return sources, places


def norm_backward(hidden, factor, gain_vec, grad_in):
    scaled = grad_in * gain_vec
    hidden_grad = factor * scaled - hidden * factor**3 * jnp.mean(
        scaled * hidden, axis=-1, keepdims=True
    )
    return hidden_grad, jnp.sum(grad_in * hidden * factor, axis=0)


def local(
    tokens,
    first_gain,
    query_weight,
    key_weight,
    value_weight,
    output_weight,
    second_gain,
    router_weight,
    gate_weight,
    up_weight,
    down_weight,
    cotangent,
    routes,
    segments,
    threshold,
):
    rows, width = tokens.shape
    query_width, kv_width = query_weight.shape[1], key_weight.shape[1]
    heads, groups = query_width // HDIM, kv_width // HDIM
    ratio = heads // groups
    local_experts = gate_weight.shape[0]
    size, dp_size = lax.axis_size("expert"), lax.axis_size("dp")
    place, dp_place = lax.axis_index("expert"), lax.axis_index("dp")
    experts = local_experts * size
    expert_pad = round_up(experts, 16)
    capacity = rows * routes.shape[1] * 9 // (experts * 8)
    slot_rows = round_up(capacity, 64)

    tables = tuple(
        lax.dynamic_slice_in_dim(jnp.asarray(table), place * rows, rows, 0) for table in rotary_tables(rows * size)
    )
    seg_block = jnp.pad(segments.reshape(rows // LANES, LANES).astype(BF16), ((0, 16 - rows // LANES), (0, 0)))

    normed, first_factor, kv_own = pl.pallas_call(
        front_kernel,
        out_shape=(
            jax.ShapeDtypeStruct((rows, width), BF16),
            jax.ShapeDtypeStruct((rows, 1), F32),
            jax.ShapeDtypeStruct((groups * rows + 16, LANES), BF16),
        ),
        in_specs=[vmem()] * 7,
        out_specs=(vmem(),) * 3,
        compiler_params=params(),
        cost_estimate=cost(4),
        name="front",
    )(tokens, first_gain.reshape(1, width), key_weight, value_weight, *tables, seg_block)
    kv_slots = [kv_own]
    for _ in range(size - 1):
        kv_slots.append(line_up(kv_slots[-1], size))

    cot_own = pl.pallas_call(
        extend_kernel,
        out_shape=jax.ShapeDtypeStruct((rows, width + LANES), BF16),
        in_specs=[vmem()] * 2,
        out_specs=vmem(),
        compiler_params=params(),
        cost_estimate=cost(2),
        name="extend",
    )(cotangent, routes)
    cots = line_gather(cot_own, size)

    query_block = 512
    queries = pl.pallas_call(
        query_kernel,
        out_shape=jax.ShapeDtypeStruct((rows, query_width), BF16),
        grid=(query_width // query_block,),
        in_specs=[
            pl.BlockSpec((rows, width), lambda s: (0, 0)),
            pl.BlockSpec((width, query_block), lambda s: (0, s)),
            pl.BlockSpec((rows, LANES), lambda s: (0, 0)),
            pl.BlockSpec((rows, LANES), lambda s: (0, 0)),
        ],
        out_specs=pl.BlockSpec((rows, query_block), lambda s: (0, s)),
        compiler_params=params(),
        cost_estimate=cost(5),
        name="queries",
    )(normed, query_weight, *tables)

    seg_column = segments.reshape(rows, 1).astype(F32)
    place_word = place.reshape(1).astype(jnp.int32)
    attended, lse, top = attend(queries, kv_slots, seg_column, place_word, groups)
    head_top = reduce_top(top, dp_size, size)[:, 0, : 2 * ratio].reshape(heads)

    hidden_in = tokens.astype(F32)
    hidden_mid = hidden_in + RESIDUAL_SCALE * dot(attended, output_weight, NT)
    second_factor = lax.rsqrt(jnp.mean(hidden_mid * hidden_mid, axis=-1, keepdims=True) + NORM_EPSILON)
    second_normed = (hidden_mid * second_factor * second_gain).astype(BF16)
    normed_blocks = line_gather(second_normed, size)

    router_t = jnp.pad(router_weight.T, ((0, expert_pad - experts), (0, 0)))
    sources, blocks_of = (jnp.asarray(table)[place] for table in arrival_order(size))
    expert_place = jnp.concatenate([(place * local_experts).reshape(1), sources, blocks_of]).astype(jnp.int32)
    expert_place, head_top = lax.optimization_barrier((expert_place, head_top))
    saved, grad_blocks, router_part = run_experts(
        expert_place, router_t, gate_weight, up_weight, down_weight, normed_blocks, cots, slot_rows
    )
    grad_blocks = lax.all_to_all(grad_blocks, "expert", 0, 0, tiled=True)

    dp_word = dp_place.reshape(1).astype(jnp.int32)
    expert_sums = run_expert_grads(saved, dp_size)
    mixture = run_mixture(blocks_of, down_weight, saved, slot_rows)
    mixture, grad_blocks, expert_sums = lax.optimization_barrier((mixture, grad_blocks, expert_sums))
    normed_grad = jnp.sum(grad_blocks.astype(F32), axis=0)
    expert_sums = lax.psum_scatter(expert_sums, "dp", scatter_dimension=0, tiled=True)[0].astype(F32)
    mixture = lax.all_to_all(mixture, "expert", 0, 0, tiled=True)

    out_grad = cotangent.astype(F32)
    mid_back, second_gain_part = norm_backward(hidden_mid, second_factor, second_gain, normed_grad)
    mid_grad = out_grad + mid_back
    branch_grad = (RESIDUAL_SCALE * mid_grad).astype(BF16)
    attended_grad = dot(branch_grad, output_weight).astype(BF16)
    query_back, dkv = attend_back(
        queries, attended, attended_grad, lse, tables, kv_slots, seg_column, place_word, groups
    )
    keep, send = dense_grads(dp_word, [(branch_grad, attended), (normed, query_back)], dp_size)
    wide = start_dense((keep, flip(send, 1, dp_size)))
    stages = dp_size.bit_length() - 2
    down = dkv[size - 1]
    for k in range(1, size):
        from_above = line_down(down, size)
        if k == 1:
            from_above, mixture = lax.optimization_barrier((from_above, mixture))
        if k == size - 2:
            from_above, wide = lax.optimization_barrier((from_above, wide))
            wide = step_spread(wide, 0, dp_size, dp_place)
        if k < size - 1:
            down = add_low(from_above, dkv[size - 1 - k])
    from_above, wide = lax.optimization_barrier((from_above, wide))
    for stage in range(1, stages):
        wide = step_spread(wide, stage, dp_size, dp_place)
    block_out = (hidden_mid + jnp.sum(mixture.astype(F32), axis=0)).astype(BF16)
    key_back, value_back = pl.pallas_call(
        unpack_kernel,
        out_shape=(jax.ShapeDtypeStruct((rows, kv_width), BF16),) * 2,
        in_specs=[vmem()] * 4,
        out_specs=(vmem(),) * 2,
        compiler_params=params(),
        cost_estimate=cost(2),
        name="unpack",
    )(dkv[0], from_above, *tables)

    first_grad = dot(query_back, query_weight, NT)
    first_grad = first_grad + dot(key_back, key_weight, NT)
    first_grad = first_grad + dot(value_back, value_weight, NT)
    input_back, first_gain_part = norm_backward(hidden_in, first_factor, first_gain, first_grad)
    input_grad = mid_grad + input_back
    keep, send = dense_grads(
        dp_word,
        [(normed, key_back), (normed, value_back)],
        dp_size,
        (router_part, second_gain_part[None], first_gain_part[None]),
    )
    keep, send, wide = lax.optimization_barrier((keep, send, wide))
    rest = start_dense((keep, flip(send, 1, dp_size)))
    for stage in range(stages):
        rest = step_spread(rest, stage, dp_size, dp_place)
    wide_grad, rest_grad = finish_dense(wide, size), finish_dense(rest, size)
    projection_grad, query_grad = wide_grad[:, :query_width], wide_grad[:, query_width:]
    key_grad = rest_grad[:, :kv_width]
    value_grad = rest_grad[:, kv_width : 2 * kv_width]
    small_grad = rest_grad[:, 2 * kv_width :]

    head_scale = threshold / jnp.maximum(head_top, threshold)
    group_scale = jnp.min(head_scale.reshape(groups, ratio), axis=1)
    row_count = width // (dp_size * size)
    row_start = (dp_place * size + place) * row_count
    query_rows = lax.dynamic_slice_in_dim(query_weight, row_start, row_count, 0).astype(F32)
    key_rows = lax.dynamic_slice_in_dim(key_weight, row_start, row_count, 0).astype(F32)
    query_clipped = (query_rows * jnp.repeat(jnp.sqrt(head_scale), HDIM)[None, :]).astype(BF16)
    key_clipped = (key_rows * jnp.repeat(jnp.sqrt(group_scale), HDIM)[None, :]).astype(BF16)
    return (
        block_out,
        input_grad,
        small_grad[:, expert_pad + 1],
        query_grad,
        key_grad,
        value_grad,
        projection_grad,
        small_grad[:, expert_pad],
        small_grad[:, :experts],
        expert_sums[0],
        expert_sums[1],
        expert_sums[2],
        head_scale,
        query_clipped,
        key_clipped,
    )


def solution(mesh):
    row = P(("dp", "expert"), None)
    vector = P(("dp", "expert"))
    expert_in = P("expert", None, None)
    expert_out = P("expert", "dp", None)
    return jax.shard_map(
        local,
        mesh=mesh,
        in_specs=(row,) + (P(),) * 7 + (expert_in,) * 3 + (row, row, vector, P()),
        out_specs=(row, row, vector)
        + (row,) * 4
        + (vector, row)
        + (expert_out,) * 3
        + (P(), row, row),
        check_vma=False,
    )
```

time: 816 us -> 572 us (0.70)
  starting transfers between devices: 246 us -> 120 us
  waiting for transfers between devices: 279 us -> 168 us
  local copies, waits for them, and re-layouts: 65.1 us -> 31.2 us
  between operations: 3.24 us -> 14.8 us
    ppermute x39 -> x9, starting transfers between devices: 161 us -> 52.2 us  [line_down(): return lax.ppermute(value, 'expert', [(i + 1, i) for i in range(size - 1)])]
    ppermute x39 -> x9, waiting for transfers between devices: 102 us -> 15.9 us  [line_down(): return lax.ppermute(value, 'expert', [(i + 1, i) for i in range(size - 1)])]
    ppermute x36 -> x13, waiting for transfers between devices: 101 us -> 46.4 us  [flip(): return lax.ppermute(value, 'dp', [(i, i ^ bit) for i in range(size)])]
    all_to_all x0 -> x4, waiting for transfers between devices: none -> 43.3 us  [the longest x1 26.6 us: local(): grad_blocks = lax.all_to_all(grad_blocks, 'expert', 0, 0, tiled=True)]
    ppermute x39 -> x9, starting transfers between devices: 52.1 us -> 11.5 us  [line_up(): return lax.ppermute(value, 'expert', [(i, i + 1) for i in range(size - 1)])]
    all_to_all x0 -> x4, starting transfers between devices: none -> 26.9 us  [the longest x2 11.6 us: finish_dense(): lax.all_to_all(block.reshape(size, -1, block.shape[-1]), 'expert', 0, 0,...]
    slice x24 -> x8, local copies, waits for them, and re-layouts: 32.1 us -> 14.8 us  [the longest x4 11.1 us: start_dense(): t[..., half:]]
    ppermute x39 -> x9, waiting for transfers between devices: 75.6 us -> 58.4 us  [line_up(): return lax.ppermute(value, 'expert', [(i, i + 1) for i in range(size - 1)])]
  transfers between devices with their start and end apart: 114 -> 38, of which waited for: 55 -> 24; matrix products, arithmetic and copies ran while one was open for 12% -> 13% of each run, Pallas kernels for 15% -> 22%
where the time goes in v2:
time: 572 us; the launch traced here: 565 us
  Pallas kernels  177 us (31%)
  waiting for transfers between devices  168 us (29%)
  starting transfers between devices  120 us (21%)
  other arithmetic  40 us (7%)
  local copies, waits for them, and re-layouts  31.2 us (5%)
  between operations  14.8 us (3%)
  matrix products  13.9 us (2%)
    ppermute x9, waiting for transfers between devices, line_up(): return lax.ppermute(value, 'expert', [(i, i + 1) for i in range(size - 1)])  58.4 us
    ppermute x9, starting transfers between devices, line_down(): return lax.ppermute(value, 'expert', [(i + 1, i) for i in range(size - 1)])  52.2 us
    ppermute x13, waiting for transfers between devices, flip(): return lax.ppermute(value, 'dp', [(i, i ^ bit) for i in range(size)])  46.4 us
    pallas_call x1, Pallas kernels, run_experts(): pl.pallas_call(functools.partial(expert_kernel, blocks, slot_rows, local_...  45.9 us
    pallas_call x1, Pallas kernels, attend(): pl.pallas_call(functools.partial(attend_kernel, slots, ratio), out_shape=...  38.8 us
    pallas_call x1, Pallas kernels, attend_back(): pl.pallas_call(functools.partial(attend_back_kernel, slots, ratio), out_s...  27.6 us
    ppermute x13, starting transfers between devices, flip(): return lax.ppermute(value, 'dp', [(i, i ^ bit) for i in range(size)])  27.1 us
    all_to_all x1, waiting for transfers between devices, local(): grad_blocks = lax.all_to_all(grad_blocks, 'expert', 0, 0, tiled=True)  26.6 us
  transfers between devices with their start and end apart: 38, of which 24 were waited for; matrix products, arithmetic and copies ran while one was open for 13% of the time, Pallas kernels for 22%

profile of v2, /device:TPU:24, one launch (start us, length us, event | category | flops | bytes accessed | tf_op | source)
XLA Modules:
  0.0 565.4 jit_solution(10669086093379861914)
XLA Ops:
  9.8 1.7 constant_dynamic-slice_fusion.2
  11.5 4.3 front.1
  17.1 14.6 %collective-permute-done.refs_1_.refs_5_ = bf16[2064,128]{1,0:T(8,128)(2,1)S(1)} collective-permute-done((bf16[2064,128]{1,0:T(8,128)(2,1)}, bf16[2064,128]{1,0:T(8,128)(2,1)S(1)}, u32[]{:S(2)}, u32[]{:S(2)}) %collective-permute-start) | collective-permute-done | bytes 528416 | tf_op jit(solution)/shard_map/ppermute | solution.py:667
  32.9 13.5 %collective-permute-done.1.refs_2_.refs_6_ = bf16[2064,128]{1,0:T(8,128)(2,1)S(1)} collective-permute-done((bf16[2064,128]{1,0:T(8,128)(2,1)S(1)}, bf16[2064,128]{1,0:T(8,128)(2,1)S(1)}, u32[]{:S(2)}, u32[]{:S(2)}) %collective-permute-start.1) | collective-permute-done | bytes 528416 | tf_op jit(solution)/shard_map/ppermute | solution.py:667
  48.5 2.7 extend.1.refs_7_
  52.4 6.6 %collective-permute-start.17 = (bf16[256,1664]{1,0:T(8,128)(2,1)}, bf16[256,1664]{1,0:T(8,128)(2,1)}, u32[]{:S(2)}, u32[]{:S(2)}) collective-permute-start(bf16[256,1664]{1,0:T(8,128)(2,1)} %extend.1.refs_7_), channel_id=1, source_target_pairs={{1,0},{2,1},{3,2},{5,4},{6,5},{7,6},{9,8},{10,9},{11,10},{13,12},{... | collective-permute-start | bytes 2555912 | tf_op jit(solution)/shard_map/ppermute | solution.py:671
  59.9 5.7 %queries.1.query_ref = bf16[256,1536]{1,0:T(8,128)(2,1)} custom-call(bf16[256,1536]{1,0:T(8,128)(2,1)} %get-tuple-element.71.normed_ref.refs_1_.refs_0_, bf16[1536,1536]{1,0:T(8,128)(2,1)} %query_ref.1, f32[256,128]{1,0:T(8,128)} %get-tuple-element.230.cos_ref, f32[256,128]{1,0:T(8,128)} %get-tuple-element.229.sin_ref), custom_call_target="tpu_custom_call" | custom-call | flops 5000000 | tf_op jit(solution)/shard_map/queries/pallas_call | solution.py:825
  66.4 38.8 %attend.1 = (bf16[256,1536]{1,0:T(8,128)(2,1)}, f32[4,256,128]{2,1,0:T(8,128)}, f32[4,8,128]{2,1,0:T(8,128)}) custom-call(s32[1]{0:T(128)} %bitcast.place_ref, bf16[256,1536]{1,0:T(8,128)(2,1)} %queries.1.query_ref, f32[256,1]{1,0:T(8,128)} %copy.58.seg_column_ref, bf16[2064,128]{1,0:T(8,128)(2,1)} %get-tuple-element.72.refs_0_.refs_4_, ...), custom_call_target="tpu_custom_call" | custom-call | flops 20000000 | tf_op jit(solution)/shard_map/attend/pallas_call | solution.py:213
  105.3 2.7 multiply_reduce_fusion.2
  109.5 4.6 collective-permute-start.11
  115.5 5.5 collective-permute-start.18
  121.0 9.6 %collective-permute-done.8.refs_1_ = bf16[256,1536]{1,0:T(8,128)(2,1)S(1)} collective-permute-done((bf16[256,1536]{1,0:T(8,128)(2,1)S(1)}, bf16[256,1536]{1,0:T(8,128)(2,1)S(1)}, u32[]{:S(2)}, u32[]{:S(2)}) %collective-permute-start.8) | collective-permute-done | bytes 786464 | tf_op jit(solution)/shard_map/ppermute | solution.py:667
  132.1 5.3 collective-permute-start.12
  137.4 11.6 %collective-permute-done.15.refs_9_ = bf16[256,1664]{1,0:T(8,128)(2,1)} collective-permute-done((bf16[256,1664]{1,0:T(8,128)(2,1)}, bf16[256,1664]{1,0:T(8,128)(2,1)}, u32[]{:S(2)}, u32[]{:S(2)}) %collective-permute-start.15) | collective-permute-done | bytes 852000 | tf_op jit(solution)/shard_map/ppermute | solution.py:667
  150.4 5.5 collective-permute-start.19
  155.9 9.1 %collective-permute-done.9.refs_2_ = bf16[256,1536]{1,0:T(8,128)(2,1)} collective-permute-done((bf16[256,1536]{1,0:T(8,128)(2,1)S(1)}, bf16[256,1536]{1,0:T(8,128)(2,1)}, u32[]{:S(2)}, u32[]{:S(2)}) %collective-permute-start.9) | collective-permute-done | bytes 786464 | tf_op jit(solution)/shard_map/ppermute | solution.py:667
  166.3 5.5 collective-permute-start.13
  174.4 2.3 collective-permute-done.4
  178.8 1.6 collective-permute-done.5
  181.7 2.5 collective-permute-done.6
  184.2 1.6 collective-permute-start.7
  187.1 1.8 collective-permute-done.7
  189.0 45.9 %experts.1 = (bf16[5,512,1536]{2,1,0:T(8,128)(2,1)}, bf16[5,512,1536]{2,1,0:T(8,128)(2,1)}, bf16[5,512,512]{2,1,0:T(8,128)(2,1)}, bf16[5,512,512]{2,1,0:T(8,128)...) custom-call(s32[9]{0:T(128)} %pad_add_fusion.place_ref, ...), custom_call_target="tpu_custom_call" | custom-call | flops 45000000 | tf_op jit(solution)/shard_map/experts/pallas_call | solution.py:480
  234.9 8.1 %all-to-all-start = ((bf16[4,256,1536]{2,1,0:T(8,128)(2,1)}), bf16[4,256,1536]{2,1,0:T(8,128)(2,1)}, u32[]{:S(2)}, u32[]{:S(2)}) async-start(bf16[4,256,1536]{2,1,0:T(8,128)(2,1)} %get-tuple-element.78), calls=%async_computation | async-start | bytes 6291456 | tf_op jit(solution)/shard_map/all_to_all | solution.py:859
  243.1 13.8 %mixture.1 = bf16[4,256,1536]{2,1,0:T(8,128)(2,1)} custom-call(s32[4]{0:T(128)} %copy-done.31, bf16[5,1536,512]{2,1,0:T(8,128)(2,1)} %down_ref.3, bf16[5,512,512]{2,1,0:T(8,128)(2,1)} %get-tuple-element.76.hs_ref, bf16[5,512,256]{2,1,0:T(8,128)(2,1)} %get-tuple-element.77.hit_ref), custom_call_target="tpu_custom_call" | custom-call | flops 10000000 | tf_op jit(solution)/shard_map/mixture/pallas_call | solution.py:554
  256.8 22.8 %expert_grads.1 = bf16[8,3,5,192,512]{4,3,2,1,0:T(8,128)(2,1)} custom-call(bf16[5,512,1536]{2,1,0:T(8,128)(2,1)} %get-tuple-element.79.xs_ref, bf16[5,512,1536]{2,1,0:T(8,128)(2,1)} %get-tuple-element.80.cs_ref, bf16[5,512,512]{2,1,0:T(8,128)(2,1)} %get-tuple-element.76.hs_ref, bf16[5,512,512]{2,1,0:T(8,128)(2,1)} %get-tuple-element.81.gate_grad_ref, ...), custom_call_target="tpu_custom_call" | custom-call | flops 30000000 | tf_op jit(solution)/shard_map/expert_grads/pallas_call | solution.py:606
  279.6 26.6 %all-to-all-done = bf16[4,256,1536]{2,1,0:T(8,128)(2,1)} async-done(((bf16[4,256,1536]{2,1,0:T(8,128)(2,1)}), bf16[4,256,1536]{2,1,0:T(8,128)(2,1)}, u32[]{:S(2)}, u32[]{:S(2)}) %all-to-all-start) | async-done | bytes 3145760 | tf_op jit(solution)/shard_map/all_to_all | solution.py:859
  306.3 7.2 %all-to-all-start.1 = ((bf16[4,256,1536]{2,1,0:T(8,128)(2,1)}), bf16[4,256,1536]{2,1,0:T(8,128)(2,1)}, u32[]{:S(2)}, u32[]{:S(2)}) async-start(bf16[4,256,1536]{2,1,0:T(8,128)(2,1)} %mixture.1), calls=%async_computation.1 | async-start | bytes 6291456 | tf_op jit(solution)/shard_map/all_to_all | solution.py:867
  313.5 2.6 convert_reduce_fusion.1
  317.2 1.7 multiply_convert_fusion
  318.9 4.9 convolution_convert_fusion.grad_ref
  323.8 27.6 %attend_back.1 = (bf16[256,1536]{1,0:T(8,128)(2,1)}, bf16[2048,128]{1,0:T(8,128)(2,1)}, bf16[2048,128]{1,0:T(8,128)(2,1)}, bf16[2048,128]{1,0:T(8,128)(2,1)}, bf16[2048,128]{1,0:T(8,128)(2,1)}) custom-call(s32[1]{0:T(128)} %bitcast.place_ref, bf16[256,1536]{1,0:T(8,128)(2,1)} %queries.1.query_ref, bf16[256,1536]{1,0:T(8,128)(2,1)} %get-tuple-element.73.attended_ref.refs_2_, ...), custom_call_target="tpu_custom_call" | custom-call | flops 2000000 | tf_op jit(solution)/shard_map/attend_back/pallas_call | solution.py:314
  351.4 8.2 %dense_grads.2 = (bf16[4,192,3072]{2,1,0:T(8,128)(2,1)}, bf16[4,192,3072]{2,1,0:T(8,128)(2,1)}) custom-call(s32[1]{0:T(128)} %bitcast.7.place_ref, bf16[256,1536]{1,0:T(8,128)(2,1)} %copy-done.14, bf16[256,1536]{1,0:T(8,128)(2,1)} %get-tuple-element.71.normed_ref.refs_1_.refs_0_, bf16[256,1536]{1,0:T(8,128)(2,1)} %get-tuple-element.73.attended_ref.refs_2_, ...), custom_call_target="tpu_custom_call" | custom-call | flops 4000000 | tf_op jit(solution)/shard_map/dense_grads/pallas_call | solution.py:654
  360.9 5.3 fusion.34
  366.2 8.6 %collective-permute-done.20 = bf16[2048,128]{1,0:T(8,128)(2,1)S(1)} collective-permute-done((bf16[2048,128]{1,0:T(8,128)(2,1)}, bf16[2048,128]{1,0:T(8,128)(2,1)S(1)}, u32[]{:S(2)}, u32[]{:S(2)}) %collective-permute-start.20) | collective-permute-done | bytes 524320 | tf_op jit(solution)/shard_map/ppermute | solution.py:671
  374.8 6.5 %all-to-all-done.1 = bf16[4,256,1536]{2,1,0:T(8,128)(2,1)} async-done(((bf16[4,256,1536]{2,1,0:T(8,128)(2,1)}), bf16[4,256,1536]{2,1,0:T(8,128)(2,1)}, u32[]{:S(2)}, u32[]{:S(2)}) %all-to-all-start.1) | async-done | bytes 3145760 | tf_op jit(solution)/shard_map/all_to_all | solution.py:867
  381.5 12.8 %collective-permute-start.21 = (bf16[2048,128]{1,0:T(8,128)(2,1)S(1)}, bf16[2048,128]{1,0:T(8,128)(2,1)S(1)}, u32[]{:S(2)}, u32[]{:S(2)}) collective-permute-start(bf16[2048,128]{1,0:T(8,128)(2,1)S(1)} %add_convert_fusion.12), channel_id=1, source_target_pairs={{1,0},{2,1},{3,2},{5,4},{6,5},{7,6},{9,8},{10,9},{11,10},{13,12},{... | collective-permute-start | bytes 1572872 | tf_op jit(solution)/shard_map/ppermute | solution.py:671
  394.3 3.4 fusion.33
  397.7 6.9 %collective-permute-done.21 = bf16[2048,128]{1,0:T(8,128)(2,1)S(1)} collective-permute-done((bf16[2048,128]{1,0:T(8,128)(2,1)S(1)}, bf16[2048,128]{1,0:T(8,128)(2,1)S(1)}, u32[]{:S(2)}, u32[]{:S(2)}) %collective-permute-start.21) | collective-permute-done | bytes 524320 | tf_op jit(solution)/shard_map/ppermute | solution.py:671
  404.6 1.7 fusion.10
  407.8 2.0 fusion.8
  409.9 16.2 %collective-permute-start.24 = (bf16[2,192,1536]{2,1,0:T(8,128)(2,1)}, bf16[2,192,1536]{2,1,0:T(8,128)(2,1)}, u32[]{:S(2)}, u32[]{:S(2)}) collective-permute-start(bf16[2,192,1536]{2,1,0:T(8,128)(2,1)} %get-tuple-element.204), channel_id=1, source_target_pairs={{0,8},{4,12},{8,0},{12,4},{16,24},{20,28},{24,16},{28,20},{1,9},{5... | collective-permute-start | bytes 3538952 | tf_op jit(solution)/shard_map/ppermute | solution.py:693
  426.8 2.1 add_convert_fusion.11
  428.9 5.2 collective-permute-start.23
  436.4 1.7 multiply_convert_fusion.2
  439.4 15.7 %collective-permute-done.25 = bf16[2,192,1536]{2,1,0:T(8,128)(2,1)} collective-permute-done((bf16[2,192,1536]{2,1,0:T(8,128)(2,1)}, bf16[2,192,1536]{2,1,0:T(8,128)(2,1)}, u32[]{:S(2)}, u32[]{:S(2)}) %collective-permute-start.25) | collective-permute-done | bytes 1179680 | tf_op jit(solution)/shard_map/ppermute | solution.py:693
  455.1 2.7 fusion.14
  459.3 2.4 fusion.12
  462.3 2.8 unpack.1
  465.0 2.2 fusion.38
  468.4 3.5 fusion.6
  472.5 4.7 dense_grads.3
  477.2 9.0 %collective-permute-done.27 = bf16[192,1536]{1,0:T(8,128)(2,1)} collective-permute-done((bf16[192,1536]{1,0:T(8,128)(2,1)}, bf16[192,1536]{1,0:T(8,128)(2,1)}, u32[]{:S(2)}, u32[]{:S(2)}) %collective-permute-start.27) | collective-permute-done | bytes 589856 | tf_op jit(solution)/shard_map/ppermute | solution.py:693
  486.2 3.9 collective-permute-done.26
  491.6 3.8 convert_reduce_fusion
  500.9 5.1 all-to-all-start.3
  512.6 8.1 %collective-permute-done.29 = bf16[2,192,512]{2,1,0:T(8,128)(2,1)S(1)} collective-permute-done((bf16[2,192,512]{2,1,0:T(8,128)(2,1)S(1)}, bf16[2,192,512]{2,1,0:T(8,128)(2,1)S(1)}, u32[]{:S(2)}, u32[]{:S(2)}) %collective-permute-start.29) | collective-permute-done | bytes 393248 | tf_op jit(solution)/shard_map/ppermute | solution.py:693
  523.9 4.2 collective-permute-done.31
  529.2 3.7 all-to-all-done.3
  532.9 6.5 %all-to-all-start.2 = ((bf16[4,48,1152]{2,1,0:T(8,128)(2,1)}), bf16[4,48,1152]{2,1,0:T(8,128)(2,1)}, u32[]{:S(2)}, u32[]{:S(2)}) async-start(bf16[4,48,1152]{2,1,0:T(8,128)(2,1)} %bitcast.94), calls=%async_computation.2 | async-start | bytes 884736 | tf_op jit(solution)/shard_map/all_to_all | solution.py:729
  539.4 3.0 fusion.3
  543.4 6.4 %all-to-all-done.2 = bf16[4,48,1152]{2,1,0:T(8,128)(2,1)} async-done(((bf16[4,48,1152]{2,1,0:T(8,128)(2,1)}), bf16[4,48,1152]{2,1,0:T(8,128)(2,1)}, u32[]{:S(2)}, u32[]{:S(2)}) %all-to-all-start.2) | async-done | bytes 442400 | tf_op jit(solution)/shard_map/all_to_all | solution.py:729
  553.0 2.6 convert_element_type.447
  555.6 2.7 slice_bitcast_fusion
  (175 shorter events, 58.7 us)
Async XLA Ops:
  11.5 36.2 %copy-start.28 = (s32[256,8]{0,1:T(8,128)S(1)}, s32[256,8]{0,1:T(8,128)}, u32[]{:S(2)}) copy-start(s32[256,8]{0,1:T(8,128)} %param.31) | copy-start | bytes 24580
  15.8 15.8 %collective-permute-start = (bf16[2064,128]{1,0:T(8,128)(2,1)}, bf16[2064,128]{1,0:T(8,128)(2,1)S(1)}, u32[]{:S(2)}, u32[]{:S(2)}) collective-permute-start(bf16[2064,128]{1,0:T(8,128)(2,1)} %get-tuple-element.72.refs_0_.refs_4_), channel_id=1, source_target_pairs={{0,1},{1,2},{2,3},{4,5},{5,6},{6,7},{8,9},{9,10},{10,11},{12,13},{... | collective-permute-start | bytes 1585160 | tf_op jit(solution)/shard_map/ppermute | solution.py:667
  31.6 34.0 %copy-start.2 = (bf16[2064,128]{1,0:T(8,128)(2,1)}, bf16[2064,128]{1,0:T(8,128)(2,1)S(1)}, u32[]{:S(2)}) copy-start(bf16[2064,128]{1,0:T(8,128)(2,1)S(1)} %collective-permute-done.refs_1_.refs_5_) | copy-start | bytes 1585156
  31.7 14.8 %collective-permute-start.1 = (bf16[2064,128]{1,0:T(8,128)(2,1)S(1)}, bf16[2064,128]{1,0:T(8,128)(2,1)S(1)}, u32[]{:S(2)}, u32[]{:S(2)}) collective-permute-start(bf16[2064,128]{1,0:T(8,128)(2,1)S(1)} %collective-permute-done.refs_1_.refs_5_), channel_id=1, source_target_pairs={{0,1},{1,2},{2,3},{4,5},{5,6},{6,7},{8,9},{9,10},{10,11},{12,13},{... | collective-permute-start | bytes 1585160 | tf_op jit(solution)/shard_map/ppermute | solution.py:667
  46.4 19.2 %copy-start.3 = (bf16[2064,128]{1,0:T(8,128)(2,1)}, bf16[2064,128]{1,0:T(8,128)(2,1)S(1)}, u32[]{:S(2)}) copy-start(bf16[2064,128]{1,0:T(8,128)(2,1)S(1)} %collective-permute-done.1.refs_2_.refs_6_) | copy-start | bytes 1585156
  46.4 19.2 %collective-permute-start.2 = (bf16[2064,128]{1,0:T(8,128)(2,1)S(1)}, bf16[2064,128]{1,0:T(8,128)(2,1)S(1)}, u32[]{:S(2)}, u32[]{:S(2)}) collective-permute-start(bf16[2064,128]{1,0:T(8,128)(2,1)S(1)} %collective-permute-done.1.refs_2_.refs_6_), channel_id=1, source_target_pairs={{0,1},{1,2},{2,3},{4,5},{5,6},{6,7},{8,9},{9,10},{10,11},{12,13},{... | collective-permute-start | bytes 1585160 | tf_op jit(solution)/shard_map/ppermute | solution.py:667
  48.5 56.7 %slice-start.2 = ((s8[4718592]{0:T(1024)(128)(4,1)}), s8[524288]{0:T(1024)(128)(4,1)S(1)}, s32[]{:S(2)}) async-start(s8[4718592]{0:T(1024)(128)(4,1)} %bitcast.97), calls=%async_computation.8 | async-start | bytes 1048576
  51.2 63.0 %collective-permute-start.14 = (bf16[256,1664]{1,0:T(8,128)(2,1)}, bf16[256,1664]{1,0:T(8,128)(2,1)}, u32[]{:S(2)}, u32[]{:S(2)}) collective-permute-start(bf16[256,1664]{1,0:T(8,128)(2,1)} %extend.1.refs_7_), channel_id=1, source_target_pairs={{0,1},{1,2},{2,3},{4,5},{5,6},{6,7},{8,9},{9,10},{10,11},{12,13},{... | collective-permute-start | bytes 2555912 | tf_op jit(solution)/shard_map/ppermute | solution.py:667
  52.4 63.0 %collective-permute-start.17 = (bf16[256,1664]{1,0:T(8,128)(2,1)}, bf16[256,1664]{1,0:T(8,128)(2,1)}, u32[]{:S(2)}, u32[]{:S(2)}) collective-permute-start(bf16[256,1664]{1,0:T(8,128)(2,1)} %extend.1.refs_7_), channel_id=1, source_target_pairs={{1,0},{2,1},{3,2},{5,4},{6,5},{7,6},{9,8},{10,9},{11,10},{13,12},{... | collective-permute-start | bytes 2555912 | tf_op jit(solution)/shard_map/ppermute | solution.py:671
  59.9 45.4 %slice-start.3 = ((s8[4718592]{0:T(1024)(128)(4,1)}), s8[4194304]{0:T(1024)(128)(4,1)S(1)}, s32[]{:S(2)}) async-start(s8[4718592]{0:T(1024)(128)(4,1)} %bitcast.97), calls=%async_computation.9 | async-start | bytes 8388608
  66.4 38.9 %copy-start.5 = (bf16[256,1536]{1,0:T(8,128)(2,1)S(1)}, bf16[256,1536]{1,0:T(8,128)(2,1)}, u32[]{:S(2)}) copy-start(bf16[256,1536]{1,0:T(8,128)(2,1)} %tokens_ref.1) | copy-start | bytes 2359300
  105.3 2.7 copy-start.25
  108.0 63.8 %copy-start.27 = (f32[4,8,128]{2,1,0:T(8,128)S(1)}, f32[4,8,128]{2,1,0:T(8,128)}, u32[]{:S(2)}) copy-start(f32[4,8,128]{2,1,0:T(8,128)} %get-tuple-element.74) | copy-start | bytes 49156
  108.0 78.4 %copy-start.26 = (bf16[1536,20]{0,1:T(8,128)(2,1)S(1)}, bf16[1536,20]{0,1:T(8,128)(2,1)}, u32[]{:S(2)}) copy-start(bf16[1536,20]{0,1:T(8,128)(2,1)} %param.26) | copy-start | bytes 184324
  108.2 80.7 %copy-start.15 = (bf16[256,1536]{1,0:T(8,128)(2,1)}, bf16[256,1536]{1,0:T(8,128)(2,1)S(1)}, u32[]{:S(2)}) copy-start(bf16[256,1536]{1,0:T(8,128)(2,1)S(1)} %multiply_convert_fusion.1.refs_0_) | copy-start | bytes 2359300
  108.2 22.4 %collective-permute-start.8 = (bf16[256,1536]{1,0:T(8,128)(2,1)S(1)}, bf16[256,1536]{1,0:T(8,128)(2,1)S(1)}, u32[]{:S(2)}, u32[]{:S(2)}) collective-permute-start(bf16[256,1536]{1,0:T(8,128)(2,1)S(1)} %multiply_convert_fusion.1.refs_0_), channel_id=1, source_target_pairs={{0,1},{1,2},{2,3},{4,5},{5,6},{6,7},{8,9},{9,10},{10,11},{12,13},{... | collective-permute-start | bytes 2359304 | tf_op jit(solution)/shard_map/ppermute | solution.py:667
  109.5 22.5 %collective-permute-start.11 = (bf16[256,1536]{1,0:T(8,128)(2,1)S(1)}, bf16[256,1536]{1,0:T(8,128)(2,1)S(1)}, u32[]{:S(2)}, u32[]{:S(2)}) collective-permute-start(bf16[256,1536]{1,0:T(8,128)(2,1)S(1)} %multiply_convert_fusion.1.refs_0_), channel_id=1, source_target_pairs={{1,0},{2,1},{3,2},{5,4},{6,5},{7,6},{9,8},{10,9},{11,10},{13,12},{... | collective-permute-start | bytes 2359304 | tf_op jit(solution)/shard_map/ppermute | solution.py:671
  114.2 34.8 %collective-permute-start.15 = (bf16[256,1664]{1,0:T(8,128)(2,1)}, bf16[256,1664]{1,0:T(8,128)(2,1)}, u32[]{:S(2)}, u32[]{:S(2)}) collective-permute-start(bf16[256,1664]{1,0:T(8,128)(2,1)} %collective-permute-done.14.refs_8_), channel_id=1, source_target_pairs={{0,1},{1,2},{2,3},{4,5},{5,6},{6,7},{8,9},{9,10},{10,11},{12,13},{... | collective-permute-start | bytes 2555912 | tf_op jit(solution)/shard_map/ppermute | solution.py:667
  115.5 35.0 %collective-permute-start.18 = (bf16[256,1664]{1,0:T(8,128)(2,1)}, bf16[256,1664]{1,0:T(8,128)(2,1)}, u32[]{:S(2)}, u32[]{:S(2)}) collective-permute-start(bf16[256,1664]{1,0:T(8,128)(2,1)} %collective-permute-done.17.refs_11_), channel_id=1, source_target_pairs={{1,0},{2,1},{3,2},{5,4},{6,5},{7,6},{9,8},{10,9},{11,10},{13,12},{... | collective-permute-start | bytes 2555912 | tf_op jit(solution)/shard_map/ppermute | solution.py:671
  130.6 34.4 %collective-permute-start.9 = (bf16[256,1536]{1,0:T(8,128)(2,1)S(1)}, bf16[256,1536]{1,0:T(8,128)(2,1)}, u32[]{:S(2)}, u32[]{:S(2)}) collective-permute-start(bf16[256,1536]{1,0:T(8,128)(2,1)S(1)} %collective-permute-done.8.refs_1_), channel_id=1, source_target_pairs={{0,1},{1,2},{2,3},{4,5},{5,6},{6,7},{8,9},{9,10},{10,11},{12,13},{... | collective-permute-start | bytes 2359304 | tf_op jit(solution)/shard_map/ppermute | solution.py:667
  132.1 32.9 %copy-start.20 = (bf16[256,1536]{1,0:T(8,128)(2,1)}, bf16[256,1536]{1,0:T(8,128)(2,1)S(1)}, u32[]{:S(2)}) copy-start(bf16[256,1536]{1,0:T(8,128)(2,1)S(1)} %collective-permute-done.11.refs_4_) | copy-start | bytes 2359300
  132.1 34.2 %collective-permute-start.12 = (bf16[256,1536]{1,0:T(8,128)(2,1)S(1)}, bf16[256,1536]{1,0:T(8,128)(2,1)}, u32[]{:S(2)}, u32[]{:S(2)}) collective-permute-start(bf16[256,1536]{1,0:T(8,128)(2,1)S(1)} %collective-permute-done.11.refs_4_), channel_id=1, source_target_pairs={{1,0},{2,1},{3,2},{5,4},{6,5},{7,6},{9,8},{10,9},{11,10},{13,12},{... | collective-permute-start | bytes 2359304 | tf_op jit(solution)/shard_map/ppermute | solution.py:671
  149.0 40.0 %collective-permute-start.16 = (bf16[256,1664]{1,0:T(8,128)(2,1)}, bf16[256,1664]{1,0:T(8,128)(2,1)}, u32[]{:S(2)}, u32[]{:S(2)}) collective-permute-start(bf16[256,1664]{1,0:T(8,128)(2,1)} %collective-permute-done.15.refs_9_), channel_id=1, source_target_pairs={{0,1},{1,2},{2,3},{4,5},{5,6},{6,7},{8,9},{9,10},{10,11},{12,13},{... | collective-permute-start | bytes 2555912 | tf_op jit(solution)/shard_map/ppermute | solution.py:667
  150.4 38.5 %collective-permute-start.19 = (bf16[256,1664]{1,0:T(8,128)(2,1)}, bf16[256,1664]{1,0:T(8,128)(2,1)}, u32[]{:S(2)}, u32[]{:S(2)}) collective-permute-start(bf16[256,1664]{1,0:T(8,128)(2,1)} %collective-permute-done.18.refs_12_), channel_id=1, source_target_pairs={{1,0},{2,1},{3,2},{5,4},{6,5},{7,6},{9,8},{10,9},{11,10},{13,12},{... | collective-permute-start | bytes 2555912 | tf_op jit(solution)/shard_map/ppermute | solution.py:671
  165.0 23.9 %collective-permute-start.10 = (bf16[256,1536]{1,0:T(8,128)(2,1)}, bf16[256,1536]{1,0:T(8,128)(2,1)}, u32[]{:S(2)}, u32[]{:S(2)}) collective-permute-start(bf16[256,1536]{1,0:T(8,128)(2,1)} %collective-permute-done.9.refs_2_), channel_id=1, source_target_pairs={{0,1},{1,2},{2,3},{4,5},{5,6},{6,7},{8,9},{9,10},{10,11},{12,13},{... | collective-permute-start | bytes 2359304 | tf_op jit(solution)/shard_map/ppermute | solution.py:667
  166.3 22.6 %collective-permute-start.13 = (bf16[256,1536]{1,0:T(8,128)(2,1)}, bf16[256,1536]{1,0:T(8,128)(2,1)}, u32[]{:S(2)}, u32[]{:S(2)}) collective-permute-start(bf16[256,1536]{1,0:T(8,128)(2,1)} %collective-permute-done.12.refs_5_), channel_id=1, source_target_pairs={{1,0},{2,1},{3,2},{5,4},{6,5},{7,6},{9,8},{10,9},{11,10},{13,12},{... | collective-permute-start | bytes 2359304 | tf_op jit(solution)/shard_map/ppermute | solution.py:671
  171.8 1.2 collective-permute-start.3
  173.0 3.7 collective-permute-start.4
  176.7 3.7 collective-permute-start.5
  178.8 56.1 %copy-start.31 = (s32[4]{0:T(128)}, s32[4]{0:T(128)S(1)}, u32[]{:S(2)}) copy-start(s32[4]{0:T(128)S(1)} %fusion.29.order_ref) | copy-start | bytes 52
  180.5 3.7 collective-permute-start.6
  184.2 4.6 collective-permute-start.7
  234.9 71.3 %all-to-all-start = ((bf16[4,256,1536]{2,1,0:T(8,128)(2,1)}), bf16[4,256,1536]{2,1,0:T(8,128)(2,1)}, u32[]{:S(2)}, u32[]{:S(2)}) async-start(bf16[4,256,1536]{2,1,0:T(8,128)(2,1)} %get-tuple-element.78), calls=%async_computation | async-start | bytes 6291456 | tf_op jit(solution)/shard_map/all_to_all | solution.py:859
  243.1 309.9 %reduce-scatter.2.cloned.1.call-start = ((), (), s32[]{:S(2)}) async-start(), calls=%async_computation.5 | async-start | bytes 26542080 | tf_op jit(solution)/shard_map/reduce_scatter | solution.py:866
  306.3 75.1 %all-to-all-start.1 = ((bf16[4,256,1536]{2,1,0:T(8,128)(2,1)}), bf16[4,256,1536]{2,1,0:T(8,128)(2,1)}, u32[]{:S(2)}, u32[]{:S(2)}) async-start(bf16[4,256,1536]{2,1,0:T(8,128)(2,1)} %mixture.1), calls=%async_computation.1 | async-start | bytes 6291456 | tf_op jit(solution)/shard_map/all_to_all | solution.py:867
  318.9 4.9 copy-start.14
  359.6 34.7 %collective-permute-start.22 = (bf16[4,192,3072]{2,1,0:T(8,128)(2,1)}, bf16[4,192,3072]{2,1,0:T(8,128)(2,1)}, u32[]{:S(2)}, u32[]{:S(2)}) collective-permute-start(bf16[4,192,3072]{2,1,0:T(8,128)(2,1)} %get-tuple-element.94), channel_id=1, source_target_pairs={{0,4},{4,0},{8,12},{12,8},{16,20},{20,16},{24,28},{28,24},{1,5},{5... | collective-permute-start | bytes 14155784 | tf_op jit(solution)/shard_map/ppermute | solution.py:693
  359.6 15.2 %collective-permute-start.20 = (bf16[2048,128]{1,0:T(8,128)(2,1)}, bf16[2048,128]{1,0:T(8,128)(2,1)S(1)}, u32[]{:S(2)}, u32[]{:S(2)}) collective-permute-start(bf16[2048,128]{1,0:T(8,128)(2,1)} %get-tuple-element.85), channel_id=1, source_target_pairs={{1,0},{2,1},{3,2},{5,4},{6,5},{7,6},{9,8},{10,9},{11,10},{13,12},{... | collective-permute-start | bytes 1572872 | tf_op jit(solution)/shard_map/ppermute | solution.py:671
  360.9 20.4 %copy-start.21 = (bf16[2048,128]{1,0:T(8,128)(2,1)S(1)}, bf16[2048,128]{1,0:T(8,128)(2,1)}, u32[]{:S(2)}) copy-start(bf16[2048,128]{1,0:T(8,128)(2,1)} %get-tuple-element.92) | copy-start | bytes 1572868
  381.5 23.1 %collective-permute-start.21 = (bf16[2048,128]{1,0:T(8,128)(2,1)S(1)}, bf16[2048,128]{1,0:T(8,128)(2,1)S(1)}, u32[]{:S(2)}, u32[]{:S(2)}) collective-permute-start(bf16[2048,128]{1,0:T(8,128)(2,1)S(1)} %add_convert_fusion.12), channel_id=1, source_target_pairs={{1,0},{2,1},{3,2},{5,4},{6,5},{7,6},{9,8},{10,9},{11,10},{13,12},{... | collective-permute-start | bytes 1572872 | tf_op jit(solution)/shard_map/ppermute | solution.py:671
  394.3 10.3 %copy-start.1 = (bf16[4,192,1536]{2,1,0:T(8,128)(2,1)S(1)}, bf16[4,192,1536]{2,1,0:T(8,128)(2,1)}, u32[]{:S(2)}) copy-start(bf16[4,192,1536]{2,1,0:T(8,128)(2,1)} %get-tuple-element.208) | copy-start | bytes 7077892
  404.6 3.2 copy-start
  406.3 19.8 %copy-start.24 = (f32[256,1]{1,0:T(8,128)S(1)}, f32[256,1]{1,0:T(8,128)}, u32[]{:S(2)}) copy-start(f32[256,1]{1,0:T(8,128)} %get-tuple-element.88) | copy-start | bytes 3076
  406.3 48.8 %collective-permute-start.25 = (bf16[2,192,1536]{2,1,0:T(8,128)(2,1)}, bf16[2,192,1536]{2,1,0:T(8,128)(2,1)}, u32[]{:S(2)}, u32[]{:S(2)}) collective-permute-start(bf16[2,192,1536]{2,1,0:T(8,128)(2,1)} %get-tuple-element.203), channel_id=1, source_target_pairs={{0,16},{4,20},{8,24},{12,28},{16,0},{20,4},{24,8},{28,12},{1,17},{... | collective-permute-start | bytes 3538952 | tf_op jit(solution)/shard_map/ppermute | solution.py:693
  409.9 24.3 %copy-start.32 = (f32[24]{0:T(128)S(1)}, f32[24]{0:T(128)}, u32[]{:S(2)}) copy-start(f32[24]{0:T(128)} %param.33) | copy-start | bytes 292
  409.9 45.2 %collective-permute-start.24 = (bf16[2,192,1536]{2,1,0:T(8,128)(2,1)}, bf16[2,192,1536]{2,1,0:T(8,128)(2,1)}, u32[]{:S(2)}, u32[]{:S(2)}) collective-permute-start(bf16[2,192,1536]{2,1,0:T(8,128)(2,1)} %get-tuple-element.204), channel_id=1, source_target_pairs={{0,8},{4,12},{8,0},{12,4},{16,24},{20,28},{24,16},{28,20},{1,9},{5... | collective-permute-start | bytes 3538952 | tf_op jit(solution)/shard_map/ppermute | solution.py:693
  428.9 26.2 %collective-permute-start.23 = (bf16[2048,128]{1,0:T(8,128)(2,1)}, bf16[2048,128]{1,0:T(8,128)(2,1)}, u32[]{:S(2)}, u32[]{:S(2)}) collective-permute-start(bf16[2048,128]{1,0:T(8,128)(2,1)} %add_convert_fusion.11), channel_id=1, source_target_pairs={{1,0},{2,1},{3,2},{5,4},{6,5},{7,6},{9,8},{10,9},{11,10},{13,12},{... | collective-permute-start | bytes 1572872 | tf_op jit(solution)/shard_map/ppermute | solution.py:671
  436.4 22.9 %copy-start.9 = (bf16[2,192,1536]{2,1,0:T(8,128)(2,1)S(1)}, bf16[2,192,1536]{2,1,0:T(8,128)(2,1)}, u32[]{:S(2)}) copy-start(bf16[2,192,1536]{2,1,0:T(8,128)(2,1)} %get-tuple-element.109) | copy-start | bytes 3538948
  455.1 12.8 %slice-start = ((s8[4718592]{0:T(1024)(128)(4,1)}), s8[4194304]{0:T(1024)(128)(4,1)S(1)}, s32[]{:S(2)}) async-start(s8[4718592]{0:T(1024)(128)(4,1)} %bitcast.83), calls=%async_computation.6 | async-start | bytes 8388608
  457.8 28.4 %collective-permute-start.27 = (bf16[192,1536]{1,0:T(8,128)(2,1)}, bf16[192,1536]{1,0:T(8,128)(2,1)}, u32[]{:S(2)}, u32[]{:S(2)}) collective-permute-start(bf16[192,1536]{1,0:T(8,128)(2,1)} %get-tuple-element.211), channel_id=1, source_target_pairs={{0,8},{4,12},{8,0},{12,4},{16,24},{20,28},{24,16},{28,20},{1,9},{5... | collective-permute-start | bytes 1769480 | tf_op jit(solution)/shard_map/ppermute | solution.py:693
  461.7 28.5 %collective-permute-start.26 = (bf16[192,1536]{1,0:T(8,128)(2,1)}, bf16[192,1536]{1,0:T(8,128)(2,1)}, u32[]{:S(2)}, u32[]{:S(2)}) collective-permute-start(bf16[192,1536]{1,0:T(8,128)(2,1)} %get-tuple-element.212), channel_id=1, source_target_pairs={{0,16},{4,20},{8,24},{12,28},{16,0},{20,4},{24,8},{28,12},{1,17},{... | collective-permute-start | bytes 1769480 | tf_op jit(solution)/shard_map/ppermute | solution.py:693
  462.2 5.7 %slice-start.1 = ((s8[4718592]{0:T(1024)(128)(4,1)}), s8[524288]{0:T(1024)(128)(4,1)S(1)}, s32[]{:S(2)}) async-start(s8[4718592]{0:T(1024)(128)(4,1)} %bitcast.83), calls=%async_computation.7 | async-start | bytes 1048576
  465.0 2.2 copy-start.18
  490.1 15.9 %collective-permute-start.28 = (bf16[4,192,1152]{2,1,0:T(8,128)(2,1)}, bf16[4,192,1152]{2,1,0:T(8,128)(2,1)}, u32[]{:S(2)}, u32[]{:S(2)}) collective-permute-start(bf16[4,192,1152]{2,1,0:T(8,128)(2,1)} %get-tuple-element.116), channel_id=1, source_target_pairs={{0,4},{4,0},{8,12},{12,8},{16,20},{20,16},{24,28},{28,24},{1,5},{5... | collective-permute-start | bytes 5308424 | tf_op jit(solution)/shard_map/ppermute | solution.py:693
  491.6 3.8 copy-start.17
  500.9 32.0 %all-to-all-start.3 = ((bf16[4,48,3072]{2,1,0:T(8,128)(2,1)}), bf16[4,48,3072]{2,1,0:T(8,128)(2,1)S(1)}, u32[]{:S(2)}, u32[]{:S(2)}) async-start(bf16[4,48,3072]{2,1,0:T(8,128)(2,1)} %bitcast.89), calls=%async_computation.3 | async-start | bytes 2359296 | tf_op jit(solution)/shard_map/all_to_all | solution.py:729
  507.8 13.2 %collective-permute-start.30 = (bf16[2,192,640]{2,1,0:T(8,128)(2,1)S(1)}, bf16[2,192,640]{2,1,0:T(8,128)(2,1)S(1)}, u32[]{:S(2)}, u32[]{:S(2)}) collective-permute-start(bf16[2,192,640]{2,1,0:T(8,128)(2,1)S(1)} %get-tuple-element.215), channel_id=1, source_target_pairs={{0,16},{4,20},{8,24},{12,28},{16,0},{20,4},{24,8},{28,12},{1,17},{... | collective-permute-start | bytes 1474568 | tf_op jit(solution)/shard_map/ppermute | solution.py:693
  509.9 13.4 %copy-start.29 = (f32[256]{0:T(256)S(1)}, f32[256]{0:T(256)}, u32[]{:S(2)}) copy-start(f32[256]{0:T(256)} %get-tuple-element.190) | copy-start | bytes 3076
  509.9 10.8 %collective-permute-start.29 = (bf16[2,192,512]{2,1,0:T(8,128)(2,1)S(1)}, bf16[2,192,512]{2,1,0:T(8,128)(2,1)S(1)}, u32[]{:S(2)}, u32[]{:S(2)}) collective-permute-start(bf16[2,192,512]{2,1,0:T(8,128)(2,1)S(1)} %get-tuple-element.217), channel_id=1, source_target_pairs={{0,8},{4,12},{8,0},{12,4},{16,24},{20,28},{24,16},{28,20},{1,9},{5... | collective-permute-start | bytes 1179656 | tf_op jit(solution)/shard_map/ppermute | solution.py:693
  521.0 7.1 %collective-permute-start.32 = (bf16[192,640]{1,0:T(8,128)(2,1)S(1)}, bf16[192,640]{1,0:T(8,128)(2,1)S(1)}, u32[]{:S(2)}, u32[]{:S(2)}) collective-permute-start(bf16[192,640]{1,0:T(8,128)(2,1)S(1)} %fusion.23), channel_id=1, source_target_pairs={{0,8},{4,12},{8,0},{12,4},{16,24},{20,28},{24,16},{28,20},{1,9},{5... | collective-permute-start | bytes 737288 | tf_op jit(solution)/shard_map/ppermute | solution.py:693
  522.4 5.7 %collective-permute-start.31 = (bf16[192,512]{1,0:T(8,128)(2,1)S(1)}, bf16[192,512]{1,0:T(8,128)(2,1)S(1)}, u32[]{:S(2)}, u32[]{:S(2)}) collective-permute-start(bf16[192,512]{1,0:T(8,128)(2,1)S(1)} %fusion.26), channel_id=1, source_target_pairs={{0,16},{4,20},{8,24},{12,28},{16,0},{20,4},{24,8},{28,12},{1,17},{... | collective-permute-start | bytes 589832 | tf_op jit(solution)/shard_map/ppermute | solution.py:693
  528.3 11.1 %copy-start.6 = (f32[256,1536]{1,0:T(8,128)S(1)}, f32[256,1536]{1,0:T(8,128)}, u32[]{:S(2)}) copy-start(f32[256,1536]{1,0:T(8,128)} %get-tuple-element.228) | copy-start | bytes 4718596
  528.3 11.1 %copy-start.30 = (f32[256]{0:T(256)S(1)}, f32[256]{0:T(256)}, u32[]{:S(2)}) copy-start(f32[256]{0:T(256)} %get-tuple-element.194) | copy-start | bytes 3076
  532.9 16.9 %all-to-all-start.2 = ((bf16[4,48,1152]{2,1,0:T(8,128)(2,1)}), bf16[4,48,1152]{2,1,0:T(8,128)(2,1)}, u32[]{:S(2)}, u32[]{:S(2)}) async-start(bf16[4,48,1152]{2,1,0:T(8,128)(2,1)} %bitcast.94), calls=%async_computation.2 | async-start | bytes 884736 | tf_op jit(solution)/shard_map/all_to_all | solution.py:729
  (11 other events, 17.3 us)
Sparse Core Ops, SparseCore 0:
  306.4 199.1 reduce-scatter.1

commit v3 on v2

--- a/solution.py
+++ b/solution.py
@@ -20,7 +20,8 @@
 NN = (((1,), (0,)), ((), ()))
 NT = (((1,), (1,)), ((), ()))
 TN = (((0,), (0,)), ((), ()))
-VMEM_LIMIT = 56 * 1024 * 1024
+VMEM_LIMIT = 60 * 1024 * 1024
+COLUMNS = 512
 
 
 def dot(left, right, dims=NN):
@@ -107,24 +108,30 @@
         out_ref[:, i * LANES : (i + 1) * LANES] = (slab.astype(BF16).astype(F32) * ATTENTION_SCALE).astype(BF16)
 
 
-def fill_bias(bias_ref, need_ref, place_ref, seg_column, seg_refs):
-    slots, rows, keys = bias_ref.shape
+def fill_bias(bias_ref, need_ref, place_ref, seg_row, seg_columns):
+    slots, keys, rows = bias_ref.shape
     for k in range(slots):
-        for j in range(keys // LANES):
-            lanes = slice(j * LANES, (j + 1) * LANES)
-            allowed = seg_column == seg_refs[k][j : j + 1, :].astype(F32)
-            if k == 0:
-                allowed = allowed & (
-                    lax.broadcasted_iota(jnp.int32, (rows, LANES), 1) + j * LANES
-                    <= lax.broadcasted_iota(jnp.int32, (rows, LANES), 0)
-                )
-            bias_ref[k, :, lanes] = jnp.where(allowed, 0.0, MASKED_SCORE)
-    first = jnp.min(seg_column)
+        allowed = seg_columns[k] == seg_row
+        if k == 0:
+            allowed = allowed & (
+                lax.broadcasted_iota(jnp.int32, (keys, rows), 0) <= lax.broadcasted_iota(jnp.int32, (keys, rows), 1)
+            )
+        bias_ref[k] = jnp.where(allowed, 0.0, MASKED_SCORE)
+    first = jnp.min(seg_row)
     need = jnp.int32(1)
     for k in range(1, slots):
-        last = jnp.max(seg_refs[k][: keys // LANES, :].astype(F32))
-        need = jnp.where((last >= first) & (k <= place_ref[0]), k + 1, need)
+        need = jnp.where((jnp.max(seg_columns[k]) >= first) & (k <= place_ref[0]), k + 1, need)
     need_ref[0] = need
+
+
+def prepare_bias(bias_ref, need_ref, place_ref, seg_refs):
+    slots, keys, _ = bias_ref.shape
+    halves = keys // LANES
+    seg_rows = [
+        jnp.concatenate([ref[j : j + 1, :].astype(F32) for j in range(halves)], axis=1) for ref in seg_refs
+    ]
+    seg_columns = [jnp.broadcast_to(row, (LANES, keys)).T[:, :1] for row in seg_rows]
+    fill_bias(bias_ref, need_ref, place_ref, seg_rows[0], seg_columns)
 
 
 def head_slab(block, head, upper):
@@ -135,22 +142,23 @@
     return jnp.where(low != upper, slab, 0.0)
 
 
-def attend_kernel(slots, ratio, place_ref, query_ref, seg_column_ref, *refs):
+def add_bias(scores, bias, ratio):
+    rows = bias.shape[1]
+    return jnp.concatenate([scores[:, r * rows : (r + 1) * rows] + bias for r in range(ratio)], axis=1)
+
+
+def attend_kernel(slots, ratio, place_ref, query_ref, *refs):
     kv_refs, seg_refs = refs[:slots], refs[slots : 2 * slots]
-    attended_ref, lse_ref, top_ref, bias_ref, stacked_ref, acc_ref, max_ref, sum_ref, need_ref = refs[2 * slots :]
+    attended_ref, lse_ref, top_ref, bias_ref, stacked_ref, scores_ref, acc_ref, max_ref, need_ref = refs[2 * slots :]
     rows = query_ref.shape[0]
     low = low_lanes(rows)
-    lane = lax.broadcasted_iota(jnp.int32, (rows, LANES), 1)
 
     @pl.when(pl.program_id(0) == 0)
     def _():
-        fill_bias(bias_ref, need_ref, place_ref, seg_column_ref[...], seg_refs)
+        prepare_bias(bias_ref, need_ref, place_ref, seg_refs)
 
     need = need_ref[0]
-
     outs = []
-    lse_all = jnp.zeros((rows, LANES), F32)
-    top_all = jnp.zeros((8, LANES), F32)
     for group in range(2):
         for r in range(ratio):
             stacked_ref[r * rows : (r + 1) * rows, :] = head_slab(
@@ -158,44 +166,39 @@
             ).astype(BF16)
         for k in range(slots):
 
-            def step(k=k):
+            def score(k=k):
                 kv = kv_refs[k][group * rows : (group + 1) * rows, :]
-                scores = dot(stacked_ref[...], kv, NT).reshape(ratio, rows, rows)
-                scores = (scores + bias_ref[k][None]).reshape(ratio * rows, rows)
-                top = jnp.max(scores, axis=-1, keepdims=True)
-                if k == 0:
-                    weights = jnp.exp(scores - top)
-                    max_ref[...] = top
-                    sum_ref[...] = jnp.sum(weights, axis=-1, keepdims=True)
-                    acc_ref[...] = dot(weights.astype(BF16), kv)
-                else:
-                    before = max_ref[...]
-                    top = jnp.maximum(top, before)
-                    shrink = jnp.exp(before - top)
-                    weights = jnp.exp(scores - top)
-                    max_ref[...] = top
-                    sum_ref[...] = sum_ref[...] * shrink + jnp.sum(weights, axis=-1, keepdims=True)
-                    acc_ref[...] = acc_ref[...] * shrink + dot(weights.astype(BF16), kv)
+                scores = add_bias(dot(kv, stacked_ref[...], NT), bias_ref[k], ratio)
+                scores_ref[k] = scores
+                top = jnp.max(scores, axis=0, keepdims=True)
+                max_ref[...] = top if k == 0 else jnp.maximum(max_ref[...], top)
 
             if k == 0:
-                step()
+                score()
             else:
-                pl.when(k < need)(step)
-        total = sum_ref[...]
-        mixed = acc_ref[...] / total
-        lse = max_ref[...] + jnp.log(total)
+                pl.when(k < need)(score)
+        for k in range(slots):
+
+            def mix(k=k):
+                kv = kv_refs[k][group * rows : (group + 1) * rows, :]
+                kv = jnp.where(low, jnp.ones_like(kv), kv)
+                weights = jnp.exp(scores_ref[k] - max_ref[...]).astype(BF16)
+                part = dot(kv, weights, TN)
+                acc_ref[...] = part if k == 0 else acc_ref[...] + part
+
+            if k == 0:
+                mix()
+            else:
+                pl.when(k < need)(mix)
+        total = acc_ref[:1, :]
+        lse_ref[0, group : group + 1, :] = max_ref[...] + jnp.log(total)
+        top_ref[0, group : group + 1, :] = max_ref[...]
+        mixed = acc_ref[HDIM:, :] / total
         for r in range(ratio):
-            head = group * ratio + r
-            outs.append(mixed[r * rows : (r + 1) * rows])
-            lse_all = jnp.where(lane == head, lse[r * rows : (r + 1) * rows], lse_all)
-            peak = jnp.max(max_ref[r * rows : (r + 1) * rows, :], axis=0, keepdims=True)
-            top_all = jnp.where(lane[:8] == head, peak, top_all)
+            outs.append(mixed[:, r * rows : (r + 1) * rows])
     for i in range(len(outs) // 2):
-        attended_ref[:, i * LANES : (i + 1) * LANES] = jnp.where(
-            low, pltpu.roll(outs[2 * i], HDIM, 1), outs[2 * i + 1]
-        ).astype(BF16)
-    lse_ref[0] = lse_all
-    top_ref[0] = top_all
+        slab = jnp.concatenate([outs[2 * i], outs[2 * i + 1]], axis=0)
+        attended_ref[:, i * LANES : (i + 1) * LANES] = slab.T.astype(BF16)
 
 
 def kv_specs(slots, groups, rows):
@@ -204,59 +207,50 @@
     ] * slots
 
 
-def attend(queries, kv_slots, seg_column, place, groups):
+def attend(queries, kv_slots, place, groups):
     slots = len(kv_slots)
     rows, width = queries.shape
     ratio = width // HDIM // groups
     steps = groups // 2
     block = 2 * ratio * HDIM
+    stats = pl.BlockSpec((1, 2, ratio * rows), lambda s: (s, 0, 0))
     return pl.pallas_call(
         functools.partial(attend_kernel, slots, ratio),
-        out_shape=(
-            jax.ShapeDtypeStruct((rows, width), BF16),
-            jax.ShapeDtypeStruct((steps, rows, LANES), F32),
-            jax.ShapeDtypeStruct((steps, 8, LANES), F32),
-        ),
+        out_shape=(jax.ShapeDtypeStruct((rows, width), BF16),)
+        + (jax.ShapeDtypeStruct((steps, 2, ratio * rows), F32),) * 2,
         grid=(steps,),
         in_specs=[
             pl.BlockSpec(memory_space=pltpu.SMEM),
             pl.BlockSpec((rows, block), lambda s: (0, s)),
-            pl.BlockSpec((rows, 1), lambda s: (0, 0)),
         ]
         + kv_specs(slots, groups, rows),
-        out_specs=(
-            pl.BlockSpec((rows, block), lambda s: (0, s)),
-            pl.BlockSpec((1, rows, LANES), lambda s: (s, 0, 0)),
-            pl.BlockSpec((1, 8, LANES), lambda s: (s, 0, 0)),
-        ),
+        out_specs=(pl.BlockSpec((rows, block), lambda s: (0, s)), stats, stats),
         scratch_shapes=[
             pltpu.VMEM((slots, rows, rows), F32),
             pltpu.VMEM((ratio * rows, LANES), BF16),
-            pltpu.VMEM((ratio * rows, LANES), F32),
-            pltpu.VMEM((ratio * rows, 1), F32),
-            pltpu.VMEM((ratio * rows, 1), F32),
+            pltpu.VMEM((slots, rows, ratio * rows), F32),
+            pltpu.VMEM((LANES, ratio * rows), F32),
+            pltpu.VMEM((1, ratio * rows), F32),
             pltpu.SMEM((1,), jnp.int32),
         ],
         compiler_params=params(),
         cost_estimate=cost(20),
         name="attend",
-    )(place, queries, seg_column, *kv_slots, *kv_slots)
-
-
-def attend_back_kernel(slots, ratio, place_ref, query_ref, attended_ref, grad_ref, lse_ref, cos_ref, sin_ref, seg_column_ref, *refs):
+    )(place, queries, *kv_slots, *kv_slots)
+
+
+def attend_back_kernel(slots, ratio, place_ref, query_ref, attended_ref, grad_ref, lse_ref, cos_ref, sin_ref, *refs):
     kv_refs, seg_refs = refs[:slots], refs[slots : 2 * slots]
     refs = refs[2 * slots :]
     back_ref, dkv_refs = refs[0], refs[1 : slots + 1]
-    bias_ref, query_s, grad_s, acc_ref, lse_s, delta_s, need_ref = refs[slots + 1 :]
+    bias_ref, query_s, grad_s, acc_ref, delta_s, need_ref = refs[slots + 1 :]
     rows = query_ref.shape[0]
-    low = low_lanes(rows)
 
     @pl.when(pl.program_id(0) == 0)
     def _():
-        fill_bias(bias_ref, need_ref, place_ref, seg_column_ref[...], seg_refs)
+        prepare_bias(bias_ref, need_ref, place_ref, seg_refs)
 
     need = need_ref[0]
-
     outs = []
     for group in range(2):
         for r in range(ratio):
@@ -265,24 +259,20 @@
             query_s[part, :] = head_slab(query_ref, head, False).astype(BF16)
             grad = head_slab(grad_ref, head, True)
             grad_s[part, :] = grad.astype(BF16)
-            delta_s[part, :] = jnp.sum(grad * head_slab(attended_ref, head, True), axis=-1, keepdims=True)
-            lse_s[part, :] = lse_ref[0, :, head : head + 1]
+            product = (grad * head_slab(attended_ref, head, True)).T
+            delta_s[:, part] = jnp.sum(product, axis=0, keepdims=True)
         for k in range(slots):
 
             def step(k=k):
                 kv = kv_refs[k][group * rows : (group + 1) * rows, :]
-                scores = dot(query_s[...], kv, NT).reshape(ratio, rows, rows)
-                scores = (scores + bias_ref[k][None]).reshape(ratio * rows, rows)
-                weights = jnp.exp(scores - lse_s[...])
-                weight_grad = dot(grad_s[...], kv, NT)
+                scores = add_bias(dot(kv, query_s[...], NT), bias_ref[k], ratio)
+                weights = jnp.exp(scores - lse_ref[0, group : group + 1, :])
+                weight_grad = dot(kv, grad_s[...], NT)
                 score_grad = (weights * (weight_grad - delta_s[...])).astype(BF16)
-                query_part = dot(score_grad, kv)
-                if k == 0:
-                    acc_ref[...] = query_part
-                else:
-                    acc_ref[...] += query_part
+                part = dot(kv, score_grad, TN)
+                acc_ref[...] = part if k == 0 else acc_ref[...] + part
                 dkv_refs[k][group * rows : (group + 1) * rows, :] = (
-                    dot(score_grad, query_s[...], TN) + dot(weights.astype(BF16), grad_s[...], TN)
+                    dot(score_grad, query_s[...]) + dot(weights.astype(BF16), grad_s[...])
                 ).astype(BF16)
 
             if k == 0:
@@ -295,15 +285,15 @@
                     dkv_refs[k][group * rows : (group + 1) * rows, :] = jnp.zeros((rows, LANES), BF16)
 
         for r in range(ratio):
-            outs.append(acc_ref[r * rows : (r + 1) * rows, :] * ATTENTION_SCALE)
+            outs.append(acc_ref[:HDIM, r * rows : (r + 1) * rows] * ATTENTION_SCALE)
     cosine, sine = cos_ref[...], sin_ref[...]
     for i in range(len(outs) // 2):
-        slab = jnp.where(low, outs[2 * i], pltpu.roll(outs[2 * i + 1], HDIM, 1))
+        slab = jnp.concatenate([outs[2 * i], outs[2 * i + 1]], axis=0).T
         slab = slab * cosine - partner_lanes(slab) * sine
         back_ref[:, i * LANES : (i + 1) * LANES] = slab.astype(BF16)
 
 
-def attend_back(queries, attended, grad, lse, tables, kv_slots, seg_column, place, groups):
+def attend_back(queries, attended, grad, lse, tables, kv_slots, place, groups):
     slots = len(kv_slots)
     rows, width = queries.shape
     ratio = width // HDIM // groups
@@ -321,10 +311,9 @@
             wide,
             wide,
             wide,
-            pl.BlockSpec((1, rows, LANES), lambda s: (s, 0, 0)),
+            pl.BlockSpec((1, 2, ratio * rows), lambda s: (s, 0, 0)),
             whole,
             whole,
-            pl.BlockSpec((rows, 1), lambda s: (0, 0)),
         ]
         + kv_specs(slots, groups, rows),
         out_specs=(wide,) + (pl.BlockSpec((2 * rows, LANES), lambda s: (s, 0)),) * slots,
@@ -332,15 +321,14 @@
             pltpu.VMEM((slots, rows, rows), F32),
             pltpu.VMEM((ratio * rows, LANES), BF16),
             pltpu.VMEM((ratio * rows, LANES), BF16),
-            pltpu.VMEM((ratio * rows, LANES), F32),
-            pltpu.VMEM((ratio * rows, 1), F32),
-            pltpu.VMEM((ratio * rows, 1), F32),
+            pltpu.VMEM((LANES, ratio * rows), F32),
+            pltpu.VMEM((1, ratio * rows), F32),
             pltpu.SMEM((1,), jnp.int32),
         ],
         compiler_params=params(),
         cost_estimate=cost(2),
         name="attend_back",
-    )(place, queries, attended, grad, lse, *tables, seg_column, *kv_slots, *kv_slots)
+    )(place, queries, attended, grad, lse, *tables, *kv_slots, *kv_slots)
     return out[0], out[1:]
 
 
@@ -364,10 +352,8 @@
 def expert_kernel(blocks, slot_rows, local_experts, place_ref, router_ref, gate_ref, up_ref, down_ref, *refs):
     sources = 2 * blocks - 1
     normed_in, cot_in = refs[:sources], refs[sources : 2 * sources]
-    refs = refs[2 * sources :]
-    xs_ref, cs_ref, hs_ref, gate_grad_ref, up_grad_ref, hit_ref = refs[:6]
-    grad_out, router_grad_ref = refs[6:8]
-    x_all, c_all, info, gates, back, grad_acc, grad_low, sems, out_sem = refs[8:]
+    xs_out, cs_out, hs_ref, gate_grad_ref, up_grad_ref, hits, grad_out, router_grad_ref = refs[2 * sources : 2 * sources + 8]
+    x_all, c_all, info, gates, back, xs_all, cs_all, gate_slots, slot_grads, sems, save_sem, out_sem = refs[2 * sources + 8 :]
     step = pl.program_id(0)
     rows, width = x_all.shape[1:]
     expert_pad = router_ref.shape[0]
@@ -380,6 +366,12 @@
             pltpu.make_async_copy(cot_in[s], c_all.at[i], sems.at[1, i]),
         )
 
+    def save_copies():
+        return (
+            pltpu.make_async_copy(xs_all, xs_out, save_sem.at[0]),
+            pltpu.make_async_copy(cs_all, cs_out, save_sem.at[1]),
+        )
+
     @pl.when(step == 0)
     def _():
         for i in range(blocks):
@@ -390,39 +382,43 @@
                     for copy in source_copies(i, s):
                         copy.start()
 
-        for i in range(blocks):
-            for copy in source_copies(i, 0):
-                copy.wait()
         same = jnp.where(
             lax.broadcasted_iota(jnp.int32, (rows, rows), 0) == lax.broadcasted_iota(jnp.int32, (rows, rows), 1),
             1.0,
             0.0,
         ).astype(BF16)
+        slot_ids = lax.broadcasted_iota(jnp.int32, (slot_rows, rows), 0).astype(F32)
+        back[...] = jnp.zeros_like(back)
         for i in range(blocks):
+            for copy in source_copies(i, 0):
+                copy.wait()
             info[i] = dot(c_all[i, :, width:], same, TN)
             logits = dot(router_ref[...], x_all[i], NT)
             logits = jnp.where(info[i, :expert_pad, :] >= 0, logits, MASKED_SCORE)
             weights = jnp.exp(logits - jnp.max(logits, axis=0, keepdims=True))
             gates[i] = weights / jnp.sum(weights, axis=0, keepdims=True)
-        back[...] = jnp.zeros_like(back)
-        grad_acc[...] = jnp.zeros_like(grad_acc)
-
-    slot_ids = lax.broadcasted_iota(jnp.int32, (slot_rows, rows), 0).astype(F32)
-    gate_slots = []
-    for i in range(blocks):
-        hit = slot_ids == info[i, mine, :]
-        part = slice(i * slot_rows, (i + 1) * slot_rows)
-        gate_slots.append(
-            jnp.sum(jnp.where(hit, gates[i, mine, :], 0.0), axis=-1, keepdims=True)
-        )
-        hit = jnp.where(hit, 1.0, 0.0).astype(BF16)
-        hit_ref[0, part, :] = hit
-        xs_ref[0, part, :] = dot(hit, x_all[i]).astype(BF16)
-        cs_ref[0, part, :] = dot(hit, c_all[i, :, :width]).astype(BF16)
-    gate_slot = jnp.concatenate(gate_slots, axis=0) * RESIDUAL_SCALE
-    gate_pre = dot(xs_ref[0], gate_ref[0])
-    up_pre = dot(xs_ref[0], up_ref[0])
-    raw_grad = dot(cs_ref[0], down_ref[0])
+            for e in range(local_experts):
+                own = pl.ds(first_expert + e, 1)
+                hit = slot_ids == info[i, own, :]
+                gate_slots[e, i * slot_rows : (i + 1) * slot_rows, :] = RESIDUAL_SCALE * jnp.sum(
+                    jnp.where(hit, gates[i, own, :], 0.0), axis=-1, keepdims=True
+                )
+                hits[i, e * slot_rows : (e + 1) * slot_rows, :] = jnp.where(hit, 1.0, 0.0).astype(BF16)
+            for source, target in ((x_all, xs_all), (c_all, cs_all)):
+                for c in range(width // COLUMNS):
+                    columns = slice(c * COLUMNS, (c + 1) * COLUMNS)
+                    picked = dot(hits[i], source[i, :, columns]).astype(BF16)
+                    for e in range(local_experts):
+                        target[e, i * slot_rows : (i + 1) * slot_rows, columns] = picked[
+                            e * slot_rows : (e + 1) * slot_rows
+                        ]
+        for copy in save_copies():
+            copy.start()
+
+    gate_slot = gate_slots[step]
+    gate_pre = dot(xs_all[step], gate_ref[0])
+    up_pre = dot(xs_all[step], up_ref[0])
+    raw_grad = dot(cs_all[step], down_ref[0])
     sigmoid = 1.0 / (1.0 + jnp.exp(-gate_pre))
     active = gate_pre * sigmoid
     expert_hidden = (active * up_pre).astype(BF16).astype(F32)
@@ -431,34 +427,44 @@
     hidden_grad = raw_grad * gate_slot
     gate_grad_ref[0] = (hidden_grad * up_pre * sigmoid * (1.0 + gate_pre * (1.0 - sigmoid))).astype(BF16)
     up_grad_ref[0] = (hidden_grad * active).astype(BF16)
-    slot_grad = (
-        dot(gate_grad_ref[0], gate_ref[0], NT) + dot(up_grad_ref[0], up_ref[0], NT)
-    ).astype(BF16)
+    spot = pl.ds(pl.multiple_of(step * slot_rows, slot_rows), slot_rows)
+    for c in range(width // COLUMNS):
+        columns = slice(c * COLUMNS, (c + 1) * COLUMNS)
+        slot_grad = (
+            dot(gate_grad_ref[0], gate_ref[0, columns, :], NT) + dot(up_grad_ref[0], up_ref[0, columns, :], NT)
+        ).astype(BF16)
+        for i in range(blocks):
+            slot_grads[i, spot, columns] = slot_grad[i * slot_rows : (i + 1) * slot_rows]
     for i in range(blocks):
         part = slice(i * slot_rows, (i + 1) * slot_rows)
-        hit = hit_ref[0, part, :]
-        back_row = jnp.sum(hit.astype(F32) * back_slot[part], axis=0, keepdims=True)
+        back_row = jnp.sum(hits[i, spot, :].astype(F32) * back_slot[part], axis=0, keepdims=True)
         back[i, mine, :] = back_row * gates[i, mine, :]
-        grad_acc[i] += dot(hit, slot_grad[part], TN)
 
     @pl.when(step == local_experts - 1)
     def _():
+        def copy(i):
+            return pltpu.make_async_copy(
+                c_all.at[i, :, pl.ds(0, width)], grad_out.at[place_ref[1 + blocks + i]], out_sem.at[i]
+            )
+
         router_sum = None
         for i in range(blocks):
             share = back[i]
             logit_grad = (share - gates[i] * jnp.sum(share, axis=0, keepdims=True)).astype(BF16)
-            grad_low[i] = (grad_acc[i] + dot(logit_grad, router_ref[...], TN)).astype(BF16)
+            turned = hits[i].T
+            for c in range(width // COLUMNS):
+                columns = slice(c * COLUMNS, (c + 1) * COLUMNS)
+                c_all[i, :, columns] = (
+                    dot(turned, slot_grads[i, :, columns]) + dot(logit_grad, router_ref[:, columns], TN)
+                ).astype(BF16)
+            copy(i).start()
             part = dot(logit_grad, x_all[i])
             router_sum = part if router_sum is None else router_sum + part
         router_grad_ref[...] = router_sum
-
-        def copy(i):
-            return pltpu.make_async_copy(grad_low.at[i], grad_out.at[place_ref[1 + blocks + i]], out_sem.at[i])
-
-        for i in range(blocks):
-            copy(i).start()
         for i in range(blocks):
             copy(i).wait()
+        for saved in save_copies():
+            saved.wait()
 
 
 def run_experts(place, router_t, gate_weight, up_weight, down_weight, normed, cots, slot_rows):
@@ -468,26 +474,24 @@
     rows = normed[0].shape[0]
     expert_pad = router_t.shape[0]
     slots = blocks * slot_rows
+    stacked = local_experts * slot_rows
     anywhere = pl.BlockSpec(memory_space=pl.ANY)
     weight_spec = pl.BlockSpec((1, width, hidden), lambda e, place: (e, 0, 0))
-
-    def slot_spec(columns):
-        return pl.BlockSpec((1, slots, columns), lambda e, place: (e, 0, 0))
-
-    def slot_shape(columns):
-        return jax.ShapeDtypeStruct((local_experts, slots, columns), BF16)
-
+    narrow = pl.BlockSpec((1, slots, hidden), lambda e, place: (e, 0, 0))
+    wide_shape = jax.ShapeDtypeStruct((local_experts, slots, width), BF16)
+    narrow_shape = jax.ShapeDtypeStruct((local_experts, slots, hidden), BF16)
     out = pl.pallas_call(
         functools.partial(expert_kernel, blocks, slot_rows, local_experts),
         out_shape=(
-            slot_shape(width),
-            slot_shape(width),
-            slot_shape(hidden),
-            slot_shape(hidden),
-            slot_shape(hidden),
-            slot_shape(rows),
-        )
-        + (jax.ShapeDtypeStruct((blocks, rows, width), BF16), jax.ShapeDtypeStruct((expert_pad, width), F32)),
+            wide_shape,
+            wide_shape,
+            narrow_shape,
+            narrow_shape,
+            narrow_shape,
+            jax.ShapeDtypeStruct((blocks, stacked, rows), BF16),
+            jax.ShapeDtypeStruct((blocks, rows, width), BF16),
+            jax.ShapeDtypeStruct((expert_pad, width), F32),
+        ),
         grid_spec=pltpu.PrefetchScalarGridSpec(
             num_scalar_prefetch=1,
             grid=(local_experts,),
@@ -495,23 +499,27 @@
             + [weight_spec] * 3
             + [anywhere] * (2 * sources),
             out_specs=(
-                slot_spec(width),
-                slot_spec(width),
-                slot_spec(hidden),
-                slot_spec(hidden),
-                slot_spec(hidden),
-                slot_spec(rows),
-            )
-            + (anywhere, pl.BlockSpec((expert_pad, width), lambda e, place: (0, 0))),
+                anywhere,
+                anywhere,
+                narrow,
+                narrow,
+                narrow,
+                pl.BlockSpec((blocks, stacked, rows), lambda e, place: (0, 0, 0)),
+                anywhere,
+                pl.BlockSpec((expert_pad, width), lambda e, place: (0, 0)),
+            ),
             scratch_shapes=[
                 pltpu.VMEM((blocks, rows, width), BF16),
                 pltpu.VMEM((blocks, rows, width + LANES), BF16),
                 pltpu.VMEM((blocks, LANES, rows), F32),
                 pltpu.VMEM((blocks, expert_pad, rows), F32),
                 pltpu.VMEM((blocks, expert_pad, rows), F32),
-                pltpu.VMEM((blocks, rows, width), F32),
-                pltpu.VMEM((blocks, rows, width), BF16),
+                pltpu.VMEM((local_experts, slots, width), BF16),
+                pltpu.VMEM((local_experts, slots, width), BF16),
+                pltpu.VMEM((local_experts, slots, 1), F32),
+                pltpu.VMEM((blocks, stacked, width), BF16),
                 pltpu.SemaphoreType.DMA((2, blocks)),
+                pltpu.SemaphoreType.DMA((2,)),
                 pltpu.SemaphoreType.DMA((blocks,)),
             ],
         ),
@@ -522,57 +530,62 @@
     return out[:6], out[6], out[7]
 
 
-def mixture_kernel(blocks, slot_rows, local_experts, order_ref, down_ref, hs_ref, hit_ref, mix_out, mix_acc, mix_low, out_sem):
+def mixture_kernel(blocks, slot_rows, local_experts, order_ref, down_ref, hs_ref, hits_ref, mix_one, mix_two, slot_outs, mix_low, out_sem):
     step = pl.program_id(0)
-
-    @pl.when(step == 0)
-    def _():
-        mix_acc[...] = jnp.zeros_like(mix_acc)
-
-    slot_out = dot(hs_ref[0], down_ref[0], NT).astype(BF16)
-    for i in range(blocks):
-        part = slice(i * slot_rows, (i + 1) * slot_rows)
-        mix_acc[i] += dot(hit_ref[0, part, :], slot_out[part], TN)
+    width = down_ref.shape[1]
+    spot = pl.ds(pl.multiple_of(step * slot_rows, slot_rows), slot_rows)
+    for c in range(width // COLUMNS):
+        columns = slice(c * COLUMNS, (c + 1) * COLUMNS)
+        slot_out = dot(hs_ref[0], down_ref[0, columns, :], NT).astype(BF16)
+        for i in range(blocks):
+            slot_outs[i, spot, columns] = slot_out[i * slot_rows : (i + 1) * slot_rows]
 
     @pl.when(step == local_experts - 1)
     def _():
-        def copy(i):
-            return pltpu.make_async_copy(mix_low.at[i], mix_out.at[order_ref[i]], out_sem.at[i])
+        def copy(i, h):
+            columns = pl.ds(h * (width // 2), width // 2)
+            return pltpu.make_async_copy(
+                mix_low.at[i, :, columns], (mix_one, mix_two)[h].at[order_ref[i]], out_sem.at[i, h]
+            )
 
         for i in range(blocks):
-            mix_low[i] = mix_acc[i].astype(BF16)
-            copy(i).start()
+            turned = hits_ref[i].T
+            for c in range(width // COLUMNS):
+                columns = slice(c * COLUMNS, (c + 1) * COLUMNS)
+                mix_low[i, :, columns] = dot(turned, slot_outs[i, :, columns]).astype(BF16)
+            for h in range(2):
+                copy(i, h).start()
         for i in range(blocks):
-            copy(i).wait()
+            for h in range(2):
+                copy(i, h).wait()
 
 
 def run_mixture(order, down_weight, saved, slot_rows):
-    hs, hit = saved[2], saved[5]
+    hs, hits = saved[2], saved[5]
     local_experts, width, hidden = down_weight.shape
-    slots, rows = hit.shape[1:]
-    blocks = slots // slot_rows
+    blocks, stacked, rows = hits.shape
     return pl.pallas_call(
         functools.partial(mixture_kernel, blocks, slot_rows, local_experts),
-        out_shape=jax.ShapeDtypeStruct((blocks, rows, width), BF16),
+        out_shape=(jax.ShapeDtypeStruct((blocks, rows, width // 2), BF16),) * 2,
         grid_spec=pltpu.PrefetchScalarGridSpec(
             num_scalar_prefetch=1,
             grid=(local_experts,),
             in_specs=[
                 pl.BlockSpec((1, width, hidden), lambda e, order: (e, 0, 0)),
-                pl.BlockSpec((1, slots, hidden), lambda e, order: (e, 0, 0)),
-                pl.BlockSpec((1, slots, rows), lambda e, order: (e, 0, 0)),
+                pl.BlockSpec((1, hs.shape[1], hidden), lambda e, order: (e, 0, 0)),
+                pl.BlockSpec((blocks, stacked, rows), lambda e, order: (0, 0, 0)),
             ],
-            out_specs=pl.BlockSpec(memory_space=pl.ANY),
+            out_specs=(pl.BlockSpec(memory_space=pl.ANY),) * 2,
             scratch_shapes=[
-                pltpu.VMEM((blocks, rows, width), F32),
+                pltpu.VMEM((blocks, stacked, width), BF16),
                 pltpu.VMEM((blocks, rows, width), BF16),
-                pltpu.SemaphoreType.DMA((blocks,)),
+                pltpu.SemaphoreType.DMA((blocks, 2)),
             ],
         ),
         compiler_params=params(),
         cost_estimate=cost(10),
         name="mixture",
-    )(order, down_weight, hs, hit)
+    )(order, down_weight, hs, hits)
 
 
 def turn_rows(block, sides_ref, owned):
@@ -586,34 +599,71 @@
             sides_ref[owner % 2, spot : spot + owned, :] = turned[o * owned : (o + 1) * owned]
 
 
-def expert_grad_kernel(xs_ref, cs_ref, hs_ref, gate_grad_ref, up_grad_ref, out_ref, turned):
-    owners, owned = out_ref.shape[0], out_ref.shape[3]
+def grad_products(side, xs_ref, cs_ref, hs_ref, gate_grad_ref, up_grad_ref, sides, owned):
     for left_ref, rights in ((xs_ref, ((0, gate_grad_ref), (1, up_grad_ref))), (cs_ref, ((2, hs_ref),))):
-        turned[...] = left_ref[0].T
+        turn_rows(left_ref[0], sides, owned)
         for w, right_ref in rights:
-            grad = dot(turned[...], right_ref[0]).astype(BF16)
-            for o in range(owners):
-                out_ref[o, w, 0] = grad[o * owned : (o + 1) * owned]
-
-
-def run_expert_grads(saved, owners):
+            yield w, dot(sides[side], right_ref[0])
+
+
+def expert_send_kernel(place_ref, xs_ref, cs_ref, hs_ref, gate_grad_ref, up_grad_ref, *refs):
+    send_refs, sides = refs[:-1], refs[-1]
+    owned = send_refs[0].shape[2]
+    side = 1 - place_ref[0] % 2
+    for w, grad in grad_products(side, xs_ref, cs_ref, hs_ref, gate_grad_ref, up_grad_ref, sides, owned):
+        for q, send_ref in enumerate(send_refs):
+            send_ref[w, 0] = grad[q * owned : (q + 1) * owned].astype(BF16)
+
+
+def expert_keep_kernel(bits, place_ref, xs_ref, cs_ref, hs_ref, gate_grad_ref, up_grad_ref, *refs):
+    count = 1 << (bits - 1)
+    received_refs, outs, sides = refs[:count], refs[count : count + 4], refs[-1]
+    owned = received_refs[0].shape[2]
+    hidden = hs_ref.shape[2] // 2
+    side = place_ref[0] % 2
+    for w, grad in grad_products(side, xs_ref, cs_ref, hs_ref, gate_grad_ref, up_grad_ref, sides, owned):
+        for q in range(count):
+            piece = (grad[q * owned : (q + 1) * owned] + received_refs[q][w, 0].astype(F32)).astype(BF16)
+            for route, bit in enumerate((1, bits - 1)):
+                part = piece[:, route * hidden : (route + 1) * hidden]
+                own = (place_ref[0] >> bit) & 1
+                spot = (q >> bit << (bit - 1)) | (q & ((1 << (bit - 1)) - 1))
+                here = q >> (bit - 1) & 1
+
+                @pl.when(own == here)
+                def _(route=route, part=part, spot=spot, w=w):
+                    outs[2 * route][spot, w, 0] = part
+
+                @pl.when(own != here)
+                def _(route=route, part=part, spot=spot, w=w):
+                    outs[2 * route + 1][spot, w, 0] = part
+
+
+def run_expert_grads(dp_word, saved, owners, received=()):
     xs, cs, hs, gate_grad, up_grad, _ = saved
     local_experts, slots, width = xs.shape
     hidden = hs.shape[2]
     owned = width // owners
-    wide = pl.BlockSpec((1, slots, width), lambda e: (e, 0, 0))
-    narrow = pl.BlockSpec((1, slots, hidden), lambda e: (e, 0, 0))
+    wide = pl.BlockSpec((1, slots, width), lambda e, place: (e, 0, 0))
+    narrow = pl.BlockSpec((1, slots, hidden), lambda e, place: (e, 0, 0))
+    pass_spec = pl.BlockSpec((3, 1, owned, hidden), lambda e, place: (0, e, 0, 0))
+    pass_shape = jax.ShapeDtypeStruct((3, local_experts, owned, hidden), BF16)
+    part_spec = pl.BlockSpec((owners // 4, 3, 1, owned, hidden // 2), lambda e, place: (0, 0, e, 0, 0))
+    part_shape = jax.ShapeDtypeStruct((owners // 4, 3, local_experts, owned, hidden // 2), BF16)
     return pl.pallas_call(
-        expert_grad_kernel,
-        out_shape=jax.ShapeDtypeStruct((owners, 3, local_experts, owned, hidden), BF16),
-        grid=(local_experts,),
-        in_specs=[wide, wide, narrow, narrow, narrow],
-        out_specs=pl.BlockSpec((owners, 3, 1, owned, hidden), lambda e: (0, 0, e, 0, 0)),
-        scratch_shapes=[pltpu.VMEM((width, slots), BF16)],
+        functools.partial(expert_keep_kernel, owners.bit_length() - 1) if received else expert_send_kernel,
+        out_shape=(part_shape,) * 4 if received else (pass_shape,) * (owners // 2),
+        grid_spec=pltpu.PrefetchScalarGridSpec(
+            num_scalar_prefetch=1,
+            grid=(local_experts,),
+            in_specs=[wide, wide, narrow, narrow, narrow] + [pass_spec] * len(received),
+            out_specs=(part_spec,) * 4 if received else (pass_spec,) * (owners // 2),
+            scratch_shapes=[pltpu.VMEM((2, width // 2, slots), BF16)],
+        ),
         compiler_params=params(),
-        cost_estimate=cost(30),
-        name="expert_grads",
-    )(xs, cs, hs, gate_grad, up_grad)
+        cost_estimate=cost(15),
+        name="expert_keep" if received else "expert_send",
+    )(dp_word, xs, cs, hs, gate_grad, up_grad, *received)
 
 
 def dense_grad_kernel(pairs, place_ref, *refs):
@@ -724,10 +774,17 @@
     return start_spread([tuple(t[..., :half] for t in terms), tuple(t[..., half:] for t in terms)])
 
 
-def finish_dense(routes, size):
+def finish_dense(routes, place, size):
     block = jnp.concatenate([add_low(*terms) for terms in routes], axis=-1)
-    parts = lax.all_to_all(block.reshape(size, -1, block.shape[-1]), "expert", 0, 0, tiled=True)
-    return jnp.sum(parts.astype(F32), axis=0)
+    parts = block.reshape(size, -1, block.shape[-1])
+    total = lax.dynamic_index_in_dim(parts, place, 0, keepdims=False).astype(F32)
+    passed = []
+    for k in range(1, size):
+        part = lax.dynamic_index_in_dim(parts, (place + k) % size, 0, keepdims=False)
+        passed.append(lax.ppermute(part, "expert", [(i, (i + k) % size) for i in range(size)]))
+    for part in lax.optimization_barrier(tuple(passed)):
+        total = total + part.astype(F32)
+    return total
 
 
 def reduce_top(top, dp_size, size):
@@ -838,10 +895,10 @@
         name="queries",
     )(normed, query_weight, *tables)
 
-    seg_column = segments.reshape(rows, 1).astype(F32)
     place_word = place.reshape(1).astype(jnp.int32)
-    attended, lse, top = attend(queries, kv_slots, seg_column, place_word, groups)
-    head_top = reduce_top(top, dp_size, size)[:, 0, : 2 * ratio].reshape(heads)
+    attended, lse, top = attend(queries, kv_slots, place_word, groups)
+    head_top = jnp.max(top.reshape(heads, rows), axis=1).reshape(1, heads)
+    head_top = reduce_top(head_top, dp_size, size).reshape(heads)
 
     hidden_in = tokens.astype(F32)
     hidden_mid = hidden_in + RESIDUAL_SCALE * dot(attended, output_weight, NT)
@@ -859,12 +916,13 @@
     grad_blocks = lax.all_to_all(grad_blocks, "expert", 0, 0, tiled=True)
 
     dp_word = dp_place.reshape(1).astype(jnp.int32)
-    expert_sums = run_expert_grads(saved, dp_size)
     mixture = run_mixture(blocks_of, down_weight, saved, slot_rows)
-    mixture, grad_blocks, expert_sums = lax.optimization_barrier((mixture, grad_blocks, expert_sums))
+    received = [flip(part, 1, dp_size) for part in run_expert_grads(dp_word, saved, dp_size)]
+    keep_a, send_a, keep_b, send_b = run_expert_grads(dp_word, saved, dp_size, received)
+    mixture, grad_blocks, send_a, send_b = lax.optimization_barrier((mixture, grad_blocks, send_a, send_b))
     normed_grad = jnp.sum(grad_blocks.astype(F32), axis=0)
-    expert_sums = lax.psum_scatter(expert_sums, "dp", scatter_dimension=0, tiled=True)[0].astype(F32)
-    mixture = lax.all_to_all(mixture, "expert", 0, 0, tiled=True)
+    passed = (flip(send_a, 2, dp_size), flip(send_b, dp_size // 2, dp_size))
+    mix_one = lax.all_to_all(mixture[0], "expert", 0, 0, tiled=True)
 
     out_grad = cotangent.astype(F32)
     mid_back, second_gain_part = norm_backward(hidden_mid, second_factor, second_gain, normed_grad)
@@ -872,25 +930,28 @@
     branch_grad = (RESIDUAL_SCALE * mid_grad).astype(BF16)
     attended_grad = dot(branch_grad, output_weight).astype(BF16)
     query_back, dkv = attend_back(
-        queries, attended, attended_grad, lse, tables, kv_slots, seg_column, place_word, groups
+        queries, attended, attended_grad, lse, tables, kv_slots, place_word, groups
     )
     keep, send = dense_grads(dp_word, [(branch_grad, attended), (normed, query_back)], dp_size)
+    stages = dp_size.bit_length() - 2
+    down, passed, mix_one, keep, send = lax.optimization_barrier((dkv[size - 1], passed, mix_one, keep, send))
+    expert_sums = step_spread(start_spread([(keep_a, passed[0]), (keep_b, passed[1])]), 1, dp_size, dp_place)
     wide = start_dense((keep, flip(send, 1, dp_size)))
-    stages = dp_size.bit_length() - 2
-    down = dkv[size - 1]
     for k in range(1, size):
         from_above = line_down(down, size)
-        if k == 1:
-            from_above, mixture = lax.optimization_barrier((from_above, mixture))
         if k == size - 2:
             from_above, wide = lax.optimization_barrier((from_above, wide))
-            wide = step_spread(wide, 0, dp_size, dp_place)
         if k < size - 1:
             down = add_low(from_above, dkv[size - 1 - k])
-    from_above, wide = lax.optimization_barrier((from_above, wide))
-    for stage in range(1, stages):
+    from_above, expert_sums, mix_two = lax.optimization_barrier((from_above, expert_sums, mixture[1]))
+    mix_two = lax.all_to_all(mix_two, "expert", 0, 0, tiled=True)
+    for stage in range(2, stages):
+        expert_sums = step_spread(expert_sums, stage, dp_size, dp_place)
+    expert_sums = [
+        jnp.concatenate([a[w].astype(F32) + b[w].astype(F32) for a, b in expert_sums], axis=-1) for w in range(3)
+    ]
+    for stage in range(stages):
         wide = step_spread(wide, stage, dp_size, dp_place)
-    block_out = (hidden_mid + jnp.sum(mixture.astype(F32), axis=0)).astype(BF16)
     key_back, value_back = pl.pallas_call(
         unpack_kernel,
         out_shape=(jax.ShapeDtypeStruct((rows, kv_width), BF16),) * 2,
@@ -916,7 +977,9 @@
     rest = start_dense((keep, flip(send, 1, dp_size)))
     for stage in range(stages):
         rest = step_spread(rest, stage, dp_size, dp_place)
-    wide_grad, rest_grad = finish_dense(wide, size), finish_dense(rest, size)
+    wide_grad, rest_grad = finish_dense(wide, place, size), finish_dense(rest, place, size)
+    mixture = jnp.concatenate([jnp.sum(part.astype(F32), axis=0) for part in (mix_one, mix_two)], axis=1)
+    block_out = (hidden_mid + mixture).astype(BF16)
     projection_grad, query_grad = wide_grad[:, :query_width], wide_grad[:, query_width:]
     key_grad = rest_grad[:, :kv_width]
     value_grad = rest_grad[:, kv_width : 2 * kv_width]

time: 572 us -> 544 us (0.951)
  the two profiles are of different devices: /device:TPU:24 before, /device:TPU:0 now
where the time goes in v3:
time: 544 us; the launch traced here: 536 us
  waiting for transfers between devices  185 us (34%)
  Pallas kernels  139 us (26%)
  starting transfers between devices  130 us (24%)
  other arithmetic  43.5 us (8%)
  local copies, waits for them, and re-layouts  19.7 us (4%)
  matrix products  16.5 us (3%)
    ppermute x21, waiting for transfers between devices, flip(): return lax.ppermute(value, 'dp', [(i, i ^ bit) for i in range(size)])  66.5 us
    ppermute x9, starting transfers between devices, line_up(): return lax.ppermute(value, 'expert', [(i, i + 1) for i in range(size - 1)])  58.7 us
    ppermute x9, waiting for transfers between devices, line_up(): return lax.ppermute(value, 'expert', [(i, i + 1) for i in range(size - 1)])  45.6 us
    pallas_call x1, Pallas kernels, run_experts(): pl.pallas_call(functools.partial(expert_kernel, blocks, slot_rows, local_...  41.5 us
    pallas_call x2, Pallas kernels, run_expert_grads(): pl.pallas_call(functools.partial(expert_keep_kernel, owners.bit_length()...  37.8 us
    ppermute x21, starting transfers between devices, flip(): return lax.ppermute(value, 'dp', [(i, i ^ bit) for i in range(size)])  26.3 us
    ppermute x6, waiting for transfers between devices, finish_dense(): lax.ppermute(part, 'expert', [(i, (i + k) % size) for i in range(size)])  23.2 us
    convert_element_type x16, other arithmetic, add_low(): return total.astype(BF16)  20.2 us
  transfers between devices with their start and end apart: 50, of which 28 were waited for; matrix products, arithmetic and copies ran while one was open for 13% of the time, Pallas kernels for 17%

profile of v3, /device:TPU:0, one launch (start us, length us, event | category | flops | bytes accessed | tf_op | source)
XLA Modules:
  0.0 535.5 jit_solution(7041075606484309094)
XLA Ops:
  4.9 4.2 front.1
  9.2 5.0 collective-permute-start
  14.1 11.5 %collective-permute-done.refs_1_.refs_5_ = bf16[2064,128]{1,0:T(8,128)(2,1)S(1)} collective-permute-done((bf16[2064,128]{1,0:T(8,128)(2,1)}, bf16[2064,128]{1,0:T(8,128)(2,1)S(1)}, u32[]{:S(2)}, u32[]{:S(2)}) %collective-permute-start) | collective-permute-done | bytes 528416 | tf_op jit(solution)/shard_map/ppermute | solution.py:717
  25.7 4.3 collective-permute-start.1
  30.0 10.3 %collective-permute-done.1.refs_2_.refs_6_ = bf16[2064,128]{1,0:T(8,128)(2,1)S(1)} collective-permute-done((bf16[2064,128]{1,0:T(8,128)(2,1)S(1)}, bf16[2064,128]{1,0:T(8,128)(2,1)S(1)}, u32[]{:S(2)}, u32[]{:S(2)}) %collective-permute-start.1) | collective-permute-done | bytes 528416 | tf_op jit(solution)/shard_map/ppermute | solution.py:717
  40.3 4.4 collective-permute-start.2
  45.5 2.6 extend.1.refs_7_
  48.1 4.4 collective-permute-start.14
  53.8 5.6 %queries.1.query_ref = bf16[256,1536]{1,0:T(8,128)(2,1)} custom-call(bf16[256,1536]{1,0:T(8,128)(2,1)} %get-tuple-element.96.normed_ref.refs_1_.refs_0_, bf16[1536,1536]{1,0:T(8,128)(2,1)} %query_ref.1, f32[256,128]{1,0:T(8,128)} %get-tuple-element.276.cos_ref, f32[256,128]{1,0:T(8,128)} %get-tuple-element.275.sin_ref), custom_call_target="tpu_custom_call" | custom-call | flops 5000000 | tf_op jit(solution)/shard_map/queries/pallas_call | solution.py:882
  60.2 8.2 %attend.1 = (bf16[256,1536]{1,0:T(8,128)(2,1)}, f32[4,2,768]{2,1,0:T(2,128)}, f32[4,2,768]{2,1,0:T(2,128)}) custom-call(s32[1]{0:T(128)} %bitcast.place_ref, bf16[256,1536]{1,0:T(8,128)(2,1)} %queries.1.query_ref, bf16[2064,128]{1,0:T(8,128)(2,1)} %get-tuple-element.97.refs_0_.refs_4_, bf16[2064,128]{1,0:T(8,128)(2,1)} %copy-done, ...), custom_call_target="tpu_custom_call" | custom-call | flops 20000000 | tf_op jit(solution)/shard_map/attend/pallas_call | solution.py:217
  68.4 4.1 multiply_reduce_fusion.2
  72.8 8.7 %collective-permute-start.8 = (bf16[256,1536]{1,0:T(8,128)(2,1)S(1)}, bf16[256,1536]{1,0:T(8,128)(2,1)S(1)}, u32[]{:S(2)}, u32[]{:S(2)}) collective-permute-start(bf16[256,1536]{1,0:T(8,128)(2,1)S(1)} %multiply_convert_fusion.1.refs_0_), channel_id=1, source_target_pairs={{0,1},{1,2},{2,3},{4,5},{5,6},{6,7},{8,9},{9,10},{10,11},{12,13},{... | collective-permute-start | bytes 2359304 | tf_op jit(solution)/shard_map/ppermute | solution.py:717
  82.9 8.5 %collective-permute-start.15 = (bf16[256,1664]{1,0:T(8,128)(2,1)}, bf16[256,1664]{1,0:T(8,128)(2,1)}, u32[]{:S(2)}, u32[]{:S(2)}) collective-permute-start(bf16[256,1664]{1,0:T(8,128)(2,1)} %collective-permute-done.14.refs_8_), channel_id=1, source_target_pairs={{0,1},{1,2},{2,3},{4,5},{5,6},{6,7},{8,9},{9,10},{10,11},{12,13},{... | collective-permute-start | bytes 2555912 | tf_op jit(solution)/shard_map/ppermute | solution.py:717
  92.6 6.9 %collective-permute-done.8.refs_1_ = bf16[256,1536]{1,0:T(8,128)(2,1)S(1)} collective-permute-done((bf16[256,1536]{1,0:T(8,128)(2,1)S(1)}, bf16[256,1536]{1,0:T(8,128)(2,1)S(1)}, u32[]{:S(2)}, u32[]{:S(2)}) %collective-permute-start.8) | collective-permute-done | bytes 786464 | tf_op jit(solution)/shard_map/ppermute | solution.py:717
  99.5 7.8 %collective-permute-start.9 = (bf16[256,1536]{1,0:T(8,128)(2,1)S(1)}, bf16[256,1536]{1,0:T(8,128)(2,1)}, u32[]{:S(2)}, u32[]{:S(2)}) collective-permute-start(bf16[256,1536]{1,0:T(8,128)(2,1)S(1)} %collective-permute-done.8.refs_1_), channel_id=1, source_target_pairs={{0,1},{1,2},{2,3},{4,5},{5,6},{6,7},{8,9},{9,10},{10,11},{12,13},{... | collective-permute-start | bytes 2359304 | tf_op jit(solution)/shard_map/ppermute | solution.py:717
  108.6 9.3 %collective-permute-done.15.refs_9_ = bf16[256,1664]{1,0:T(8,128)(2,1)} collective-permute-done((bf16[256,1664]{1,0:T(8,128)(2,1)}, bf16[256,1664]{1,0:T(8,128)(2,1)}, u32[]{:S(2)}, u32[]{:S(2)}) %collective-permute-start.15) | collective-permute-done | bytes 852000 | tf_op jit(solution)/shard_map/ppermute | solution.py:717
  117.9 7.8 %collective-permute-start.16 = (bf16[256,1664]{1,0:T(8,128)(2,1)}, bf16[256,1664]{1,0:T(8,128)(2,1)}, u32[]{:S(2)}, u32[]{:S(2)}) collective-permute-start(bf16[256,1664]{1,0:T(8,128)(2,1)} %collective-permute-done.15.refs_9_), channel_id=1, source_target_pairs={{0,1},{1,2},{2,3},{4,5},{5,6},{6,7},{8,9},{9,10},{10,11},{12,13},{... | collective-permute-start | bytes 2555912 | tf_op jit(solution)/shard_map/ppermute | solution.py:717
  127.0 7.6 %collective-permute-done.9.refs_2_ = bf16[256,1536]{1,0:T(8,128)(2,1)} collective-permute-done((bf16[256,1536]{1,0:T(8,128)(2,1)S(1)}, bf16[256,1536]{1,0:T(8,128)(2,1)}, u32[]{:S(2)}, u32[]{:S(2)}) %collective-permute-start.9) | collective-permute-done | bytes 786464 | tf_op jit(solution)/shard_map/ppermute | solution.py:717
  134.6 7.9 %collective-permute-start.10 = (bf16[256,1536]{1,0:T(8,128)(2,1)}, bf16[256,1536]{1,0:T(8,128)(2,1)}, u32[]{:S(2)}, u32[]{:S(2)}) collective-permute-start(bf16[256,1536]{1,0:T(8,128)(2,1)} %collective-permute-done.9.refs_2_), channel_id=1, source_target_pairs={{0,1},{1,2},{2,3},{4,5},{5,6},{6,7},{8,9},{9,10},{10,11},{12,13},{... | collective-permute-start | bytes 2359304 | tf_op jit(solution)/shard_map/ppermute | solution.py:717
  149.9 2.5 collective-permute-done.5
  152.4 2.6 collective-permute-start.6
  155.7 14.5 %collective-permute-done.6 = f32[1,24]{1,0:T(1,128)S(1)} collective-permute-done((f32[1,24]{1,0:T(1,128)S(1)}, f32[1,24]{1,0:T(1,128)S(1)}, u32[]{:S(2)}, u32[]{:S(2)}) %collective-permute-start.6) | collective-permute-done | bytes 128 | tf_op jit(solution)/shard_map/ppermute | solution.py:794
  172.1 2.6 collective-permute-done.7
  174.7 41.5 %experts.1 = (bf16[5,512,1536]{2,1,0:T(8,128)(2,1)}, bf16[5,512,1536]{2,1,0:T(8,128)(2,1)}, bf16[5,512,512]{2,1,0:T(8,128)(2,1)}, bf16[5,512,512]{2,1,0:T(8,128)...) custom-call(s32[9]{0:T(128)} %pad_add_fusion.place_ref, ...), custom_call_target="tpu_custom_call" | custom-call | flops 45000000 | tf_op jit(solution)/shard_map/experts/pallas_call | solution.py:483
  216.2 5.1 all-to-all-start
  221.2 16.7 %expert_send.1 = (bf16[3,5,192,512]{3,2,1,0:T(8,128)(2,1)}, bf16[3,5,192,512]{3,2,1,0:T(8,128)(2,1)}, bf16[3,5,192,512]{3,2,1,0:T(8,128)(2,1)}, bf16[3,5,192,512]{3,2,1,0:T(8,128)(2,1)}) custom-call(s32[1]{0:T(128)} %bitcast.8.place_ref, bf16[5,512,1536]{2,1,0:T(8,128)(2,1)} %get-tuple-element.106.xs_ref, bf16[5,512,1536]{2,1,0:T(8,128)(2,1)} %get-tuple-element.107.cs_ref, ...), custom_call_target="tpu_custom_call" | custom-call | flops 15000000 | tf_op jit(solution)/shard_map/expert_send/pallas_call | solution.py:653
  239.0 12.3 %mixture.1 = (bf16[4,256,768]{2,1,0:T(8,128)(2,1)}, bf16[4,256,768]{2,1,0:T(8,128)(2,1)}) custom-call(s32[4]{0:T(128)} %copy-done.38, bf16[5,1536,512]{2,1,0:T(8,128)(2,1)} %down_ref.3, bf16[5,512,512]{2,1,0:T(8,128)(2,1)} %get-tuple-element.101.hs_ref, bf16[4,640,256]{2,1,0:T(8,128)(2,1)} %get-tuple-element.102.hits_ref), custom_call_target="tpu_custom_call" | custom-call | flops 10000000 | tf_op jit(solution)/shard_map/mixture/pallas_call | solution.py:567
  252.1 4.2 collective-permute-done.23.refs_3_
  256.3 21.1 %expert_keep.1 = (bf16[2,3,5,192,256]{4,3,2,1,0:T(8,128)(2,1)}, bf16[2,3,5,192,256]{4,3,2,1,0:T(8,128)(2,1)}, bf16[2,3,5,192,256]{4,3,2,1,0:T(8,128)(2,1)}, bf16[2,3,5,192,256]{4,3,2,1,0:T(8,128)(2,1)}) custom-call(s32[1]{0:T(128)} %bitcast.8.place_ref, bf16[5,512,1536]{2,1,0:T(8,128)(2,1)} %get-tuple-element.106.xs_ref, ...), custom_call_target="tpu_custom_call" | custom-call | flops 15000000 | tf_op jit(solution)/shard_map/expert_keep/pallas_call | solution.py:653
  277.4 6.9 %all-to-all-done = bf16[4,256,1536]{2,1,0:T(8,128)(2,1)} async-done(((bf16[4,256,1536]{2,1,0:T(8,128)(2,1)}), bf16[4,256,1536]{2,1,0:T(8,128)(2,1)}, u32[]{:S(2)}, u32[]{:S(2)}) %all-to-all-start) | async-done | bytes 3145760 | tf_op jit(solution)/shard_map/all_to_all | solution.py:916
  285.9 9.2 %collective-permute-start.25 = (bf16[2,3,5,192,256]{4,3,2,1,0:T(8,128)(2,1)}, bf16[2,3,5,192,256]{4,3,2,1,0:T(8,128)(2,1)}, u32[]{:S(2)}, u32[]{:S(2)}) collective-permute-start(bf16[2,3,5,192,256]{4,3,2,1,0:T(8,128)(2,1)} %get-tuple-element.120), channel_id=1, source_target_pairs={{0,16},{4,20},{8,24},{12,28},{16,0},{20,4},{24,8},{28,12},{1,17},{... | collective-permute-start | bytes 8847368 | tf_op jit(solution)/shard_map/ppermute | solution.py:743
  295.0 4.5 all-to-all-start.1
  299.5 2.6 convert_reduce_fusion
  304.9 4.9 convolution_convert_fusion.grad_ref
  309.8 11.7 %attend_back.1 = (bf16[256,1536]{1,0:T(8,128)(2,1)}, bf16[2048,128]{1,0:T(8,128)(2,1)}, bf16[2048,128]{1,0:T(8,128)(2,1)}, bf16[2048,128]{1,0:T(8,128)(2,1)}, bf16[2048,128]{1,0:T(8,128)(2,1)}) custom-call(s32[1]{0:T(128)} %bitcast.place_ref, bf16[256,1536]{1,0:T(8,128)(2,1)} %queries.1.query_ref, bf16[256,1536]{1,0:T(8,128)(2,1)} %get-tuple-element.98.attended_ref.refs_2_, ...), custom_call_target="tpu_custom_call" | custom-call | flops 2000000 | tf_op jit(solution)/shard_map/attend_back/pallas_call | solution.py:304
  321.5 7.9 %dense_grads.2 = (bf16[4,192,3072]{2,1,0:T(8,128)(2,1)}, bf16[4,192,3072]{2,1,0:T(8,128)(2,1)}) custom-call(s32[1]{0:T(128)} %bitcast.8.place_ref, bf16[256,1536]{1,0:T(8,128)(2,1)} %copy-done.14, bf16[256,1536]{1,0:T(8,128)(2,1)} %get-tuple-element.96.normed_ref.refs_1_.refs_0_, bf16[256,1536]{1,0:T(8,128)(2,1)} %get-tuple-element.98.attended_ref.refs_2_, ...), custom_call_target="tpu_custom_call" | custom-call | flops 4000000 | tf_op jit(solution)/shard_map/dense_grads/pallas_call | solution.py:704
  329.3 6.5 %all-to-all-done.1 = bf16[4,256,768]{2,1,0:T(8,128)(2,1)} async-done(((bf16[4,256,768]{2,1,0:T(8,128)(2,1)}), bf16[4,256,768]{2,1,0:T(8,128)(2,1)}, u32[]{:S(2)}, u32[]{:S(2)}) %all-to-all-start.1) | async-done | bytes 1572896 | tf_op jit(solution)/shard_map/all_to_all | solution.py:925
  335.8 13.7 %collective-permute-done.24 = bf16[2,3,5,192,256]{4,3,2,1,0:T(8,128)(2,1)} collective-permute-done((bf16[2,3,5,192,256]{4,3,2,1,0:T(8,128)(2,1)}, bf16[2,3,5,192,256]{4,3,2,1,0:T(8,128)(2,1)}, u32[]{:S(2)}, u32[]{:S(2)}) %collective-permute-start.24) | collective-permute-done | bytes 2949152 | tf_op jit(solution)/shard_map/ppermute | solution.py:743
  349.5 9.0 %collective-permute-done.25 = bf16[2,3,5,192,256]{4,3,2,1,0:T(8,128)(2,1)} collective-permute-done((bf16[2,3,5,192,256]{4,3,2,1,0:T(8,128)(2,1)}, bf16[2,3,5,192,256]{4,3,2,1,0:T(8,128)(2,1)}, u32[]{:S(2)}, u32[]{:S(2)}) %collective-permute-start.25) | collective-permute-done | bytes 2949152 | tf_op jit(solution)/shard_map/ppermute | solution.py:743
  360.8 5.0 fusion.11
  367.6 4.1 fusion.9
  376.0 2.6 convert_reduce_fusion.2
  379.0 11.3 %collective-permute-done.26 = bf16[2048,128]{1,0:T(8,128)(2,1)S(1)} collective-permute-done((bf16[2048,128]{1,0:T(8,128)(2,1)S(1)}, bf16[2048,128]{1,0:T(8,128)(2,1)S(1)}, u32[]{:S(2)}, u32[]{:S(2)}) %collective-permute-start.26) | collective-permute-done | bytes 524320 | tf_op jit(solution)/shard_map/ppermute | solution.py:721
  391.9 8.6 %collective-permute-done.31 = bf16[3,5,192,256]{3,2,1,0:T(8,128)(2,1)S(1)} collective-permute-done((bf16[3,5,192,256]{3,2,1,0:T(8,128)(2,1)S(1)}, bf16[3,5,192,256]{3,2,1,0:T(8,128)(2,1)S(1)}, u32[]{:S(2)}, u32[]{:S(2)}) %collective-permute-start.31) | collective-permute-done | bytes 1474592 | tf_op jit(solution)/shard_map/ppermute | solution.py:743
  400.5 5.6 %collective-permute-done.30 = bf16[3,5,192,256]{3,2,1,0:T(8,128)(2,1)S(1)} collective-permute-done((bf16[3,5,192,256]{3,2,1,0:T(8,128)(2,1)S(1)}, bf16[3,5,192,256]{3,2,1,0:T(8,128)(2,1)S(1)}, u32[]{:S(2)}, u32[]{:S(2)}) %collective-permute-start.30) | collective-permute-done | bytes 1474592 | tf_op jit(solution)/shard_map/ppermute | solution.py:743
  406.1 3.4 fusion.43
  411.0 2.1 add_convert_fusion.4
  414.8 2.0 add_convert_fusion.7
  417.2 7.7 %collective-permute-done.29.above_ref = bf16[2048,128]{1,0:T(8,128)(2,1)S(1)} collective-permute-done((bf16[2048,128]{1,0:T(8,128)(2,1)S(1)}, bf16[2048,128]{1,0:T(8,128)(2,1)S(1)}, u32[]{:S(2)}, u32[]{:S(2)}) %collective-permute-start.29) | collective-permute-done | bytes 524320 | tf_op jit(solution)/shard_map/ppermute | solution.py:721
  425.6 2.7 unpack.1
  431.2 5.2 fusion.6
  437.0 4.6 all-to-all-start.2
  441.6 4.8 dense_grads.3
  446.4 1.9 add_bitcast_fusion.1
  457.8 8.4 %collective-permute-done.35 = bf16[192,1536]{1,0:T(8,128)(2,1)S(1)} collective-permute-done((bf16[192,1536]{1,0:T(8,128)(2,1)S(1)}, bf16[192,1536]{1,0:T(8,128)(2,1)S(1)}, u32[]{:S(2)}, u32[]{:S(2)}) %collective-permute-start.35) | collective-permute-done | bytes 589856 | tf_op jit(solution)/shard_map/ppermute | solution.py:743
  466.2 1.9 collective-permute-done.34
  470.3 2.4 collective-permute-start.45
  477.9 2.4 collective-permute-done.44
  480.4 17.2 %collective-permute-done.45 = bf16[48,3072]{1,0:T(8,128)(2,1)S(1)} collective-permute-done((bf16[48,3072]{1,0:T(8,128)(2,1)S(1)}, bf16[48,3072]{1,0:T(8,128)(2,1)S(1)}, u32[]{:S(2)}, u32[]{:S(2)}) %collective-permute-start.45) | collective-permute-done | bytes 294944 | tf_op jit(solution)/shard_map/ppermute | solution.py:784
  498.0 1.8 collective-permute-start.38
  500.6 8.2 %collective-permute-done.37 = bf16[2,192,512]{2,1,0:T(8,128)(2,1)S(1)} collective-permute-done((bf16[2,192,512]{2,1,0:T(8,128)(2,1)S(1)}, bf16[2,192,512]{2,1,0:T(8,128)(2,1)S(1)}, u32[]{:S(2)}, u32[]{:S(2)}) %collective-permute-start.37) | collective-permute-done | bytes 393248 | tf_op jit(solution)/shard_map/ppermute | solution.py:743
  519.0 6.9 %collective-permute-start.41 = (bf16[48,1152]{1,0:T(8,128)(2,1)S(1)}, bf16[48,1152]{1,0:T(8,128)(2,1)S(1)}, u32[]{:S(2)}, u32[]{:S(2)}) collective-permute-start(bf16[48,1152]{1,0:T(8,128)(2,1)S(1)} %get-tuple-element.267), channel_id=1, source_target_pairs={{0,1},{1,2},{2,3},{3,0},{4,5},{5,6},{6,7},{7,4},{8,9},{9,10},{10,1... | collective-permute-start | bytes 331784 | tf_op jit(solution)/shard_map/ppermute | solution.py:784
  526.0 2.4 collective-permute-start.43
  529.4 3.5 collective-permute-done.42
  (222 shorter events, 78.0 us)
Async XLA Ops:
  4.9 39.8 %copy-start.37 = (s32[256,8]{0,1:T(8,128)S(1)}, s32[256,8]{0,1:T(8,128)}, u32[]{:S(2)}) copy-start(s32[256,8]{0,1:T(8,128)} %param.31) | copy-start | bytes 24580
  9.2 16.5 %collective-permute-start = (bf16[2064,128]{1,0:T(8,128)(2,1)}, bf16[2064,128]{1,0:T(8,128)(2,1)S(1)}, u32[]{:S(2)}, u32[]{:S(2)}) collective-permute-start(bf16[2064,128]{1,0:T(8,128)(2,1)} %get-tuple-element.97.refs_0_.refs_4_), channel_id=1, source_target_pairs={{0,1},{1,2},{2,3},{4,5},{5,6},{6,7},{8,9},{9,10},{10,11},{12,13},{... | collective-permute-start | bytes 1585160 | tf_op jit(solution)/shard_map/ppermute | solution.py:717
  25.7 33.7 %copy-start = (bf16[2064,128]{1,0:T(8,128)(2,1)}, bf16[2064,128]{1,0:T(8,128)(2,1)S(1)}, u32[]{:S(2)}) copy-start(bf16[2064,128]{1,0:T(8,128)(2,1)S(1)} %collective-permute-done.refs_1_.refs_5_) | copy-start | bytes 1585156
  25.7 14.7 %collective-permute-start.1 = (bf16[2064,128]{1,0:T(8,128)(2,1)S(1)}, bf16[2064,128]{1,0:T(8,128)(2,1)S(1)}, u32[]{:S(2)}, u32[]{:S(2)}) collective-permute-start(bf16[2064,128]{1,0:T(8,128)(2,1)S(1)} %collective-permute-done.refs_1_.refs_5_), channel_id=1, source_target_pairs={{0,1},{1,2},{2,3},{4,5},{5,6},{6,7},{8,9},{9,10},{10,11},{12,13},{... | collective-permute-start | bytes 1585160 | tf_op jit(solution)/shard_map/ppermute | solution.py:717
  40.3 19.1 %copy-start.1 = (bf16[2064,128]{1,0:T(8,128)(2,1)}, bf16[2064,128]{1,0:T(8,128)(2,1)S(1)}, u32[]{:S(2)}) copy-start(bf16[2064,128]{1,0:T(8,128)(2,1)S(1)} %collective-permute-done.1.refs_2_.refs_6_) | copy-start | bytes 1585156
  40.3 19.1 %collective-permute-start.2 = (bf16[2064,128]{1,0:T(8,128)(2,1)S(1)}, bf16[2064,128]{1,0:T(8,128)(2,1)S(1)}, u32[]{:S(2)}, u32[]{:S(2)}) collective-permute-start(bf16[2064,128]{1,0:T(8,128)(2,1)S(1)} %collective-permute-done.1.refs_2_.refs_6_), channel_id=1, source_target_pairs={{0,1},{1,2},{2,3},{4,5},{5,6},{6,7},{8,9},{9,10},{10,11},{12,13},{... | collective-permute-start | bytes 1585160 | tf_op jit(solution)/shard_map/ppermute | solution.py:717
  48.1 34.7 %collective-permute-start.14 = (bf16[256,1664]{1,0:T(8,128)(2,1)}, bf16[256,1664]{1,0:T(8,128)(2,1)}, u32[]{:S(2)}, u32[]{:S(2)}) collective-permute-start(bf16[256,1664]{1,0:T(8,128)(2,1)} %extend.1.refs_7_), channel_id=1, source_target_pairs={{0,1},{1,2},{2,3},{4,5},{5,6},{6,7},{8,9},{9,10},{10,11},{12,13},{... | collective-permute-start | bytes 2555912 | tf_op jit(solution)/shard_map/ppermute | solution.py:717
  52.5 38.8 %collective-permute-start.17 = (bf16[256,1664]{1,0:T(8,128)(2,1)}, bf16[256,1664]{1,0:T(8,128)(2,1)}, u32[]{:S(2)}, u32[]{:S(2)}) collective-permute-start(bf16[256,1664]{1,0:T(8,128)(2,1)} %extend.1.refs_7_), channel_id=1, source_target_pairs={{1,0},{2,1},{3,2},{5,4},{6,5},{7,6},{9,8},{10,9},{11,10},{13,12},{... | collective-permute-start | bytes 2555912 | tf_op jit(solution)/shard_map/ppermute | solution.py:721
  72.6 71.4 %copy-start.36 = (f32[4,2,768]{2,1,0:T(2,128)S(1)}, f32[4,2,768]{2,1,0:T(2,128)}, u32[]{:S(2)}) copy-start(f32[4,2,768]{2,1,0:T(2,128)} %get-tuple-element.99) | copy-start | bytes 73732
  72.6 98.8 %copy-start.35 = (bf16[1536,20]{0,1:T(8,128)(2,1)S(1)}, bf16[1536,20]{0,1:T(8,128)(2,1)}, u32[]{:S(2)}) copy-start(bf16[1536,20]{0,1:T(8,128)(2,1)} %param.26) | copy-start | bytes 184324
  72.8 101.8 %copy-start.16 = (bf16[256,1536]{1,0:T(8,128)(2,1)}, bf16[256,1536]{1,0:T(8,128)(2,1)S(1)}, u32[]{:S(2)}) copy-start(bf16[256,1536]{1,0:T(8,128)(2,1)S(1)} %multiply_convert_fusion.1.refs_0_) | copy-start | bytes 2359300
  72.8 26.6 %collective-permute-start.8 = (bf16[256,1536]{1,0:T(8,128)(2,1)S(1)}, bf16[256,1536]{1,0:T(8,128)(2,1)S(1)}, u32[]{:S(2)}, u32[]{:S(2)}) collective-permute-start(bf16[256,1536]{1,0:T(8,128)(2,1)S(1)} %multiply_convert_fusion.1.refs_0_), channel_id=1, source_target_pairs={{0,1},{1,2},{2,3},{4,5},{5,6},{6,7},{8,9},{9,10},{10,11},{12,13},{... | collective-permute-start | bytes 2359304 | tf_op jit(solution)/shard_map/ppermute | solution.py:717
  81.6 25.7 %collective-permute-start.11 = (bf16[256,1536]{1,0:T(8,128)(2,1)S(1)}, bf16[256,1536]{1,0:T(8,128)(2,1)S(1)}, u32[]{:S(2)}, u32[]{:S(2)}) collective-permute-start(bf16[256,1536]{1,0:T(8,128)(2,1)S(1)} %multiply_convert_fusion.1.refs_0_), channel_id=1, source_target_pairs={{1,0},{2,1},{3,2},{5,4},{6,5},{7,6},{9,8},{10,9},{11,10},{13,12},{... | collective-permute-start | bytes 2359304 | tf_op jit(solution)/shard_map/ppermute | solution.py:721
  82.9 35.0 %collective-permute-start.15 = (bf16[256,1664]{1,0:T(8,128)(2,1)}, bf16[256,1664]{1,0:T(8,128)(2,1)}, u32[]{:S(2)}, u32[]{:S(2)}) collective-permute-start(bf16[256,1664]{1,0:T(8,128)(2,1)} %collective-permute-done.14.refs_8_), channel_id=1, source_target_pairs={{0,1},{1,2},{2,3},{4,5},{5,6},{6,7},{8,9},{9,10},{10,11},{12,13},{... | collective-permute-start | bytes 2555912 | tf_op jit(solution)/shard_map/ppermute | solution.py:717
  91.3 34.4 %collective-permute-start.18 = (bf16[256,1664]{1,0:T(8,128)(2,1)}, bf16[256,1664]{1,0:T(8,128)(2,1)}, u32[]{:S(2)}, u32[]{:S(2)}) collective-permute-start(bf16[256,1664]{1,0:T(8,128)(2,1)} %collective-permute-done.17.refs_11_), channel_id=1, source_target_pairs={{1,0},{2,1},{3,2},{5,4},{6,5},{7,6},{9,8},{10,9},{11,10},{13,12},{... | collective-permute-start | bytes 2555912 | tf_op jit(solution)/shard_map/ppermute | solution.py:721
  99.5 35.1 %collective-permute-start.9 = (bf16[256,1536]{1,0:T(8,128)(2,1)S(1)}, bf16[256,1536]{1,0:T(8,128)(2,1)}, u32[]{:S(2)}, u32[]{:S(2)}) collective-permute-start(bf16[256,1536]{1,0:T(8,128)(2,1)S(1)} %collective-permute-done.8.refs_1_), channel_id=1, source_target_pairs={{0,1},{1,2},{2,3},{4,5},{5,6},{6,7},{8,9},{9,10},{10,11},{12,13},{... | collective-permute-start | bytes 2359304 | tf_op jit(solution)/shard_map/ppermute | solution.py:717
  107.3 27.3 %copy-start.24 = (bf16[256,1536]{1,0:T(8,128)(2,1)}, bf16[256,1536]{1,0:T(8,128)(2,1)S(1)}, u32[]{:S(2)}) copy-start(bf16[256,1536]{1,0:T(8,128)(2,1)S(1)} %collective-permute-done.11.refs_4_) | copy-start | bytes 2359300
  107.3 35.2 %collective-permute-start.12 = (bf16[256,1536]{1,0:T(8,128)(2,1)S(1)}, bf16[256,1536]{1,0:T(8,128)(2,1)}, u32[]{:S(2)}, u32[]{:S(2)}) collective-permute-start(bf16[256,1536]{1,0:T(8,128)(2,1)S(1)} %collective-permute-done.11.refs_4_), channel_id=1, source_target_pairs={{1,0},{2,1},{3,2},{5,4},{6,5},{7,6},{9,8},{10,9},{11,10},{13,12},{... | collective-permute-start | bytes 2359304 | tf_op jit(solution)/shard_map/ppermute | solution.py:721
  117.9 56.8 %collective-permute-start.16 = (bf16[256,1664]{1,0:T(8,128)(2,1)}, bf16[256,1664]{1,0:T(8,128)(2,1)}, u32[]{:S(2)}, u32[]{:S(2)}) collective-permute-start(bf16[256,1664]{1,0:T(8,128)(2,1)} %collective-permute-done.15.refs_9_), channel_id=1, source_target_pairs={{0,1},{1,2},{2,3},{4,5},{5,6},{6,7},{8,9},{9,10},{10,11},{12,13},{... | collective-permute-start | bytes 2555912 | tf_op jit(solution)/shard_map/ppermute | solution.py:717
  125.7 48.9 %collective-permute-start.19 = (bf16[256,1664]{1,0:T(8,128)(2,1)}, bf16[256,1664]{1,0:T(8,128)(2,1)}, u32[]{:S(2)}, u32[]{:S(2)}) collective-permute-start(bf16[256,1664]{1,0:T(8,128)(2,1)} %collective-permute-done.18.refs_12_), channel_id=1, source_target_pairs={{1,0},{2,1},{3,2},{5,4},{6,5},{7,6},{9,8},{10,9},{11,10},{13,12},{... | collective-permute-start | bytes 2555912 | tf_op jit(solution)/shard_map/ppermute | solution.py:721
  134.6 40.0 %collective-permute-start.10 = (bf16[256,1536]{1,0:T(8,128)(2,1)}, bf16[256,1536]{1,0:T(8,128)(2,1)}, u32[]{:S(2)}, u32[]{:S(2)}) collective-permute-start(bf16[256,1536]{1,0:T(8,128)(2,1)} %collective-permute-done.9.refs_2_), channel_id=1, source_target_pairs={{0,1},{1,2},{2,3},{4,5},{5,6},{6,7},{8,9},{9,10},{10,11},{12,13},{... | collective-permute-start | bytes 2359304 | tf_op jit(solution)/shard_map/ppermute | solution.py:717
  142.5 32.1 %collective-permute-start.13 = (bf16[256,1536]{1,0:T(8,128)(2,1)}, bf16[256,1536]{1,0:T(8,128)(2,1)}, u32[]{:S(2)}, u32[]{:S(2)}) collective-permute-start(bf16[256,1536]{1,0:T(8,128)(2,1)} %collective-permute-done.12.refs_5_), channel_id=1, source_target_pairs={{1,0},{2,1},{3,2},{5,4},{6,5},{7,6},{9,8},{10,9},{11,10},{13,12},{... | collective-permute-start | bytes 2359304 | tf_op jit(solution)/shard_map/ppermute | solution.py:721
  144.1 1.2 collective-permute-start.3
  144.9 71.2 %copy-start.38 = (s32[4]{0:T(128)}, s32[4]{0:T(128)S(1)}, u32[]{:S(2)}) copy-start(s32[4]{0:T(128)S(1)} %fusion.39.order_ref) | copy-start | bytes 52
  145.3 3.5 collective-permute-start.4
  148.9 3.5 collective-permute-start.5
  152.4 17.7 %collective-permute-start.6 = (f32[1,24]{1,0:T(1,128)S(1)}, f32[1,24]{1,0:T(1,128)S(1)}, u32[]{:S(2)}, u32[]{:S(2)}) collective-permute-start(f32[1,24]{1,0:T(1,128)S(1)} %max.20), channel_id=1, source_target_pairs={{0,1},{1,0},{2,3},{3,2},{4,5},{5,4},{6,7},{7,6},{8,9},{9,8},{10,11... | collective-permute-start | bytes 296 | tf_op jit(solution)/shard_map/ppermute | solution.py:794
  170.2 4.4 collective-permute-start.7
  216.2 68.2 %all-to-all-start = ((bf16[4,256,1536]{2,1,0:T(8,128)(2,1)}), bf16[4,256,1536]{2,1,0:T(8,128)(2,1)}, u32[]{:S(2)}, u32[]{:S(2)}) async-start(bf16[4,256,1536]{2,1,0:T(8,128)(2,1)} %get-tuple-element.105), calls=%async_computation | async-start | bytes 6291456 | tf_op jit(solution)/shard_map/all_to_all | solution.py:916
  237.9 13.4 %collective-permute-start.20 = (bf16[3,5,192,512]{3,2,1,0:T(8,128)(2,1)}, bf16[3,5,192,512]{3,2,1,0:T(8,128)(2,1)}, u32[]{:S(2)}, u32[]{:S(2)}) collective-permute-start(bf16[3,5,192,512]{3,2,1,0:T(8,128)(2,1)} %get-tuple-element.110), channel_id=1, source_target_pairs={{0,4},{4,0},{8,12},{12,8},{16,20},{20,16},{24,28},{28,24},{1,5},{5... | collective-permute-start | bytes 8847368 | tf_op jit(solution)/shard_map/ppermute | solution.py:743
  238.0 13.4 %collective-permute-start.21 = (bf16[3,5,192,512]{3,2,1,0:T(8,128)(2,1)}, bf16[3,5,192,512]{3,2,1,0:T(8,128)(2,1)}, u32[]{:S(2)}, u32[]{:S(2)}) collective-permute-start(bf16[3,5,192,512]{3,2,1,0:T(8,128)(2,1)} %get-tuple-element.111), channel_id=1, source_target_pairs={{0,4},{4,0},{8,12},{12,8},{16,20},{20,16},{24,28},{28,24},{1,5},{5... | collective-permute-start | bytes 8847368 | tf_op jit(solution)/shard_map/ppermute | solution.py:743
  238.5 13.6 %collective-permute-start.22 = (bf16[3,5,192,512]{3,2,1,0:T(8,128)(2,1)}, bf16[3,5,192,512]{3,2,1,0:T(8,128)(2,1)}, u32[]{:S(2)}, u32[]{:S(2)}) collective-permute-start(bf16[3,5,192,512]{3,2,1,0:T(8,128)(2,1)} %get-tuple-element.112), channel_id=1, source_target_pairs={{0,4},{4,0},{8,12},{12,8},{16,20},{20,16},{24,28},{28,24},{1,5},{5... | collective-permute-start | bytes 8847368 | tf_op jit(solution)/shard_map/ppermute | solution.py:743
  238.5 17.8 %collective-permute-start.23 = (bf16[3,5,192,512]{3,2,1,0:T(8,128)(2,1)}, bf16[3,5,192,512]{3,2,1,0:T(8,128)(2,1)}, u32[]{:S(2)}, u32[]{:S(2)}) collective-permute-start(bf16[3,5,192,512]{3,2,1,0:T(8,128)(2,1)} %get-tuple-element.113), channel_id=1, source_target_pairs={{0,4},{4,0},{8,12},{12,8},{16,20},{20,16},{24,28},{28,24},{1,5},{5... | collective-permute-start | bytes 8847368 | tf_op jit(solution)/shard_map/ppermute | solution.py:743
  284.4 65.2 %collective-permute-start.24 = (bf16[2,3,5,192,256]{4,3,2,1,0:T(8,128)(2,1)}, bf16[2,3,5,192,256]{4,3,2,1,0:T(8,128)(2,1)}, u32[]{:S(2)}, u32[]{:S(2)}) collective-permute-start(bf16[2,3,5,192,256]{4,3,2,1,0:T(8,128)(2,1)} %get-tuple-element.119), channel_id=1, source_target_pairs={{0,8},{4,12},{8,0},{12,4},{16,24},{20,28},{24,16},{28,20},{1,9},{5... | collective-permute-start | bytes 8847368 | tf_op jit(solution)/shard_map/ppermute | solution.py:743
  285.9 72.6 %collective-permute-start.25 = (bf16[2,3,5,192,256]{4,3,2,1,0:T(8,128)(2,1)}, bf16[2,3,5,192,256]{4,3,2,1,0:T(8,128)(2,1)}, u32[]{:S(2)}, u32[]{:S(2)}) collective-permute-start(bf16[2,3,5,192,256]{4,3,2,1,0:T(8,128)(2,1)} %get-tuple-element.120), channel_id=1, source_target_pairs={{0,16},{4,20},{8,24},{12,28},{16,0},{20,4},{24,8},{28,12},{1,17},{... | collective-permute-start | bytes 8847368 | tf_op jit(solution)/shard_map/ppermute | solution.py:743
  295.0 40.8 %all-to-all-start.1 = ((bf16[4,256,768]{2,1,0:T(8,128)(2,1)}), bf16[4,256,768]{2,1,0:T(8,128)(2,1)}, u32[]{:S(2)}, u32[]{:S(2)}) async-start(bf16[4,256,768]{2,1,0:T(8,128)(2,1)} %get-tuple-element.121), calls=%async_computation.1 | async-start | bytes 3145728 | tf_op jit(solution)/shard_map/all_to_all | solution.py:925
  321.5 37.0 %copy-start.33 = (f32[256,1]{1,0:T(8,128)S(1)}, f32[256,1]{1,0:T(8,128)}, u32[]{:S(2)}) copy-start(f32[256,1]{1,0:T(8,128)} %get-tuple-element.140) | copy-start | bytes 3076
  321.5 37.1 %copy-start.40 = (f32[24]{0:T(128)S(1)}, f32[24]{0:T(128)}, u32[]{:S(2)}) copy-start(f32[24]{0:T(128)} %param.33) | copy-start | bytes 292
  358.5 47.6 %collective-permute-start.28 = (bf16[4,192,3072]{2,1,0:T(8,128)(2,1)}, bf16[4,192,3072]{2,1,0:T(8,128)(2,1)}, u32[]{:S(2)}, u32[]{:S(2)}) collective-permute-start(bf16[4,192,3072]{2,1,0:T(8,128)(2,1)} %get-tuple-element.129), channel_id=1, source_target_pairs={{0,4},{4,0},{8,12},{12,8},{16,20},{20,16},{24,28},{28,24},{1,5},{5... | collective-permute-start | bytes 14155784 | tf_op jit(solution)/shard_map/ppermute | solution.py:743
  360.8 17.8 %slice-start = ((s8[4718592]{0:T(1024)(128)(4,1)}), s8[4194304]{0:T(1024)(128)(4,1)S(1)}, s32[]{:S(2)}) async-start(s8[4718592]{0:T(1024)(128)(4,1)} %bitcast.132), calls=%async_computation.3 | async-start | bytes 8388608
  365.8 34.7 %collective-permute-start.31 = (bf16[3,5,192,256]{3,2,1,0:T(8,128)(2,1)S(1)}, bf16[3,5,192,256]{3,2,1,0:T(8,128)(2,1)S(1)}, u32[]{:S(2)}, u32[]{:S(2)}) collective-permute-start(bf16[3,5,192,256]{3,2,1,0:T(8,128)(2,1)S(1)} %get-tuple-element.235), channel_id=1, source_target_pairs={{0,8},{4,12},{8,0},{12,4},{16,24},{20,28},{24,16},{28,20},{1,9},{5... | collective-permute-start | bytes 4423688 | tf_op jit(solution)/shard_map/ppermute | solution.py:743
  371.7 34.4 %collective-permute-start.30 = (bf16[3,5,192,256]{3,2,1,0:T(8,128)(2,1)S(1)}, bf16[3,5,192,256]{3,2,1,0:T(8,128)(2,1)S(1)}, u32[]{:S(2)}, u32[]{:S(2)}) collective-permute-start(bf16[3,5,192,256]{3,2,1,0:T(8,128)(2,1)S(1)} %get-tuple-element.236), channel_id=1, source_target_pairs={{0,16},{4,20},{8,24},{12,28},{16,0},{20,4},{24,8},{28,12},{1,17},{... | collective-permute-start | bytes 4423688 | tf_op jit(solution)/shard_map/ppermute | solution.py:743
  374.7 15.7 %collective-permute-start.26 = (bf16[2048,128]{1,0:T(8,128)(2,1)S(1)}, bf16[2048,128]{1,0:T(8,128)(2,1)S(1)}, u32[]{:S(2)}, u32[]{:S(2)}) collective-permute-start(bf16[2048,128]{1,0:T(8,128)(2,1)S(1)} %copy-done.42), channel_id=1, source_target_pairs={{1,0},{2,1},{3,2},{5,4},{6,5},{7,6},{9,8},{10,9},{11,10},{13,12},{... | collective-permute-start | bytes 1572872 | tf_op jit(solution)/shard_map/ppermute | solution.py:721
  390.5 19.1 %copy-start.25 = (bf16[2048,128]{1,0:T(8,128)(2,1)S(1)}, bf16[2048,128]{1,0:T(8,128)(2,1)}, u32[]{:S(2)}) copy-start(bf16[2048,128]{1,0:T(8,128)(2,1)} %get-tuple-element.131) | copy-start | bytes 1572868
  390.5 19.1 %collective-permute-start.27 = (bf16[2048,128]{1,0:T(8,128)(2,1)S(1)}, bf16[2048,128]{1,0:T(8,128)(2,1)S(1)}, u32[]{:S(2)}, u32[]{:S(2)}) collective-permute-start(bf16[2048,128]{1,0:T(8,128)(2,1)S(1)} %add_convert_fusion.11), channel_id=1, source_target_pairs={{1,0},{2,1},{3,2},{5,4},{6,5},{7,6},{9,8},{10,9},{11,10},{13,12},{... | collective-permute-start | bytes 1572872 | tf_op jit(solution)/shard_map/ppermute | solution.py:721
  409.7 15.1 %collective-permute-start.29 = (bf16[2048,128]{1,0:T(8,128)(2,1)S(1)}, bf16[2048,128]{1,0:T(8,128)(2,1)S(1)}, u32[]{:S(2)}, u32[]{:S(2)}) collective-permute-start(bf16[2048,128]{1,0:T(8,128)(2,1)S(1)} %add_convert_fusion.10), channel_id=1, source_target_pairs={{1,0},{2,1},{3,2},{5,4},{6,5},{7,6},{9,8},{10,9},{11,10},{13,12},{... | collective-permute-start | bytes 1572872 | tf_op jit(solution)/shard_map/ppermute | solution.py:721
  413.1 37.5 %collective-permute-start.33 = (bf16[2,192,1536]{2,1,0:T(8,128)(2,1)}, bf16[2,192,1536]{2,1,0:T(8,128)(2,1)}, u32[]{:S(2)}, u32[]{:S(2)}) collective-permute-start(bf16[2,192,1536]{2,1,0:T(8,128)(2,1)} %get-tuple-element.239), channel_id=1, source_target_pairs={{0,16},{4,20},{8,24},{12,28},{16,0},{20,4},{24,8},{28,12},{1,17},{... | collective-permute-start | bytes 3538952 | tf_op jit(solution)/shard_map/ppermute | solution.py:743
  416.9 33.8 %collective-permute-start.32 = (bf16[2,192,1536]{2,1,0:T(8,128)(2,1)}, bf16[2,192,1536]{2,1,0:T(8,128)(2,1)}, u32[]{:S(2)}, u32[]{:S(2)}) collective-permute-start(bf16[2,192,1536]{2,1,0:T(8,128)(2,1)} %get-tuple-element.241), channel_id=1, source_target_pairs={{0,8},{4,12},{8,0},{12,4},{16,24},{20,28},{24,16},{28,20},{1,9},{5... | collective-permute-start | bytes 3538952 | tf_op jit(solution)/shard_map/ppermute | solution.py:743
  437.0 77.4 %all-to-all-start.2 = ((bf16[4,256,768]{2,1,0:T(8,128)(2,1)}), bf16[4,256,768]{2,1,0:T(8,128)(2,1)}, u32[]{:S(2)}, u32[]{:S(2)}) async-start(bf16[4,256,768]{2,1,0:T(8,128)(2,1)} %get-tuple-element.139), calls=%async_computation.2 | async-start | bytes 3145728 | tf_op jit(solution)/shard_map/all_to_all | solution.py:947
  452.3 13.9 %collective-permute-start.35 = (bf16[192,1536]{1,0:T(8,128)(2,1)S(1)}, bf16[192,1536]{1,0:T(8,128)(2,1)S(1)}, u32[]{:S(2)}, u32[]{:S(2)}) collective-permute-start(bf16[192,1536]{1,0:T(8,128)(2,1)S(1)} %get-tuple-element.253), channel_id=1, source_target_pairs={{0,8},{4,12},{8,0},{12,4},{16,24},{20,28},{24,16},{28,20},{1,9},{5... | collective-permute-start | bytes 1769480 | tf_op jit(solution)/shard_map/ppermute | solution.py:743
  454.4 13.6 %collective-permute-start.34 = (bf16[192,1536]{1,0:T(8,128)(2,1)S(1)}, bf16[192,1536]{1,0:T(8,128)(2,1)S(1)}, u32[]{:S(2)}, u32[]{:S(2)}) collective-permute-start(bf16[192,1536]{1,0:T(8,128)(2,1)S(1)} %get-tuple-element.254), channel_id=1, source_target_pairs={{0,16},{4,20},{8,24},{12,28},{16,0},{20,4},{24,8},{28,12},{1,17},{... | collective-permute-start | bytes 1769480 | tf_op jit(solution)/shard_map/ppermute | solution.py:743
  456.2 11.8 %copy-start.41 = (bf16[4,192,1152]{2,1,0:T(8,128)(2,1)S(1)}, bf16[4,192,1152]{2,1,0:T(8,128)(2,1)}, u32[]{:S(2)}) copy-start(bf16[4,192,1152]{2,1,0:T(8,128)(2,1)} %get-tuple-element.157) | copy-start | bytes 5308420
  468.0 29.6 %collective-permute-start.36 = (bf16[4,192,1152]{2,1,0:T(8,128)(2,1)S(1)}, bf16[4,192,1152]{2,1,0:T(8,128)(2,1)S(1)}, u32[]{:S(2)}, u32[]{:S(2)}) collective-permute-start(bf16[4,192,1152]{2,1,0:T(8,128)(2,1)S(1)} %copy-done.41), channel_id=1, source_target_pairs={{0,4},{4,0},{8,12},{12,8},{16,20},{20,16},{24,28},{28,24},{1,5},{5... | collective-permute-start | bytes 5308424 | tf_op jit(solution)/shard_map/ppermute | solution.py:743
  468.6 11.8 %collective-permute-start.44 = (bf16[48,3072]{1,0:T(8,128)(2,1)S(1)}, bf16[48,3072]{1,0:T(8,128)(2,1)S(1)}, u32[]{:S(2)}, u32[]{:S(2)}) collective-permute-start(bf16[48,3072]{1,0:T(8,128)(2,1)S(1)} %get-tuple-element.262), channel_id=1, source_target_pairs={{0,1},{1,2},{2,3},{3,0},{4,5},{5,6},{6,7},{7,4},{8,9},{9,10},{10,1... | collective-permute-start | bytes 884744 | tf_op jit(solution)/shard_map/ppermute | solution.py:784
  470.3 27.3 %collective-permute-start.45 = (bf16[48,3072]{1,0:T(8,128)(2,1)S(1)}, bf16[48,3072]{1,0:T(8,128)(2,1)S(1)}, u32[]{:S(2)}, u32[]{:S(2)}) collective-permute-start(bf16[48,3072]{1,0:T(8,128)(2,1)S(1)} %get-tuple-element.261), channel_id=1, source_target_pairs={{0,2},{1,3},{2,0},{3,1},{4,6},{5,7},{6,4},{7,5},{8,10},{9,11},{10,... | collective-permute-start | bytes 884744 | tf_op jit(solution)/shard_map/ppermute | solution.py:784
  472.7 24.9 %collective-permute-start.46 = (bf16[48,3072]{1,0:T(8,128)(2,1)S(1)}, bf16[48,3072]{1,0:T(8,128)(2,1)S(1)}, u32[]{:S(2)}, u32[]{:S(2)}) collective-permute-start(bf16[48,3072]{1,0:T(8,128)(2,1)S(1)} %get-tuple-element.260), channel_id=1, source_target_pairs={{0,3},{1,0},{2,1},{3,2},{4,7},{5,4},{6,5},{7,6},{8,11},{9,8},{10,9... | collective-permute-start | bytes 884744 | tf_op jit(solution)/shard_map/ppermute | solution.py:784
  498.0 11.2 %collective-permute-start.38 = (bf16[2,192,640]{2,1,0:T(8,128)(2,1)S(1)}, bf16[2,192,640]{2,1,0:T(8,128)(2,1)S(1)}, u32[]{:S(2)}, u32[]{:S(2)}) collective-permute-start(bf16[2,192,640]{2,1,0:T(8,128)(2,1)S(1)} %get-tuple-element.257), channel_id=1, source_target_pairs={{0,16},{4,20},{8,24},{12,28},{16,0},{20,4},{24,8},{28,12},{1,17},{... | collective-permute-start | bytes 1474568 | tf_op jit(solution)/shard_map/ppermute | solution.py:743
  500.1 8.8 %collective-permute-start.37 = (bf16[2,192,512]{2,1,0:T(8,128)(2,1)S(1)}, bf16[2,192,512]{2,1,0:T(8,128)(2,1)S(1)}, u32[]{:S(2)}, u32[]{:S(2)}) collective-permute-start(bf16[2,192,512]{2,1,0:T(8,128)(2,1)S(1)} %get-tuple-element.259), channel_id=1, source_target_pairs={{0,8},{4,12},{8,0},{12,4},{16,24},{20,28},{24,16},{28,20},{1,9},{5... | collective-permute-start | bytes 1179656 | tf_op jit(solution)/shard_map/ppermute | solution.py:743
  510.7 7.1 %collective-permute-start.40 = (bf16[192,640]{1,0:T(8,128)(2,1)}, bf16[192,640]{1,0:T(8,128)(2,1)S(1)}, u32[]{:S(2)}, u32[]{:S(2)}) collective-permute-start(bf16[192,640]{1,0:T(8,128)(2,1)} %fusion.32), channel_id=1, source_target_pairs={{0,8},{4,12},{8,0},{12,4},{16,24},{20,28},{24,16},{28,20},{1,9},{5... | collective-permute-start | bytes 737288 | tf_op jit(solution)/shard_map/ppermute | solution.py:743
  511.8 6.0 %collective-permute-start.39 = (bf16[192,512]{1,0:T(8,128)(2,1)}, bf16[192,512]{1,0:T(8,128)(2,1)}, u32[]{:S(2)}, u32[]{:S(2)}) collective-permute-start(bf16[192,512]{1,0:T(8,128)(2,1)} %fusion.37), channel_id=1, source_target_pairs={{0,16},{4,20},{8,24},{12,28},{16,0},{20,4},{24,8},{28,12},{1,17},{... | collective-permute-start | bytes 589832 | tf_op jit(solution)/shard_map/ppermute | solution.py:743
  516.2 12.2 %copy-start.15 = (f32[256,768]{1,0:T(8,128)S(1)}, f32[256,768]{1,0:T(8,128)}, u32[]{:S(2)}) copy-start(f32[256,768]{1,0:T(8,128)} %convert_reduce_fusion.2) | copy-start | bytes 2359300
  519.0 10.4 %collective-permute-start.41 = (bf16[48,1152]{1,0:T(8,128)(2,1)S(1)}, bf16[48,1152]{1,0:T(8,128)(2,1)S(1)}, u32[]{:S(2)}, u32[]{:S(2)}) collective-permute-start(bf16[48,1152]{1,0:T(8,128)(2,1)S(1)} %get-tuple-element.267), channel_id=1, source_target_pairs={{0,1},{1,2},{2,3},{3,0},{4,5},{5,6},{6,7},{7,4},{8,9},{9,10},{10,1... | collective-permute-start | bytes 331784 | tf_op jit(solution)/shard_map/ppermute | solution.py:784
  525.9 7.0 %collective-permute-start.42 = (bf16[48,1152]{1,0:T(8,128)(2,1)S(1)}, bf16[48,1152]{1,0:T(8,128)(2,1)S(1)}, u32[]{:S(2)}, u32[]{:S(2)}) collective-permute-start(bf16[48,1152]{1,0:T(8,128)(2,1)S(1)} %get-tuple-element.266), channel_id=1, source_target_pairs={{0,2},{1,3},{2,0},{3,1},{4,6},{5,7},{6,4},{7,5},{8,10},{9,11},{10,... | collective-permute-start | bytes 331784 | tf_op jit(solution)/shard_map/ppermute | solution.py:784
  526.0 7.0 %collective-permute-start.43 = (bf16[48,1152]{1,0:T(8,128)(2,1)S(1)}, bf16[48,1152]{1,0:T(8,128)(2,1)S(1)}, u32[]{:S(2)}, u32[]{:S(2)}) collective-permute-start(bf16[48,1152]{1,0:T(8,128)(2,1)S(1)} %get-tuple-element.265), channel_id=1, source_target_pairs={{0,3},{1,0},{2,1},{3,2},{4,7},{5,4},{6,5},{7,6},{8,11},{9,8},{10,9... | collective-permute-start | bytes 331784 | tf_op jit(solution)/shard_map/ppermute | solution.py:784
  (31 other events, 128.1 us)

commit v4 on v3

--- a/solution.py
+++ b/solution.py
@@ -774,25 +774,39 @@
     return start_spread([tuple(t[..., :half] for t in terms), tuple(t[..., half:] for t in terms)])
 
 
-def finish_dense(routes, place, size):
+def pass_line(routes, place, size):
     block = jnp.concatenate([add_low(*terms) for terms in routes], axis=-1)
     parts = block.reshape(size, -1, block.shape[-1])
-    total = lax.dynamic_index_in_dim(parts, place, 0, keepdims=False).astype(F32)
-    passed = []
+    passed = [lax.dynamic_index_in_dim(parts, place, 0, keepdims=False)]
     for k in range(1, size):
         part = lax.dynamic_index_in_dim(parts, (place + k) % size, 0, keepdims=False)
         passed.append(lax.ppermute(part, "expert", [(i, (i + k) % size) for i in range(size)]))
-    for part in lax.optimization_barrier(tuple(passed)):
+    return passed
+
+
+def total_of(parts):
+    total = parts[0].astype(F32)
+    for part in parts[1:]:
         total = total + part.astype(F32)
     return total
 
 
-def reduce_top(top, dp_size, size):
-    for bit in range(dp_size.bit_length() - 1):
-        top = jnp.maximum(top, flip(top, 1 << bit, dp_size))
+def swap_top(top, axis, size):
     for bit in range(size.bit_length() - 1):
-        top = jnp.maximum(top, lax.ppermute(top, "expert", [(i, i ^ (1 << bit)) for i in range(size)]))
+        top = jnp.maximum(top, lax.ppermute(top, axis, [(i, i ^ (1 << bit)) for i in range(size)]))
     return top
+
+
+def gather_and_top(value, top, dp_size, size):
+    below, above = [], []
+    up, down = value, value
+    for k in range(1, size):
+        up, down = line_up(up, size), line_down(down, size)
+        if k == 1:
+            up, down, top = lax.optimization_barrier((up, down, swap_top(top, "dp", dp_size)))
+        below.append(up)
+        above.append(down)
+    return [value] + below + above, top
 
 
 def arrival_order(size):
@@ -898,18 +912,16 @@
     place_word = place.reshape(1).astype(jnp.int32)
     attended, lse, top = attend(queries, kv_slots, place_word, groups)
     head_top = jnp.max(top.reshape(heads, rows), axis=1).reshape(1, heads)
-    head_top = reduce_top(head_top, dp_size, size).reshape(heads)
 
     hidden_in = tokens.astype(F32)
     hidden_mid = hidden_in + RESIDUAL_SCALE * dot(attended, output_weight, NT)
     second_factor = lax.rsqrt(jnp.mean(hidden_mid * hidden_mid, axis=-1, keepdims=True) + NORM_EPSILON)
     second_normed = (hidden_mid * second_factor * second_gain).astype(BF16)
-    normed_blocks = line_gather(second_normed, size)
+    normed_blocks, head_top = gather_and_top(second_normed, head_top, dp_size, size)
 
     router_t = jnp.pad(router_weight.T, ((0, expert_pad - experts), (0, 0)))
     sources, blocks_of = (jnp.asarray(table)[place] for table in arrival_order(size))
     expert_place = jnp.concatenate([(place * local_experts).reshape(1), sources, blocks_of]).astype(jnp.int32)
-    expert_place, head_top = lax.optimization_barrier((expert_place, head_top))
     saved, grad_blocks, router_part = run_experts(
         expert_place, router_t, gate_weight, up_weight, down_weight, normed_blocks, cots, slot_rows
     )
@@ -934,22 +946,22 @@
     )
     keep, send = dense_grads(dp_word, [(branch_grad, attended), (normed, query_back)], dp_size)
     stages = dp_size.bit_length() - 2
-    down, passed, mix_one, keep, send = lax.optimization_barrier((dkv[size - 1], passed, mix_one, keep, send))
-    expert_sums = step_spread(start_spread([(keep_a, passed[0]), (keep_b, passed[1])]), 1, dp_size, dp_place)
+    from_above = line_down(dkv[size - 1], size)
+    from_above, passed, mix_one, keep, send = lax.optimization_barrier((from_above, passed, mix_one, keep, send))
     wide = start_dense((keep, flip(send, 1, dp_size)))
     for k in range(1, size):
-        from_above = line_down(down, size)
+        if k > 1:
+            from_above = line_down(down, size)
         if k == size - 2:
             from_above, wide = lax.optimization_barrier((from_above, wide))
         if k < size - 1:
             down = add_low(from_above, dkv[size - 1 - k])
-    from_above, expert_sums, mix_two = lax.optimization_barrier((from_above, expert_sums, mixture[1]))
+    from_above, passed, head_top = lax.optimization_barrier((from_above, passed, head_top))
+    head_top = swap_top(head_top, "expert", size)
+    mix_two, head_top = lax.optimization_barrier((mixture[1], head_top))
+    head_top = head_top.reshape(heads)
+    expert_sums = step_spread(start_spread([(keep_a, passed[0]), (keep_b, passed[1])]), 1, dp_size, dp_place)
     mix_two = lax.all_to_all(mix_two, "expert", 0, 0, tiled=True)
-    for stage in range(2, stages):
-        expert_sums = step_spread(expert_sums, stage, dp_size, dp_place)
-    expert_sums = [
-        jnp.concatenate([a[w].astype(F32) + b[w].astype(F32) for a, b in expert_sums], axis=-1) for w in range(3)
-    ]
     for stage in range(stages):
         wide = step_spread(wide, stage, dp_size, dp_place)
     key_back, value_back = pl.pallas_call(
@@ -973,11 +985,21 @@
         dp_size,
         (router_part, second_gain_part[None], first_gain_part[None]),
     )
-    keep, send, wide = lax.optimization_barrier((keep, send, wide))
+    keep, send, wide, expert_sums = lax.optimization_barrier((keep, send, wide, expert_sums))
     rest = start_dense((keep, flip(send, 1, dp_size)))
-    for stage in range(stages):
+    rest = step_spread(rest, 0, dp_size, dp_place)
+    wide_parts, rest, expert_sums, mix_two = lax.optimization_barrier(
+        (pass_line(wide, place, size), rest, expert_sums, mix_two)
+    )
+    for stage in range(2, stages):
+        expert_sums = step_spread(expert_sums, stage, dp_size, dp_place)
+    expert_sums = [
+        jnp.concatenate([a[w].astype(F32) + b[w].astype(F32) for a, b in expert_sums], axis=-1) for w in range(3)
+    ]
+    for stage in range(1, stages):
         rest = step_spread(rest, stage, dp_size, dp_place)
-    wide_grad, rest_grad = finish_dense(wide, place, size), finish_dense(rest, place, size)
+    rest_parts = lax.optimization_barrier(pass_line(rest, place, size))
+    wide_grad, rest_grad = total_of(wide_parts), total_of(rest_parts)
     mixture = jnp.concatenate([jnp.sum(part.astype(F32), axis=0) for part in (mix_one, mix_two)], axis=1)
     block_out = (hidden_mid + mixture).astype(BF16)
     projection_grad, query_grad = wide_grad[:, :query_width], wide_grad[:, query_width:]

time: 544 us -> 543 us (level)
  the two profiles are of different devices: /device:TPU:0 before, /device:TPU:24 now
where the time goes in v4:
time: 543 us; the launch traced here: 534 us
  waiting for transfers between devices  161 us (30%)
  Pallas kernels  149 us (27%)
  starting transfers between devices  127 us (23%)
  other arithmetic  54 us (10%)
  local copies, waits for them, and re-layouts  25.6 us (5%)
  matrix products  15.5 us (3%)
    ppermute x9, starting transfers between devices, line_down(): return lax.ppermute(value, 'expert', [(i + 1, i) for i in range(size - 1)])  56 us
    ppermute x9, waiting for transfers between devices, line_up(): return lax.ppermute(value, 'expert', [(i, i + 1) for i in range(size - 1)])  51.6 us
    pallas_call x1, Pallas kernels, run_experts(): pl.pallas_call(functools.partial(expert_kernel, blocks, slot_rows, local_...  41.5 us
    ppermute x18, waiting for transfers between devices, flip(): return lax.ppermute(value, 'dp', [(i, i ^ bit) for i in range(size)])  38 us
    pallas_call x2, Pallas kernels, run_expert_grads(): pl.pallas_call(functools.partial(expert_keep_kernel, owners.bit_length()...  37.9 us
    ppermute x6, waiting for transfers between devices, pass_line(): lax.ppermute(part, 'expert', [(i, (i + k) % size) for i in range(size)])  31.7 us
    ppermute x9, waiting for transfers between devices, line_down(): return lax.ppermute(value, 'expert', [(i + 1, i) for i in range(size - 1)])  26.7 us
    convert_element_type x16, other arithmetic, add_low(): return total.astype(BF16)  25.5 us
  transfers between devices with their start and end apart: 50, of which 21 were waited for; matrix products, arithmetic and copies ran while one was open for 15% of the time, Pallas kernels for 19%

profile of v4, /device:TPU:24, one launch (start us, length us, event | category | flops | bytes accessed | tf_op | source)
XLA Modules:
  0.0 533.6 jit_solution(11894067762547337252)
XLA Ops:
  4.9 4.2 front.1
  10.4 14.6 %collective-permute-done.refs_1_.refs_5_ = bf16[2064,128]{1,0:T(8,128)(2,1)S(1)} collective-permute-done((bf16[2064,128]{1,0:T(8,128)(2,1)}, bf16[2064,128]{1,0:T(8,128)(2,1)S(1)}, u32[]{:S(2)}, u32[]{:S(2)}) %collective-permute-start) | collective-permute-done | bytes 528416 | tf_op jit(solution)/shard_map/ppermute | solution.py:717
  26.3 13.5 %collective-permute-done.1.refs_2_.refs_6_ = bf16[2064,128]{1,0:T(8,128)(2,1)S(1)} collective-permute-done((bf16[2064,128]{1,0:T(8,128)(2,1)S(1)}, bf16[2064,128]{1,0:T(8,128)(2,1)S(1)}, u32[]{:S(2)}, u32[]{:S(2)}) %collective-permute-start.1) | collective-permute-done | bytes 528416 | tf_op jit(solution)/shard_map/ppermute | solution.py:717
  41.9 2.6 extend.1.refs_7_
  45.7 6.1 %collective-permute-start.15 = (bf16[256,1664]{1,0:T(8,128)(2,1)}, bf16[256,1664]{1,0:T(8,128)(2,1)}, u32[]{:S(2)}, u32[]{:S(2)}) collective-permute-start(bf16[256,1664]{1,0:T(8,128)(2,1)} %extend.1.refs_7_), channel_id=1, source_target_pairs={{1,0},{2,1},{3,2},{5,4},{6,5},{7,6},{9,8},{10,9},{11,10},{13,12},{... | collective-permute-start | bytes 2555912 | tf_op jit(solution)/shard_map/ppermute | solution.py:721
  51.8 5.6 %queries.1.query_ref = bf16[256,1536]{1,0:T(8,128)(2,1)} custom-call(bf16[256,1536]{1,0:T(8,128)(2,1)} %get-tuple-element.112.normed_ref.refs_1_.refs_0_, bf16[1536,1536]{1,0:T(8,128)(2,1)} %query_ref.1, f32[256,128]{1,0:T(8,128)} %get-tuple-element.295.cos_ref, f32[256,128]{1,0:T(8,128)} %get-tuple-element.294.sin_ref), custom_call_target="tpu_custom_call" | custom-call | flops 5000000 | tf_op jit(solution)/shard_map/queries/pallas_call | solution.py:896
  58.2 12.3 %attend.1 = (bf16[256,1536]{1,0:T(8,128)(2,1)}, f32[4,2,768]{2,1,0:T(2,128)}, f32[4,2,768]{2,1,0:T(2,128)}) custom-call(s32[1]{0:T(128)} %bitcast.place_ref, bf16[256,1536]{1,0:T(8,128)(2,1)} %queries.1.query_ref, bf16[2064,128]{1,0:T(8,128)(2,1)} %get-tuple-element.113.refs_0_.refs_4_, bf16[2064,128]{1,0:T(8,128)(2,1)} %copy-done, ...), custom_call_target="tpu_custom_call" | custom-call | flops 20000000 | tf_op jit(solution)/shard_map/attend/pallas_call | solution.py:217
  70.6 4.1 multiply_reduce_fusion.2
  76.3 8.9 %collective-permute-start.4 = (bf16[256,1536]{1,0:T(8,128)(2,1)S(1)}, bf16[256,1536]{1,0:T(8,128)(2,1)}, u32[]{:S(2)}, u32[]{:S(2)}) collective-permute-start(bf16[256,1536]{1,0:T(8,128)(2,1)S(1)} %multiply_convert_fusion.1.refs_0_), channel_id=1, source_target_pairs={{1,0},{2,1},{3,2},{5,4},{6,5},{7,6},{9,8},{10,9},{11,10},{13,12},{... | collective-permute-start | bytes 2359304 | tf_op jit(solution)/shard_map/ppermute | solution.py:721
  86.8 5.5 %collective-permute-start.16 = (bf16[256,1664]{1,0:T(8,128)(2,1)}, bf16[256,1664]{1,0:T(8,128)(2,1)}, u32[]{:S(2)}, u32[]{:S(2)}) collective-permute-start(bf16[256,1664]{1,0:T(8,128)(2,1)} %collective-permute-done.15.refs_11_), channel_id=1, source_target_pairs={{1,0},{2,1},{3,2},{5,4},{6,5},{7,6},{9,8},{10,9},{11,10},{13,12},{... | collective-permute-start | bytes 2555912 | tf_op jit(solution)/shard_map/ppermute | solution.py:721
  93.7 2.1 collective-permute-done.6
  95.8 1.8 collective-permute-start.7
  101.0 4.8 collective-permute-start.10
  107.1 11.0 %collective-permute-done.13.refs_9_ = bf16[256,1664]{1,0:T(8,128)(2,1)} collective-permute-done((bf16[256,1664]{1,0:T(8,128)(2,1)}, bf16[256,1664]{1,0:T(8,128)(2,1)}, u32[]{:S(2)}, u32[]{:S(2)}) %collective-permute-start.13) | collective-permute-done | bytes 852000 | tf_op jit(solution)/shard_map/ppermute | solution.py:717
  119.4 5.5 %collective-permute-start.17 = (bf16[256,1664]{1,0:T(8,128)(2,1)}, bf16[256,1664]{1,0:T(8,128)(2,1)}, u32[]{:S(2)}, u32[]{:S(2)}) collective-permute-start(bf16[256,1664]{1,0:T(8,128)(2,1)} %collective-permute-done.16.refs_12_), channel_id=1, source_target_pairs={{1,0},{2,1},{3,2},{5,4},{6,5},{7,6},{9,8},{10,9},{11,10},{13,12},{... | collective-permute-start | bytes 2555912 | tf_op jit(solution)/shard_map/ppermute | solution.py:721
  125.0 8.1 %collective-permute-done.10.refs_5_ = bf16[256,1536]{1,0:T(8,128)(2,1)} collective-permute-done((bf16[256,1536]{1,0:T(8,128)(2,1)}, bf16[256,1536]{1,0:T(8,128)(2,1)}, u32[]{:S(2)}, u32[]{:S(2)}) %collective-permute-start.10) | collective-permute-done | bytes 786464 | tf_op jit(solution)/shard_map/ppermute | solution.py:721
  133.1 5.3 collective-permute-start.11
  141.8 11.4 %collective-permute-done.14.refs_10_ = bf16[256,1664]{1,0:T(8,128)(2,1)} collective-permute-done((bf16[256,1664]{1,0:T(8,128)(2,1)}, bf16[256,1664]{1,0:T(8,128)(2,1)}, u32[]{:S(2)}, u32[]{:S(2)}) %collective-permute-start.14) | collective-permute-done | bytes 852000 | tf_op jit(solution)/shard_map/ppermute | solution.py:717
  153.2 12.1 %collective-permute-done.11.refs_6_ = bf16[256,1536]{1,0:T(8,128)(2,1)} collective-permute-done((bf16[256,1536]{1,0:T(8,128)(2,1)}, bf16[256,1536]{1,0:T(8,128)(2,1)}, u32[]{:S(2)}, u32[]{:S(2)}) %collective-permute-start.11) | collective-permute-done | bytes 786464 | tf_op jit(solution)/shard_map/ppermute | solution.py:721
  165.3 41.5 %experts.1 = (bf16[5,512,1536]{2,1,0:T(8,128)(2,1)}, bf16[5,512,1536]{2,1,0:T(8,128)(2,1)}, bf16[5,512,512]{2,1,0:T(8,128)(2,1)}, bf16[5,512,512]{2,1,0:T(8,128)...) custom-call(s32[9]{0:T(128)} %pad_add_fusion.place_ref, ...), custom_call_target="tpu_custom_call" | custom-call | flops 45000000 | tf_op jit(solution)/shard_map/experts/pallas_call | solution.py:483
  206.8 9.5 %all-to-all-start = ((bf16[4,256,1536]{2,1,0:T(8,128)(2,1)}), bf16[4,256,1536]{2,1,0:T(8,128)(2,1)}, u32[]{:S(2)}, u32[]{:S(2)}) async-start(bf16[4,256,1536]{2,1,0:T(8,128)(2,1)} %get-tuple-element.122), calls=%async_computation | async-start | bytes 6291456 | tf_op jit(solution)/shard_map/all_to_all | solution.py:928
  216.3 16.7 %expert_send.1 = (bf16[3,5,192,512]{3,2,1,0:T(8,128)(2,1)}, bf16[3,5,192,512]{3,2,1,0:T(8,128)(2,1)}, bf16[3,5,192,512]{3,2,1,0:T(8,128)(2,1)}, bf16[3,5,192,512]{3,2,1,0:T(8,128)(2,1)}) custom-call(s32[1]{0:T(128)} %bitcast.7.place_ref, bf16[5,512,1536]{2,1,0:T(8,128)(2,1)} %get-tuple-element.123.xs_ref, bf16[5,512,1536]{2,1,0:T(8,128)(2,1)} %get-tuple-element.124.cs_ref, ...), custom_call_target="tpu_custom_call" | custom-call | flops 15000000 | tf_op jit(solution)/shard_map/expert_send/pallas_call | solution.py:653
  234.1 12.3 %mixture.1 = (bf16[4,256,768]{2,1,0:T(8,128)(2,1)}, bf16[4,256,768]{2,1,0:T(8,128)(2,1)}) custom-call(s32[4]{0:T(128)} %copy-done.36, bf16[5,1536,512]{2,1,0:T(8,128)(2,1)} %down_ref.3, bf16[5,512,512]{2,1,0:T(8,128)(2,1)} %get-tuple-element.118.hs_ref, bf16[4,640,256]{2,1,0:T(8,128)(2,1)} %get-tuple-element.119.hits_ref), custom_call_target="tpu_custom_call" | custom-call | flops 10000000 | tf_op jit(solution)/shard_map/mixture/pallas_call | solution.py:567
  247.2 4.2 collective-permute-done.21.refs_3_
  251.5 21.1 %expert_keep.1 = (bf16[2,3,5,192,256]{4,3,2,1,0:T(8,128)(2,1)}, bf16[2,3,5,192,256]{4,3,2,1,0:T(8,128)(2,1)}, bf16[2,3,5,192,256]{4,3,2,1,0:T(8,128)(2,1)}, bf16[2,3,5,192,256]{4,3,2,1,0:T(8,128)(2,1)}) custom-call(s32[1]{0:T(128)} %bitcast.7.place_ref, bf16[5,512,1536]{2,1,0:T(8,128)(2,1)} %get-tuple-element.123.xs_ref, ...), custom_call_target="tpu_custom_call" | custom-call | flops 15000000 | tf_op jit(solution)/shard_map/expert_keep/pallas_call | solution.py:653
  272.6 8.8 %all-to-all-done = bf16[4,256,1536]{2,1,0:T(8,128)(2,1)} async-done(((bf16[4,256,1536]{2,1,0:T(8,128)(2,1)}), bf16[4,256,1536]{2,1,0:T(8,128)(2,1)}, u32[]{:S(2)}, u32[]{:S(2)}) %all-to-all-start) | async-done | bytes 3145760 | tf_op jit(solution)/shard_map/all_to_all | solution.py:928
  282.8 2.2 collective-permute-start.24
  285.0 7.7 %all-to-all-start.1 = ((bf16[4,256,768]{2,1,0:T(8,128)(2,1)}), bf16[4,256,768]{2,1,0:T(8,128)(2,1)}, u32[]{:S(2)}, u32[]{:S(2)}) async-start(bf16[4,256,768]{2,1,0:T(8,128)(2,1)} %get-tuple-element.138), calls=%async_computation.1 | async-start | bytes 3145728 | tf_op jit(solution)/shard_map/all_to_all | solution.py:937
  292.7 2.6 convert_reduce_fusion
  298.1 4.9 convolution_convert_fusion.grad_ref
  303.0 17.6 %attend_back.1 = (bf16[256,1536]{1,0:T(8,128)(2,1)}, bf16[2048,128]{1,0:T(8,128)(2,1)}, bf16[2048,128]{1,0:T(8,128)(2,1)}, bf16[2048,128]{1,0:T(8,128)(2,1)}, bf16[2048,128]{1,0:T(8,128)(2,1)}) custom-call(s32[1]{0:T(128)} %bitcast.place_ref, bf16[256,1536]{1,0:T(8,128)(2,1)} %queries.1.query_ref, bf16[256,1536]{1,0:T(8,128)(2,1)} %get-tuple-element.114.attended_ref.refs_2_, ...), custom_call_target="tpu_custom_call" | custom-call | flops 2000000 | tf_op jit(solution)/shard_map/attend_back/pallas_call | solution.py:304
  320.6 8.6 %collective-permute-start.22 = (bf16[2048,128]{1,0:T(8,128)(2,1)}, bf16[2048,128]{1,0:T(8,128)(2,1)S(1)}, u32[]{:S(2)}, u32[]{:S(2)}) collective-permute-start(bf16[2048,128]{1,0:T(8,128)(2,1)} %get-tuple-element.135), channel_id=1, source_target_pairs={{1,0},{2,1},{3,2},{5,4},{6,5},{7,6},{9,8},{10,9},{11,10},{13,12},{... | collective-permute-start | bytes 1572872 | tf_op jit(solution)/shard_map/ppermute | solution.py:721
  329.3 7.9 %dense_grads.2 = (bf16[4,192,3072]{2,1,0:T(8,128)(2,1)}, bf16[4,192,3072]{2,1,0:T(8,128)(2,1)}) custom-call(s32[1]{0:T(128)} %bitcast.7.place_ref, bf16[256,1536]{1,0:T(8,128)(2,1)} %copy-done.14, bf16[256,1536]{1,0:T(8,128)(2,1)} %get-tuple-element.112.normed_ref.refs_1_.refs_0_, bf16[256,1536]{1,0:T(8,128)(2,1)} %get-tuple-element.114.attended_ref.refs_2_, ...), custom_call_target="tpu_custom_call" | custom-call | flops 4000000 | tf_op jit(solution)/shard_map/dense_grads/pallas_call | solution.py:704
  337.2 5.6 %collective-permute-done.23 = bf16[2,3,5,192,256]{4,3,2,1,0:T(8,128)(2,1)} collective-permute-done((bf16[2,3,5,192,256]{4,3,2,1,0:T(8,128)(2,1)}, bf16[2,3,5,192,256]{4,3,2,1,0:T(8,128)(2,1)}, u32[]{:S(2)}, u32[]{:S(2)}) %collective-permute-start.23) | collective-permute-done | bytes 2949152 | tf_op jit(solution)/shard_map/ppermute | solution.py:743
  342.8 2.4 collective-permute-done.24
  346.1 6.8 %collective-permute-start.25 = (bf16[2048,128]{1,0:T(8,128)(2,1)S(1)}, bf16[2048,128]{1,0:T(8,128)(2,1)S(1)}, u32[]{:S(2)}, u32[]{:S(2)}) collective-permute-start(bf16[2048,128]{1,0:T(8,128)(2,1)S(1)} %add_convert_fusion.11), channel_id=1, source_target_pairs={{1,0},{2,1},{3,2},{5,4},{6,5},{7,6},{9,8},{10,9},{11,10},{13,12},{... | collective-permute-start | bytes 1572872 | tf_op jit(solution)/shard_map/ppermute | solution.py:721
  352.9 2.6 convert_reduce_fusion.2
  355.5 2.9 fusion.37
  358.4 2.9 fusion.36
  361.3 3.2 collective-permute-done.25
  364.6 4.4 collective-permute-start.27
  369.0 2.1 add_convert_fusion.4
  372.9 2.1 add_convert_fusion.7
  376.7 3.4 collective-permute-done.27.above_ref
  380.1 2.5 collective-permute-start.40
  382.6 4.6 fusion.11
  388.9 4.7 fusion.9
  395.4 2.7 unpack.1
  400.9 4.2 fusion.6
  405.2 2.5 fusion.21
  408.4 2.5 fusion.19
  414.0 3.4 collective-permute-start.41
  417.4 4.7 dense_grads.3
  422.1 5.1 all-to-all-start.2
  427.2 19.4 %collective-permute-done.31 = bf16[192,1536]{1,0:T(8,128)(2,1)} collective-permute-done((bf16[192,1536]{1,0:T(8,128)(2,1)}, bf16[192,1536]{1,0:T(8,128)(2,1)}, u32[]{:S(2)}, u32[]{:S(2)}) %collective-permute-start.31) | collective-permute-done | bytes 589856 | tf_op jit(solution)/shard_map/ppermute | solution.py:743
  450.9 2.4 collective-permute-start.34
  454.3 2.3 collective-permute-start.36
  466.4 5.6 %collective-permute-done.38 = bf16[2,192,512]{2,1,0:T(8,128)(2,1)S(1)} collective-permute-done((bf16[2,192,512]{2,1,0:T(8,128)(2,1)}, bf16[2,192,512]{2,1,0:T(8,128)(2,1)S(1)}, u32[]{:S(2)}, u32[]{:S(2)}) %collective-permute-start.38) | collective-permute-done | bytes 393248 | tf_op jit(solution)/shard_map/ppermute | solution.py:743
  472.1 12.4 %collective-permute-done.35 = bf16[48,3072]{1,0:T(8,128)(2,1)} collective-permute-done((bf16[48,3072]{1,0:T(8,128)(2,1)}, bf16[48,3072]{1,0:T(8,128)(2,1)}, u32[]{:S(2)}, u32[]{:S(2)}) %collective-permute-start.35) | collective-permute-done | bytes 294944 | tf_op jit(solution)/shard_map/ppermute | solution.py:783
  487.7 1.8 collective-permute-start.43
  493.1 1.8 add_bitcast_fusion.1
  494.9 2.7 add_bitcast_fusion
  507.3 2.0 collective-permute-start.46
  511.8 18.5 %collective-permute-done.45 = bf16[48,1152]{0,1:T(8,128)(2,1)S(1)} collective-permute-done((bf16[48,1152]{0,1:T(8,128)(2,1)}, bf16[48,1152]{0,1:T(8,128)(2,1)S(1)}, u32[]{:S(2)}, u32[]{:S(2)}) %collective-permute-start.45) | collective-permute-done | bytes 110624 | tf_op jit(solution)/shard_map/ppermute | solution.py:783
  (215 shorter events, 82.4 us)
Async XLA Ops:
  4.9 36.1 %copy-start.35 = (s32[256,8]{0,1:T(8,128)S(1)}, s32[256,8]{0,1:T(8,128)}, u32[]{:S(2)}) copy-start(s32[256,8]{0,1:T(8,128)} %param.31) | copy-start | bytes 24580
  9.2 15.8 %collective-permute-start = (bf16[2064,128]{1,0:T(8,128)(2,1)}, bf16[2064,128]{1,0:T(8,128)(2,1)S(1)}, u32[]{:S(2)}, u32[]{:S(2)}) collective-permute-start(bf16[2064,128]{1,0:T(8,128)(2,1)} %get-tuple-element.113.refs_0_.refs_4_), channel_id=1, source_target_pairs={{0,1},{1,2},{2,3},{4,5},{5,6},{6,7},{8,9},{9,10},{10,11},{12,13},{... | collective-permute-start | bytes 1585160 | tf_op jit(solution)/shard_map/ppermute | solution.py:717
  25.0 32.4 %copy-start = (bf16[2064,128]{1,0:T(8,128)(2,1)}, bf16[2064,128]{1,0:T(8,128)(2,1)S(1)}, u32[]{:S(2)}) copy-start(bf16[2064,128]{1,0:T(8,128)(2,1)S(1)} %collective-permute-done.refs_1_.refs_5_) | copy-start | bytes 1585156
  25.0 14.8 %collective-permute-start.1 = (bf16[2064,128]{1,0:T(8,128)(2,1)S(1)}, bf16[2064,128]{1,0:T(8,128)(2,1)S(1)}, u32[]{:S(2)}, u32[]{:S(2)}) collective-permute-start(bf16[2064,128]{1,0:T(8,128)(2,1)S(1)} %collective-permute-done.refs_1_.refs_5_), channel_id=1, source_target_pairs={{0,1},{1,2},{2,3},{4,5},{5,6},{6,7},{8,9},{9,10},{10,11},{12,13},{... | collective-permute-start | bytes 1585160 | tf_op jit(solution)/shard_map/ppermute | solution.py:717
  39.8 17.7 %copy-start.1 = (bf16[2064,128]{1,0:T(8,128)(2,1)}, bf16[2064,128]{1,0:T(8,128)(2,1)S(1)}, u32[]{:S(2)}) copy-start(bf16[2064,128]{1,0:T(8,128)(2,1)S(1)} %collective-permute-done.1.refs_2_.refs_6_) | copy-start | bytes 1585156
  39.8 17.7 %collective-permute-start.2 = (bf16[2064,128]{1,0:T(8,128)(2,1)S(1)}, bf16[2064,128]{1,0:T(8,128)(2,1)S(1)}, u32[]{:S(2)}, u32[]{:S(2)}) collective-permute-start(bf16[2064,128]{1,0:T(8,128)(2,1)S(1)} %collective-permute-done.1.refs_2_.refs_6_), channel_id=1, source_target_pairs={{0,1},{1,2},{2,3},{4,5},{5,6},{6,7},{8,9},{9,10},{10,11},{12,13},{... | collective-permute-start | bytes 1585160 | tf_op jit(solution)/shard_map/ppermute | solution.py:717
  44.4 40.8 %collective-permute-start.12 = (bf16[256,1664]{1,0:T(8,128)(2,1)}, bf16[256,1664]{1,0:T(8,128)(2,1)}, u32[]{:S(2)}, u32[]{:S(2)}) collective-permute-start(bf16[256,1664]{1,0:T(8,128)(2,1)} %extend.1.refs_7_), channel_id=1, source_target_pairs={{0,1},{1,2},{2,3},{4,5},{5,6},{6,7},{8,9},{9,10},{10,11},{12,13},{... | collective-permute-start | bytes 2555912 | tf_op jit(solution)/shard_map/ppermute | solution.py:717
  45.7 41.0 %collective-permute-start.15 = (bf16[256,1664]{1,0:T(8,128)(2,1)}, bf16[256,1664]{1,0:T(8,128)(2,1)}, u32[]{:S(2)}, u32[]{:S(2)}) collective-permute-start(bf16[256,1664]{1,0:T(8,128)(2,1)} %extend.1.refs_7_), channel_id=1, source_target_pairs={{1,0},{2,1},{3,2},{5,4},{6,5},{7,6},{9,8},{10,9},{11,10},{13,12},{... | collective-permute-start | bytes 2555912 | tf_op jit(solution)/shard_map/ppermute | solution.py:721
  58.2 12.3 %copy-start.3 = (bf16[256,1536]{1,0:T(8,128)(2,1)S(1)}, bf16[256,1536]{1,0:T(8,128)(2,1)}, u32[]{:S(2)}) copy-start(bf16[256,1536]{1,0:T(8,128)(2,1)} %tokens_ref.1) | copy-start | bytes 2359300
  74.7 65.2 %copy-start.33 = (bf16[1536,20]{0,1:T(8,128)(2,1)S(1)}, bf16[1536,20]{0,1:T(8,128)(2,1)}, u32[]{:S(2)}) copy-start(bf16[1536,20]{0,1:T(8,128)(2,1)} %param.26) | copy-start | bytes 184324
  75.0 90.4 %copy-start.16 = (bf16[256,1536]{1,0:T(8,128)(2,1)}, bf16[256,1536]{1,0:T(8,128)(2,1)S(1)}, u32[]{:S(2)}) copy-start(bf16[256,1536]{1,0:T(8,128)(2,1)S(1)} %multiply_convert_fusion.1.refs_0_) | copy-start | bytes 2359300
  75.0 26.0 %collective-permute-start.3 = (bf16[256,1536]{1,0:T(8,128)(2,1)S(1)}, bf16[256,1536]{1,0:T(8,128)(2,1)}, u32[]{:S(2)}, u32[]{:S(2)}) collective-permute-start(bf16[256,1536]{1,0:T(8,128)(2,1)S(1)} %multiply_convert_fusion.1.refs_0_), channel_id=1, source_target_pairs={{0,1},{1,2},{2,3},{4,5},{5,6},{6,7},{8,9},{9,10},{10,11},{12,13},{... | collective-permute-start | bytes 2359304 | tf_op jit(solution)/shard_map/ppermute | solution.py:717
  76.3 24.7 %collective-permute-start.4 = (bf16[256,1536]{1,0:T(8,128)(2,1)S(1)}, bf16[256,1536]{1,0:T(8,128)(2,1)}, u32[]{:S(2)}, u32[]{:S(2)}) collective-permute-start(bf16[256,1536]{1,0:T(8,128)(2,1)S(1)} %multiply_convert_fusion.1.refs_0_), channel_id=1, source_target_pairs={{1,0},{2,1},{3,2},{5,4},{6,5},{7,6},{9,8},{10,9},{11,10},{13,12},{... | collective-permute-start | bytes 2359304 | tf_op jit(solution)/shard_map/ppermute | solution.py:721
  85.2 32.9 %collective-permute-start.13 = (bf16[256,1664]{1,0:T(8,128)(2,1)}, bf16[256,1664]{1,0:T(8,128)(2,1)}, u32[]{:S(2)}, u32[]{:S(2)}) collective-permute-start(bf16[256,1664]{1,0:T(8,128)(2,1)} %collective-permute-done.12.refs_8_), channel_id=1, source_target_pairs={{0,1},{1,2},{2,3},{4,5},{5,6},{6,7},{8,9},{9,10},{10,11},{12,13},{... | collective-permute-start | bytes 2555912 | tf_op jit(solution)/shard_map/ppermute | solution.py:717
  86.7 5.5 %collective-permute-start.5 = (f32[1,24]{1,0:T(1,128)S(1)}, f32[1,24]{1,0:T(1,128)S(1)}, u32[]{:S(2)}, u32[]{:S(2)}) collective-permute-start(f32[1,24]{1,0:T(1,128)S(1)} %bitcast.138), channel_id=1, source_target_pairs={{0,4},{4,0},{8,12},{12,8},{16,20},{20,16},{24,28},{28,24},{1,5},{5... | collective-permute-start | bytes 296 | tf_op jit(solution)/shard_map/ppermute | solution.py:796
  86.8 32.7 %collective-permute-start.16 = (bf16[256,1664]{1,0:T(8,128)(2,1)}, bf16[256,1664]{1,0:T(8,128)(2,1)}, u32[]{:S(2)}, u32[]{:S(2)}) collective-permute-start(bf16[256,1664]{1,0:T(8,128)(2,1)} %collective-permute-done.15.refs_11_), channel_id=1, source_target_pairs={{1,0},{2,1},{3,2},{5,4},{6,5},{7,6},{9,8},{10,9},{11,10},{13,12},{... | collective-permute-start | bytes 2555912 | tf_op jit(solution)/shard_map/ppermute | solution.py:721
  92.2 3.5 collective-permute-start.6
  95.8 3.5 collective-permute-start.7
  101.0 32.1 %collective-permute-start.10 = (bf16[256,1536]{1,0:T(8,128)(2,1)}, bf16[256,1536]{1,0:T(8,128)(2,1)}, u32[]{:S(2)}, u32[]{:S(2)}) collective-permute-start(bf16[256,1536]{1,0:T(8,128)(2,1)} %collective-permute-done.4.refs_4_), channel_id=1, source_target_pairs={{1,0},{2,1},{3,2},{5,4},{6,5},{7,6},{9,8},{10,9},{11,10},{13,12},{... | collective-permute-start | bytes 2359304 | tf_op jit(solution)/shard_map/ppermute | solution.py:721
  105.8 32.6 %collective-permute-start.8 = (bf16[256,1536]{1,0:T(8,128)(2,1)}, bf16[256,1536]{1,0:T(8,128)(2,1)}, u32[]{:S(2)}, u32[]{:S(2)}) collective-permute-start(bf16[256,1536]{1,0:T(8,128)(2,1)} %collective-permute-done.3.refs_1_), channel_id=1, source_target_pairs={{0,1},{1,2},{2,3},{4,5},{5,6},{6,7},{8,9},{9,10},{10,11},{12,13},{... | collective-permute-start | bytes 2359304 | tf_op jit(solution)/shard_map/ppermute | solution.py:717
  118.1 35.1 %collective-permute-start.14 = (bf16[256,1664]{1,0:T(8,128)(2,1)}, bf16[256,1664]{1,0:T(8,128)(2,1)}, u32[]{:S(2)}, u32[]{:S(2)}) collective-permute-start(bf16[256,1664]{1,0:T(8,128)(2,1)} %collective-permute-done.13.refs_9_), channel_id=1, source_target_pairs={{0,1},{1,2},{2,3},{4,5},{5,6},{6,7},{8,9},{9,10},{10,11},{12,13},{... | collective-permute-start | bytes 2555912 | tf_op jit(solution)/shard_map/ppermute | solution.py:717
  119.4 33.8 %collective-permute-start.17 = (bf16[256,1664]{1,0:T(8,128)(2,1)}, bf16[256,1664]{1,0:T(8,128)(2,1)}, u32[]{:S(2)}, u32[]{:S(2)}) collective-permute-start(bf16[256,1664]{1,0:T(8,128)(2,1)} %collective-permute-done.16.refs_12_), channel_id=1, source_target_pairs={{1,0},{2,1},{3,2},{5,4},{6,5},{7,6},{9,8},{10,9},{11,10},{13,12},{... | collective-permute-start | bytes 2555912 | tf_op jit(solution)/shard_map/ppermute | solution.py:721
  133.1 32.3 %collective-permute-start.11 = (bf16[256,1536]{1,0:T(8,128)(2,1)}, bf16[256,1536]{1,0:T(8,128)(2,1)}, u32[]{:S(2)}, u32[]{:S(2)}) collective-permute-start(bf16[256,1536]{1,0:T(8,128)(2,1)} %collective-permute-done.10.refs_5_), channel_id=1, source_target_pairs={{1,0},{2,1},{3,2},{5,4},{6,5},{7,6},{9,8},{10,9},{11,10},{13,12},{... | collective-permute-start | bytes 2359304 | tf_op jit(solution)/shard_map/ppermute | solution.py:721
  138.4 27.0 %collective-permute-start.9 = (bf16[256,1536]{1,0:T(8,128)(2,1)}, bf16[256,1536]{1,0:T(8,128)(2,1)}, u32[]{:S(2)}, u32[]{:S(2)}) collective-permute-start(bf16[256,1536]{1,0:T(8,128)(2,1)} %collective-permute-done.8.refs_2_), channel_id=1, source_target_pairs={{0,1},{1,2},{2,3},{4,5},{5,6},{6,7},{8,9},{9,10},{10,11},{12,13},{... | collective-permute-start | bytes 2359304 | tf_op jit(solution)/shard_map/ppermute | solution.py:717
  141.2 65.6 %copy-start.36 = (s32[4]{0:T(128)}, s32[4]{0:T(128)S(1)}, u32[]{:S(2)}) copy-start(s32[4]{0:T(128)S(1)} %get-tuple-element.296.order_ref) | copy-start | bytes 52
  206.8 74.6 %all-to-all-start = ((bf16[4,256,1536]{2,1,0:T(8,128)(2,1)}), bf16[4,256,1536]{2,1,0:T(8,128)(2,1)}, u32[]{:S(2)}, u32[]{:S(2)}) async-start(bf16[4,256,1536]{2,1,0:T(8,128)(2,1)} %get-tuple-element.122), calls=%async_computation | async-start | bytes 6291456 | tf_op jit(solution)/shard_map/all_to_all | solution.py:928
  233.1 13.4 %collective-permute-start.18 = (bf16[3,5,192,512]{3,2,1,0:T(8,128)(2,1)}, bf16[3,5,192,512]{3,2,1,0:T(8,128)(2,1)}, u32[]{:S(2)}, u32[]{:S(2)}) collective-permute-start(bf16[3,5,192,512]{3,2,1,0:T(8,128)(2,1)} %get-tuple-element.127), channel_id=1, source_target_pairs={{0,4},{4,0},{8,12},{12,8},{16,20},{20,16},{24,28},{28,24},{1,5},{5... | collective-permute-start | bytes 8847368 | tf_op jit(solution)/shard_map/ppermute | solution.py:743
  233.1 13.4 %collective-permute-start.19 = (bf16[3,5,192,512]{3,2,1,0:T(8,128)(2,1)}, bf16[3,5,192,512]{3,2,1,0:T(8,128)(2,1)}, u32[]{:S(2)}, u32[]{:S(2)}) collective-permute-start(bf16[3,5,192,512]{3,2,1,0:T(8,128)(2,1)} %get-tuple-element.128), channel_id=1, source_target_pairs={{0,4},{4,0},{8,12},{12,8},{16,20},{20,16},{24,28},{28,24},{1,5},{5... | collective-permute-start | bytes 8847368 | tf_op jit(solution)/shard_map/ppermute | solution.py:743
  233.6 13.6 %collective-permute-start.20 = (bf16[3,5,192,512]{3,2,1,0:T(8,128)(2,1)}, bf16[3,5,192,512]{3,2,1,0:T(8,128)(2,1)}, u32[]{:S(2)}, u32[]{:S(2)}) collective-permute-start(bf16[3,5,192,512]{3,2,1,0:T(8,128)(2,1)} %get-tuple-element.129), channel_id=1, source_target_pairs={{0,4},{4,0},{8,12},{12,8},{16,20},{20,16},{24,28},{28,24},{1,5},{5... | collective-permute-start | bytes 8847368 | tf_op jit(solution)/shard_map/ppermute | solution.py:743
  233.7 17.8 %collective-permute-start.21 = (bf16[3,5,192,512]{3,2,1,0:T(8,128)(2,1)}, bf16[3,5,192,512]{3,2,1,0:T(8,128)(2,1)}, u32[]{:S(2)}, u32[]{:S(2)}) collective-permute-start(bf16[3,5,192,512]{3,2,1,0:T(8,128)(2,1)} %get-tuple-element.130), channel_id=1, source_target_pairs={{0,4},{4,0},{8,12},{12,8},{16,20},{20,16},{24,28},{28,24},{1,5},{5... | collective-permute-start | bytes 8847368 | tf_op jit(solution)/shard_map/ppermute | solution.py:743
  281.4 61.4 %collective-permute-start.23 = (bf16[2,3,5,192,256]{4,3,2,1,0:T(8,128)(2,1)}, bf16[2,3,5,192,256]{4,3,2,1,0:T(8,128)(2,1)}, u32[]{:S(2)}, u32[]{:S(2)}) collective-permute-start(bf16[2,3,5,192,256]{4,3,2,1,0:T(8,128)(2,1)} %get-tuple-element.136), channel_id=1, source_target_pairs={{0,8},{4,12},{8,0},{12,4},{16,24},{20,28},{24,16},{28,20},{1,9},{5... | collective-permute-start | bytes 8847368 | tf_op jit(solution)/shard_map/ppermute | solution.py:743
  282.8 62.4 %collective-permute-start.24 = (bf16[2,3,5,192,256]{4,3,2,1,0:T(8,128)(2,1)}, bf16[2,3,5,192,256]{4,3,2,1,0:T(8,128)(2,1)}, u32[]{:S(2)}, u32[]{:S(2)}) collective-permute-start(bf16[2,3,5,192,256]{4,3,2,1,0:T(8,128)(2,1)} %get-tuple-element.137), channel_id=1, source_target_pairs={{0,16},{4,20},{8,24},{12,28},{16,0},{20,4},{24,8},{28,12},{1,17},{... | collective-permute-start | bytes 8847368 | tf_op jit(solution)/shard_map/ppermute | solution.py:743
  285.0 52.2 %all-to-all-start.1 = ((bf16[4,256,768]{2,1,0:T(8,128)(2,1)}), bf16[4,256,768]{2,1,0:T(8,128)(2,1)}, u32[]{:S(2)}, u32[]{:S(2)}) async-start(bf16[4,256,768]{2,1,0:T(8,128)(2,1)} %get-tuple-element.138), calls=%async_computation.1 | async-start | bytes 3145728 | tf_op jit(solution)/shard_map/all_to_all | solution.py:937
  320.6 16.5 %collective-permute-start.22 = (bf16[2048,128]{1,0:T(8,128)(2,1)}, bf16[2048,128]{1,0:T(8,128)(2,1)S(1)}, u32[]{:S(2)}, u32[]{:S(2)}) collective-permute-start(bf16[2048,128]{1,0:T(8,128)(2,1)} %get-tuple-element.135), channel_id=1, source_target_pairs={{1,0},{2,1},{3,2},{5,4},{6,5},{7,6},{9,8},{10,9},{11,10},{13,12},{... | collective-permute-start | bytes 1572872 | tf_op jit(solution)/shard_map/ppermute | solution.py:721
  329.3 15.9 %copy-start.31 = (f32[256,1]{1,0:T(8,128)S(1)}, f32[256,1]{1,0:T(8,128)}, u32[]{:S(2)}) copy-start(f32[256,1]{1,0:T(8,128)} %get-tuple-element.157) | copy-start | bytes 3076
  329.3 16.7 %copy-start.26 = (bf16[2048,128]{1,0:T(8,128)(2,1)S(1)}, bf16[2048,128]{1,0:T(8,128)(2,1)}, u32[]{:S(2)}) copy-start(bf16[2048,128]{1,0:T(8,128)(2,1)} %get-tuple-element.145) | copy-start | bytes 1572868
  345.2 13.2 %collective-permute-start.26 = (bf16[4,192,3072]{2,1,0:T(8,128)(2,1)}, bf16[4,192,3072]{2,1,0:T(8,128)(2,1)}, u32[]{:S(2)}, u32[]{:S(2)}) collective-permute-start(bf16[4,192,3072]{2,1,0:T(8,128)(2,1)} %get-tuple-element.147), channel_id=1, source_target_pairs={{0,4},{4,0},{8,12},{12,8},{16,20},{20,16},{24,28},{28,24},{1,5},{5... | collective-permute-start | bytes 14155784 | tf_op jit(solution)/shard_map/ppermute | solution.py:743
  346.1 18.4 %collective-permute-start.25 = (bf16[2048,128]{1,0:T(8,128)(2,1)S(1)}, bf16[2048,128]{1,0:T(8,128)(2,1)S(1)}, u32[]{:S(2)}, u32[]{:S(2)}) collective-permute-start(bf16[2048,128]{1,0:T(8,128)(2,1)S(1)} %add_convert_fusion.11), channel_id=1, source_target_pairs={{1,0},{2,1},{3,2},{5,4},{6,5},{7,6},{9,8},{10,9},{11,10},{13,12},{... | collective-permute-start | bytes 1572872 | tf_op jit(solution)/shard_map/ppermute | solution.py:721
  364.6 15.4 %collective-permute-start.27 = (bf16[2048,128]{1,0:T(8,128)(2,1)S(1)}, bf16[2048,128]{1,0:T(8,128)(2,1)S(1)}, u32[]{:S(2)}, u32[]{:S(2)}) collective-permute-start(bf16[2048,128]{1,0:T(8,128)(2,1)S(1)} %add_convert_fusion.10), channel_id=1, source_target_pairs={{1,0},{2,1},{3,2},{5,4},{6,5},{7,6},{9,8},{10,9},{11,10},{13,12},{... | collective-permute-start | bytes 1572872 | tf_op jit(solution)/shard_map/ppermute | solution.py:721
  371.1 34.1 %collective-permute-start.29 = (bf16[2,192,1536]{2,1,0:T(8,128)(2,1)}, bf16[2,192,1536]{2,1,0:T(8,128)(2,1)}, u32[]{:S(2)}, u32[]{:S(2)}) collective-permute-start(bf16[2,192,1536]{2,1,0:T(8,128)(2,1)} %get-tuple-element.254), channel_id=1, source_target_pairs={{0,16},{4,20},{8,24},{12,28},{16,0},{20,4},{24,8},{28,12},{1,17},{... | collective-permute-start | bytes 3538952 | tf_op jit(solution)/shard_map/ppermute | solution.py:743
  374.9 30.2 %collective-permute-start.28 = (bf16[2,192,1536]{2,1,0:T(8,128)(2,1)}, bf16[2,192,1536]{2,1,0:T(8,128)(2,1)}, u32[]{:S(2)}, u32[]{:S(2)}) collective-permute-start(bf16[2,192,1536]{2,1,0:T(8,128)(2,1)} %get-tuple-element.256), channel_id=1, source_target_pairs={{0,8},{4,12},{8,0},{12,4},{16,24},{20,28},{24,16},{28,20},{1,9},{5... | collective-permute-start | bytes 3538952 | tf_op jit(solution)/shard_map/ppermute | solution.py:743
  380.1 33.3 %collective-permute-start.40 = (f32[1,24]{1,0:T(1,128)S(1)}, f32[1,24]{1,0:T(1,128)}, u32[]{:S(2)}, u32[]{:S(2)}) collective-permute-start(f32[1,24]{1,0:T(1,128)S(1)} %copy-done.39), channel_id=1, source_target_pairs={{0,1},{1,0},{2,3},{3,2},{4,5},{5,4},{6,7},{7,6},{8,9},{9,8},{10,11... | collective-permute-start | bytes 296 | tf_op jit(solution)/shard_map/ppermute | solution.py:796
  387.2 59.4 %collective-permute-start.33 = (bf16[3,5,192,256]{3,2,1,0:T(8,128)(2,1)}, bf16[3,5,192,256]{3,2,1,0:T(8,128)(2,1)}, u32[]{:S(2)}, u32[]{:S(2)}) collective-permute-start(bf16[3,5,192,256]{3,2,1,0:T(8,128)(2,1)} %get-tuple-element.250), channel_id=1, source_target_pairs={{0,8},{4,12},{8,0},{12,4},{16,24},{20,28},{24,16},{28,20},{1,9},{5... | collective-permute-start | bytes 4423688 | tf_op jit(solution)/shard_map/ppermute | solution.py:743
  393.6 52.9 %collective-permute-start.32 = (bf16[3,5,192,256]{3,2,1,0:T(8,128)(2,1)}, bf16[3,5,192,256]{3,2,1,0:T(8,128)(2,1)}, u32[]{:S(2)}, u32[]{:S(2)}) collective-permute-start(bf16[3,5,192,256]{3,2,1,0:T(8,128)(2,1)} %get-tuple-element.251), channel_id=1, source_target_pairs={{0,16},{4,20},{8,24},{12,28},{16,0},{20,4},{24,8},{28,12},{1,17},{... | collective-permute-start | bytes 4423688 | tf_op jit(solution)/shard_map/ppermute | solution.py:743
  407.7 38.8 %collective-permute-start.31 = (bf16[192,1536]{1,0:T(8,128)(2,1)}, bf16[192,1536]{1,0:T(8,128)(2,1)}, u32[]{:S(2)}, u32[]{:S(2)}) collective-permute-start(bf16[192,1536]{1,0:T(8,128)(2,1)} %get-tuple-element.268), channel_id=1, source_target_pairs={{0,8},{4,12},{8,0},{12,4},{16,24},{20,28},{24,16},{28,20},{1,9},{5... | collective-permute-start | bytes 1769480 | tf_op jit(solution)/shard_map/ppermute | solution.py:743
  410.9 35.7 %collective-permute-start.30 = (bf16[192,1536]{1,0:T(8,128)(2,1)}, bf16[192,1536]{1,0:T(8,128)(2,1)}, u32[]{:S(2)}, u32[]{:S(2)}) collective-permute-start(bf16[192,1536]{1,0:T(8,128)(2,1)} %get-tuple-element.269), channel_id=1, source_target_pairs={{0,16},{4,20},{8,24},{12,28},{16,0},{20,4},{24,8},{28,12},{1,17},{... | collective-permute-start | bytes 1769480 | tf_op jit(solution)/shard_map/ppermute | solution.py:743
  414.0 8.0 %collective-permute-start.41 = (f32[1,24]{1,0:T(1,128)S(1)}, f32[1,24]{1,0:T(1,128)S(1)}, u32[]{:S(2)}, u32[]{:S(2)}) collective-permute-start(f32[1,24]{1,0:T(1,128)S(1)} %max.21), channel_id=1, source_target_pairs={{0,2},{1,3},{2,0},{3,1},{4,6},{5,7},{6,4},{7,5},{8,10},{9,11},{10,... | collective-permute-start | bytes 296 | tf_op jit(solution)/shard_map/ppermute | solution.py:796
  422.0 24.6 %copy-start.38 = (f32[24]{0:T(128)S(1)}, f32[24]{0:T(128)}, u32[]{:S(2)}) copy-start(f32[24]{0:T(128)} %param.33) | copy-start | bytes 292
  422.1 62.5 %all-to-all-start.2 = ((bf16[4,256,768]{2,1,0:T(8,128)(2,1)}), bf16[4,256,768]{2,1,0:T(8,128)(2,1)}, u32[]{:S(2)}, u32[]{:S(2)}) async-start(bf16[4,256,768]{2,1,0:T(8,128)(2,1)} %get-tuple-element.188), calls=%async_computation.2 | async-start | bytes 3145728 | tf_op jit(solution)/shard_map/all_to_all | solution.py:964
  446.6 10.0 %collective-permute-start.37 = (bf16[4,192,1152]{2,1,0:T(8,128)(2,1)}, bf16[4,192,1152]{2,1,0:T(8,128)(2,1)}, u32[]{:S(2)}, u32[]{:S(2)}) collective-permute-start(bf16[4,192,1152]{2,1,0:T(8,128)(2,1)} %get-tuple-element.179), channel_id=1, source_target_pairs={{0,4},{4,0},{8,12},{12,8},{16,20},{20,16},{24,28},{28,24},{1,5},{5... | collective-permute-start | bytes 5308424 | tf_op jit(solution)/shard_map/ppermute | solution.py:743
  446.7 18.0 %copy-start.37 = (f32[24]{0:T(128)}, f32[24]{0:T(128)S(1)}, u32[]{:S(2)}) copy-start(f32[24]{0:T(128)S(1)} %get-tuple-element.246) | copy-start | bytes 292
  450.9 21.2 %collective-permute-start.34 = (bf16[48,3072]{1,0:T(8,128)(2,1)}, bf16[48,3072]{1,0:T(8,128)(2,1)}, u32[]{:S(2)}, u32[]{:S(2)}) collective-permute-start(bf16[48,3072]{1,0:T(8,128)(2,1)} %get-tuple-element.277), channel_id=1, source_target_pairs={{0,1},{1,2},{2,3},{3,0},{4,5},{5,6},{6,7},{7,4},{8,9},{9,10},{10,1... | collective-permute-start | bytes 884744 | tf_op jit(solution)/shard_map/ppermute | solution.py:783
  453.4 31.1 %collective-permute-start.35 = (bf16[48,3072]{1,0:T(8,128)(2,1)}, bf16[48,3072]{1,0:T(8,128)(2,1)}, u32[]{:S(2)}, u32[]{:S(2)}) collective-permute-start(bf16[48,3072]{1,0:T(8,128)(2,1)} %get-tuple-element.276), channel_id=1, source_target_pairs={{0,2},{1,3},{2,0},{3,1},{4,6},{5,7},{6,4},{7,5},{8,10},{9,11},{10,... | collective-permute-start | bytes 884744 | tf_op jit(solution)/shard_map/ppermute | solution.py:783
  454.3 30.2 %collective-permute-start.36 = (bf16[48,3072]{1,0:T(8,128)(2,1)}, bf16[48,3072]{1,0:T(8,128)(2,1)}, u32[]{:S(2)}, u32[]{:S(2)}) collective-permute-start(bf16[48,3072]{1,0:T(8,128)(2,1)} %get-tuple-element.275), channel_id=1, source_target_pairs={{0,3},{1,0},{2,1},{3,2},{4,7},{5,4},{6,5},{7,6},{8,11},{9,8},{10,9... | collective-permute-start | bytes 884744 | tf_op jit(solution)/shard_map/ppermute | solution.py:783
  458.9 27.9 %copy-start.19 = (bf16[2,192,640]{2,1,0:T(8,128)(2,1)}, bf16[2,192,640]{2,1,0:T(8,128)(2,1)S(1)}, u32[]{:S(2)}) copy-start(bf16[2,192,640]{2,1,0:T(8,128)(2,1)S(1)} %get-tuple-element.192) | copy-start | bytes 1474564
  458.9 13.2 %collective-permute-start.39 = (bf16[2,192,640]{2,1,0:T(8,128)(2,1)}, bf16[2,192,640]{2,1,0:T(8,128)(2,1)}, u32[]{:S(2)}, u32[]{:S(2)}) collective-permute-start(bf16[2,192,640]{2,1,0:T(8,128)(2,1)} %get-tuple-element.272), channel_id=1, source_target_pairs={{0,16},{4,20},{8,24},{12,28},{16,0},{20,4},{24,8},{28,12},{1,17},{... | collective-permute-start | bytes 1474568 | tf_op jit(solution)/shard_map/ppermute | solution.py:743
  461.3 28.2 %copy-start.22 = (bf16[2,192,512]{2,1,0:T(8,128)(2,1)}, bf16[2,192,512]{2,1,0:T(8,128)(2,1)S(1)}, u32[]{:S(2)}) copy-start(bf16[2,192,512]{2,1,0:T(8,128)(2,1)S(1)} %get-tuple-element.190) | copy-start | bytes 1179652
  461.3 10.8 %collective-permute-start.38 = (bf16[2,192,512]{2,1,0:T(8,128)(2,1)}, bf16[2,192,512]{2,1,0:T(8,128)(2,1)S(1)}, u32[]{:S(2)}, u32[]{:S(2)}) collective-permute-start(bf16[2,192,512]{2,1,0:T(8,128)(2,1)} %get-tuple-element.273), channel_id=1, source_target_pairs={{0,8},{4,12},{8,0},{12,4},{16,24},{20,28},{24,16},{28,20},{1,9},{5... | collective-permute-start | bytes 1179656 | tf_op jit(solution)/shard_map/ppermute | solution.py:743
  472.1 12.4 %copy-start.28 = (bf16[2,192,512]{2,1,0:T(8,128)(2,1)}, bf16[2,192,512]{2,1,0:T(8,128)(2,1)S(1)}, u32[]{:S(2)}) copy-start(bf16[2,192,512]{2,1,0:T(8,128)(2,1)S(1)} %collective-permute-done.38) | copy-start | bytes 1179652
  487.7 14.0 %collective-permute-start.43 = (bf16[192,640]{1,0:T(8,128)(2,1)S(1)}, bf16[192,640]{1,0:T(8,128)(2,1)S(1)}, u32[]{:S(2)}, u32[]{:S(2)}) collective-permute-start(bf16[192,640]{1,0:T(8,128)(2,1)S(1)} %fusion.28), channel_id=1, source_target_pairs={{0,8},{4,12},{8,0},{12,4},{16,24},{20,28},{24,16},{28,20},{1,9},{5... | collective-permute-start | bytes 737288 | tf_op jit(solution)/shard_map/ppermute | solution.py:743
  489.6 12.2 %collective-permute-start.42 = (bf16[192,512]{1,0:T(8,128)(2,1)S(1)}, bf16[192,512]{1,0:T(8,128)(2,1)S(1)}, u32[]{:S(2)}, u32[]{:S(2)}) collective-permute-start(bf16[192,512]{1,0:T(8,128)(2,1)S(1)} %fusion.31), channel_id=1, source_target_pairs={{0,16},{4,20},{8,24},{12,28},{16,0},{20,4},{24,8},{28,12},{1,17},{... | collective-permute-start | bytes 589832 | tf_op jit(solution)/shard_map/ppermute | solution.py:743
  504.0 7.8 %collective-permute-start.44 = (bf16[48,1152]{0,1:T(8,128)(2,1)}, bf16[48,1152]{0,1:T(8,128)(2,1)S(1)}, u32[]{:S(2)}, u32[]{:S(2)}) collective-permute-start(bf16[48,1152]{0,1:T(8,128)(2,1)} %bitcast.45), channel_id=1, source_target_pairs={{0,1},{1,2},{2,3},{3,0},{4,5},{5,6},{6,7},{7,4},{8,9},{9,10},{10,1... | collective-permute-start | bytes 331784 | tf_op jit(solution)/shard_map/ppermute | solution.py:783
  504.9 25.5 %collective-permute-start.45 = (bf16[48,1152]{0,1:T(8,128)(2,1)}, bf16[48,1152]{0,1:T(8,128)(2,1)S(1)}, u32[]{:S(2)}, u32[]{:S(2)}) collective-permute-start(bf16[48,1152]{0,1:T(8,128)(2,1)} %bitcast.46), channel_id=1, source_target_pairs={{0,2},{1,3},{2,0},{3,1},{4,6},{5,7},{6,4},{7,5},{8,10},{9,11},{10,... | collective-permute-start | bytes 331784 | tf_op jit(solution)/shard_map/ppermute | solution.py:783
  507.3 23.1 %collective-permute-start.46 = (bf16[48,1152]{0,1:T(8,128)(2,1)}, bf16[48,1152]{0,1:T(8,128)(2,1)S(1)}, u32[]{:S(2)}, u32[]{:S(2)}) collective-permute-start(bf16[48,1152]{0,1:T(8,128)(2,1)} %bitcast.136), channel_id=1, source_target_pairs={{0,3},{1,0},{2,1},{3,2},{4,7},{5,4},{6,5},{7,6},{8,11},{9,8},{10,9... | collective-permute-start | bytes 331784 | tf_op jit(solution)/shard_map/ppermute | solution.py:783
  (26 other events, 107.6 us)

commit v5 on v4

--- a/solution.py
+++ b/solution.py
@@ -988,6 +988,9 @@
     keep, send, wide, expert_sums = lax.optimization_barrier((keep, send, wide, expert_sums))
     rest = start_dense((keep, flip(send, 1, dp_size)))
     rest = step_spread(rest, 0, dp_size, dp_place)
+    rest, expert_sums, mix_two = lax.optimization_barrier((rest, expert_sums, mix_two))
+    for stage in range(1, stages):
+        rest = step_spread(rest, stage, dp_size, dp_place)
     wide_parts, rest, expert_sums, mix_two = lax.optimization_barrier(
         (pass_line(wide, place, size), rest, expert_sums, mix_two)
     )
@@ -996,8 +999,6 @@
     expert_sums = [
         jnp.concatenate([a[w].astype(F32) + b[w].astype(F32) for a, b in expert_sums], axis=-1) for w in range(3)
     ]
-    for stage in range(1, stages):
-        rest = step_spread(rest, stage, dp_size, dp_place)
     rest_parts = lax.optimization_barrier(pass_line(rest, place, size))
     wide_grad, rest_grad = total_of(wide_parts), total_of(rest_parts)
     mixture = jnp.concatenate([jnp.sum(part.astype(F32), axis=0) for part in (mix_one, mix_two)], axis=1)

time: 543 us -> 563 us (1.037)
  the two profiles are of different devices: /device:TPU:24 before, /device:TPU:11 now
where the time goes in v5:
time: 563 us; the launch traced here: 554 us
  waiting for transfers between devices  188 us (33%)
  Pallas kernels  149 us (26%)
  starting transfers between devices  120 us (21%)
  other arithmetic  51.7 us (9%)
  local copies, waits for them, and re-layouts  27.1 us (5%)
  matrix products  16.3 us (3%)
    ppermute x18, waiting for transfers between devices, flip(): return lax.ppermute(value, 'dp', [(i, i ^ bit) for i in range(size)])  53.3 us
    ppermute x9, waiting for transfers between devices, line_down(): return lax.ppermute(value, 'expert', [(i + 1, i) for i in range(size - 1)])  49.9 us
    pallas_call x1, Pallas kernels, run_experts(): pl.pallas_call(functools.partial(expert_kernel, blocks, slot_rows, local_...  41.5 us
    pallas_call x2, Pallas kernels, run_expert_grads(): pl.pallas_call(functools.partial(expert_keep_kernel, owners.bit_length()...  37.8 us
    ppermute x9, waiting for transfers between devices, line_up(): return lax.ppermute(value, 'expert', [(i, i + 1) for i in range(size - 1)])  37.5 us
    ppermute x9, starting transfers between devices, line_down(): return lax.ppermute(value, 'expert', [(i + 1, i) for i in range(size - 1)])  33.2 us
    ppermute x18, starting transfers between devices, flip(): return lax.ppermute(value, 'dp', [(i, i ^ bit) for i in range(size)])  25.7 us
    ppermute x9, starting transfers between devices, line_up(): return lax.ppermute(value, 'expert', [(i, i + 1) for i in range(size - 1)])  25.5 us
  transfers between devices with their start and end apart: 50, of which 27 were waited for; matrix products, arithmetic and copies ran while one was open for 15% of the time, Pallas kernels for 19%

profile of v5, /device:TPU:11, one launch (start us, length us, event | category | flops | bytes accessed | tf_op | source)
XLA Modules:
  0.0 554.3 jit_solution(9504673106698842544)
XLA Ops:
  4.9 4.2 front.1
  9.2 3.2 collective-permute-start
  12.4 11.8 %collective-permute-done.refs_1_.refs_5_ = bf16[2064,128]{1,0:T(8,128)(2,1)S(1)} collective-permute-done((bf16[2064,128]{1,0:T(8,128)(2,1)}, bf16[2064,128]{1,0:T(8,128)(2,1)S(1)}, u32[]{:S(2)}, u32[]{:S(2)}) %collective-permute-start) | collective-permute-done | bytes 528416 | tf_op jit(solution)/shard_map/ppermute | solution.py:717
  24.1 3.2 collective-permute-start.1
  27.3 10.6 %collective-permute-done.1.refs_2_.refs_6_ = bf16[2064,128]{1,0:T(8,128)(2,1)S(1)} collective-permute-done((bf16[2064,128]{1,0:T(8,128)(2,1)S(1)}, bf16[2064,128]{1,0:T(8,128)(2,1)S(1)}, u32[]{:S(2)}, u32[]{:S(2)}) %collective-permute-start.1) | collective-permute-done | bytes 528416 | tf_op jit(solution)/shard_map/ppermute | solution.py:717
  38.0 3.2 collective-permute-start.2
  42.0 2.6 extend.1.refs_7_
  44.6 3.2 collective-permute-start.12
  47.8 3.0 collective-permute-start.15
  50.8 5.6 %queries.1.query_ref = bf16[256,1536]{1,0:T(8,128)(2,1)} custom-call(bf16[256,1536]{1,0:T(8,128)(2,1)} %get-tuple-element.121.normed_ref.refs_1_.refs_0_, bf16[1536,1536]{1,0:T(8,128)(2,1)} %query_ref.1, f32[256,128]{1,0:T(8,128)} %get-tuple-element.317.cos_ref, f32[256,128]{1,0:T(8,128)} %get-tuple-element.316.sin_ref), custom_call_target="tpu_custom_call" | custom-call | flops 5000000 | tf_op jit(solution)/shard_map/queries/pallas_call | solution.py:896
  57.2 12.3 %attend.1 = (bf16[256,1536]{1,0:T(8,128)(2,1)}, f32[4,2,768]{2,1,0:T(2,128)}, f32[4,2,768]{2,1,0:T(2,128)}) custom-call(s32[1]{0:T(128)} %bitcast.place_ref, bf16[256,1536]{1,0:T(8,128)(2,1)} %queries.1.query_ref, bf16[2064,128]{1,0:T(8,128)(2,1)} %get-tuple-element.122.refs_0_.refs_4_, bf16[2064,128]{1,0:T(8,128)(2,1)} %copy-done, ...), custom_call_target="tpu_custom_call" | custom-call | flops 20000000 | tf_op jit(solution)/shard_map/attend/pallas_call | solution.py:217
  69.5 4.1 multiply_reduce_fusion.2
  73.9 2.3 collective-permute-start.3
  76.2 4.0 collective-permute-start.4
  82.3 3.9 collective-permute-start.5
  86.2 4.6 collective-permute-start.16
  98.9 4.2 collective-permute-start.8
  103.0 6.9 %collective-permute-done.13.refs_9_ = bf16[256,1664]{1,0:T(8,128)(2,1)} collective-permute-done((bf16[256,1664]{1,0:T(8,128)(2,1)}, bf16[256,1664]{1,0:T(8,128)(2,1)}, u32[]{:S(2)}, u32[]{:S(2)}) %collective-permute-start.13) | collective-permute-done | bytes 852000 | tf_op jit(solution)/shard_map/ppermute | solution.py:717
  112.2 3.9 collective-permute-start.17
  116.1 12.6 %collective-permute-done.10.refs_5_ = bf16[256,1536]{1,0:T(8,128)(2,1)} collective-permute-done((bf16[256,1536]{1,0:T(8,128)(2,1)}, bf16[256,1536]{1,0:T(8,128)(2,1)}, u32[]{:S(2)}, u32[]{:S(2)}) %collective-permute-start.10) | collective-permute-done | bytes 786464 | tf_op jit(solution)/shard_map/ppermute | solution.py:721
  128.7 4.0 collective-permute-start.11
  136.8 8.2 %collective-permute-done.14.refs_10_ = bf16[256,1664]{1,0:T(8,128)(2,1)} collective-permute-done((bf16[256,1664]{1,0:T(8,128)(2,1)}, bf16[256,1664]{1,0:T(8,128)(2,1)}, u32[]{:S(2)}, u32[]{:S(2)}) %collective-permute-start.14) | collective-permute-done | bytes 852000 | tf_op jit(solution)/shard_map/ppermute | solution.py:717
  147.0 16.9 %collective-permute-done.11.refs_6_ = bf16[256,1536]{1,0:T(8,128)(2,1)} collective-permute-done((bf16[256,1536]{1,0:T(8,128)(2,1)}, bf16[256,1536]{1,0:T(8,128)(2,1)}, u32[]{:S(2)}, u32[]{:S(2)}) %collective-permute-start.11) | collective-permute-done | bytes 786464 | tf_op jit(solution)/shard_map/ppermute | solution.py:721
  163.9 41.5 %experts.1 = (bf16[5,512,1536]{2,1,0:T(8,128)(2,1)}, bf16[5,512,1536]{2,1,0:T(8,128)(2,1)}, bf16[5,512,512]{2,1,0:T(8,128)(2,1)}, bf16[5,512,512]{2,1,0:T(8,128)...) custom-call(s32[9]{0:T(128)} %pad_add_fusion.place_ref, ...), custom_call_target="tpu_custom_call" | custom-call | flops 45000000 | tf_op jit(solution)/shard_map/experts/pallas_call | solution.py:483
  205.4 7.1 %all-to-all-start = ((bf16[4,256,1536]{2,1,0:T(8,128)(2,1)}), bf16[4,256,1536]{2,1,0:T(8,128)(2,1)}, u32[]{:S(2)}, u32[]{:S(2)}) async-start(bf16[4,256,1536]{2,1,0:T(8,128)(2,1)} %get-tuple-element.131), calls=%async_computation | async-start | bytes 6291456 | tf_op jit(solution)/shard_map/all_to_all | solution.py:928
  212.5 16.8 %expert_send.1 = (bf16[3,5,192,512]{3,2,1,0:T(8,128)(2,1)}, bf16[3,5,192,512]{3,2,1,0:T(8,128)(2,1)}, bf16[3,5,192,512]{3,2,1,0:T(8,128)(2,1)}, bf16[3,5,192,512]{3,2,1,0:T(8,128)(2,1)}) custom-call(s32[1]{0:T(128)} %bitcast.7.place_ref, bf16[5,512,1536]{2,1,0:T(8,128)(2,1)} %get-tuple-element.132.xs_ref, bf16[5,512,1536]{2,1,0:T(8,128)(2,1)} %get-tuple-element.133.cs_ref, ...), custom_call_target="tpu_custom_call" | custom-call | flops 15000000 | tf_op jit(solution)/shard_map/expert_send/pallas_call | solution.py:653
  229.2 4.8 collective-permute-start.18
  234.6 12.3 %mixture.1 = (bf16[4,256,768]{2,1,0:T(8,128)(2,1)}, bf16[4,256,768]{2,1,0:T(8,128)(2,1)}) custom-call(s32[4]{0:T(128)} %copy-done.25, bf16[5,1536,512]{2,1,0:T(8,128)(2,1)} %down_ref.3, bf16[5,512,512]{2,1,0:T(8,128)(2,1)} %get-tuple-element.127.hs_ref, bf16[4,640,256]{2,1,0:T(8,128)(2,1)} %get-tuple-element.128.hits_ref), custom_call_target="tpu_custom_call" | custom-call | flops 10000000 | tf_op jit(solution)/shard_map/mixture/pallas_call | solution.py:567
  247.8 4.2 collective-permute-done.21.refs_3_
  252.0 21.0 %expert_keep.1 = (bf16[2,3,5,192,256]{4,3,2,1,0:T(8,128)(2,1)}, bf16[2,3,5,192,256]{4,3,2,1,0:T(8,128)(2,1)}, bf16[2,3,5,192,256]{4,3,2,1,0:T(8,128)(2,1)}, bf16[2,3,5,192,256]{4,3,2,1,0:T(8,128)(2,1)}) custom-call(s32[1]{0:T(128)} %bitcast.7.place_ref, bf16[5,512,1536]{2,1,0:T(8,128)(2,1)} %get-tuple-element.132.xs_ref, ...), custom_call_target="tpu_custom_call" | custom-call | flops 15000000 | tf_op jit(solution)/shard_map/expert_keep/pallas_call | solution.py:653
  273.0 2.6 all-to-all-done
  275.6 9.6 %collective-permute-start.23 = (bf16[2,3,5,192,256]{4,3,2,1,0:T(8,128)(2,1)}, bf16[2,3,5,192,256]{4,3,2,1,0:T(8,128)(2,1)}, u32[]{:S(2)}, u32[]{:S(2)}) collective-permute-start(bf16[2,3,5,192,256]{4,3,2,1,0:T(8,128)(2,1)} %get-tuple-element.145), channel_id=1, source_target_pairs={{0,8},{4,12},{8,0},{12,4},{16,24},{20,28},{24,16},{28,20},{1,9},{5... | collective-permute-start | bytes 8847368 | tf_op jit(solution)/shard_map/ppermute | solution.py:743
  285.2 8.2 %all-to-all-start.1 = ((bf16[4,256,768]{2,1,0:T(8,128)(2,1)}), bf16[4,256,768]{2,1,0:T(8,128)(2,1)}, u32[]{:S(2)}, u32[]{:S(2)}) async-start(bf16[4,256,768]{2,1,0:T(8,128)(2,1)} %get-tuple-element.147), calls=%async_computation.1 | async-start | bytes 3145728 | tf_op jit(solution)/shard_map/all_to_all | solution.py:937
  293.5 2.6 convert_reduce_fusion
  298.9 4.9 convolution_convert_fusion.grad_ref
  303.8 17.6 %attend_back.1 = (bf16[256,1536]{1,0:T(8,128)(2,1)}, bf16[2048,128]{1,0:T(8,128)(2,1)}, bf16[2048,128]{1,0:T(8,128)(2,1)}, bf16[2048,128]{1,0:T(8,128)(2,1)}, bf16[2048,128]{1,0:T(8,128)(2,1)}) custom-call(s32[1]{0:T(128)} %bitcast.place_ref, bf16[256,1536]{1,0:T(8,128)(2,1)} %queries.1.query_ref, bf16[256,1536]{1,0:T(8,128)(2,1)} %get-tuple-element.123.attended_ref.refs_2_, ...), custom_call_target="tpu_custom_call" | custom-call | flops 2000000 | tf_op jit(solution)/shard_map/attend_back/pallas_call | solution.py:304
  323.3 7.9 %dense_grads.2 = (bf16[4,192,3072]{2,1,0:T(8,128)(2,1)}, bf16[4,192,3072]{2,1,0:T(8,128)(2,1)}) custom-call(s32[1]{0:T(128)} %bitcast.7.place_ref, bf16[256,1536]{1,0:T(8,128)(2,1)} %copy-done.9, bf16[256,1536]{1,0:T(8,128)(2,1)} %get-tuple-element.121.normed_ref.refs_1_.refs_0_, bf16[256,1536]{1,0:T(8,128)(2,1)} %get-tuple-element.123.attended_ref.refs_2_, ...), custom_call_target="tpu_custom_call" | custom-call | flops 4000000 | tf_op jit(solution)/shard_map/dense_grads/pallas_call | solution.py:704
  331.2 8.9 %collective-permute-done.22 = bf16[2048,128]{1,0:T(8,128)(2,1)S(1)} collective-permute-done((bf16[2048,128]{1,0:T(8,128)(2,1)}, bf16[2048,128]{1,0:T(8,128)(2,1)S(1)}, u32[]{:S(2)}, u32[]{:S(2)}) %collective-permute-start.22) | collective-permute-done | bytes 524320 | tf_op jit(solution)/shard_map/ppermute | solution.py:721
  340.1 7.7 %collective-permute-done.23 = bf16[2,3,5,192,256]{4,3,2,1,0:T(8,128)(2,1)} collective-permute-done((bf16[2,3,5,192,256]{4,3,2,1,0:T(8,128)(2,1)}, bf16[2,3,5,192,256]{4,3,2,1,0:T(8,128)(2,1)}, u32[]{:S(2)}, u32[]{:S(2)}) %collective-permute-start.23) | collective-permute-done | bytes 2949152 | tf_op jit(solution)/shard_map/ppermute | solution.py:743
  348.7 3.1 collective-permute-start.26
  352.7 5.9 %collective-permute-start.25 = (bf16[2048,128]{1,0:T(8,128)(2,1)S(1)}, bf16[2048,128]{1,0:T(8,128)(2,1)S(1)}, u32[]{:S(2)}, u32[]{:S(2)}) collective-permute-start(bf16[2048,128]{1,0:T(8,128)(2,1)S(1)} %add_convert_fusion.11), channel_id=1, source_target_pairs={{1,0},{2,1},{3,2},{5,4},{6,5},{7,6},{9,8},{10,9},{11,10},{13,12},{... | collective-permute-start | bytes 1572872 | tf_op jit(solution)/shard_map/ppermute | solution.py:721
  358.6 2.9 fusion.35
  361.5 2.9 fusion.34
  364.5 5.3 collective-permute-done.25
  369.9 4.1 collective-permute-start.27
  377.7 2.6 convert_reduce_fusion.2
  380.3 4.2 collective-permute-done.27.above_ref
  386.8 4.6 fusion.11
  391.4 4.7 fusion.9
  396.1 2.7 unpack.1
  404.2 2.6 fusion.21
  407.4 2.6 fusion.19
  411.5 2.9 fusion.6
  415.0 4.7 dense_grads.3
  419.7 28.7 %collective-permute-done.31 = bf16[192,1536]{1,0:T(8,128)(2,1)} collective-permute-done((bf16[192,1536]{1,0:T(8,128)(2,1)}, bf16[192,1536]{1,0:T(8,128)(2,1)}, u32[]{:S(2)}, u32[]{:S(2)}) %collective-permute-start.31) | collective-permute-done | bytes 589856 | tf_op jit(solution)/shard_map/ppermute | solution.py:743
  448.4 2.3 collective-permute-start.37
  450.7 3.0 fusion.5
  453.7 4.7 all-to-all-start.2
  474.3 6.5 %collective-permute-done.38 = bf16[2,192,512]{2,1,0:T(8,128)(2,1)S(1)} collective-permute-done((bf16[2,192,512]{2,1,0:T(8,128)(2,1)S(1)}, bf16[2,192,512]{2,1,0:T(8,128)(2,1)S(1)}, u32[]{:S(2)}, u32[]{:S(2)}) %collective-permute-start.38) | collective-permute-done | bytes 393248 | tf_op jit(solution)/shard_map/ppermute | solution.py:743
  480.8 24.6 %all-to-all-done.2 = bf16[4,256,768]{2,1,0:T(8,128)(2,1)} async-done(((bf16[4,256,768]{2,1,0:T(8,128)(2,1)}), bf16[4,256,768]{2,1,0:T(8,128)(2,1)}, u32[]{:S(2)}, u32[]{:S(2)}) %all-to-all-start.2) | async-done | bytes 1572896 | tf_op jit(solution)/shard_map/all_to_all | solution.py:964
  509.7 2.4 collective-permute-done.42
  513.3 4.7 collective-permute-done.35
  539.4 8.2 %collective-permute-done.45 = bf16[48,1152]{0,1:T(8,128)(2,1)S(1)} collective-permute-done((bf16[48,1152]{0,1:T(8,128)(2,1)}, bf16[48,1152]{0,1:T(8,128)(2,1)S(1)}, u32[]{:S(2)}, u32[]{:S(2)}) %collective-permute-start.45) | collective-permute-done | bytes 110624 | tf_op jit(solution)/shard_map/ppermute | solution.py:783
  547.5 3.6 collective-permute-done.46
  (198 shorter events, 91.9 us)
Async XLA Ops:
  4.9 36.3 %copy-start.24 = (s32[256,8]{0,1:T(8,128)S(1)}, s32[256,8]{0,1:T(8,128)}, u32[]{:S(2)}) copy-start(s32[256,8]{0,1:T(8,128)} %param.31) | copy-start | bytes 24580
  9.2 15.0 %collective-permute-start = (bf16[2064,128]{1,0:T(8,128)(2,1)}, bf16[2064,128]{1,0:T(8,128)(2,1)S(1)}, u32[]{:S(2)}, u32[]{:S(2)}) collective-permute-start(bf16[2064,128]{1,0:T(8,128)(2,1)} %get-tuple-element.122.refs_0_.refs_4_), channel_id=1, source_target_pairs={{0,1},{1,2},{2,3},{4,5},{5,6},{6,7},{8,9},{9,10},{10,11},{12,13},{... | collective-permute-start | bytes 1585160 | tf_op jit(solution)/shard_map/ppermute | solution.py:717
  24.1 32.3 %copy-start = (bf16[2064,128]{1,0:T(8,128)(2,1)}, bf16[2064,128]{1,0:T(8,128)(2,1)S(1)}, u32[]{:S(2)}) copy-start(bf16[2064,128]{1,0:T(8,128)(2,1)S(1)} %collective-permute-done.refs_1_.refs_5_) | copy-start | bytes 1585156
  24.1 13.8 %collective-permute-start.1 = (bf16[2064,128]{1,0:T(8,128)(2,1)S(1)}, bf16[2064,128]{1,0:T(8,128)(2,1)S(1)}, u32[]{:S(2)}, u32[]{:S(2)}) collective-permute-start(bf16[2064,128]{1,0:T(8,128)(2,1)S(1)} %collective-permute-done.refs_1_.refs_5_), channel_id=1, source_target_pairs={{0,1},{1,2},{2,3},{4,5},{5,6},{6,7},{8,9},{9,10},{10,11},{12,13},{... | collective-permute-start | bytes 1585160 | tf_op jit(solution)/shard_map/ppermute | solution.py:717
  38.0 18.4 %copy-start.1 = (bf16[2064,128]{1,0:T(8,128)(2,1)}, bf16[2064,128]{1,0:T(8,128)(2,1)S(1)}, u32[]{:S(2)}) copy-start(bf16[2064,128]{1,0:T(8,128)(2,1)S(1)} %collective-permute-done.1.refs_2_.refs_6_) | copy-start | bytes 1585156
  38.0 18.4 %collective-permute-start.2 = (bf16[2064,128]{1,0:T(8,128)(2,1)S(1)}, bf16[2064,128]{1,0:T(8,128)(2,1)S(1)}, u32[]{:S(2)}, u32[]{:S(2)}) collective-permute-start(bf16[2064,128]{1,0:T(8,128)(2,1)S(1)} %collective-permute-done.1.refs_2_.refs_6_), channel_id=1, source_target_pairs={{0,1},{1,2},{2,3},{4,5},{5,6},{6,7},{8,9},{9,10},{10,11},{12,13},{... | collective-permute-start | bytes 1585160 | tf_op jit(solution)/shard_map/ppermute | solution.py:717
  44.6 35.6 %collective-permute-start.12 = (bf16[256,1664]{1,0:T(8,128)(2,1)}, bf16[256,1664]{1,0:T(8,128)(2,1)}, u32[]{:S(2)}, u32[]{:S(2)}) collective-permute-start(bf16[256,1664]{1,0:T(8,128)(2,1)} %extend.1.refs_7_), channel_id=1, source_target_pairs={{0,1},{1,2},{2,3},{4,5},{5,6},{6,7},{8,9},{9,10},{10,11},{12,13},{... | collective-permute-start | bytes 2555912 | tf_op jit(solution)/shard_map/ppermute | solution.py:717
  47.8 38.4 %collective-permute-start.15 = (bf16[256,1664]{1,0:T(8,128)(2,1)}, bf16[256,1664]{1,0:T(8,128)(2,1)}, u32[]{:S(2)}, u32[]{:S(2)}) collective-permute-start(bf16[256,1664]{1,0:T(8,128)(2,1)} %extend.1.refs_7_), channel_id=1, source_target_pairs={{1,0},{2,1},{3,2},{5,4},{6,5},{7,6},{9,8},{10,9},{11,10},{13,12},{... | collective-permute-start | bytes 2555912 | tf_op jit(solution)/shard_map/ppermute | solution.py:721
  57.2 12.3 %copy-start.3 = (bf16[256,1536]{1,0:T(8,128)(2,1)S(1)}, bf16[256,1536]{1,0:T(8,128)(2,1)}, u32[]{:S(2)}) copy-start(bf16[256,1536]{1,0:T(8,128)(2,1)} %tokens_ref.1) | copy-start | bytes 2359300
  73.7 8.5 %copy-start.23 = (f32[4,2,768]{2,1,0:T(2,128)S(1)}, f32[4,2,768]{2,1,0:T(2,128)}, u32[]{:S(2)}) copy-start(f32[4,2,768]{2,1,0:T(2,128)} %get-tuple-element.124) | copy-start | bytes 73732
  73.7 61.2 %copy-start.22 = (bf16[1536,20]{0,1:T(8,128)(2,1)S(1)}, bf16[1536,20]{0,1:T(8,128)(2,1)}, u32[]{:S(2)}) copy-start(bf16[1536,20]{0,1:T(8,128)(2,1)} %param.26) | copy-start | bytes 184324
  73.9 90.0 %copy-start.11 = (bf16[256,1536]{1,0:T(8,128)(2,1)}, bf16[256,1536]{1,0:T(8,128)(2,1)S(1)}, u32[]{:S(2)}) copy-start(bf16[256,1536]{1,0:T(8,128)(2,1)S(1)} %multiply_convert_fusion.1.refs_0_) | copy-start | bytes 2359300
  73.9 23.0 %collective-permute-start.3 = (bf16[256,1536]{1,0:T(8,128)(2,1)S(1)}, bf16[256,1536]{1,0:T(8,128)(2,1)}, u32[]{:S(2)}, u32[]{:S(2)}) collective-permute-start(bf16[256,1536]{1,0:T(8,128)(2,1)S(1)} %multiply_convert_fusion.1.refs_0_), channel_id=1, source_target_pairs={{0,1},{1,2},{2,3},{4,5},{5,6},{6,7},{8,9},{9,10},{10,11},{12,13},{... | collective-permute-start | bytes 2359304 | tf_op jit(solution)/shard_map/ppermute | solution.py:717
  76.2 20.7 %collective-permute-start.4 = (bf16[256,1536]{1,0:T(8,128)(2,1)S(1)}, bf16[256,1536]{1,0:T(8,128)(2,1)}, u32[]{:S(2)}, u32[]{:S(2)}) collective-permute-start(bf16[256,1536]{1,0:T(8,128)(2,1)S(1)} %multiply_convert_fusion.1.refs_0_), channel_id=1, source_target_pairs={{1,0},{2,1},{3,2},{5,4},{6,5},{7,6},{9,8},{10,9},{11,10},{13,12},{... | collective-permute-start | bytes 2359304 | tf_op jit(solution)/shard_map/ppermute | solution.py:721
  80.2 29.7 %collective-permute-start.13 = (bf16[256,1664]{1,0:T(8,128)(2,1)}, bf16[256,1664]{1,0:T(8,128)(2,1)}, u32[]{:S(2)}, u32[]{:S(2)}) collective-permute-start(bf16[256,1664]{1,0:T(8,128)(2,1)} %collective-permute-done.12.refs_8_), channel_id=1, source_target_pairs={{0,1},{1,2},{2,3},{4,5},{5,6},{6,7},{8,9},{9,10},{10,11},{12,13},{... | collective-permute-start | bytes 2555912 | tf_op jit(solution)/shard_map/ppermute | solution.py:717
  82.3 8.5 %collective-permute-start.5 = (f32[1,24]{1,0:T(1,128)S(1)}, f32[1,24]{1,0:T(1,128)S(1)}, u32[]{:S(2)}, u32[]{:S(2)}) collective-permute-start(f32[1,24]{1,0:T(1,128)S(1)} %bitcast.133), channel_id=1, source_target_pairs={{0,4},{4,0},{8,12},{12,8},{16,20},{20,16},{24,28},{28,24},{1,5},{5... | collective-permute-start | bytes 296 | tf_op jit(solution)/shard_map/ppermute | solution.py:796
  86.2 26.0 %collective-permute-start.16 = (bf16[256,1664]{1,0:T(8,128)(2,1)}, bf16[256,1664]{1,0:T(8,128)(2,1)}, u32[]{:S(2)}, u32[]{:S(2)}) collective-permute-start(bf16[256,1664]{1,0:T(8,128)(2,1)} %collective-permute-done.15.refs_11_), channel_id=1, source_target_pairs={{1,0},{2,1},{3,2},{5,4},{6,5},{7,6},{9,8},{10,9},{11,10},{13,12},{... | collective-permute-start | bytes 2555912 | tf_op jit(solution)/shard_map/ppermute | solution.py:721
  90.8 2.9 collective-permute-start.6
  93.6 2.8 collective-permute-start.7
  96.9 31.8 %collective-permute-start.10 = (bf16[256,1536]{1,0:T(8,128)(2,1)}, bf16[256,1536]{1,0:T(8,128)(2,1)}, u32[]{:S(2)}, u32[]{:S(2)}) collective-permute-start(bf16[256,1536]{1,0:T(8,128)(2,1)} %collective-permute-done.4.refs_4_), channel_id=1, source_target_pairs={{1,0},{2,1},{3,2},{5,4},{6,5},{7,6},{9,8},{10,9},{11,10},{13,12},{... | collective-permute-start | bytes 2359304 | tf_op jit(solution)/shard_map/ppermute | solution.py:721
  98.9 33.9 %collective-permute-start.8 = (bf16[256,1536]{1,0:T(8,128)(2,1)}, bf16[256,1536]{1,0:T(8,128)(2,1)}, u32[]{:S(2)}, u32[]{:S(2)}) collective-permute-start(bf16[256,1536]{1,0:T(8,128)(2,1)} %collective-permute-done.3.refs_1_), channel_id=1, source_target_pairs={{0,1},{1,2},{2,3},{4,5},{5,6},{6,7},{8,9},{9,10},{10,11},{12,13},{... | collective-permute-start | bytes 2359304 | tf_op jit(solution)/shard_map/ppermute | solution.py:717
  109.9 35.1 %collective-permute-start.14 = (bf16[256,1664]{1,0:T(8,128)(2,1)}, bf16[256,1664]{1,0:T(8,128)(2,1)}, u32[]{:S(2)}, u32[]{:S(2)}) collective-permute-start(bf16[256,1664]{1,0:T(8,128)(2,1)} %collective-permute-done.13.refs_9_), channel_id=1, source_target_pairs={{0,1},{1,2},{2,3},{4,5},{5,6},{6,7},{8,9},{9,10},{10,11},{12,13},{... | collective-permute-start | bytes 2555912 | tf_op jit(solution)/shard_map/ppermute | solution.py:717
  112.2 34.8 %collective-permute-start.17 = (bf16[256,1664]{1,0:T(8,128)(2,1)}, bf16[256,1664]{1,0:T(8,128)(2,1)}, u32[]{:S(2)}, u32[]{:S(2)}) collective-permute-start(bf16[256,1664]{1,0:T(8,128)(2,1)} %collective-permute-done.16.refs_12_), channel_id=1, source_target_pairs={{1,0},{2,1},{3,2},{5,4},{6,5},{7,6},{9,8},{10,9},{11,10},{13,12},{... | collective-permute-start | bytes 2555912 | tf_op jit(solution)/shard_map/ppermute | solution.py:721
  128.7 35.1 %collective-permute-start.11 = (bf16[256,1536]{1,0:T(8,128)(2,1)}, bf16[256,1536]{1,0:T(8,128)(2,1)}, u32[]{:S(2)}, u32[]{:S(2)}) collective-permute-start(bf16[256,1536]{1,0:T(8,128)(2,1)} %collective-permute-done.10.refs_5_), channel_id=1, source_target_pairs={{1,0},{2,1},{3,2},{5,4},{6,5},{7,6},{9,8},{10,9},{11,10},{13,12},{... | collective-permute-start | bytes 2359304 | tf_op jit(solution)/shard_map/ppermute | solution.py:721
  132.7 31.1 %collective-permute-start.9 = (bf16[256,1536]{1,0:T(8,128)(2,1)}, bf16[256,1536]{1,0:T(8,128)(2,1)}, u32[]{:S(2)}, u32[]{:S(2)}) collective-permute-start(bf16[256,1536]{1,0:T(8,128)(2,1)} %collective-permute-done.8.refs_2_), channel_id=1, source_target_pairs={{0,1},{1,2},{2,3},{4,5},{5,6},{6,7},{8,9},{9,10},{10,11},{12,13},{... | collective-permute-start | bytes 2359304 | tf_op jit(solution)/shard_map/ppermute | solution.py:717
  136.2 69.1 %copy-start.25 = (s32[4]{0:T(128)}, s32[4]{0:T(128)S(1)}, u32[]{:S(2)}) copy-start(s32[4]{0:T(128)S(1)} %get-tuple-element.318.order_ref) | copy-start | bytes 52
  205.4 70.3 %all-to-all-start = ((bf16[4,256,1536]{2,1,0:T(8,128)(2,1)}), bf16[4,256,1536]{2,1,0:T(8,128)(2,1)}, u32[]{:S(2)}, u32[]{:S(2)}) async-start(bf16[4,256,1536]{2,1,0:T(8,128)(2,1)} %get-tuple-element.131), calls=%async_computation | async-start | bytes 6291456 | tf_op jit(solution)/shard_map/all_to_all | solution.py:928
  229.2 17.7 %collective-permute-start.18 = (bf16[3,5,192,512]{3,2,1,0:T(8,128)(2,1)}, bf16[3,5,192,512]{3,2,1,0:T(8,128)(2,1)}, u32[]{:S(2)}, u32[]{:S(2)}) collective-permute-start(bf16[3,5,192,512]{3,2,1,0:T(8,128)(2,1)} %get-tuple-element.136), channel_id=1, source_target_pairs={{0,4},{4,0},{8,12},{12,8},{16,20},{20,16},{24,28},{28,24},{1,5},{5... | collective-permute-start | bytes 8847368 | tf_op jit(solution)/shard_map/ppermute | solution.py:743
  234.0 12.9 %collective-permute-start.19 = (bf16[3,5,192,512]{3,2,1,0:T(8,128)(2,1)}, bf16[3,5,192,512]{3,2,1,0:T(8,128)(2,1)}, u32[]{:S(2)}, u32[]{:S(2)}) collective-permute-start(bf16[3,5,192,512]{3,2,1,0:T(8,128)(2,1)} %get-tuple-element.137), channel_id=1, source_target_pairs={{0,4},{4,0},{8,12},{12,8},{16,20},{20,16},{24,28},{28,24},{1,5},{5... | collective-permute-start | bytes 8847368 | tf_op jit(solution)/shard_map/ppermute | solution.py:743
  234.1 13.7 %collective-permute-start.20 = (bf16[3,5,192,512]{3,2,1,0:T(8,128)(2,1)}, bf16[3,5,192,512]{3,2,1,0:T(8,128)(2,1)}, u32[]{:S(2)}, u32[]{:S(2)}) collective-permute-start(bf16[3,5,192,512]{3,2,1,0:T(8,128)(2,1)} %get-tuple-element.138), channel_id=1, source_target_pairs={{0,4},{4,0},{8,12},{12,8},{16,20},{20,16},{24,28},{28,24},{1,5},{5... | collective-permute-start | bytes 8847368 | tf_op jit(solution)/shard_map/ppermute | solution.py:743
  234.5 17.5 %collective-permute-start.21 = (bf16[3,5,192,512]{3,2,1,0:T(8,128)(2,1)}, bf16[3,5,192,512]{3,2,1,0:T(8,128)(2,1)}, u32[]{:S(2)}, u32[]{:S(2)}) collective-permute-start(bf16[3,5,192,512]{3,2,1,0:T(8,128)(2,1)} %get-tuple-element.139), channel_id=1, source_target_pairs={{0,4},{4,0},{8,12},{12,8},{16,20},{20,16},{24,28},{28,24},{1,5},{5... | collective-permute-start | bytes 8847368 | tf_op jit(solution)/shard_map/ppermute | solution.py:743
  275.6 72.2 %collective-permute-start.23 = (bf16[2,3,5,192,256]{4,3,2,1,0:T(8,128)(2,1)}, bf16[2,3,5,192,256]{4,3,2,1,0:T(8,128)(2,1)}, u32[]{:S(2)}, u32[]{:S(2)}) collective-permute-start(bf16[2,3,5,192,256]{4,3,2,1,0:T(8,128)(2,1)} %get-tuple-element.145), channel_id=1, source_target_pairs={{0,8},{4,12},{8,0},{12,4},{16,24},{20,28},{24,16},{28,20},{1,9},{5... | collective-permute-start | bytes 8847368 | tf_op jit(solution)/shard_map/ppermute | solution.py:743
  285.2 63.5 %collective-permute-start.24 = (bf16[2,3,5,192,256]{4,3,2,1,0:T(8,128)(2,1)}, bf16[2,3,5,192,256]{4,3,2,1,0:T(8,128)(2,1)}, u32[]{:S(2)}, u32[]{:S(2)}) collective-permute-start(bf16[2,3,5,192,256]{4,3,2,1,0:T(8,128)(2,1)} %get-tuple-element.146), channel_id=1, source_target_pairs={{0,16},{4,20},{8,24},{12,28},{16,0},{20,4},{24,8},{28,12},{1,17},{... | collective-permute-start | bytes 8847368 | tf_op jit(solution)/shard_map/ppermute | solution.py:743
  285.2 54.9 %all-to-all-start.1 = ((bf16[4,256,768]{2,1,0:T(8,128)(2,1)}), bf16[4,256,768]{2,1,0:T(8,128)(2,1)}, u32[]{:S(2)}, u32[]{:S(2)}) async-start(bf16[4,256,768]{2,1,0:T(8,128)(2,1)} %get-tuple-element.147), calls=%async_computation.1 | async-start | bytes 3145728 | tf_op jit(solution)/shard_map/all_to_all | solution.py:937
  321.4 18.8 %collective-permute-start.22 = (bf16[2048,128]{1,0:T(8,128)(2,1)}, bf16[2048,128]{1,0:T(8,128)(2,1)S(1)}, u32[]{:S(2)}, u32[]{:S(2)}) collective-permute-start(bf16[2048,128]{1,0:T(8,128)(2,1)} %get-tuple-element.144), channel_id=1, source_target_pairs={{1,0},{2,1},{3,2},{5,4},{6,5},{7,6},{9,8},{10,9},{11,10},{13,12},{... | collective-permute-start | bytes 1572872 | tf_op jit(solution)/shard_map/ppermute | solution.py:721
  323.3 28.6 %copy-start.20 = (f32[256,1]{1,0:T(8,128)S(1)}, f32[256,1]{1,0:T(8,128)}, u32[]{:S(2)}) copy-start(f32[256,1]{1,0:T(8,128)} %get-tuple-element.166) | copy-start | bytes 3076
  323.3 29.3 %copy-start.17 = (bf16[2048,128]{1,0:T(8,128)(2,1)S(1)}, bf16[2048,128]{1,0:T(8,128)(2,1)}, u32[]{:S(2)}) copy-start(bf16[2048,128]{1,0:T(8,128)(2,1)} %get-tuple-element.154) | copy-start | bytes 1572868
  348.7 12.8 %collective-permute-start.26 = (bf16[4,192,3072]{2,1,0:T(8,128)(2,1)}, bf16[4,192,3072]{2,1,0:T(8,128)(2,1)}, u32[]{:S(2)}, u32[]{:S(2)}) collective-permute-start(bf16[4,192,3072]{2,1,0:T(8,128)(2,1)} %get-tuple-element.156), channel_id=1, source_target_pairs={{0,4},{4,0},{8,12},{12,8},{16,20},{20,16},{24,28},{28,24},{1,5},{5... | collective-permute-start | bytes 14155784 | tf_op jit(solution)/shard_map/ppermute | solution.py:743
  352.7 17.0 %collective-permute-start.25 = (bf16[2048,128]{1,0:T(8,128)(2,1)S(1)}, bf16[2048,128]{1,0:T(8,128)(2,1)S(1)}, u32[]{:S(2)}, u32[]{:S(2)}) collective-permute-start(bf16[2048,128]{1,0:T(8,128)(2,1)S(1)} %add_convert_fusion.11), channel_id=1, source_target_pairs={{1,0},{2,1},{3,2},{5,4},{6,5},{7,6},{9,8},{10,9},{11,10},{13,12},{... | collective-permute-start | bytes 1572872 | tf_op jit(solution)/shard_map/ppermute | solution.py:721
  369.9 14.7 %collective-permute-start.27 = (bf16[2048,128]{1,0:T(8,128)(2,1)S(1)}, bf16[2048,128]{1,0:T(8,128)(2,1)S(1)}, u32[]{:S(2)}, u32[]{:S(2)}) collective-permute-start(bf16[2048,128]{1,0:T(8,128)(2,1)S(1)} %add_convert_fusion.10), channel_id=1, source_target_pairs={{1,0},{2,1},{3,2},{5,4},{6,5},{7,6},{9,8},{10,9},{11,10},{13,12},{... | collective-permute-start | bytes 1572872 | tf_op jit(solution)/shard_map/ppermute | solution.py:721
  376.1 27.2 %collective-permute-start.29 = (bf16[2,192,1536]{2,1,0:T(8,128)(2,1)}, bf16[2,192,1536]{2,1,0:T(8,128)(2,1)}, u32[]{:S(2)}, u32[]{:S(2)}) collective-permute-start(bf16[2,192,1536]{2,1,0:T(8,128)(2,1)} %get-tuple-element.272), channel_id=1, source_target_pairs={{0,16},{4,20},{8,24},{12,28},{16,0},{20,4},{24,8},{28,12},{1,17},{... | collective-permute-start | bytes 3538952 | tf_op jit(solution)/shard_map/ppermute | solution.py:743
  376.1 10.7 %copy-start.13 = (bf16[2,3,5,192,256]{4,3,2,1,0:T(8,128)(2,1)S(1)}, bf16[2,3,5,192,256]{4,3,2,1,0:T(8,128)(2,1)}, u32[]{:S(2)}) copy-start(bf16[2,3,5,192,256]{4,3,2,1,0:T(8,128)(2,1)} %get-tuple-element.179) | copy-start | bytes 8847364
  377.7 26.4 %collective-permute-start.28 = (bf16[2,192,1536]{2,1,0:T(8,128)(2,1)}, bf16[2,192,1536]{2,1,0:T(8,128)(2,1)}, u32[]{:S(2)}, u32[]{:S(2)}) collective-permute-start(bf16[2,192,1536]{2,1,0:T(8,128)(2,1)} %get-tuple-element.274), channel_id=1, source_target_pairs={{0,8},{4,12},{8,0},{12,4},{16,24},{20,28},{24,16},{28,20},{1,9},{5... | collective-permute-start | bytes 3538952 | tf_op jit(solution)/shard_map/ppermute | solution.py:743
  384.6 35.1 %collective-permute-start.40 = (f32[1,24]{1,0:T(1,128)S(1)}, f32[1,24]{1,0:T(1,128)S(1)}, u32[]{:S(2)}, u32[]{:S(2)}) collective-permute-start(f32[1,24]{1,0:T(1,128)S(1)} %copy-done.28), channel_id=1, source_target_pairs={{0,1},{1,0},{2,3},{3,2},{4,5},{5,4},{6,7},{7,6},{8,9},{9,8},{10,11... | collective-permute-start | bytes 296 | tf_op jit(solution)/shard_map/ppermute | solution.py:796
  391.4 57.0 %collective-permute-start.33 = (bf16[3,5,192,256]{3,2,1,0:T(8,128)(2,1)}, bf16[3,5,192,256]{3,2,1,0:T(8,128)(2,1)}, u32[]{:S(2)}, u32[]{:S(2)}) collective-permute-start(bf16[3,5,192,256]{3,2,1,0:T(8,128)(2,1)} %get-tuple-element.268), channel_id=1, source_target_pairs={{0,8},{4,12},{8,0},{12,4},{16,24},{20,28},{24,16},{28,20},{1,9},{5... | collective-permute-start | bytes 4423688 | tf_op jit(solution)/shard_map/ppermute | solution.py:743
  391.4 20.1 %slice-start = ((s8[4718592]{0:T(1024)(128)(4,1)}), s8[524288]{0:T(1024)(128)(4,1)S(1)}, s32[]{:S(2)}) async-start(s8[4718592]{0:T(1024)(128)(4,1)} %bitcast.119), calls=%async_computation.3 | async-start | bytes 1048576
  396.1 52.3 %collective-permute-start.32 = (bf16[3,5,192,256]{3,2,1,0:T(8,128)(2,1)}, bf16[3,5,192,256]{3,2,1,0:T(8,128)(2,1)}, u32[]{:S(2)}, u32[]{:S(2)}) collective-permute-start(bf16[3,5,192,256]{3,2,1,0:T(8,128)(2,1)} %get-tuple-element.269), channel_id=1, source_target_pairs={{0,16},{4,20},{8,24},{12,28},{16,0},{20,4},{24,8},{28,12},{1,17},{... | collective-permute-start | bytes 4423688 | tf_op jit(solution)/shard_map/ppermute | solution.py:743
  398.8 12.6 %slice-start.1 = ((s8[4718592]{0:T(1024)(128)(4,1)}), s8[4194304]{0:T(1024)(128)(4,1)S(1)}, s32[]{:S(2)}) async-start(s8[4718592]{0:T(1024)(128)(4,1)} %bitcast.119), calls=%async_computation.4 | async-start | bytes 8388608
  406.7 41.7 %collective-permute-start.31 = (bf16[192,1536]{1,0:T(8,128)(2,1)}, bf16[192,1536]{1,0:T(8,128)(2,1)}, u32[]{:S(2)}, u32[]{:S(2)}) collective-permute-start(bf16[192,1536]{1,0:T(8,128)(2,1)} %get-tuple-element.286), channel_id=1, source_target_pairs={{0,8},{4,12},{8,0},{12,4},{16,24},{20,28},{24,16},{28,20},{1,9},{5... | collective-permute-start | bytes 1769480 | tf_op jit(solution)/shard_map/ppermute | solution.py:743
  410.0 38.4 %collective-permute-start.30 = (bf16[192,1536]{1,0:T(8,128)(2,1)}, bf16[192,1536]{1,0:T(8,128)(2,1)}, u32[]{:S(2)}, u32[]{:S(2)}) collective-permute-start(bf16[192,1536]{1,0:T(8,128)(2,1)} %get-tuple-element.287), channel_id=1, source_target_pairs={{0,16},{4,20},{8,24},{12,28},{16,0},{20,4},{24,8},{28,12},{1,17},{... | collective-permute-start | bytes 1769480 | tf_op jit(solution)/shard_map/ppermute | solution.py:743
  414.4 36.4 %copy-start.4 = (f32[256,1536]{1,0:T(8,128)S(1)}, f32[256,1536]{1,0:T(8,128)}, u32[]{:S(2)}) copy-start(f32[256,1536]{1,0:T(8,128)} %get-tuple-element.315) | copy-start | bytes 4718596
  419.7 34.1 %collective-permute-start.41 = (f32[1,24]{1,0:T(1,128)S(1)}, f32[1,24]{1,0:T(1,128)S(1)}, u32[]{:S(2)}, u32[]{:S(2)}) collective-permute-start(f32[1,24]{1,0:T(1,128)S(1)} %max.21), channel_id=1, source_target_pairs={{0,2},{1,3},{2,0},{3,1},{4,6},{5,7},{6,4},{7,5},{8,10},{9,11},{10,... | collective-permute-start | bytes 296 | tf_op jit(solution)/shard_map/ppermute | solution.py:796
  448.4 17.3 %collective-permute-start.37 = (bf16[4,192,1152]{2,1,0:T(8,128)(2,1)}, bf16[4,192,1152]{2,1,0:T(8,128)(2,1)}, u32[]{:S(2)}, u32[]{:S(2)}) collective-permute-start(bf16[4,192,1152]{2,1,0:T(8,128)(2,1)} %get-tuple-element.188), channel_id=1, source_target_pairs={{0,4},{4,0},{8,12},{12,8},{16,20},{20,16},{24,28},{28,24},{1,5},{5... | collective-permute-start | bytes 5308424 | tf_op jit(solution)/shard_map/ppermute | solution.py:743
  453.7 51.7 %all-to-all-start.2 = ((bf16[4,256,768]{2,1,0:T(8,128)(2,1)}), bf16[4,256,768]{2,1,0:T(8,128)(2,1)}, u32[]{:S(2)}, u32[]{:S(2)}) async-start(bf16[4,256,768]{2,1,0:T(8,128)(2,1)} %get-tuple-element.197), calls=%async_computation.2 | async-start | bytes 3145728 | tf_op jit(solution)/shard_map/all_to_all | solution.py:964
  467.2 13.5 %collective-permute-start.39 = (bf16[2,192,640]{2,1,0:T(8,128)(2,1)S(1)}, bf16[2,192,640]{2,1,0:T(8,128)(2,1)}, u32[]{:S(2)}, u32[]{:S(2)}) collective-permute-start(bf16[2,192,640]{2,1,0:T(8,128)(2,1)S(1)} %get-tuple-element.290), channel_id=1, source_target_pairs={{0,16},{4,20},{8,24},{12,28},{16,0},{20,4},{24,8},{28,12},{1,17},{... | collective-permute-start | bytes 1474568 | tf_op jit(solution)/shard_map/ppermute | solution.py:743
  470.2 10.6 %collective-permute-start.38 = (bf16[2,192,512]{2,1,0:T(8,128)(2,1)S(1)}, bf16[2,192,512]{2,1,0:T(8,128)(2,1)S(1)}, u32[]{:S(2)}, u32[]{:S(2)}) collective-permute-start(bf16[2,192,512]{2,1,0:T(8,128)(2,1)S(1)} %get-tuple-element.291), channel_id=1, source_target_pairs={{0,8},{4,12},{8,0},{12,4},{16,24},{20,28},{24,16},{28,20},{1,9},{5... | collective-permute-start | bytes 1179656 | tf_op jit(solution)/shard_map/ppermute | solution.py:743
  471.3 42.0 %collective-permute-start.34 = (bf16[48,3072]{1,0:T(8,128)(2,1)}, bf16[48,3072]{1,0:T(8,128)(2,1)}, u32[]{:S(2)}, u32[]{:S(2)}) collective-permute-start(bf16[48,3072]{1,0:T(8,128)(2,1)} %get-tuple-element.295), channel_id=1, source_target_pairs={{0,1},{1,2},{2,3},{3,0},{4,5},{5,6},{6,7},{7,4},{8,9},{9,10},{10,1... | collective-permute-start | bytes 884744 | tf_op jit(solution)/shard_map/ppermute | solution.py:783
  471.9 46.1 %collective-permute-start.35 = (bf16[48,3072]{1,0:T(8,128)(2,1)}, bf16[48,3072]{1,0:T(8,128)(2,1)}, u32[]{:S(2)}, u32[]{:S(2)}) collective-permute-start(bf16[48,3072]{1,0:T(8,128)(2,1)} %get-tuple-element.294), channel_id=1, source_target_pairs={{0,2},{1,3},{2,0},{3,1},{4,6},{5,7},{6,4},{7,5},{8,10},{9,11},{10,... | collective-permute-start | bytes 884744 | tf_op jit(solution)/shard_map/ppermute | solution.py:783
  472.8 46.3 %collective-permute-start.36 = (bf16[48,3072]{1,0:T(8,128)(2,1)}, bf16[48,3072]{1,0:T(8,128)(2,1)}, u32[]{:S(2)}, u32[]{:S(2)}) collective-permute-start(bf16[48,3072]{1,0:T(8,128)(2,1)} %get-tuple-element.293), channel_id=1, source_target_pairs={{0,3},{1,0},{2,1},{3,2},{4,7},{5,4},{6,5},{7,6},{8,11},{9,8},{10,9... | collective-permute-start | bytes 884744 | tf_op jit(solution)/shard_map/ppermute | solution.py:783
  506.6 6.7 %collective-permute-start.43 = (bf16[192,640]{1,0:T(8,128)(2,1)S(1)}, bf16[192,640]{1,0:T(8,128)(2,1)S(1)}, u32[]{:S(2)}, u32[]{:S(2)}) collective-permute-start(bf16[192,640]{1,0:T(8,128)(2,1)S(1)} %get-tuple-element.298), channel_id=1, source_target_pairs={{0,8},{4,12},{8,0},{12,4},{16,24},{20,28},{24,16},{28,20},{1,9},{5... | collective-permute-start | bytes 737288 | tf_op jit(solution)/shard_map/ppermute | solution.py:743
  506.8 5.4 collective-permute-start.42
  522.4 17.0 %collective-permute-start.44 = (bf16[48,1152]{0,1:T(8,128)(2,1)}, bf16[48,1152]{0,1:T(8,128)(2,1)S(1)}, u32[]{:S(2)}, u32[]{:S(2)}) collective-permute-start(bf16[48,1152]{0,1:T(8,128)(2,1)} %bitcast.45), channel_id=1, source_target_pairs={{0,1},{1,2},{2,3},{3,0},{4,5},{5,6},{6,7},{7,4},{8,9},{9,10},{10,1... | collective-permute-start | bytes 331784 | tf_op jit(solution)/shard_map/ppermute | solution.py:783
  523.3 24.2 %collective-permute-start.45 = (bf16[48,1152]{0,1:T(8,128)(2,1)}, bf16[48,1152]{0,1:T(8,128)(2,1)S(1)}, u32[]{:S(2)}, u32[]{:S(2)}) collective-permute-start(bf16[48,1152]{0,1:T(8,128)(2,1)} %bitcast.46), channel_id=1, source_target_pairs={{0,2},{1,3},{2,0},{3,1},{4,6},{5,7},{6,4},{7,5},{8,10},{9,11},{10,... | collective-permute-start | bytes 331784 | tf_op jit(solution)/shard_map/ppermute | solution.py:783
  526.2 24.9 %collective-permute-start.46 = (bf16[48,1152]{0,1:T(8,128)(2,1)}, bf16[48,1152]{0,1:T(8,128)(2,1)S(1)}, u32[]{:S(2)}, u32[]{:S(2)}) collective-permute-start(bf16[48,1152]{0,1:T(8,128)(2,1)} %bitcast.47), channel_id=1, source_target_pairs={{0,3},{1,0},{2,1},{3,2},{4,7},{5,4},{6,5},{7,6},{8,11},{9,8},{10,9... | collective-permute-start | bytes 331784 | tf_op jit(solution)/shard_map/ppermute | solution.py:783
  (17 other events, 62.6 us)

commit v6 on v4

--- a/solution.py
+++ b/solution.py
@@ -986,16 +986,14 @@
         (router_part, second_gain_part[None], first_gain_part[None]),
     )
     keep, send, wide, expert_sums = lax.optimization_barrier((keep, send, wide, expert_sums))
-    rest = start_dense((keep, flip(send, 1, dp_size)))
-    rest = step_spread(rest, 0, dp_size, dp_place)
-    wide_parts, rest, expert_sums, mix_two = lax.optimization_barrier(
-        (pass_line(wide, place, size), rest, expert_sums, mix_two)
-    )
     for stage in range(2, stages):
         expert_sums = step_spread(expert_sums, stage, dp_size, dp_place)
     expert_sums = [
         jnp.concatenate([a[w].astype(F32) + b[w].astype(F32) for a, b in expert_sums], axis=-1) for w in range(3)
     ]
+    rest = start_dense((keep, flip(send, 1, dp_size)))
+    rest = step_spread(rest, 0, dp_size, dp_place)
+    wide_parts, rest = lax.optimization_barrier((pass_line(wide, place, size), rest))
     for stage in range(1, stages):
         rest = step_spread(rest, stage, dp_size, dp_place)
     rest_parts = lax.optimization_barrier(pass_line(rest, place, size))

time: 543 us -> 527 us (0.971)
  other arithmetic: 54 us -> 44.8 us
  starting transfers between devices: 127 us -> 118 us
    ppermute x9, waiting for transfers between devices: 26.7 us -> 37 us  [line_down(): return lax.ppermute(value, 'expert', [(i + 1, i) for i in range(size - 1)])]
    ppermute x18, waiting for transfers between devices: 38 us -> 48.3 us  [flip(): return lax.ppermute(value, 'dp', [(i, i ^ bit) for i in range(size)])]
    ppermute x9, starting transfers between devices: 56 us -> 46.3 us  [line_down(): return lax.ppermute(value, 'expert', [(i + 1, i) for i in range(size - 1)])]
    ppermute x6, waiting for transfers between devices: 31.7 us -> 22.1 us  [pass_line(): lax.ppermute(part, 'expert', [(i, (i + k) % size) for i in range(size)])]
    convert_element_type x16, other arithmetic: 25.5 us -> 18 us  [add_low(): return total.astype(BF16)]
  transfers between devices with their start and end apart: 50 -> 50, of which waited for: 21 -> 26; matrix products, arithmetic and copies ran while one was open for 15% -> 14% of each run, Pallas kernels for 19% -> 20%
where the time goes in v6:
time: 527 us; the launch traced here: 520 us
  waiting for transfers between devices  165 us (31%)
  Pallas kernels  149 us (28%)
  starting transfers between devices  118 us (22%)
  other arithmetic  44.8 us (9%)
  local copies, waits for them, and re-layouts  25.5 us (5%)
  matrix products  15.5 us (3%)
    ppermute x18, waiting for transfers between devices, flip(): return lax.ppermute(value, 'dp', [(i, i ^ bit) for i in range(size)])  48.3 us
    ppermute x9, waiting for transfers between devices, line_up(): return lax.ppermute(value, 'expert', [(i, i + 1) for i in range(size - 1)])  46.3 us
    ppermute x9, starting transfers between devices, line_down(): return lax.ppermute(value, 'expert', [(i + 1, i) for i in range(size - 1)])  46.3 us
    pallas_call x1, Pallas kernels, run_experts(): pl.pallas_call(functools.partial(expert_kernel, blocks, slot_rows, local_...  41.5 us
    pallas_call x2, Pallas kernels, run_expert_grads(): pl.pallas_call(functools.partial(expert_keep_kernel, owners.bit_length()...  37.9 us
    ppermute x9, waiting for transfers between devices, line_down(): return lax.ppermute(value, 'expert', [(i + 1, i) for i in range(size - 1)])  37 us
    ppermute x6, waiting for transfers between devices, pass_line(): lax.ppermute(part, 'expert', [(i, (i + k) % size) for i in range(size)])  22.1 us
    convert_element_type x16, other arithmetic, add_low(): return total.astype(BF16)  18 us
  transfers between devices with their start and end apart: 50, of which 26 were waited for; matrix products, arithmetic and copies ran while one was open for 14% of the time, Pallas kernels for 20%

profile of v6, /device:TPU:24, one launch (start us, length us, event | category | flops | bytes accessed | tf_op | source)
XLA Modules:
  0.0 520.0 jit_solution(6973634588976180445)
XLA Ops:
  4.9 4.2 front.1
  10.4 14.6 %collective-permute-done.refs_1_.refs_5_ = bf16[2064,128]{1,0:T(8,128)(2,1)S(1)} collective-permute-done((bf16[2064,128]{1,0:T(8,128)(2,1)}, bf16[2064,128]{1,0:T(8,128)(2,1)S(1)}, u32[]{:S(2)}, u32[]{:S(2)}) %collective-permute-start) | collective-permute-done | bytes 528416 | tf_op jit(solution)/shard_map/ppermute | solution.py:717
  26.3 13.5 %collective-permute-done.1.refs_2_.refs_6_ = bf16[2064,128]{1,0:T(8,128)(2,1)S(1)} collective-permute-done((bf16[2064,128]{1,0:T(8,128)(2,1)S(1)}, bf16[2064,128]{1,0:T(8,128)(2,1)S(1)}, u32[]{:S(2)}, u32[]{:S(2)}) %collective-permute-start.1) | collective-permute-done | bytes 528416 | tf_op jit(solution)/shard_map/ppermute | solution.py:717
  41.9 2.6 extend.1.refs_7_
  45.7 6.1 %collective-permute-start.15 = (bf16[256,1664]{1,0:T(8,128)(2,1)}, bf16[256,1664]{1,0:T(8,128)(2,1)}, u32[]{:S(2)}, u32[]{:S(2)}) collective-permute-start(bf16[256,1664]{1,0:T(8,128)(2,1)} %extend.1.refs_7_), channel_id=1, source_target_pairs={{1,0},{2,1},{3,2},{5,4},{6,5},{7,6},{9,8},{10,9},{11,10},{13,12},{... | collective-permute-start | bytes 2555912 | tf_op jit(solution)/shard_map/ppermute | solution.py:721
  51.8 5.6 %queries.1.query_ref = bf16[256,1536]{1,0:T(8,128)(2,1)} custom-call(bf16[256,1536]{1,0:T(8,128)(2,1)} %get-tuple-element.107.normed_ref.refs_1_.refs_0_, bf16[1536,1536]{1,0:T(8,128)(2,1)} %query_ref.1, f32[256,128]{1,0:T(8,128)} %get-tuple-element.285.cos_ref, f32[256,128]{1,0:T(8,128)} %get-tuple-element.284.sin_ref), custom_call_target="tpu_custom_call" | custom-call | flops 5000000 | tf_op jit(solution)/shard_map/queries/pallas_call | solution.py:896
  58.3 12.3 %attend.1 = (bf16[256,1536]{1,0:T(8,128)(2,1)}, f32[4,2,768]{2,1,0:T(2,128)}, f32[4,2,768]{2,1,0:T(2,128)}) custom-call(s32[1]{0:T(128)} %bitcast.place_ref, bf16[256,1536]{1,0:T(8,128)(2,1)} %queries.1.query_ref, bf16[2064,128]{1,0:T(8,128)(2,1)} %get-tuple-element.108.refs_0_.refs_4_, bf16[2064,128]{1,0:T(8,128)(2,1)} %copy-done, ...), custom_call_target="tpu_custom_call" | custom-call | flops 20000000 | tf_op jit(solution)/shard_map/attend/pallas_call | solution.py:217
  70.6 4.1 multiply_reduce_fusion.2
  76.3 5.4 %collective-permute-start.4 = (bf16[256,1536]{1,0:T(8,128)(2,1)S(1)}, bf16[256,1536]{1,0:T(8,128)(2,1)}, u32[]{:S(2)}, u32[]{:S(2)}) collective-permute-start(bf16[256,1536]{1,0:T(8,128)(2,1)S(1)} %multiply_convert_fusion.1.refs_0_), channel_id=1, source_target_pairs={{1,0},{2,1},{3,2},{5,4},{6,5},{7,6},{9,8},{10,9},{11,10},{13,12},{... | collective-permute-start | bytes 2359304 | tf_op jit(solution)/shard_map/ppermute | solution.py:721
  83.2 5.5 %collective-permute-start.16 = (bf16[256,1664]{1,0:T(8,128)(2,1)}, bf16[256,1664]{1,0:T(8,128)(2,1)}, u32[]{:S(2)}, u32[]{:S(2)}) collective-permute-start(bf16[256,1664]{1,0:T(8,128)(2,1)} %collective-permute-done.15.refs_11_), channel_id=1, source_target_pairs={{1,0},{2,1},{3,2},{5,4},{6,5},{7,6},{9,8},{10,9},{11,10},{13,12},{... | collective-permute-start | bytes 2555912 | tf_op jit(solution)/shard_map/ppermute | solution.py:721
  88.7 4.9 collective-permute-start.6
  95.2 2.1 collective-permute-start.7
  99.3 4.9 collective-permute-start.10
  105.5 10.2 %collective-permute-done.13.refs_9_ = bf16[256,1664]{1,0:T(8,128)(2,1)} collective-permute-done((bf16[256,1664]{1,0:T(8,128)(2,1)}, bf16[256,1664]{1,0:T(8,128)(2,1)}, u32[]{:S(2)}, u32[]{:S(2)}) %collective-permute-start.13) | collective-permute-done | bytes 852000 | tf_op jit(solution)/shard_map/ppermute | solution.py:717
  117.2 5.3 %collective-permute-start.17 = (bf16[256,1664]{1,0:T(8,128)(2,1)}, bf16[256,1664]{1,0:T(8,128)(2,1)}, u32[]{:S(2)}, u32[]{:S(2)}) collective-permute-start(bf16[256,1664]{1,0:T(8,128)(2,1)} %collective-permute-done.16.refs_12_), channel_id=1, source_target_pairs={{1,0},{2,1},{3,2},{5,4},{6,5},{7,6},{9,8},{10,9},{11,10},{13,12},{... | collective-permute-start | bytes 2555912 | tf_op jit(solution)/shard_map/ppermute | solution.py:721
  122.5 11.5 %collective-permute-done.10.refs_5_ = bf16[256,1536]{1,0:T(8,128)(2,1)} collective-permute-done((bf16[256,1536]{1,0:T(8,128)(2,1)}, bf16[256,1536]{1,0:T(8,128)(2,1)}, u32[]{:S(2)}, u32[]{:S(2)}) %collective-permute-start.10) | collective-permute-done | bytes 786464 | tf_op jit(solution)/shard_map/ppermute | solution.py:721
  134.0 5.3 %collective-permute-start.11 = (bf16[256,1536]{1,0:T(8,128)(2,1)}, bf16[256,1536]{1,0:T(8,128)(2,1)}, u32[]{:S(2)}, u32[]{:S(2)}) collective-permute-start(bf16[256,1536]{1,0:T(8,128)(2,1)} %collective-permute-done.10.refs_5_), channel_id=1, source_target_pairs={{1,0},{2,1},{3,2},{5,4},{6,5},{7,6},{9,8},{10,9},{11,10},{13,12},{... | collective-permute-start | bytes 2359304 | tf_op jit(solution)/shard_map/ppermute | solution.py:721
  142.7 8.1 %collective-permute-done.14.refs_10_ = bf16[256,1664]{1,0:T(8,128)(2,1)} collective-permute-done((bf16[256,1664]{1,0:T(8,128)(2,1)}, bf16[256,1664]{1,0:T(8,128)(2,1)}, u32[]{:S(2)}, u32[]{:S(2)}) %collective-permute-start.14) | collective-permute-done | bytes 852000 | tf_op jit(solution)/shard_map/ppermute | solution.py:717
  152.3 13.0 %collective-permute-done.11.refs_6_ = bf16[256,1536]{1,0:T(8,128)(2,1)} collective-permute-done((bf16[256,1536]{1,0:T(8,128)(2,1)}, bf16[256,1536]{1,0:T(8,128)(2,1)}, u32[]{:S(2)}, u32[]{:S(2)}) %collective-permute-start.11) | collective-permute-done | bytes 786464 | tf_op jit(solution)/shard_map/ppermute | solution.py:721
  165.3 41.5 %experts.1 = (bf16[5,512,1536]{2,1,0:T(8,128)(2,1)}, bf16[5,512,1536]{2,1,0:T(8,128)(2,1)}, bf16[5,512,512]{2,1,0:T(8,128)(2,1)}, bf16[5,512,512]{2,1,0:T(8,128)...) custom-call(s32[9]{0:T(128)} %pad_add_fusion.place_ref, ...), custom_call_target="tpu_custom_call" | custom-call | flops 45000000 | tf_op jit(solution)/shard_map/experts/pallas_call | solution.py:483
  206.8 9.5 %all-to-all-start = ((bf16[4,256,1536]{2,1,0:T(8,128)(2,1)}), bf16[4,256,1536]{2,1,0:T(8,128)(2,1)}, u32[]{:S(2)}, u32[]{:S(2)}) async-start(bf16[4,256,1536]{2,1,0:T(8,128)(2,1)} %get-tuple-element.117), calls=%async_computation | async-start | bytes 6291456 | tf_op jit(solution)/shard_map/all_to_all | solution.py:928
  216.3 16.8 %expert_send.1 = (bf16[3,5,192,512]{3,2,1,0:T(8,128)(2,1)}, bf16[3,5,192,512]{3,2,1,0:T(8,128)(2,1)}, bf16[3,5,192,512]{3,2,1,0:T(8,128)(2,1)}, bf16[3,5,192,512]{3,2,1,0:T(8,128)(2,1)}) custom-call(s32[1]{0:T(128)} %bitcast.7.place_ref, bf16[5,512,1536]{2,1,0:T(8,128)(2,1)} %get-tuple-element.118.xs_ref, bf16[5,512,1536]{2,1,0:T(8,128)(2,1)} %get-tuple-element.119.cs_ref, ...), custom_call_target="tpu_custom_call" | custom-call | flops 15000000 | tf_op jit(solution)/shard_map/expert_send/pallas_call | solution.py:653
  234.0 12.3 %mixture.1 = (bf16[4,256,768]{2,1,0:T(8,128)(2,1)}, bf16[4,256,768]{2,1,0:T(8,128)(2,1)}) custom-call(s32[4]{0:T(128)} %copy-done.30, bf16[5,1536,512]{2,1,0:T(8,128)(2,1)} %down_ref.3, bf16[5,512,512]{2,1,0:T(8,128)(2,1)} %get-tuple-element.113.hs_ref, bf16[4,640,256]{2,1,0:T(8,128)(2,1)} %get-tuple-element.114.hits_ref), custom_call_target="tpu_custom_call" | custom-call | flops 10000000 | tf_op jit(solution)/shard_map/mixture/pallas_call | solution.py:567
  247.2 4.2 collective-permute-done.21.refs_3_
  251.4 21.1 %expert_keep.1 = (bf16[2,3,5,192,256]{4,3,2,1,0:T(8,128)(2,1)}, bf16[2,3,5,192,256]{4,3,2,1,0:T(8,128)(2,1)}, bf16[2,3,5,192,256]{4,3,2,1,0:T(8,128)(2,1)}, bf16[2,3,5,192,256]{4,3,2,1,0:T(8,128)(2,1)}) custom-call(s32[1]{0:T(128)} %bitcast.7.place_ref, bf16[5,512,1536]{2,1,0:T(8,128)(2,1)} %get-tuple-element.118.xs_ref, ...), custom_call_target="tpu_custom_call" | custom-call | flops 15000000 | tf_op jit(solution)/shard_map/expert_keep/pallas_call | solution.py:653
  272.5 8.6 %all-to-all-done = bf16[4,256,1536]{2,1,0:T(8,128)(2,1)} async-done(((bf16[4,256,1536]{2,1,0:T(8,128)(2,1)}), bf16[4,256,1536]{2,1,0:T(8,128)(2,1)}, u32[]{:S(2)}, u32[]{:S(2)}) %all-to-all-start) | async-done | bytes 3145760 | tf_op jit(solution)/shard_map/all_to_all | solution.py:928
  281.1 1.8 collective-permute-start.23
  282.8 3.6 collective-permute-start.24
  286.5 7.7 %all-to-all-start.1 = ((bf16[4,256,768]{2,1,0:T(8,128)(2,1)}), bf16[4,256,768]{2,1,0:T(8,128)(2,1)}, u32[]{:S(2)}, u32[]{:S(2)}) async-start(bf16[4,256,768]{2,1,0:T(8,128)(2,1)} %get-tuple-element.133), calls=%async_computation.1 | async-start | bytes 3145728 | tf_op jit(solution)/shard_map/all_to_all | solution.py:937
  294.2 2.6 convert_reduce_fusion
  299.6 4.9 convolution_convert_fusion.grad_ref
  304.5 17.6 %attend_back.1 = (bf16[256,1536]{1,0:T(8,128)(2,1)}, bf16[2048,128]{1,0:T(8,128)(2,1)}, bf16[2048,128]{1,0:T(8,128)(2,1)}, bf16[2048,128]{1,0:T(8,128)(2,1)}, bf16[2048,128]{1,0:T(8,128)(2,1)}) custom-call(s32[1]{0:T(128)} %bitcast.place_ref, bf16[256,1536]{1,0:T(8,128)(2,1)} %queries.1.query_ref, bf16[256,1536]{1,0:T(8,128)(2,1)} %get-tuple-element.109.attended_ref.refs_2_, ...), custom_call_target="tpu_custom_call" | custom-call | flops 2000000 | tf_op jit(solution)/shard_map/attend_back/pallas_call | solution.py:304
  322.1 2.5 collective-permute-start.22
  324.7 7.9 %dense_grads.2 = (bf16[4,192,3072]{2,1,0:T(8,128)(2,1)}, bf16[4,192,3072]{2,1,0:T(8,128)(2,1)}) custom-call(s32[1]{0:T(128)} %bitcast.7.place_ref, bf16[256,1536]{1,0:T(8,128)(2,1)} %copy-done.13, bf16[256,1536]{1,0:T(8,128)(2,1)} %get-tuple-element.107.normed_ref.refs_1_.refs_0_, bf16[256,1536]{1,0:T(8,128)(2,1)} %get-tuple-element.109.attended_ref.refs_2_, ...), custom_call_target="tpu_custom_call" | custom-call | flops 4000000 | tf_op jit(solution)/shard_map/dense_grads/pallas_call | solution.py:704
  332.6 2.9 collective-permute-done.22
  335.4 7.1 %collective-permute-done.23 = bf16[2,3,5,192,256]{4,3,2,1,0:T(8,128)(2,1)} collective-permute-done((bf16[2,3,5,192,256]{4,3,2,1,0:T(8,128)(2,1)}, bf16[2,3,5,192,256]{4,3,2,1,0:T(8,128)(2,1)}, u32[]{:S(2)}, u32[]{:S(2)}) %collective-permute-start.23) | collective-permute-done | bytes 2949152 | tf_op jit(solution)/shard_map/ppermute | solution.py:743
  342.5 3.8 collective-permute-done.24
  347.3 6.8 %collective-permute-start.25 = (bf16[2048,128]{1,0:T(8,128)(2,1)S(1)}, bf16[2048,128]{1,0:T(8,128)(2,1)S(1)}, u32[]{:S(2)}, u32[]{:S(2)}) collective-permute-start(bf16[2048,128]{1,0:T(8,128)(2,1)S(1)} %add_convert_fusion.11), channel_id=1, source_target_pairs={{1,0},{2,1},{3,2},{5,4},{6,5},{7,6},{9,8},{10,9},{11,10},{13,12},{... | collective-permute-start | bytes 1572872 | tf_op jit(solution)/shard_map/ppermute | solution.py:721
  354.1 2.6 convert_reduce_fusion.2
  356.7 2.9 fusion.38
  359.6 2.9 fusion.37
  362.5 3.1 collective-permute-done.25
  365.8 4.4 collective-permute-start.27
  370.2 2.1 add_convert_fusion.4
  374.0 2.1 add_convert_fusion.7
  376.4 4.8 collective-permute-done.27.above_ref
  382.1 4.6 fusion.11
  387.0 4.7 fusion.9
  391.6 1.7 collective-permute-start.34
  393.4 2.7 unpack.1
  398.5 2.5 collective-permute-start.28
  401.0 4.2 fusion.6
  407.5 3.4 collective-permute-start.29
  410.9 4.7 dense_grads.3
  415.6 5.2 %all-to-all-start.2 = ((bf16[4,256,768]{2,1,0:T(8,128)(2,1)}), bf16[4,256,768]{2,1,0:T(8,128)(2,1)}, u32[]{:S(2)}, u32[]{:S(2)}) async-start(bf16[4,256,768]{2,1,0:T(8,128)(2,1)} %get-tuple-element.149), calls=%async_computation.2 | async-start | bytes 3145728 | tf_op jit(solution)/shard_map/all_to_all | solution.py:964
  423.0 1.8 collective-permute-start.33
  429.8 17.9 %collective-permute-done.33 = bf16[192,1536]{1,0:T(8,128)(2,1)S(1)} collective-permute-done((bf16[192,1536]{1,0:T(8,128)(2,1)S(1)}, bf16[192,1536]{1,0:T(8,128)(2,1)S(1)}, u32[]{:S(2)}, u32[]{:S(2)}) %collective-permute-start.33) | collective-permute-done | bytes 589856 | tf_op jit(solution)/shard_map/ppermute | solution.py:743
  450.7 2.4 collective-permute-start.36
  454.0 2.3 collective-permute-start.38
  471.4 8.5 %collective-permute-done.40 = bf16[2,192,512]{2,1,0:T(8,128)(2,1)S(1)} collective-permute-done((bf16[2,192,512]{2,1,0:T(8,128)(2,1)S(1)}, bf16[2,192,512]{2,1,0:T(8,128)(2,1)S(1)}, u32[]{:S(2)}, u32[]{:S(2)}) %collective-permute-start.40) | collective-permute-done | bytes 393248 | tf_op jit(solution)/shard_map/ppermute | solution.py:743
  483.5 4.5 collective-permute-done.42
  492.0 2.1 collective-permute-start.46
  495.1 3.1 collective-permute-done.44
  498.2 18.6 %collective-permute-done.45 = bf16[48,1152]{0,1:T(8,128)(2,1)S(1)} collective-permute-done((bf16[48,1152]{0,1:T(8,128)(2,1)S(1)}, bf16[48,1152]{0,1:T(8,128)(2,1)S(1)}, u32[]{:S(2)}, u32[]{:S(2)}) %collective-permute-start.45) | collective-permute-done | bytes 110624 | tf_op jit(solution)/shard_map/ppermute | solution.py:783
  (203 shorter events, 76.0 us)
Async XLA Ops:
  4.9 36.2 %copy-start.29 = (s32[256,8]{0,1:T(8,128)S(1)}, s32[256,8]{0,1:T(8,128)}, u32[]{:S(2)}) copy-start(s32[256,8]{0,1:T(8,128)} %param.31) | copy-start | bytes 24580
  9.2 15.8 %collective-permute-start = (bf16[2064,128]{1,0:T(8,128)(2,1)}, bf16[2064,128]{1,0:T(8,128)(2,1)S(1)}, u32[]{:S(2)}, u32[]{:S(2)}) collective-permute-start(bf16[2064,128]{1,0:T(8,128)(2,1)} %get-tuple-element.108.refs_0_.refs_4_), channel_id=1, source_target_pairs={{0,1},{1,2},{2,3},{4,5},{5,6},{6,7},{8,9},{9,10},{10,11},{12,13},{... | collective-permute-start | bytes 1585160 | tf_op jit(solution)/shard_map/ppermute | solution.py:717
  25.0 32.4 %copy-start = (bf16[2064,128]{1,0:T(8,128)(2,1)}, bf16[2064,128]{1,0:T(8,128)(2,1)S(1)}, u32[]{:S(2)}) copy-start(bf16[2064,128]{1,0:T(8,128)(2,1)S(1)} %collective-permute-done.refs_1_.refs_5_) | copy-start | bytes 1585156
  25.0 14.8 %collective-permute-start.1 = (bf16[2064,128]{1,0:T(8,128)(2,1)S(1)}, bf16[2064,128]{1,0:T(8,128)(2,1)S(1)}, u32[]{:S(2)}, u32[]{:S(2)}) collective-permute-start(bf16[2064,128]{1,0:T(8,128)(2,1)S(1)} %collective-permute-done.refs_1_.refs_5_), channel_id=1, source_target_pairs={{0,1},{1,2},{2,3},{4,5},{5,6},{6,7},{8,9},{9,10},{10,11},{12,13},{... | collective-permute-start | bytes 1585160 | tf_op jit(solution)/shard_map/ppermute | solution.py:717
  39.8 17.7 %copy-start.1 = (bf16[2064,128]{1,0:T(8,128)(2,1)}, bf16[2064,128]{1,0:T(8,128)(2,1)S(1)}, u32[]{:S(2)}) copy-start(bf16[2064,128]{1,0:T(8,128)(2,1)S(1)} %collective-permute-done.1.refs_2_.refs_6_) | copy-start | bytes 1585156
  39.8 17.7 %collective-permute-start.2 = (bf16[2064,128]{1,0:T(8,128)(2,1)S(1)}, bf16[2064,128]{1,0:T(8,128)(2,1)S(1)}, u32[]{:S(2)}, u32[]{:S(2)}) collective-permute-start(bf16[2064,128]{1,0:T(8,128)(2,1)S(1)} %collective-permute-done.1.refs_2_.refs_6_), channel_id=1, source_target_pairs={{0,1},{1,2},{2,3},{4,5},{5,6},{6,7},{8,9},{9,10},{10,11},{12,13},{... | collective-permute-start | bytes 1585160 | tf_op jit(solution)/shard_map/ppermute | solution.py:717
  44.5 37.3 %collective-permute-start.12 = (bf16[256,1664]{1,0:T(8,128)(2,1)}, bf16[256,1664]{1,0:T(8,128)(2,1)}, u32[]{:S(2)}, u32[]{:S(2)}) collective-permute-start(bf16[256,1664]{1,0:T(8,128)(2,1)} %extend.1.refs_7_), channel_id=1, source_target_pairs={{0,1},{1,2},{2,3},{4,5},{5,6},{6,7},{8,9},{9,10},{10,11},{12,13},{... | collective-permute-start | bytes 2555912 | tf_op jit(solution)/shard_map/ppermute | solution.py:717
  45.7 37.5 %collective-permute-start.15 = (bf16[256,1664]{1,0:T(8,128)(2,1)}, bf16[256,1664]{1,0:T(8,128)(2,1)}, u32[]{:S(2)}, u32[]{:S(2)}) collective-permute-start(bf16[256,1664]{1,0:T(8,128)(2,1)} %extend.1.refs_7_), channel_id=1, source_target_pairs={{1,0},{2,1},{3,2},{5,4},{6,5},{7,6},{9,8},{10,9},{11,10},{13,12},{... | collective-permute-start | bytes 2555912 | tf_op jit(solution)/shard_map/ppermute | solution.py:721
  58.3 12.3 %copy-start.3 = (bf16[256,1536]{1,0:T(8,128)(2,1)S(1)}, bf16[256,1536]{1,0:T(8,128)(2,1)}, u32[]{:S(2)}) copy-start(bf16[256,1536]{1,0:T(8,128)(2,1)} %tokens_ref.1) | copy-start | bytes 2359300
  74.7 8.3 %copy-start.28 = (f32[4,2,768]{2,1,0:T(2,128)S(1)}, f32[4,2,768]{2,1,0:T(2,128)}, u32[]{:S(2)}) copy-start(f32[4,2,768]{2,1,0:T(2,128)} %get-tuple-element.110) | copy-start | bytes 73732
  74.7 66.1 %copy-start.27 = (bf16[1536,20]{0,1:T(8,128)(2,1)S(1)}, bf16[1536,20]{0,1:T(8,128)(2,1)}, u32[]{:S(2)}) copy-start(bf16[1536,20]{0,1:T(8,128)(2,1)} %param.26) | copy-start | bytes 184324
  75.0 90.4 %copy-start.15 = (bf16[256,1536]{1,0:T(8,128)(2,1)}, bf16[256,1536]{1,0:T(8,128)(2,1)S(1)}, u32[]{:S(2)}) copy-start(bf16[256,1536]{1,0:T(8,128)(2,1)S(1)} %multiply_convert_fusion.1.refs_0_) | copy-start | bytes 2359300
  75.0 24.3 %collective-permute-start.3 = (bf16[256,1536]{1,0:T(8,128)(2,1)S(1)}, bf16[256,1536]{1,0:T(8,128)(2,1)}, u32[]{:S(2)}, u32[]{:S(2)}) collective-permute-start(bf16[256,1536]{1,0:T(8,128)(2,1)S(1)} %multiply_convert_fusion.1.refs_0_), channel_id=1, source_target_pairs={{0,1},{1,2},{2,3},{4,5},{5,6},{6,7},{8,9},{9,10},{10,11},{12,13},{... | collective-permute-start | bytes 2359304 | tf_op jit(solution)/shard_map/ppermute | solution.py:717
  76.3 23.0 %collective-permute-start.4 = (bf16[256,1536]{1,0:T(8,128)(2,1)S(1)}, bf16[256,1536]{1,0:T(8,128)(2,1)}, u32[]{:S(2)}, u32[]{:S(2)}) collective-permute-start(bf16[256,1536]{1,0:T(8,128)(2,1)S(1)} %multiply_convert_fusion.1.refs_0_), channel_id=1, source_target_pairs={{1,0},{2,1},{3,2},{5,4},{6,5},{7,6},{9,8},{10,9},{11,10},{13,12},{... | collective-permute-start | bytes 2359304 | tf_op jit(solution)/shard_map/ppermute | solution.py:721
  81.7 34.0 %collective-permute-start.13 = (bf16[256,1664]{1,0:T(8,128)(2,1)}, bf16[256,1664]{1,0:T(8,128)(2,1)}, u32[]{:S(2)}, u32[]{:S(2)}) collective-permute-start(bf16[256,1664]{1,0:T(8,128)(2,1)} %collective-permute-done.12.refs_8_), channel_id=1, source_target_pairs={{0,1},{1,2},{2,3},{4,5},{5,6},{6,7},{8,9},{9,10},{10,11},{12,13},{... | collective-permute-start | bytes 2555912 | tf_op jit(solution)/shard_map/ppermute | solution.py:717
  83.2 5.6 %collective-permute-start.5 = (f32[1,24]{1,0:T(1,128)S(1)}, f32[1,24]{1,0:T(1,128)S(1)}, u32[]{:S(2)}, u32[]{:S(2)}) collective-permute-start(f32[1,24]{1,0:T(1,128)S(1)} %bitcast.140), channel_id=1, source_target_pairs={{0,4},{4,0},{8,12},{12,8},{16,20},{20,16},{24,28},{28,24},{1,5},{5... | collective-permute-start | bytes 296 | tf_op jit(solution)/shard_map/ppermute | solution.py:796
  83.2 33.9 %collective-permute-start.16 = (bf16[256,1664]{1,0:T(8,128)(2,1)}, bf16[256,1664]{1,0:T(8,128)(2,1)}, u32[]{:S(2)}, u32[]{:S(2)}) collective-permute-start(bf16[256,1664]{1,0:T(8,128)(2,1)} %collective-permute-done.15.refs_11_), channel_id=1, source_target_pairs={{1,0},{2,1},{3,2},{5,4},{6,5},{7,6},{9,8},{10,9},{11,10},{13,12},{... | collective-permute-start | bytes 2555912 | tf_op jit(solution)/shard_map/ppermute | solution.py:721
  88.7 6.5 %collective-permute-start.6 = (f32[1,24]{1,0:T(1,128)S(1)}, f32[1,24]{1,0:T(1,128)S(1)}, u32[]{:S(2)}, u32[]{:S(2)}) collective-permute-start(f32[1,24]{1,0:T(1,128)S(1)} %bitcast_maximum_fusion), channel_id=1, source_target_pairs={{0,8},{4,12},{8,0},{12,4},{16,24},{20,28},{24,16},{28,20},{1,9},{5... | collective-permute-start | bytes 296 | tf_op jit(solution)/shard_map/ppermute | solution.py:796
  95.2 3.6 collective-permute-start.7
  99.3 34.7 %collective-permute-start.10 = (bf16[256,1536]{1,0:T(8,128)(2,1)}, bf16[256,1536]{1,0:T(8,128)(2,1)}, u32[]{:S(2)}, u32[]{:S(2)}) collective-permute-start(bf16[256,1536]{1,0:T(8,128)(2,1)} %collective-permute-done.4.refs_4_), channel_id=1, source_target_pairs={{1,0},{2,1},{3,2},{5,4},{6,5},{7,6},{9,8},{10,9},{11,10},{13,12},{... | collective-permute-start | bytes 2359304 | tf_op jit(solution)/shard_map/ppermute | solution.py:721
  104.2 35.1 %collective-permute-start.8 = (bf16[256,1536]{1,0:T(8,128)(2,1)}, bf16[256,1536]{1,0:T(8,128)(2,1)}, u32[]{:S(2)}, u32[]{:S(2)}) collective-permute-start(bf16[256,1536]{1,0:T(8,128)(2,1)} %collective-permute-done.3.refs_1_), channel_id=1, source_target_pairs={{0,1},{1,2},{2,3},{4,5},{5,6},{6,7},{8,9},{9,10},{10,11},{12,13},{... | collective-permute-start | bytes 2359304 | tf_op jit(solution)/shard_map/ppermute | solution.py:717
  115.7 35.1 %collective-permute-start.14 = (bf16[256,1664]{1,0:T(8,128)(2,1)}, bf16[256,1664]{1,0:T(8,128)(2,1)}, u32[]{:S(2)}, u32[]{:S(2)}) collective-permute-start(bf16[256,1664]{1,0:T(8,128)(2,1)} %collective-permute-done.13.refs_9_), channel_id=1, source_target_pairs={{0,1},{1,2},{2,3},{4,5},{5,6},{6,7},{8,9},{9,10},{10,11},{12,13},{... | collective-permute-start | bytes 2555912 | tf_op jit(solution)/shard_map/ppermute | solution.py:717
  117.2 35.1 %collective-permute-start.17 = (bf16[256,1664]{1,0:T(8,128)(2,1)}, bf16[256,1664]{1,0:T(8,128)(2,1)}, u32[]{:S(2)}, u32[]{:S(2)}) collective-permute-start(bf16[256,1664]{1,0:T(8,128)(2,1)} %collective-permute-done.16.refs_12_), channel_id=1, source_target_pairs={{1,0},{2,1},{3,2},{5,4},{6,5},{7,6},{9,8},{10,9},{11,10},{13,12},{... | collective-permute-start | bytes 2555912 | tf_op jit(solution)/shard_map/ppermute | solution.py:721
  134.0 31.3 %collective-permute-start.11 = (bf16[256,1536]{1,0:T(8,128)(2,1)}, bf16[256,1536]{1,0:T(8,128)(2,1)}, u32[]{:S(2)}, u32[]{:S(2)}) collective-permute-start(bf16[256,1536]{1,0:T(8,128)(2,1)} %collective-permute-done.10.refs_5_), channel_id=1, source_target_pairs={{1,0},{2,1},{3,2},{5,4},{6,5},{7,6},{9,8},{10,9},{11,10},{13,12},{... | collective-permute-start | bytes 2359304 | tf_op jit(solution)/shard_map/ppermute | solution.py:721
  139.3 26.0 %collective-permute-start.9 = (bf16[256,1536]{1,0:T(8,128)(2,1)}, bf16[256,1536]{1,0:T(8,128)(2,1)}, u32[]{:S(2)}, u32[]{:S(2)}) collective-permute-start(bf16[256,1536]{1,0:T(8,128)(2,1)} %collective-permute-done.8.refs_2_), channel_id=1, source_target_pairs={{0,1},{1,2},{2,3},{4,5},{5,6},{6,7},{8,9},{9,10},{10,11},{12,13},{... | collective-permute-start | bytes 2359304 | tf_op jit(solution)/shard_map/ppermute | solution.py:717
  142.2 64.6 %copy-start.30 = (s32[4]{0:T(128)}, s32[4]{0:T(128)S(1)}, u32[]{:S(2)}) copy-start(s32[4]{0:T(128)S(1)} %get-tuple-element.286.order_ref) | copy-start | bytes 52
  206.8 74.3 %all-to-all-start = ((bf16[4,256,1536]{2,1,0:T(8,128)(2,1)}), bf16[4,256,1536]{2,1,0:T(8,128)(2,1)}, u32[]{:S(2)}, u32[]{:S(2)}) async-start(bf16[4,256,1536]{2,1,0:T(8,128)(2,1)} %get-tuple-element.117), calls=%async_computation | async-start | bytes 6291456 | tf_op jit(solution)/shard_map/all_to_all | solution.py:928
  233.0 13.4 %collective-permute-start.18 = (bf16[3,5,192,512]{3,2,1,0:T(8,128)(2,1)}, bf16[3,5,192,512]{3,2,1,0:T(8,128)(2,1)}, u32[]{:S(2)}, u32[]{:S(2)}) collective-permute-start(bf16[3,5,192,512]{3,2,1,0:T(8,128)(2,1)} %get-tuple-element.122), channel_id=1, source_target_pairs={{0,4},{4,0},{8,12},{12,8},{16,20},{20,16},{24,28},{28,24},{1,5},{5... | collective-permute-start | bytes 8847368 | tf_op jit(solution)/shard_map/ppermute | solution.py:743
  233.0 13.4 %collective-permute-start.19 = (bf16[3,5,192,512]{3,2,1,0:T(8,128)(2,1)}, bf16[3,5,192,512]{3,2,1,0:T(8,128)(2,1)}, u32[]{:S(2)}, u32[]{:S(2)}) collective-permute-start(bf16[3,5,192,512]{3,2,1,0:T(8,128)(2,1)} %get-tuple-element.123), channel_id=1, source_target_pairs={{0,4},{4,0},{8,12},{12,8},{16,20},{20,16},{24,28},{28,24},{1,5},{5... | collective-permute-start | bytes 8847368 | tf_op jit(solution)/shard_map/ppermute | solution.py:743
  233.5 13.6 %collective-permute-start.20 = (bf16[3,5,192,512]{3,2,1,0:T(8,128)(2,1)}, bf16[3,5,192,512]{3,2,1,0:T(8,128)(2,1)}, u32[]{:S(2)}, u32[]{:S(2)}) collective-permute-start(bf16[3,5,192,512]{3,2,1,0:T(8,128)(2,1)} %get-tuple-element.124), channel_id=1, source_target_pairs={{0,4},{4,0},{8,12},{12,8},{16,20},{20,16},{24,28},{28,24},{1,5},{5... | collective-permute-start | bytes 8847368 | tf_op jit(solution)/shard_map/ppermute | solution.py:743
  233.6 17.8 %collective-permute-start.21 = (bf16[3,5,192,512]{3,2,1,0:T(8,128)(2,1)}, bf16[3,5,192,512]{3,2,1,0:T(8,128)(2,1)}, u32[]{:S(2)}, u32[]{:S(2)}) collective-permute-start(bf16[3,5,192,512]{3,2,1,0:T(8,128)(2,1)} %get-tuple-element.125), channel_id=1, source_target_pairs={{0,4},{4,0},{8,12},{12,8},{16,20},{20,16},{24,28},{28,24},{1,5},{5... | collective-permute-start | bytes 8847368 | tf_op jit(solution)/shard_map/ppermute | solution.py:743
  281.1 61.4 %collective-permute-start.23 = (bf16[2,3,5,192,256]{4,3,2,1,0:T(8,128)(2,1)}, bf16[2,3,5,192,256]{4,3,2,1,0:T(8,128)(2,1)}, u32[]{:S(2)}, u32[]{:S(2)}) collective-permute-start(bf16[2,3,5,192,256]{4,3,2,1,0:T(8,128)(2,1)} %get-tuple-element.131), channel_id=1, source_target_pairs={{0,8},{4,12},{8,0},{12,4},{16,24},{20,28},{24,16},{28,20},{1,9},{5... | collective-permute-start | bytes 8847368 | tf_op jit(solution)/shard_map/ppermute | solution.py:743
  282.8 63.5 %collective-permute-start.24 = (bf16[2,3,5,192,256]{4,3,2,1,0:T(8,128)(2,1)}, bf16[2,3,5,192,256]{4,3,2,1,0:T(8,128)(2,1)}, u32[]{:S(2)}, u32[]{:S(2)}) collective-permute-start(bf16[2,3,5,192,256]{4,3,2,1,0:T(8,128)(2,1)} %get-tuple-element.132), channel_id=1, source_target_pairs={{0,16},{4,20},{8,24},{12,28},{16,0},{20,4},{24,8},{28,12},{1,17},{... | collective-permute-start | bytes 8847368 | tf_op jit(solution)/shard_map/ppermute | solution.py:743
  286.5 49.0 %all-to-all-start.1 = ((bf16[4,256,768]{2,1,0:T(8,128)(2,1)}), bf16[4,256,768]{2,1,0:T(8,128)(2,1)}, u32[]{:S(2)}, u32[]{:S(2)}) async-start(bf16[4,256,768]{2,1,0:T(8,128)(2,1)} %get-tuple-element.133), calls=%async_computation.1 | async-start | bytes 3145728 | tf_op jit(solution)/shard_map/all_to_all | solution.py:937
  322.1 13.3 %collective-permute-start.22 = (bf16[2048,128]{1,0:T(8,128)(2,1)}, bf16[2048,128]{1,0:T(8,128)(2,1)S(1)}, u32[]{:S(2)}, u32[]{:S(2)}) collective-permute-start(bf16[2048,128]{1,0:T(8,128)(2,1)} %get-tuple-element.130), channel_id=1, source_target_pairs={{1,0},{2,1},{3,2},{5,4},{6,5},{7,6},{9,8},{10,9},{11,10},{13,12},{... | collective-permute-start | bytes 1572872 | tf_op jit(solution)/shard_map/ppermute | solution.py:721
  324.6 21.7 %copy-start.25 = (f32[256,1]{1,0:T(8,128)S(1)}, f32[256,1]{1,0:T(8,128)}, u32[]{:S(2)}) copy-start(f32[256,1]{1,0:T(8,128)} %get-tuple-element.150) | copy-start | bytes 3076
  324.7 22.5 %copy-start.22 = (bf16[2048,128]{1,0:T(8,128)(2,1)S(1)}, bf16[2048,128]{1,0:T(8,128)(2,1)}, u32[]{:S(2)}) copy-start(bf16[2048,128]{1,0:T(8,128)(2,1)} %get-tuple-element.140) | copy-start | bytes 1572868
  346.3 13.2 %collective-permute-start.26 = (bf16[4,192,3072]{2,1,0:T(8,128)(2,1)}, bf16[4,192,3072]{2,1,0:T(8,128)(2,1)}, u32[]{:S(2)}, u32[]{:S(2)}) collective-permute-start(bf16[4,192,3072]{2,1,0:T(8,128)(2,1)} %get-tuple-element.142), channel_id=1, source_target_pairs={{0,4},{4,0},{8,12},{12,8},{16,20},{20,16},{24,28},{28,24},{1,5},{5... | collective-permute-start | bytes 14155784 | tf_op jit(solution)/shard_map/ppermute | solution.py:743
  347.3 18.4 %collective-permute-start.25 = (bf16[2048,128]{1,0:T(8,128)(2,1)S(1)}, bf16[2048,128]{1,0:T(8,128)(2,1)S(1)}, u32[]{:S(2)}, u32[]{:S(2)}) collective-permute-start(bf16[2048,128]{1,0:T(8,128)(2,1)S(1)} %add_convert_fusion.11), channel_id=1, source_target_pairs={{1,0},{2,1},{3,2},{5,4},{6,5},{7,6},{9,8},{10,9},{11,10},{13,12},{... | collective-permute-start | bytes 1572872 | tf_op jit(solution)/shard_map/ppermute | solution.py:721
  365.8 15.4 %collective-permute-start.27 = (bf16[2048,128]{1,0:T(8,128)(2,1)S(1)}, bf16[2048,128]{1,0:T(8,128)(2,1)S(1)}, u32[]{:S(2)}, u32[]{:S(2)}) collective-permute-start(bf16[2048,128]{1,0:T(8,128)(2,1)S(1)} %add_convert_fusion.10), channel_id=1, source_target_pairs={{1,0},{2,1},{3,2},{5,4},{6,5},{7,6},{9,8},{10,9},{11,10},{13,12},{... | collective-permute-start | bytes 1572872 | tf_op jit(solution)/shard_map/ppermute | solution.py:721
  372.3 49.1 %collective-permute-start.31 = (bf16[2,192,1536]{2,1,0:T(8,128)(2,1)}, bf16[2,192,1536]{2,1,0:T(8,128)(2,1)}, u32[]{:S(2)}, u32[]{:S(2)}) collective-permute-start(bf16[2,192,1536]{2,1,0:T(8,128)(2,1)} %get-tuple-element.244), channel_id=1, source_target_pairs={{0,16},{4,20},{8,24},{12,28},{16,0},{20,4},{24,8},{28,12},{1,17},{... | collective-permute-start | bytes 3538952 | tf_op jit(solution)/shard_map/ppermute | solution.py:743
  374.0 8.0 %copy-start.17 = (bf16[2,3,5,192,256]{4,3,2,1,0:T(8,128)(2,1)S(1)}, bf16[2,3,5,192,256]{4,3,2,1,0:T(8,128)(2,1)}, u32[]{:S(2)}) copy-start(bf16[2,3,5,192,256]{4,3,2,1,0:T(8,128)(2,1)} %get-tuple-element.168) | copy-start | bytes 8847364
  376.1 45.2 %collective-permute-start.30 = (bf16[2,192,1536]{2,1,0:T(8,128)(2,1)}, bf16[2,192,1536]{2,1,0:T(8,128)(2,1)}, u32[]{:S(2)}, u32[]{:S(2)}) collective-permute-start(bf16[2,192,1536]{2,1,0:T(8,128)(2,1)} %get-tuple-element.246), channel_id=1, source_target_pairs={{0,8},{4,12},{8,0},{12,4},{16,24},{20,28},{24,16},{28,20},{1,9},{5... | collective-permute-start | bytes 3538952 | tf_op jit(solution)/shard_map/ppermute | solution.py:743
  386.7 60.9 %collective-permute-start.35 = (bf16[3,5,192,256]{3,2,1,0:T(8,128)(2,1)}, bf16[3,5,192,256]{3,2,1,0:T(8,128)(2,1)}, u32[]{:S(2)}, u32[]{:S(2)}) collective-permute-start(bf16[3,5,192,256]{3,2,1,0:T(8,128)(2,1)} %get-tuple-element.240), channel_id=1, source_target_pairs={{0,8},{4,12},{8,0},{12,4},{16,24},{20,28},{24,16},{28,20},{1,9},{5... | collective-permute-start | bytes 4423688 | tf_op jit(solution)/shard_map/ppermute | solution.py:743
  387.0 9.1 %copy-start.4 = (bf16[1536,512]{1,0:T(8,128)(2,1)S(1)}, bf16[1536,512]{1,0:T(8,128)(2,1)}, u32[]{:S(2)}) copy-start(bf16[1536,512]{1,0:T(8,128)(2,1)} %key_ref.1) | copy-start | bytes 4718596
  391.6 56.0 %collective-permute-start.34 = (bf16[3,5,192,256]{3,2,1,0:T(8,128)(2,1)}, bf16[3,5,192,256]{3,2,1,0:T(8,128)(2,1)}, u32[]{:S(2)}, u32[]{:S(2)}) collective-permute-start(bf16[3,5,192,256]{3,2,1,0:T(8,128)(2,1)} %get-tuple-element.241), channel_id=1, source_target_pairs={{0,16},{4,20},{8,24},{12,28},{16,0},{20,4},{24,8},{28,12},{1,17},{... | collective-permute-start | bytes 4423688 | tf_op jit(solution)/shard_map/ppermute | solution.py:743
  398.5 9.0 %collective-permute-start.28 = (f32[1,24]{1,0:T(1,128)S(1)}, f32[1,24]{1,0:T(1,128)S(1)}, u32[]{:S(2)}, u32[]{:S(2)}) collective-permute-start(f32[1,24]{1,0:T(1,128)S(1)} %copy-done.33), channel_id=1, source_target_pairs={{0,1},{1,0},{2,3},{3,2},{4,5},{5,4},{6,7},{7,6},{8,9},{9,8},{10,11... | collective-permute-start | bytes 296 | tf_op jit(solution)/shard_map/ppermute | solution.py:796
  407.5 8.1 %collective-permute-start.29 = (f32[1,24]{1,0:T(1,128)S(1)}, f32[1,24]{1,0:T(1,128)S(1)}, u32[]{:S(2)}, u32[]{:S(2)}) collective-permute-start(f32[1,24]{1,0:T(1,128)S(1)} %max.21), channel_id=1, source_target_pairs={{0,2},{1,3},{2,0},{3,1},{4,6},{5,7},{6,4},{7,5},{8,10},{9,11},{10,... | collective-permute-start | bytes 296 | tf_op jit(solution)/shard_map/ppermute | solution.py:796
  415.6 48.8 %all-to-all-start.2 = ((bf16[4,256,768]{2,1,0:T(8,128)(2,1)}), bf16[4,256,768]{2,1,0:T(8,128)(2,1)}, u32[]{:S(2)}, u32[]{:S(2)}) async-start(bf16[4,256,768]{2,1,0:T(8,128)(2,1)} %get-tuple-element.149), calls=%async_computation.2 | async-start | bytes 3145728 | tf_op jit(solution)/shard_map/all_to_all | solution.py:964
  423.0 24.6 %collective-permute-start.33 = (bf16[192,1536]{1,0:T(8,128)(2,1)S(1)}, bf16[192,1536]{1,0:T(8,128)(2,1)S(1)}, u32[]{:S(2)}, u32[]{:S(2)}) collective-permute-start(bf16[192,1536]{1,0:T(8,128)(2,1)S(1)} %get-tuple-element.258), channel_id=1, source_target_pairs={{0,8},{4,12},{8,0},{12,4},{16,24},{20,28},{24,16},{28,20},{1,9},{5... | collective-permute-start | bytes 1769480 | tf_op jit(solution)/shard_map/ppermute | solution.py:743
  426.4 21.2 %collective-permute-start.32 = (bf16[192,1536]{1,0:T(8,128)(2,1)S(1)}, bf16[192,1536]{1,0:T(8,128)(2,1)S(1)}, u32[]{:S(2)}, u32[]{:S(2)}) collective-permute-start(bf16[192,1536]{1,0:T(8,128)(2,1)S(1)} %get-tuple-element.259), channel_id=1, source_target_pairs={{0,16},{4,20},{8,24},{12,28},{16,0},{20,4},{24,8},{28,12},{1,17},{... | collective-permute-start | bytes 1769480 | tf_op jit(solution)/shard_map/ppermute | solution.py:743
  447.6 18.5 %collective-permute-start.39 = (bf16[4,192,1152]{2,1,0:T(8,128)(2,1)}, bf16[4,192,1152]{2,1,0:T(8,128)(2,1)}, u32[]{:S(2)}, u32[]{:S(2)}) collective-permute-start(bf16[4,192,1152]{2,1,0:T(8,128)(2,1)} %get-tuple-element.177), channel_id=1, source_target_pairs={{0,4},{4,0},{8,12},{12,8},{16,20},{20,16},{24,28},{28,24},{1,5},{5... | collective-permute-start | bytes 5308424 | tf_op jit(solution)/shard_map/ppermute | solution.py:743
  449.6 6.7 %copy-start.8 = (bf16[3,5,192,256]{3,2,1,0:T(8,128)(2,1)S(1)}, bf16[3,5,192,256]{3,2,1,0:T(8,128)(2,1)}, u32[]{:S(2)}) copy-start(bf16[3,5,192,256]{3,2,1,0:T(8,128)(2,1)} %get-tuple-element.194) | copy-start | bytes 4423684
  450.7 29.8 %collective-permute-start.36 = (bf16[48,3072]{1,0:T(8,128)(2,1)}, bf16[48,3072]{1,0:T(8,128)(2,1)}, u32[]{:S(2)}, u32[]{:S(2)}) collective-permute-start(bf16[48,3072]{1,0:T(8,128)(2,1)} %get-tuple-element.267), channel_id=1, source_target_pairs={{0,1},{1,2},{2,3},{3,0},{4,5},{5,6},{6,7},{7,4},{8,9},{9,10},{10,1... | collective-permute-start | bytes 884744 | tf_op jit(solution)/shard_map/ppermute | solution.py:783
  453.1 27.8 %collective-permute-start.37 = (bf16[48,3072]{1,0:T(8,128)(2,1)}, bf16[48,3072]{1,0:T(8,128)(2,1)}, u32[]{:S(2)}, u32[]{:S(2)}) collective-permute-start(bf16[48,3072]{1,0:T(8,128)(2,1)} %get-tuple-element.266), channel_id=1, source_target_pairs={{0,2},{1,3},{2,0},{3,1},{4,6},{5,7},{6,4},{7,5},{8,10},{9,11},{10,... | collective-permute-start | bytes 884744 | tf_op jit(solution)/shard_map/ppermute | solution.py:783
  454.0 26.9 %collective-permute-start.38 = (bf16[48,3072]{1,0:T(8,128)(2,1)}, bf16[48,3072]{1,0:T(8,128)(2,1)}, u32[]{:S(2)}, u32[]{:S(2)}) collective-permute-start(bf16[48,3072]{1,0:T(8,128)(2,1)} %get-tuple-element.265), channel_id=1, source_target_pairs={{0,3},{1,0},{2,1},{3,2},{4,7},{5,4},{6,5},{7,6},{8,11},{9,8},{10,9... | collective-permute-start | bytes 884744 | tf_op jit(solution)/shard_map/ppermute | solution.py:783
  467.6 12.8 %collective-permute-start.41 = (bf16[2,192,640]{2,1,0:T(8,128)(2,1)S(1)}, bf16[2,192,640]{2,1,0:T(8,128)(2,1)S(1)}, u32[]{:S(2)}, u32[]{:S(2)}) collective-permute-start(bf16[2,192,640]{2,1,0:T(8,128)(2,1)S(1)} %get-tuple-element.262), channel_id=1, source_target_pairs={{0,16},{4,20},{8,24},{12,28},{16,0},{20,4},{24,8},{28,12},{1,17},{... | collective-permute-start | bytes 1474568 | tf_op jit(solution)/shard_map/ppermute | solution.py:743
  469.4 12.8 %copy-start.19 = (bf16[48,3072]{1,0:T(8,128)(2,1)S(1)}, bf16[48,3072]{1,0:T(8,128)(2,1)}, u32[]{:S(2)}) copy-start(bf16[48,3072]{1,0:T(8,128)(2,1)} %get-tuple-element.190) | copy-start | bytes 884740
  469.4 10.5 %collective-permute-start.40 = (bf16[2,192,512]{2,1,0:T(8,128)(2,1)S(1)}, bf16[2,192,512]{2,1,0:T(8,128)(2,1)S(1)}, u32[]{:S(2)}, u32[]{:S(2)}) collective-permute-start(bf16[2,192,512]{2,1,0:T(8,128)(2,1)S(1)} %get-tuple-element.263), channel_id=1, source_target_pairs={{0,8},{4,12},{8,0},{12,4},{16,24},{20,28},{24,16},{28,20},{1,9},{5... | collective-permute-start | bytes 1179656 | tf_op jit(solution)/shard_map/ppermute | solution.py:743
  481.0 7.8 %collective-permute-start.43 = (bf16[192,640]{1,0:T(8,128)(2,1)S(1)}, bf16[192,640]{1,0:T(8,128)(2,1)S(1)}, u32[]{:S(2)}, u32[]{:S(2)}) collective-permute-start(bf16[192,640]{1,0:T(8,128)(2,1)S(1)} %fusion.28), channel_id=1, source_target_pairs={{0,8},{4,12},{8,0},{12,4},{16,24},{20,28},{24,16},{28,20},{1,9},{5... | collective-permute-start | bytes 737288 | tf_op jit(solution)/shard_map/ppermute | solution.py:743
  481.5 6.5 %collective-permute-start.42 = (bf16[192,512]{1,0:T(8,128)(2,1)S(1)}, bf16[192,512]{1,0:T(8,128)(2,1)S(1)}, u32[]{:S(2)}, u32[]{:S(2)}) collective-permute-start(bf16[192,512]{1,0:T(8,128)(2,1)S(1)} %fusion.31), channel_id=1, source_target_pairs={{0,16},{4,20},{8,24},{12,28},{16,0},{20,4},{24,8},{28,12},{1,17},{... | collective-permute-start | bytes 589832 | tf_op jit(solution)/shard_map/ppermute | solution.py:743
  489.4 8.7 %collective-permute-start.44 = (bf16[48,1152]{0,1:T(8,128)(2,1)S(1)}, bf16[48,1152]{0,1:T(8,128)(2,1)S(1)}, u32[]{:S(2)}, u32[]{:S(2)}) collective-permute-start(bf16[48,1152]{0,1:T(8,128)(2,1)S(1)} %bitcast.136), channel_id=1, source_target_pairs={{0,1},{1,2},{2,3},{3,0},{4,5},{5,6},{6,7},{7,4},{8,9},{9,10},{10,1... | collective-permute-start | bytes 331784 | tf_op jit(solution)/shard_map/ppermute | solution.py:783
  490.5 26.2 %collective-permute-start.45 = (bf16[48,1152]{0,1:T(8,128)(2,1)S(1)}, bf16[48,1152]{0,1:T(8,128)(2,1)S(1)}, u32[]{:S(2)}, u32[]{:S(2)}) collective-permute-start(bf16[48,1152]{0,1:T(8,128)(2,1)S(1)} %bitcast.137), channel_id=1, source_target_pairs={{0,2},{1,3},{2,0},{3,1},{4,6},{5,7},{6,4},{7,5},{8,10},{9,11},{10,... | collective-permute-start | bytes 331784 | tf_op jit(solution)/shard_map/ppermute | solution.py:783
  492.0 24.8 %collective-permute-start.46 = (bf16[48,1152]{0,1:T(8,128)(2,1)S(1)}, bf16[48,1152]{0,1:T(8,128)(2,1)S(1)}, u32[]{:S(2)}, u32[]{:S(2)}) collective-permute-start(bf16[48,1152]{0,1:T(8,128)(2,1)S(1)} %bitcast.138), channel_id=1, source_target_pairs={{0,3},{1,0},{2,1},{3,2},{4,7},{5,4},{6,5},{7,6},{8,11},{9,8},{10,9... | collective-permute-start | bytes 331784 | tf_op jit(solution)/shard_map/ppermute | solution.py:783
  (20 other events, 60.8 us)

commit v7 on v6

--- a/solution.py
+++ b/solution.py
@@ -993,7 +993,7 @@
     ]
     rest = start_dense((keep, flip(send, 1, dp_size)))
     rest = step_spread(rest, 0, dp_size, dp_place)
-    wide_parts, rest = lax.optimization_barrier((pass_line(wide, place, size), rest))
+    wide_parts, rest, mix_two = lax.optimization_barrier((pass_line(wide, place, size), rest, mix_two))
     for stage in range(1, stages):
         rest = step_spread(rest, stage, dp_size, dp_place)
     rest_parts = lax.optimization_barrier(pass_line(rest, place, size))

time: 527 us -> 529 us (level)
    ppermute x9, starting transfers between devices: 46.3 us -> 38.7 us  [line_down(): return lax.ppermute(value, 'expert', [(i + 1, i) for i in range(size - 1)])]
    ppermute x6, waiting for transfers between devices: 22.1 us -> 29.3 us  [pass_line(): lax.ppermute(part, 'expert', [(i, (i + k) % size) for i in range(size)])]
    ppermute x9, waiting for transfers between devices: 46.3 us -> 39.6 us  [line_up(): return lax.ppermute(value, 'expert', [(i, i + 1) for i in range(size - 1)])]
    ppermute x9, waiting for transfers between devices: 37 us -> 42.5 us  [line_down(): return lax.ppermute(value, 'expert', [(i + 1, i) for i in range(size - 1)])]
    ppermute x5, starting transfers between devices: 13 us -> 18.3 us  [swap_top(): lax.ppermute(top, axis, [(i, i ^ 1 << bit) for i in range(size)])]
  transfers between devices with their start and end apart: 50 -> 50, of which waited for: 26 -> 25; matrix products, arithmetic and copies ran while one was open for 14% -> 14% of each run, Pallas kernels for 20% -> 20%
where the time goes in v7:
time: 529 us; the launch traced here: 521 us
  waiting for transfers between devices  167 us (32%)
  Pallas kernels  149 us (28%)
  starting transfers between devices  119 us (22%)
  other arithmetic  46.8 us (9%)
  local copies, waits for them, and re-layouts  22.2 us (4%)
  matrix products  15.5 us (3%)
    ppermute x18, waiting for transfers between devices, flip(): return lax.ppermute(value, 'dp', [(i, i ^ bit) for i in range(size)])  43.4 us
    ppermute x9, waiting for transfers between devices, line_down(): return lax.ppermute(value, 'expert', [(i + 1, i) for i in range(size - 1)])  42.5 us
    pallas_call x1, Pallas kernels, run_experts(): pl.pallas_call(functools.partial(expert_kernel, blocks, slot_rows, local_...  41.5 us
    ppermute x9, waiting for transfers between devices, line_up(): return lax.ppermute(value, 'expert', [(i, i + 1) for i in range(size - 1)])  39.6 us
    ppermute x9, starting transfers between devices, line_down(): return lax.ppermute(value, 'expert', [(i + 1, i) for i in range(size - 1)])  38.7 us
    pallas_call x2, Pallas kernels, run_expert_grads(): pl.pallas_call(functools.partial(expert_keep_kernel, owners.bit_length()...  37.8 us
    ppermute x6, waiting for transfers between devices, pass_line(): lax.ppermute(part, 'expert', [(i, (i + k) % size) for i in range(size)])  29.3 us
    convert_element_type x16, other arithmetic, add_low(): return total.astype(BF16)  20 us
  transfers between devices with their start and end apart: 50, of which 25 were waited for; matrix products, arithmetic and copies ran while one was open for 14% of the time, Pallas kernels for 20%

profile of v7, /device:TPU:24, one launch (start us, length us, event | category | flops | bytes accessed | tf_op | source)
XLA Modules:
  0.0 521.0 jit_solution(10564654508961291241)
XLA Ops:
  4.9 4.3 front.1
  10.5 14.6 %collective-permute-done.refs_1_.refs_5_ = bf16[2064,128]{1,0:T(8,128)(2,1)S(1)} collective-permute-done((bf16[2064,128]{1,0:T(8,128)(2,1)}, bf16[2064,128]{1,0:T(8,128)(2,1)S(1)}, u32[]{:S(2)}, u32[]{:S(2)}) %collective-permute-start) | collective-permute-done | bytes 528416 | tf_op jit(solution)/shard_map/ppermute | solution.py:717
  26.3 13.5 %collective-permute-done.1.refs_2_.refs_6_ = bf16[2064,128]{1,0:T(8,128)(2,1)S(1)} collective-permute-done((bf16[2064,128]{1,0:T(8,128)(2,1)S(1)}, bf16[2064,128]{1,0:T(8,128)(2,1)S(1)}, u32[]{:S(2)}, u32[]{:S(2)}) %collective-permute-start.1) | collective-permute-done | bytes 528416 | tf_op jit(solution)/shard_map/ppermute | solution.py:717
  41.9 2.6 extend.1.refs_7_
  45.8 6.1 %collective-permute-start.15 = (bf16[256,1664]{1,0:T(8,128)(2,1)}, bf16[256,1664]{1,0:T(8,128)(2,1)}, u32[]{:S(2)}, u32[]{:S(2)}) collective-permute-start(bf16[256,1664]{1,0:T(8,128)(2,1)} %extend.1.refs_7_), channel_id=1, source_target_pairs={{1,0},{2,1},{3,2},{5,4},{6,5},{7,6},{9,8},{10,9},{11,10},{13,12},{... | collective-permute-start | bytes 2555912 | tf_op jit(solution)/shard_map/ppermute | solution.py:721
  51.9 5.6 %queries.1.query_ref = bf16[256,1536]{1,0:T(8,128)(2,1)} custom-call(bf16[256,1536]{1,0:T(8,128)(2,1)} %get-tuple-element.108.normed_ref.refs_1_.refs_0_, bf16[1536,1536]{1,0:T(8,128)(2,1)} %query_ref.1, f32[256,128]{1,0:T(8,128)} %get-tuple-element.287.cos_ref, f32[256,128]{1,0:T(8,128)} %get-tuple-element.286.sin_ref), custom_call_target="tpu_custom_call" | custom-call | flops 5000000 | tf_op jit(solution)/shard_map/queries/pallas_call | solution.py:896
  58.3 12.3 %attend.1 = (bf16[256,1536]{1,0:T(8,128)(2,1)}, f32[4,2,768]{2,1,0:T(2,128)}, f32[4,2,768]{2,1,0:T(2,128)}) custom-call(s32[1]{0:T(128)} %bitcast.place_ref, bf16[256,1536]{1,0:T(8,128)(2,1)} %queries.1.query_ref, bf16[2064,128]{1,0:T(8,128)(2,1)} %get-tuple-element.109.refs_0_.refs_4_, bf16[2064,128]{1,0:T(8,128)(2,1)} %copy-done, ...), custom_call_target="tpu_custom_call" | custom-call | flops 20000000 | tf_op jit(solution)/shard_map/attend/pallas_call | solution.py:217
  70.6 4.1 multiply_reduce_fusion.2
  76.3 5.5 %collective-permute-start.4 = (bf16[256,1536]{1,0:T(8,128)(2,1)S(1)}, bf16[256,1536]{1,0:T(8,128)(2,1)}, u32[]{:S(2)}, u32[]{:S(2)}) collective-permute-start(bf16[256,1536]{1,0:T(8,128)(2,1)S(1)} %multiply_convert_fusion.1.refs_0_), channel_id=1, source_target_pairs={{1,0},{2,1},{3,2},{5,4},{6,5},{7,6},{9,8},{10,9},{11,10},{13,12},{... | collective-permute-start | bytes 2359304 | tf_op jit(solution)/shard_map/ppermute | solution.py:721
  83.3 5.5 %collective-permute-start.16 = (bf16[256,1664]{1,0:T(8,128)(2,1)}, bf16[256,1664]{1,0:T(8,128)(2,1)}, u32[]{:S(2)}, u32[]{:S(2)}) collective-permute-start(bf16[256,1664]{1,0:T(8,128)(2,1)} %collective-permute-done.15.refs_11_), channel_id=1, source_target_pairs={{1,0},{2,1},{3,2},{5,4},{6,5},{7,6},{9,8},{10,9},{11,10},{13,12},{... | collective-permute-start | bytes 2555912 | tf_op jit(solution)/shard_map/ppermute | solution.py:721
  88.8 2.5 collective-permute-start.6
  92.8 9.8 %collective-permute-start.7 = (f32[1,24]{1,0:T(1,128)S(1)}, f32[1,24]{1,0:T(1,128)S(1)}, u32[]{:S(2)}, u32[]{:S(2)}) collective-permute-start(f32[1,24]{1,0:T(1,128)S(1)} %max.19), channel_id=1, source_target_pairs={{0,16},{4,20},{8,24},{12,28},{16,0},{20,4},{24,8},{28,12},{1,17},{... | collective-permute-start | bytes 296 | tf_op jit(solution)/shard_map/ppermute | solution.py:796
  104.6 2.2 collective-permute-start.10
  108.1 5.5 %collective-permute-done.13.refs_9_ = bf16[256,1664]{1,0:T(8,128)(2,1)} collective-permute-done((bf16[256,1664]{1,0:T(8,128)(2,1)}, bf16[256,1664]{1,0:T(8,128)(2,1)}, u32[]{:S(2)}, u32[]{:S(2)}) %collective-permute-start.13) | collective-permute-done | bytes 852000 | tf_op jit(solution)/shard_map/ppermute | solution.py:717
  115.0 2.2 collective-permute-done.16.refs_12_
  117.2 5.4 %collective-permute-start.17 = (bf16[256,1664]{1,0:T(8,128)(2,1)}, bf16[256,1664]{1,0:T(8,128)(2,1)}, u32[]{:S(2)}, u32[]{:S(2)}) collective-permute-start(bf16[256,1664]{1,0:T(8,128)(2,1)} %collective-permute-done.16.refs_12_), channel_id=1, source_target_pairs={{1,0},{2,1},{3,2},{5,4},{6,5},{7,6},{9,8},{10,9},{11,10},{13,12},{... | collective-permute-start | bytes 2555912 | tf_op jit(solution)/shard_map/ppermute | solution.py:721
  122.6 11.5 %collective-permute-done.10.refs_5_ = bf16[256,1536]{1,0:T(8,128)(2,1)} collective-permute-done((bf16[256,1536]{1,0:T(8,128)(2,1)}, bf16[256,1536]{1,0:T(8,128)(2,1)}, u32[]{:S(2)}, u32[]{:S(2)}) %collective-permute-start.10) | collective-permute-done | bytes 786464 | tf_op jit(solution)/shard_map/ppermute | solution.py:721
  134.1 5.3 %collective-permute-start.11 = (bf16[256,1536]{1,0:T(8,128)(2,1)}, bf16[256,1536]{1,0:T(8,128)(2,1)}, u32[]{:S(2)}, u32[]{:S(2)}) collective-permute-start(bf16[256,1536]{1,0:T(8,128)(2,1)} %collective-permute-done.10.refs_5_), channel_id=1, source_target_pairs={{1,0},{2,1},{3,2},{5,4},{6,5},{7,6},{9,8},{10,9},{11,10},{13,12},{... | collective-permute-start | bytes 2359304 | tf_op jit(solution)/shard_map/ppermute | solution.py:721
  142.8 6.0 %collective-permute-done.14.refs_10_ = bf16[256,1664]{1,0:T(8,128)(2,1)} collective-permute-done((bf16[256,1664]{1,0:T(8,128)(2,1)}, bf16[256,1664]{1,0:T(8,128)(2,1)}, u32[]{:S(2)}, u32[]{:S(2)}) %collective-permute-start.14) | collective-permute-done | bytes 852000 | tf_op jit(solution)/shard_map/ppermute | solution.py:717
  148.8 3.5 collective-permute-done.17.refs_13_
  152.3 13.0 %collective-permute-done.11.refs_6_ = bf16[256,1536]{1,0:T(8,128)(2,1)} collective-permute-done((bf16[256,1536]{1,0:T(8,128)(2,1)}, bf16[256,1536]{1,0:T(8,128)(2,1)}, u32[]{:S(2)}, u32[]{:S(2)}) %collective-permute-start.11) | collective-permute-done | bytes 786464 | tf_op jit(solution)/shard_map/ppermute | solution.py:721
  165.3 41.5 %experts.1 = (bf16[5,512,1536]{2,1,0:T(8,128)(2,1)}, bf16[5,512,1536]{2,1,0:T(8,128)(2,1)}, bf16[5,512,512]{2,1,0:T(8,128)(2,1)}, bf16[5,512,512]{2,1,0:T(8,128)...) custom-call(s32[9]{0:T(128)} %pad_add_fusion.place_ref, ...), custom_call_target="tpu_custom_call" | custom-call | flops 45000000 | tf_op jit(solution)/shard_map/experts/pallas_call | solution.py:483
  206.8 9.5 %all-to-all-start = ((bf16[4,256,1536]{2,1,0:T(8,128)(2,1)}), bf16[4,256,1536]{2,1,0:T(8,128)(2,1)}, u32[]{:S(2)}, u32[]{:S(2)}) async-start(bf16[4,256,1536]{2,1,0:T(8,128)(2,1)} %get-tuple-element.118), calls=%async_computation | async-start | bytes 6291456 | tf_op jit(solution)/shard_map/all_to_all | solution.py:928
  216.3 16.7 %expert_send.1 = (bf16[3,5,192,512]{3,2,1,0:T(8,128)(2,1)}, bf16[3,5,192,512]{3,2,1,0:T(8,128)(2,1)}, bf16[3,5,192,512]{3,2,1,0:T(8,128)(2,1)}, bf16[3,5,192,512]{3,2,1,0:T(8,128)(2,1)}) custom-call(s32[1]{0:T(128)} %bitcast.7.place_ref, bf16[5,512,1536]{2,1,0:T(8,128)(2,1)} %get-tuple-element.119.xs_ref, bf16[5,512,1536]{2,1,0:T(8,128)(2,1)} %get-tuple-element.120.cs_ref, ...), custom_call_target="tpu_custom_call" | custom-call | flops 15000000 | tf_op jit(solution)/shard_map/expert_send/pallas_call | solution.py:653
  234.1 12.3 %mixture.1 = (bf16[4,256,768]{2,1,0:T(8,128)(2,1)}, bf16[4,256,768]{2,1,0:T(8,128)(2,1)}) custom-call(s32[4]{0:T(128)} %copy-done.34, bf16[5,1536,512]{2,1,0:T(8,128)(2,1)} %down_ref.3, bf16[5,512,512]{2,1,0:T(8,128)(2,1)} %get-tuple-element.114.hs_ref, bf16[4,640,256]{2,1,0:T(8,128)(2,1)} %get-tuple-element.115.hits_ref), custom_call_target="tpu_custom_call" | custom-call | flops 10000000 | tf_op jit(solution)/shard_map/mixture/pallas_call | solution.py:567
  247.2 4.2 collective-permute-done.21.refs_3_
  251.4 21.1 %expert_keep.1 = (bf16[2,3,5,192,256]{4,3,2,1,0:T(8,128)(2,1)}, bf16[2,3,5,192,256]{4,3,2,1,0:T(8,128)(2,1)}, bf16[2,3,5,192,256]{4,3,2,1,0:T(8,128)(2,1)}, bf16[2,3,5,192,256]{4,3,2,1,0:T(8,128)(2,1)}) custom-call(s32[1]{0:T(128)} %bitcast.7.place_ref, bf16[5,512,1536]{2,1,0:T(8,128)(2,1)} %get-tuple-element.119.xs_ref, ...), custom_call_target="tpu_custom_call" | custom-call | flops 15000000 | tf_op jit(solution)/shard_map/expert_keep/pallas_call | solution.py:653
  272.5 8.6 %all-to-all-done = bf16[4,256,1536]{2,1,0:T(8,128)(2,1)} async-done(((bf16[4,256,1536]{2,1,0:T(8,128)(2,1)}), bf16[4,256,1536]{2,1,0:T(8,128)(2,1)}, u32[]{:S(2)}, u32[]{:S(2)}) %all-to-all-start) | async-done | bytes 3145760 | tf_op jit(solution)/shard_map/all_to_all | solution.py:928
  281.1 7.3 %collective-permute-start.23 = (bf16[2,3,5,192,256]{4,3,2,1,0:T(8,128)(2,1)}, bf16[2,3,5,192,256]{4,3,2,1,0:T(8,128)(2,1)}, u32[]{:S(2)}, u32[]{:S(2)}) collective-permute-start(bf16[2,3,5,192,256]{4,3,2,1,0:T(8,128)(2,1)} %get-tuple-element.132), channel_id=1, source_target_pairs={{0,8},{4,12},{8,0},{12,4},{16,24},{20,28},{24,16},{28,20},{1,9},{5... | collective-permute-start | bytes 8847368 | tf_op jit(solution)/shard_map/ppermute | solution.py:743
  288.4 6.4 %all-to-all-start.1 = ((bf16[4,256,768]{2,1,0:T(8,128)(2,1)}), bf16[4,256,768]{2,1,0:T(8,128)(2,1)}, u32[]{:S(2)}, u32[]{:S(2)}) async-start(bf16[4,256,768]{2,1,0:T(8,128)(2,1)} %get-tuple-element.134), calls=%async_computation.1 | async-start | bytes 3145728 | tf_op jit(solution)/shard_map/all_to_all | solution.py:937
  294.8 2.6 convert_reduce_fusion
  300.2 4.9 convolution_convert_fusion.grad_ref
  305.1 17.6 %attend_back.1 = (bf16[256,1536]{1,0:T(8,128)(2,1)}, bf16[2048,128]{1,0:T(8,128)(2,1)}, bf16[2048,128]{1,0:T(8,128)(2,1)}, bf16[2048,128]{1,0:T(8,128)(2,1)}, bf16[2048,128]{1,0:T(8,128)(2,1)}) custom-call(s32[1]{0:T(128)} %bitcast.place_ref, bf16[256,1536]{1,0:T(8,128)(2,1)} %queries.1.query_ref, bf16[256,1536]{1,0:T(8,128)(2,1)} %get-tuple-element.110.attended_ref.refs_2_, ...), custom_call_target="tpu_custom_call" | custom-call | flops 2000000 | tf_op jit(solution)/shard_map/attend_back/pallas_call | solution.py:304
  322.7 2.5 collective-permute-start.22
  325.2 7.9 %dense_grads.2 = (bf16[4,192,3072]{2,1,0:T(8,128)(2,1)}, bf16[4,192,3072]{2,1,0:T(8,128)(2,1)}) custom-call(s32[1]{0:T(128)} %bitcast.7.place_ref, bf16[256,1536]{1,0:T(8,128)(2,1)} %copy-done.13, bf16[256,1536]{1,0:T(8,128)(2,1)} %get-tuple-element.108.normed_ref.refs_1_.refs_0_, bf16[256,1536]{1,0:T(8,128)(2,1)} %get-tuple-element.110.attended_ref.refs_2_, ...), custom_call_target="tpu_custom_call" | custom-call | flops 4000000 | tf_op jit(solution)/shard_map/dense_grads/pallas_call | solution.py:704
  333.1 3.2 collective-permute-done.22
  336.3 15.8 %collective-permute-done.23 = bf16[2,3,5,192,256]{4,3,2,1,0:T(8,128)(2,1)} collective-permute-done((bf16[2,3,5,192,256]{4,3,2,1,0:T(8,128)(2,1)}, bf16[2,3,5,192,256]{4,3,2,1,0:T(8,128)(2,1)}, u32[]{:S(2)}, u32[]{:S(2)}) %collective-permute-start.23) | collective-permute-done | bytes 2949152 | tf_op jit(solution)/shard_map/ppermute | solution.py:743
  354.5 2.0 collective-permute-start.25
  356.4 2.6 convert_reduce_fusion.2
  359.0 2.9 fusion.37
  361.9 2.9 fusion.36
  364.9 3.2 collective-permute-done.25
  368.2 4.4 collective-permute-start.27
  372.6 2.1 add_convert_fusion.4
  375.0 2.1 add_convert_fusion.7
  377.7 5.9 %collective-permute-done.27.above_ref = bf16[2048,128]{1,0:T(8,128)(2,1)S(1)} collective-permute-done((bf16[2048,128]{1,0:T(8,128)(2,1)S(1)}, bf16[2048,128]{1,0:T(8,128)(2,1)S(1)}, u32[]{:S(2)}, u32[]{:S(2)}) %collective-permute-start.27) | collective-permute-done | bytes 524320 | tf_op jit(solution)/shard_map/ppermute | solution.py:721
  384.4 4.6 fusion.11
  389.3 4.7 fusion.9
  394.7 2.7 unpack.1
  399.8 2.5 collective-permute-start.40
  402.4 4.2 fusion.6
  408.8 3.4 collective-permute-start.41
  412.2 4.7 dense_grads.3
  416.9 5.2 %all-to-all-start.2 = ((bf16[4,256,768]{2,1,0:T(8,128)(2,1)}), bf16[4,256,768]{2,1,0:T(8,128)(2,1)}, u32[]{:S(2)}, u32[]{:S(2)}) async-start(bf16[4,256,768]{2,1,0:T(8,128)(2,1)} %get-tuple-element.180), calls=%async_computation.2 | async-start | bytes 3145728 | tf_op jit(solution)/shard_map/all_to_all | solution.py:964
  432.3 16.3 %collective-permute-done.31 = bf16[192,1536]{1,0:T(8,128)(2,1)S(1)} collective-permute-done((bf16[192,1536]{1,0:T(8,128)(2,1)S(1)}, bf16[192,1536]{1,0:T(8,128)(2,1)S(1)}, u32[]{:S(2)}, u32[]{:S(2)}) %collective-permute-start.31) | collective-permute-done | bytes 589856 | tf_op jit(solution)/shard_map/ppermute | solution.py:743
  451.1 2.4 collective-permute-start.34
  454.5 2.3 collective-permute-start.36
  460.5 1.8 collective-permute-start.39
  467.7 4.4 collective-permute-done.38
  472.4 7.7 %collective-permute-done.35 = bf16[48,3072]{1,0:T(8,128)(2,1)} collective-permute-done((bf16[48,3072]{1,0:T(8,128)(2,1)S(1)}, bf16[48,3072]{1,0:T(8,128)(2,1)}, u32[]{:S(2)}, u32[]{:S(2)}) %collective-permute-start.35) | collective-permute-done | bytes 294944 | tf_op jit(solution)/shard_map/ppermute | solution.py:783
  490.5 2.3 collective-permute-start.45
  493.0 2.1 collective-permute-start.46
  496.1 2.0 collective-permute-done.44
  498.1 19.7 %collective-permute-done.45 = bf16[48,1152]{0,1:T(8,128)(2,1)S(1)} collective-permute-done((bf16[48,1152]{0,1:T(8,128)(2,1)S(1)}, bf16[48,1152]{0,1:T(8,128)(2,1)S(1)}, u32[]{:S(2)}, u32[]{:S(2)}) %collective-permute-start.45) | collective-permute-done | bytes 110624 | tf_op jit(solution)/shard_map/ppermute | solution.py:783
  (213 shorter events, 75.2 us)
Async XLA Ops:
  4.9 36.2 %copy-start.33 = (s32[256,8]{0,1:T(8,128)S(1)}, s32[256,8]{0,1:T(8,128)}, u32[]{:S(2)}) copy-start(s32[256,8]{0,1:T(8,128)} %param.31) | copy-start | bytes 24580
  9.2 15.8 %collective-permute-start = (bf16[2064,128]{1,0:T(8,128)(2,1)}, bf16[2064,128]{1,0:T(8,128)(2,1)S(1)}, u32[]{:S(2)}, u32[]{:S(2)}) collective-permute-start(bf16[2064,128]{1,0:T(8,128)(2,1)} %get-tuple-element.109.refs_0_.refs_4_), channel_id=1, source_target_pairs={{0,1},{1,2},{2,3},{4,5},{5,6},{6,7},{8,9},{9,10},{10,11},{12,13},{... | collective-permute-start | bytes 1585160 | tf_op jit(solution)/shard_map/ppermute | solution.py:717
  25.1 32.4 %copy-start = (bf16[2064,128]{1,0:T(8,128)(2,1)}, bf16[2064,128]{1,0:T(8,128)(2,1)S(1)}, u32[]{:S(2)}) copy-start(bf16[2064,128]{1,0:T(8,128)(2,1)S(1)} %collective-permute-done.refs_1_.refs_5_) | copy-start | bytes 1585156
  25.1 14.8 %collective-permute-start.1 = (bf16[2064,128]{1,0:T(8,128)(2,1)S(1)}, bf16[2064,128]{1,0:T(8,128)(2,1)S(1)}, u32[]{:S(2)}, u32[]{:S(2)}) collective-permute-start(bf16[2064,128]{1,0:T(8,128)(2,1)S(1)} %collective-permute-done.refs_1_.refs_5_), channel_id=1, source_target_pairs={{0,1},{1,2},{2,3},{4,5},{5,6},{6,7},{8,9},{9,10},{10,11},{12,13},{... | collective-permute-start | bytes 1585160 | tf_op jit(solution)/shard_map/ppermute | solution.py:717
  39.8 17.7 %copy-start.1 = (bf16[2064,128]{1,0:T(8,128)(2,1)}, bf16[2064,128]{1,0:T(8,128)(2,1)S(1)}, u32[]{:S(2)}) copy-start(bf16[2064,128]{1,0:T(8,128)(2,1)S(1)} %collective-permute-done.1.refs_2_.refs_6_) | copy-start | bytes 1585156
  39.8 17.7 %collective-permute-start.2 = (bf16[2064,128]{1,0:T(8,128)(2,1)S(1)}, bf16[2064,128]{1,0:T(8,128)(2,1)S(1)}, u32[]{:S(2)}, u32[]{:S(2)}) collective-permute-start(bf16[2064,128]{1,0:T(8,128)(2,1)S(1)} %collective-permute-done.1.refs_2_.refs_6_), channel_id=1, source_target_pairs={{0,1},{1,2},{2,3},{4,5},{5,6},{6,7},{8,9},{9,10},{10,11},{12,13},{... | collective-permute-start | bytes 1585160 | tf_op jit(solution)/shard_map/ppermute | solution.py:717
  44.5 37.3 %collective-permute-start.12 = (bf16[256,1664]{1,0:T(8,128)(2,1)}, bf16[256,1664]{1,0:T(8,128)(2,1)}, u32[]{:S(2)}, u32[]{:S(2)}) collective-permute-start(bf16[256,1664]{1,0:T(8,128)(2,1)} %extend.1.refs_7_), channel_id=1, source_target_pairs={{0,1},{1,2},{2,3},{4,5},{5,6},{6,7},{8,9},{9,10},{10,11},{12,13},{... | collective-permute-start | bytes 2555912 | tf_op jit(solution)/shard_map/ppermute | solution.py:717
  45.8 37.5 %collective-permute-start.15 = (bf16[256,1664]{1,0:T(8,128)(2,1)}, bf16[256,1664]{1,0:T(8,128)(2,1)}, u32[]{:S(2)}, u32[]{:S(2)}) collective-permute-start(bf16[256,1664]{1,0:T(8,128)(2,1)} %extend.1.refs_7_), channel_id=1, source_target_pairs={{1,0},{2,1},{3,2},{5,4},{6,5},{7,6},{9,8},{10,9},{11,10},{13,12},{... | collective-permute-start | bytes 2555912 | tf_op jit(solution)/shard_map/ppermute | solution.py:721
  58.3 12.3 %copy-start.3 = (bf16[256,1536]{1,0:T(8,128)(2,1)S(1)}, bf16[256,1536]{1,0:T(8,128)(2,1)}, u32[]{:S(2)}) copy-start(bf16[256,1536]{1,0:T(8,128)(2,1)} %tokens_ref.1) | copy-start | bytes 2359300
  74.7 8.3 %copy-start.32 = (f32[4,2,768]{2,1,0:T(2,128)S(1)}, f32[4,2,768]{2,1,0:T(2,128)}, u32[]{:S(2)}) copy-start(f32[4,2,768]{2,1,0:T(2,128)} %get-tuple-element.111) | copy-start | bytes 73732
  74.7 66.1 %copy-start.31 = (bf16[1536,20]{0,1:T(8,128)(2,1)S(1)}, bf16[1536,20]{0,1:T(8,128)(2,1)}, u32[]{:S(2)}) copy-start(bf16[1536,20]{0,1:T(8,128)(2,1)} %param.26) | copy-start | bytes 184324
  75.0 90.3 %copy-start.15 = (bf16[256,1536]{1,0:T(8,128)(2,1)}, bf16[256,1536]{1,0:T(8,128)(2,1)S(1)}, u32[]{:S(2)}) copy-start(bf16[256,1536]{1,0:T(8,128)(2,1)S(1)} %multiply_convert_fusion.1.refs_0_) | copy-start | bytes 2359300
  75.0 29.6 %collective-permute-start.3 = (bf16[256,1536]{1,0:T(8,128)(2,1)S(1)}, bf16[256,1536]{1,0:T(8,128)(2,1)}, u32[]{:S(2)}, u32[]{:S(2)}) collective-permute-start(bf16[256,1536]{1,0:T(8,128)(2,1)S(1)} %multiply_convert_fusion.1.refs_0_), channel_id=1, source_target_pairs={{0,1},{1,2},{2,3},{4,5},{5,6},{6,7},{8,9},{9,10},{10,11},{12,13},{... | collective-permute-start | bytes 2359304 | tf_op jit(solution)/shard_map/ppermute | solution.py:717
  76.3 28.3 %collective-permute-start.4 = (bf16[256,1536]{1,0:T(8,128)(2,1)S(1)}, bf16[256,1536]{1,0:T(8,128)(2,1)}, u32[]{:S(2)}, u32[]{:S(2)}) collective-permute-start(bf16[256,1536]{1,0:T(8,128)(2,1)S(1)} %multiply_convert_fusion.1.refs_0_), channel_id=1, source_target_pairs={{1,0},{2,1},{3,2},{5,4},{6,5},{7,6},{9,8},{10,9},{11,10},{13,12},{... | collective-permute-start | bytes 2359304 | tf_op jit(solution)/shard_map/ppermute | solution.py:721
  81.8 31.9 %collective-permute-start.13 = (bf16[256,1664]{1,0:T(8,128)(2,1)}, bf16[256,1664]{1,0:T(8,128)(2,1)}, u32[]{:S(2)}, u32[]{:S(2)}) collective-permute-start(bf16[256,1664]{1,0:T(8,128)(2,1)} %collective-permute-done.12.refs_8_), channel_id=1, source_target_pairs={{0,1},{1,2},{2,3},{4,5},{5,6},{6,7},{8,9},{9,10},{10,11},{12,13},{... | collective-permute-start | bytes 2555912 | tf_op jit(solution)/shard_map/ppermute | solution.py:717
  83.2 5.5 %collective-permute-start.5 = (f32[1,24]{1,0:T(1,128)S(1)}, f32[1,24]{1,0:T(1,128)S(1)}, u32[]{:S(2)}, u32[]{:S(2)}) collective-permute-start(f32[1,24]{1,0:T(1,128)S(1)} %bitcast.140), channel_id=1, source_target_pairs={{0,4},{4,0},{8,12},{12,8},{16,20},{20,16},{24,28},{28,24},{1,5},{5... | collective-permute-start | bytes 296 | tf_op jit(solution)/shard_map/ppermute | solution.py:796
  83.3 33.9 %collective-permute-start.16 = (bf16[256,1664]{1,0:T(8,128)(2,1)}, bf16[256,1664]{1,0:T(8,128)(2,1)}, u32[]{:S(2)}, u32[]{:S(2)}) collective-permute-start(bf16[256,1664]{1,0:T(8,128)(2,1)} %collective-permute-done.15.refs_11_), channel_id=1, source_target_pairs={{1,0},{2,1},{3,2},{5,4},{6,5},{7,6},{9,8},{10,9},{11,10},{13,12},{... | collective-permute-start | bytes 2555912 | tf_op jit(solution)/shard_map/ppermute | solution.py:721
  88.8 4.0 collective-permute-start.6
  92.8 11.4 %collective-permute-start.7 = (f32[1,24]{1,0:T(1,128)S(1)}, f32[1,24]{1,0:T(1,128)S(1)}, u32[]{:S(2)}, u32[]{:S(2)}) collective-permute-start(f32[1,24]{1,0:T(1,128)S(1)} %max.19), channel_id=1, source_target_pairs={{0,16},{4,20},{8,24},{12,28},{16,0},{20,4},{24,8},{28,12},{1,17},{... | collective-permute-start | bytes 296 | tf_op jit(solution)/shard_map/ppermute | solution.py:796
  104.6 29.4 %collective-permute-start.10 = (bf16[256,1536]{1,0:T(8,128)(2,1)}, bf16[256,1536]{1,0:T(8,128)(2,1)}, u32[]{:S(2)}, u32[]{:S(2)}) collective-permute-start(bf16[256,1536]{1,0:T(8,128)(2,1)} %collective-permute-done.4.refs_4_), channel_id=1, source_target_pairs={{1,0},{2,1},{3,2},{5,4},{6,5},{7,6},{9,8},{10,9},{11,10},{13,12},{... | collective-permute-start | bytes 2359304 | tf_op jit(solution)/shard_map/ppermute | solution.py:721
  106.8 32.5 %collective-permute-start.8 = (bf16[256,1536]{1,0:T(8,128)(2,1)}, bf16[256,1536]{1,0:T(8,128)(2,1)}, u32[]{:S(2)}, u32[]{:S(2)}) collective-permute-start(bf16[256,1536]{1,0:T(8,128)(2,1)} %collective-permute-done.3.refs_1_), channel_id=1, source_target_pairs={{0,1},{1,2},{2,3},{4,5},{5,6},{6,7},{8,9},{9,10},{10,11},{12,13},{... | collective-permute-start | bytes 2359304 | tf_op jit(solution)/shard_map/ppermute | solution.py:717
  113.7 35.1 %collective-permute-start.14 = (bf16[256,1664]{1,0:T(8,128)(2,1)}, bf16[256,1664]{1,0:T(8,128)(2,1)}, u32[]{:S(2)}, u32[]{:S(2)}) collective-permute-start(bf16[256,1664]{1,0:T(8,128)(2,1)} %collective-permute-done.13.refs_9_), channel_id=1, source_target_pairs={{0,1},{1,2},{2,3},{4,5},{5,6},{6,7},{8,9},{9,10},{10,11},{12,13},{... | collective-permute-start | bytes 2555912 | tf_op jit(solution)/shard_map/ppermute | solution.py:717
  117.2 35.1 %collective-permute-start.17 = (bf16[256,1664]{1,0:T(8,128)(2,1)}, bf16[256,1664]{1,0:T(8,128)(2,1)}, u32[]{:S(2)}, u32[]{:S(2)}) collective-permute-start(bf16[256,1664]{1,0:T(8,128)(2,1)} %collective-permute-done.16.refs_12_), channel_id=1, source_target_pairs={{1,0},{2,1},{3,2},{5,4},{6,5},{7,6},{9,8},{10,9},{11,10},{13,12},{... | collective-permute-start | bytes 2555912 | tf_op jit(solution)/shard_map/ppermute | solution.py:721
  134.1 31.3 %collective-permute-start.11 = (bf16[256,1536]{1,0:T(8,128)(2,1)}, bf16[256,1536]{1,0:T(8,128)(2,1)}, u32[]{:S(2)}, u32[]{:S(2)}) collective-permute-start(bf16[256,1536]{1,0:T(8,128)(2,1)} %collective-permute-done.10.refs_5_), channel_id=1, source_target_pairs={{1,0},{2,1},{3,2},{5,4},{6,5},{7,6},{9,8},{10,9},{11,10},{13,12},{... | collective-permute-start | bytes 2359304 | tf_op jit(solution)/shard_map/ppermute | solution.py:721
  139.3 26.0 %collective-permute-start.9 = (bf16[256,1536]{1,0:T(8,128)(2,1)}, bf16[256,1536]{1,0:T(8,128)(2,1)}, u32[]{:S(2)}, u32[]{:S(2)}) collective-permute-start(bf16[256,1536]{1,0:T(8,128)(2,1)} %collective-permute-done.8.refs_2_), channel_id=1, source_target_pairs={{0,1},{1,2},{2,3},{4,5},{5,6},{6,7},{8,9},{9,10},{10,11},{12,13},{... | collective-permute-start | bytes 2359304 | tf_op jit(solution)/shard_map/ppermute | solution.py:717
  142.2 64.7 %copy-start.34 = (s32[4]{0:T(128)}, s32[4]{0:T(128)S(1)}, u32[]{:S(2)}) copy-start(s32[4]{0:T(128)S(1)} %get-tuple-element.288.order_ref) | copy-start | bytes 52
  206.8 74.3 %all-to-all-start = ((bf16[4,256,1536]{2,1,0:T(8,128)(2,1)}), bf16[4,256,1536]{2,1,0:T(8,128)(2,1)}, u32[]{:S(2)}, u32[]{:S(2)}) async-start(bf16[4,256,1536]{2,1,0:T(8,128)(2,1)} %get-tuple-element.118), calls=%async_computation | async-start | bytes 6291456 | tf_op jit(solution)/shard_map/all_to_all | solution.py:928
  233.1 13.4 %collective-permute-start.18 = (bf16[3,5,192,512]{3,2,1,0:T(8,128)(2,1)}, bf16[3,5,192,512]{3,2,1,0:T(8,128)(2,1)}, u32[]{:S(2)}, u32[]{:S(2)}) collective-permute-start(bf16[3,5,192,512]{3,2,1,0:T(8,128)(2,1)} %get-tuple-element.123), channel_id=1, source_target_pairs={{0,4},{4,0},{8,12},{12,8},{16,20},{20,16},{24,28},{28,24},{1,5},{5... | collective-permute-start | bytes 8847368 | tf_op jit(solution)/shard_map/ppermute | solution.py:743
  233.1 13.4 %collective-permute-start.19 = (bf16[3,5,192,512]{3,2,1,0:T(8,128)(2,1)}, bf16[3,5,192,512]{3,2,1,0:T(8,128)(2,1)}, u32[]{:S(2)}, u32[]{:S(2)}) collective-permute-start(bf16[3,5,192,512]{3,2,1,0:T(8,128)(2,1)} %get-tuple-element.124), channel_id=1, source_target_pairs={{0,4},{4,0},{8,12},{12,8},{16,20},{20,16},{24,28},{28,24},{1,5},{5... | collective-permute-start | bytes 8847368 | tf_op jit(solution)/shard_map/ppermute | solution.py:743
  233.6 13.6 %collective-permute-start.20 = (bf16[3,5,192,512]{3,2,1,0:T(8,128)(2,1)}, bf16[3,5,192,512]{3,2,1,0:T(8,128)(2,1)}, u32[]{:S(2)}, u32[]{:S(2)}) collective-permute-start(bf16[3,5,192,512]{3,2,1,0:T(8,128)(2,1)} %get-tuple-element.125), channel_id=1, source_target_pairs={{0,4},{4,0},{8,12},{12,8},{16,20},{20,16},{24,28},{28,24},{1,5},{5... | collective-permute-start | bytes 8847368 | tf_op jit(solution)/shard_map/ppermute | solution.py:743
  233.6 17.8 %collective-permute-start.21 = (bf16[3,5,192,512]{3,2,1,0:T(8,128)(2,1)}, bf16[3,5,192,512]{3,2,1,0:T(8,128)(2,1)}, u32[]{:S(2)}, u32[]{:S(2)}) collective-permute-start(bf16[3,5,192,512]{3,2,1,0:T(8,128)(2,1)} %get-tuple-element.126), channel_id=1, source_target_pairs={{0,4},{4,0},{8,12},{12,8},{16,20},{20,16},{24,28},{28,24},{1,5},{5... | collective-permute-start | bytes 8847368 | tf_op jit(solution)/shard_map/ppermute | solution.py:743
  281.1 71.0 %collective-permute-start.23 = (bf16[2,3,5,192,256]{4,3,2,1,0:T(8,128)(2,1)}, bf16[2,3,5,192,256]{4,3,2,1,0:T(8,128)(2,1)}, u32[]{:S(2)}, u32[]{:S(2)}) collective-permute-start(bf16[2,3,5,192,256]{4,3,2,1,0:T(8,128)(2,1)} %get-tuple-element.132), channel_id=1, source_target_pairs={{0,8},{4,12},{8,0},{12,4},{16,24},{20,28},{24,16},{28,20},{1,9},{5... | collective-permute-start | bytes 8847368 | tf_op jit(solution)/shard_map/ppermute | solution.py:743
  288.4 65.2 %collective-permute-start.24 = (bf16[2,3,5,192,256]{4,3,2,1,0:T(8,128)(2,1)}, bf16[2,3,5,192,256]{4,3,2,1,0:T(8,128)(2,1)}, u32[]{:S(2)}, u32[]{:S(2)}) collective-permute-start(bf16[2,3,5,192,256]{4,3,2,1,0:T(8,128)(2,1)} %get-tuple-element.133), channel_id=1, source_target_pairs={{0,16},{4,20},{8,24},{12,28},{16,0},{20,4},{24,8},{28,12},{1,17},{... | collective-permute-start | bytes 8847368 | tf_op jit(solution)/shard_map/ppermute | solution.py:743
  288.4 47.9 %all-to-all-start.1 = ((bf16[4,256,768]{2,1,0:T(8,128)(2,1)}), bf16[4,256,768]{2,1,0:T(8,128)(2,1)}, u32[]{:S(2)}, u32[]{:S(2)}) async-start(bf16[4,256,768]{2,1,0:T(8,128)(2,1)} %get-tuple-element.134), calls=%async_computation.1 | async-start | bytes 3145728 | tf_op jit(solution)/shard_map/all_to_all | solution.py:937
  322.7 13.6 %collective-permute-start.22 = (bf16[2048,128]{1,0:T(8,128)(2,1)}, bf16[2048,128]{1,0:T(8,128)(2,1)S(1)}, u32[]{:S(2)}, u32[]{:S(2)}) collective-permute-start(bf16[2048,128]{1,0:T(8,128)(2,1)} %get-tuple-element.131), channel_id=1, source_target_pairs={{1,0},{2,1},{3,2},{5,4},{6,5},{7,6},{9,8},{10,9},{11,10},{13,12},{... | collective-permute-start | bytes 1572872 | tf_op jit(solution)/shard_map/ppermute | solution.py:721
  325.2 28.4 %copy-start.29 = (f32[256,1]{1,0:T(8,128)S(1)}, f32[256,1]{1,0:T(8,128)}, u32[]{:S(2)}) copy-start(f32[256,1]{1,0:T(8,128)} %get-tuple-element.153) | copy-start | bytes 3076
  325.2 29.1 %copy-start.24 = (bf16[2048,128]{1,0:T(8,128)(2,1)S(1)}, bf16[2048,128]{1,0:T(8,128)(2,1)}, u32[]{:S(2)}) copy-start(bf16[2048,128]{1,0:T(8,128)(2,1)} %get-tuple-element.141) | copy-start | bytes 1572868
  353.6 8.3 %collective-permute-start.26 = (bf16[4,192,3072]{2,1,0:T(8,128)(2,1)}, bf16[4,192,3072]{2,1,0:T(8,128)(2,1)}, u32[]{:S(2)}, u32[]{:S(2)}) collective-permute-start(bf16[4,192,3072]{2,1,0:T(8,128)(2,1)} %get-tuple-element.143), channel_id=1, source_target_pairs={{0,4},{4,0},{8,12},{12,8},{16,20},{20,16},{24,28},{28,24},{1,5},{5... | collective-permute-start | bytes 14155784 | tf_op jit(solution)/shard_map/ppermute | solution.py:743
  354.5 13.6 %collective-permute-start.25 = (bf16[2048,128]{1,0:T(8,128)(2,1)S(1)}, bf16[2048,128]{1,0:T(8,128)(2,1)S(1)}, u32[]{:S(2)}, u32[]{:S(2)}) collective-permute-start(bf16[2048,128]{1,0:T(8,128)(2,1)S(1)} %add_convert_fusion.11), channel_id=1, source_target_pairs={{1,0},{2,1},{3,2},{5,4},{6,5},{7,6},{9,8},{10,9},{11,10},{13,12},{... | collective-permute-start | bytes 1572872 | tf_op jit(solution)/shard_map/ppermute | solution.py:721
  368.2 15.4 %collective-permute-start.27 = (bf16[2048,128]{1,0:T(8,128)(2,1)S(1)}, bf16[2048,128]{1,0:T(8,128)(2,1)S(1)}, u32[]{:S(2)}, u32[]{:S(2)}) collective-permute-start(bf16[2048,128]{1,0:T(8,128)(2,1)S(1)} %add_convert_fusion.10), channel_id=1, source_target_pairs={{1,0},{2,1},{3,2},{5,4},{6,5},{7,6},{9,8},{10,9},{11,10},{13,12},{... | collective-permute-start | bytes 1572872 | tf_op jit(solution)/shard_map/ppermute | solution.py:721
  374.7 48.0 %collective-permute-start.29 = (bf16[2,192,1536]{2,1,0:T(8,128)(2,1)}, bf16[2,192,1536]{2,1,0:T(8,128)(2,1)}, u32[]{:S(2)}, u32[]{:S(2)}) collective-permute-start(bf16[2,192,1536]{2,1,0:T(8,128)(2,1)} %get-tuple-element.246), channel_id=1, source_target_pairs={{0,16},{4,20},{8,24},{12,28},{16,0},{20,4},{24,8},{28,12},{1,17},{... | collective-permute-start | bytes 3538952 | tf_op jit(solution)/shard_map/ppermute | solution.py:743
  375.0 9.4 %copy-start.17 = (bf16[2,3,5,192,256]{4,3,2,1,0:T(8,128)(2,1)S(1)}, bf16[2,3,5,192,256]{4,3,2,1,0:T(8,128)(2,1)}, u32[]{:S(2)}) copy-start(bf16[2,3,5,192,256]{4,3,2,1,0:T(8,128)(2,1)} %get-tuple-element.166) | copy-start | bytes 8847364
  377.0 45.6 %collective-permute-start.28 = (bf16[2,192,1536]{2,1,0:T(8,128)(2,1)}, bf16[2,192,1536]{2,1,0:T(8,128)(2,1)}, u32[]{:S(2)}, u32[]{:S(2)}) collective-permute-start(bf16[2,192,1536]{2,1,0:T(8,128)(2,1)} %get-tuple-element.248), channel_id=1, source_target_pairs={{0,8},{4,12},{8,0},{12,4},{16,24},{20,28},{24,16},{28,20},{1,9},{5... | collective-permute-start | bytes 3538952 | tf_op jit(solution)/shard_map/ppermute | solution.py:743
  389.0 59.5 %collective-permute-start.33 = (bf16[3,5,192,256]{3,2,1,0:T(8,128)(2,1)}, bf16[3,5,192,256]{3,2,1,0:T(8,128)(2,1)}, u32[]{:S(2)}, u32[]{:S(2)}) collective-permute-start(bf16[3,5,192,256]{3,2,1,0:T(8,128)(2,1)} %get-tuple-element.242), channel_id=1, source_target_pairs={{0,8},{4,12},{8,0},{12,4},{16,24},{20,28},{24,16},{28,20},{1,9},{5... | collective-permute-start | bytes 4423688 | tf_op jit(solution)/shard_map/ppermute | solution.py:743
  394.0 54.5 %collective-permute-start.32 = (bf16[3,5,192,256]{3,2,1,0:T(8,128)(2,1)}, bf16[3,5,192,256]{3,2,1,0:T(8,128)(2,1)}, u32[]{:S(2)}, u32[]{:S(2)}) collective-permute-start(bf16[3,5,192,256]{3,2,1,0:T(8,128)(2,1)} %get-tuple-element.243), channel_id=1, source_target_pairs={{0,16},{4,20},{8,24},{12,28},{16,0},{20,4},{24,8},{28,12},{1,17},{... | collective-permute-start | bytes 4423688 | tf_op jit(solution)/shard_map/ppermute | solution.py:743
  399.8 9.0 %collective-permute-start.40 = (f32[1,24]{1,0:T(1,128)S(1)}, f32[1,24]{1,0:T(1,128)S(1)}, u32[]{:S(2)}, u32[]{:S(2)}) collective-permute-start(f32[1,24]{1,0:T(1,128)S(1)} %copy-done.38), channel_id=1, source_target_pairs={{0,1},{1,0},{2,3},{3,2},{4,5},{5,4},{6,7},{7,6},{8,9},{9,8},{10,11... | collective-permute-start | bytes 296 | tf_op jit(solution)/shard_map/ppermute | solution.py:796
  408.8 8.1 %collective-permute-start.41 = (f32[1,24]{1,0:T(1,128)S(1)}, f32[1,24]{1,0:T(1,128)S(1)}, u32[]{:S(2)}, u32[]{:S(2)}) collective-permute-start(f32[1,24]{1,0:T(1,128)S(1)} %max.21), channel_id=1, source_target_pairs={{0,2},{1,3},{2,0},{3,1},{4,6},{5,7},{6,4},{7,5},{8,10},{9,11},{10,... | collective-permute-start | bytes 296 | tf_op jit(solution)/shard_map/ppermute | solution.py:796
  416.9 63.3 %all-to-all-start.2 = ((bf16[4,256,768]{2,1,0:T(8,128)(2,1)}), bf16[4,256,768]{2,1,0:T(8,128)(2,1)}, u32[]{:S(2)}, u32[]{:S(2)}) async-start(bf16[4,256,768]{2,1,0:T(8,128)(2,1)} %get-tuple-element.180), calls=%async_computation.2 | async-start | bytes 3145728 | tf_op jit(solution)/shard_map/all_to_all | solution.py:964
  424.3 24.2 %collective-permute-start.31 = (bf16[192,1536]{1,0:T(8,128)(2,1)S(1)}, bf16[192,1536]{1,0:T(8,128)(2,1)S(1)}, u32[]{:S(2)}, u32[]{:S(2)}) collective-permute-start(bf16[192,1536]{1,0:T(8,128)(2,1)S(1)} %get-tuple-element.260), channel_id=1, source_target_pairs={{0,8},{4,12},{8,0},{12,4},{16,24},{20,28},{24,16},{28,20},{1,9},{5... | collective-permute-start | bytes 1769480 | tf_op jit(solution)/shard_map/ppermute | solution.py:743
  425.7 22.8 %copy-start.37 = (bf16[4,192,1152]{2,1,0:T(8,128)(2,1)S(1)}, bf16[4,192,1152]{2,1,0:T(8,128)(2,1)}, u32[]{:S(2)}) copy-start(bf16[4,192,1152]{2,1,0:T(8,128)(2,1)} %get-tuple-element.175) | copy-start | bytes 5308420
  427.4 21.1 %collective-permute-start.30 = (bf16[192,1536]{1,0:T(8,128)(2,1)S(1)}, bf16[192,1536]{1,0:T(8,128)(2,1)S(1)}, u32[]{:S(2)}, u32[]{:S(2)}) collective-permute-start(bf16[192,1536]{1,0:T(8,128)(2,1)S(1)} %get-tuple-element.261), channel_id=1, source_target_pairs={{0,16},{4,20},{8,24},{12,28},{16,0},{20,4},{24,8},{28,12},{1,17},{... | collective-permute-start | bytes 1769480 | tf_op jit(solution)/shard_map/ppermute | solution.py:743
  448.6 11.6 %collective-permute-start.37 = (bf16[4,192,1152]{2,1,0:T(8,128)(2,1)S(1)}, bf16[4,192,1152]{2,1,0:T(8,128)(2,1)S(1)}, u32[]{:S(2)}, u32[]{:S(2)}) collective-permute-start(bf16[4,192,1152]{2,1,0:T(8,128)(2,1)S(1)} %copy-done.37), channel_id=1, source_target_pairs={{0,4},{4,0},{8,12},{12,8},{16,20},{20,16},{24,28},{28,24},{1,5},{5... | collective-permute-start | bytes 5308424 | tf_op jit(solution)/shard_map/ppermute | solution.py:743
  451.1 21.3 %collective-permute-start.34 = (bf16[48,3072]{1,0:T(8,128)(2,1)S(1)}, bf16[48,3072]{1,0:T(8,128)(2,1)}, u32[]{:S(2)}, u32[]{:S(2)}) collective-permute-start(bf16[48,3072]{1,0:T(8,128)(2,1)S(1)} %get-tuple-element.269), channel_id=1, source_target_pairs={{0,1},{1,2},{2,3},{3,0},{4,5},{5,6},{6,7},{7,4},{8,9},{9,10},{10,1... | collective-permute-start | bytes 884744 | tf_op jit(solution)/shard_map/ppermute | solution.py:783
  453.6 26.5 %collective-permute-start.35 = (bf16[48,3072]{1,0:T(8,128)(2,1)S(1)}, bf16[48,3072]{1,0:T(8,128)(2,1)}, u32[]{:S(2)}, u32[]{:S(2)}) collective-permute-start(bf16[48,3072]{1,0:T(8,128)(2,1)S(1)} %get-tuple-element.268), channel_id=1, source_target_pairs={{0,2},{1,3},{2,0},{3,1},{4,6},{5,7},{6,4},{7,5},{8,10},{9,11},{10,... | collective-permute-start | bytes 884744 | tf_op jit(solution)/shard_map/ppermute | solution.py:783
  454.5 25.6 %collective-permute-start.36 = (bf16[48,3072]{1,0:T(8,128)(2,1)S(1)}, bf16[48,3072]{1,0:T(8,128)(2,1)}, u32[]{:S(2)}, u32[]{:S(2)}) collective-permute-start(bf16[48,3072]{1,0:T(8,128)(2,1)S(1)} %get-tuple-element.267), channel_id=1, source_target_pairs={{0,3},{1,0},{2,1},{3,2},{4,7},{5,4},{6,5},{7,6},{8,11},{9,8},{10,9... | collective-permute-start | bytes 884744 | tf_op jit(solution)/shard_map/ppermute | solution.py:783
  460.5 11.9 %collective-permute-start.39 = (bf16[2,192,640]{2,1,0:T(8,128)(2,1)S(1)}, bf16[2,192,640]{2,1,0:T(8,128)(2,1)}, u32[]{:S(2)}, u32[]{:S(2)}) collective-permute-start(bf16[2,192,640]{2,1,0:T(8,128)(2,1)S(1)} %get-tuple-element.264), channel_id=1, source_target_pairs={{0,16},{4,20},{8,24},{12,28},{16,0},{20,4},{24,8},{28,12},{1,17},{... | collective-permute-start | bytes 1474568 | tf_op jit(solution)/shard_map/ppermute | solution.py:743
  462.7 19.9 %copy-start.19 = (bf16[2,192,512]{2,1,0:T(8,128)(2,1)}, bf16[2,192,512]{2,1,0:T(8,128)(2,1)S(1)}, u32[]{:S(2)}) copy-start(bf16[2,192,512]{2,1,0:T(8,128)(2,1)S(1)} %get-tuple-element.182) | copy-start | bytes 1179652
  462.7 9.4 %collective-permute-start.38 = (bf16[2,192,512]{2,1,0:T(8,128)(2,1)S(1)}, bf16[2,192,512]{2,1,0:T(8,128)(2,1)S(1)}, u32[]{:S(2)}, u32[]{:S(2)}) collective-permute-start(bf16[2,192,512]{2,1,0:T(8,128)(2,1)S(1)} %get-tuple-element.265), channel_id=1, source_target_pairs={{0,8},{4,12},{8,0},{12,4},{16,24},{20,28},{24,16},{28,20},{1,9},{5... | collective-permute-start | bytes 1179656 | tf_op jit(solution)/shard_map/ppermute | solution.py:743
  472.0 10.5 %copy-start.26 = (bf16[2,192,512]{2,1,0:T(8,128)(2,1)}, bf16[2,192,512]{2,1,0:T(8,128)(2,1)S(1)}, u32[]{:S(2)}) copy-start(bf16[2,192,512]{2,1,0:T(8,128)(2,1)S(1)} %collective-permute-done.38) | copy-start | bytes 1179652
  481.2 7.5 %collective-permute-start.43 = (bf16[192,640]{1,0:T(8,128)(2,1)S(1)}, bf16[192,640]{1,0:T(8,128)(2,1)S(1)}, u32[]{:S(2)}, u32[]{:S(2)}) collective-permute-start(bf16[192,640]{1,0:T(8,128)(2,1)S(1)} %fusion.28), channel_id=1, source_target_pairs={{0,8},{4,12},{8,0},{12,4},{16,24},{20,28},{24,16},{28,20},{1,9},{5... | collective-permute-start | bytes 737288 | tf_op jit(solution)/shard_map/ppermute | solution.py:743
  482.6 6.0 %collective-permute-start.42 = (bf16[192,512]{1,0:T(8,128)(2,1)S(1)}, bf16[192,512]{1,0:T(8,128)(2,1)S(1)}, u32[]{:S(2)}, u32[]{:S(2)}) collective-permute-start(bf16[192,512]{1,0:T(8,128)(2,1)S(1)} %fusion.31), channel_id=1, source_target_pairs={{0,16},{4,20},{8,24},{12,28},{16,0},{20,4},{24,8},{28,12},{1,17},{... | collective-permute-start | bytes 589832 | tf_op jit(solution)/shard_map/ppermute | solution.py:743
  490.1 7.9 %collective-permute-start.44 = (bf16[48,1152]{0,1:T(8,128)(2,1)S(1)}, bf16[48,1152]{0,1:T(8,128)(2,1)S(1)}, u32[]{:S(2)}, u32[]{:S(2)}) collective-permute-start(bf16[48,1152]{0,1:T(8,128)(2,1)S(1)} %bitcast.136), channel_id=1, source_target_pairs={{0,1},{1,2},{2,3},{3,0},{4,5},{5,6},{6,7},{7,4},{8,9},{9,10},{10,1... | collective-permute-start | bytes 331784 | tf_op jit(solution)/shard_map/ppermute | solution.py:783
  490.5 27.3 %collective-permute-start.45 = (bf16[48,1152]{0,1:T(8,128)(2,1)S(1)}, bf16[48,1152]{0,1:T(8,128)(2,1)S(1)}, u32[]{:S(2)}, u32[]{:S(2)}) collective-permute-start(bf16[48,1152]{0,1:T(8,128)(2,1)S(1)} %bitcast.137), channel_id=1, source_target_pairs={{0,2},{1,3},{2,0},{3,1},{4,6},{5,7},{6,4},{7,5},{8,10},{9,11},{10,... | collective-permute-start | bytes 331784 | tf_op jit(solution)/shard_map/ppermute | solution.py:783
  493.0 24.8 %collective-permute-start.46 = (bf16[48,1152]{0,1:T(8,128)(2,1)S(1)}, bf16[48,1152]{0,1:T(8,128)(2,1)S(1)}, u32[]{:S(2)}, u32[]{:S(2)}) collective-permute-start(bf16[48,1152]{0,1:T(8,128)(2,1)S(1)} %bitcast.138), channel_id=1, source_target_pairs={{0,3},{1,0},{2,1},{3,2},{4,7},{5,4},{6,5},{7,6},{8,11},{9,8},{10,9... | collective-permute-start | bytes 331784 | tf_op jit(solution)/shard_map/ppermute | solution.py:783
  (25 other events, 86.0 us)
